TPU v7x, 32 devices: a whole 2x2x4 slice. The times are simulated.
32 devices in a mesh: chan: 8 (over y, x, core), batch: 4 (over z).
Axes of the slice: x: 2, y: 2, z: 4, core: 2. Of those that a mesh axis runs over, the one named last changes fastest.
Arguments:
- images: bfloat16 [256, 2, 13, 13, 384], P(('batch', 'chan')), may hold values from -6 to 6
- conv_weight: float32 [2, 3, 3, 384, 256], P(None, None, None, None, 'chan'), may hold values from -0.109375 to 0.109375
- conv_bias: float32 [2, 256], P(None, 'chan'), may hold values from -3 to 3
- stitch_conv: float32 [2, 2, 256], P(None, None, 'chan'), may hold values from 0.1 to 1
- fc_weight: float32 [2, 9216, 4096], P(None, 'batch', 'chan'), may hold values from -0.0625 to 0.0625
- fc_bias: float32 [2, 4096], P(None, 'chan'), may hold values from -3 to 3
- stitch_fc: float32 [2, 2, 4096], P(None, None, 'chan'), may hold values from 0.1 to 1
- conv_moment: float32 [2, 3, 3, 384, 256], P(None, None, None, None, 'chan'), may hold values from -6 to 6
- bias_moment: float32 [2, 256], P(None, 'chan'), may hold values from -6 to 6
- stitch_conv_moment: float32 [2, 2, 256], P(None, None, 'chan'), may hold values from -6 to 6
- fc_moment: float32 [2, 9216, 4096], P(None, 'batch', 'chan'), may hold values from -6 to 6
- fc_bias_moment: float32 [2, 4096], P(None, 'chan'), may hold values from -6 to 6
- stitch_fc_moment: float32 [2, 2, 4096], P(None, None, 'chan'), may hold values from -6 to 6
- cotangent: bfloat16 [256, 2, 4096], P('batch', None, 'chan'), may hold values from -6 to 6
- task_mask: int32 [256, 2], P('batch'), may hold values 0 or 1
Outputs:
- features_out: bfloat16 [256, 2, 4096], P('batch', None, 'chan')
- images_grad: bfloat16 [256, 2, 13, 13, 384], P(('batch', 'chan'))
- new_conv_weight: float32 [2, 3, 3, 384, 256], P(None, None, None, None, 'chan')
- new_conv_bias: float32 [2, 256], P(None, 'chan')
- new_stitch_conv: float32 [2, 2, 256], P(None, None, 'chan')
- new_fc_weight: float32 [2, 9216, 4096], P(None, 'batch', 'chan')
- new_fc_bias: float32 [2, 4096], P(None, 'chan')
- new_stitch_fc: float32 [2, 2, 4096], P(None, None, 'chan')
- new_conv_moment: float32 [2, 3, 3, 384, 256], P(None, None, None, None, 'chan')
- new_bias_moment: float32 [2, 256], P(None, 'chan')
- new_stitch_conv_moment: float32 [2, 2, 256], P(None, None, 'chan')
- new_fc_moment: float32 [2, 9216, 4096], P(None, 'batch', 'chan')
- new_fc_bias_moment: float32 [2, 4096], P(None, 'chan')
- new_stitch_fc_moment: float32 [2, 2, 4096], P(None, None, 'chan')
All inputs are finite; a program needn't handle non-finite values. No bound on the sum of `task_mask` on one device may be relied on, other than what follows from the above.
Results may differ from a plain program's by a relative error of at most 0.015.
Values may be sent and summed in bfloat16 or wider, within the bound.
No kernel may reach another device: no remote copies, remote signals or barrier semaphores. Data moves between devices by JAX's collectives and lax.ppermute only.
A program may use at most 128 MiB of HBM per device.

v0:
```python
import functools

import jax
import jax.numpy as jnp
from jax import lax
from jax.experimental import pallas as pl
from jax.experimental.pallas import tpu as pltpu
from jax.sharding import PartitionSpec as P

MOMENTUM = 0.9
LEARN_RATE = 0.002
BIAS_RATE = 0.02
STITCH_RATE = 0.02
LOW = jnp.bfloat16
WIDE = jnp.float32
TAPS = 9
CELLS = 36
EXTRA = 16
LANES = 128
WHOLE = pl.BlockSpec(memory_space=pltpu.VMEM)
SCALARS = pl.BlockSpec(memory_space=pltpu.SMEM)
NN = (((1,), (0,)), ((), ()))
NT = (((1,), (1,)), ((), ()))
TN = (((0,), (0,)), ((), ()))


def like(shape, dtype):
    return jax.ShapeDtypeStruct(shape, dtype)


def dot(a, b, dims):
    return lax.dot_general(a, b, dims, preferred_element_type=WIDE)


def trade(value, axis, bit):
    size = lax.axis_size(axis)
    return lax.ppermute(value, axis, [(i, i ^ bit) for i in range(size)])


def gather_chips(first, second, chips):
    if chips == 4:
        second_x = trade(second, "chan", 2)
        first_y = trade(first, "chan", 4)
        first_x = trade(first, "chan", 2)
        second_y = trade(second, "chan", 4)
        first_d = trade(first_y, "chan", 2)
        second_d = trade(second_x, "chan", 4)
        return [(first, second), (first_x, second_x), (first_y, second_y), (first_d, second_d)]
    return [(first, second)] + [
        (trade(first, "chan", 2 * j), trade(second, "chan", 2 * j)) for j in range(1, chips)
    ]


def add_low(a, b):
    return (a.astype(WIDE) + b.astype(WIDE)).astype(LOW)


def scatter_chips(parts, chips):
    if chips == 4:
        from_x = trade(parts[3][0], "chan", 2)
        from_y = trade(parts[3][1], "chan", 4)
        first_x = trade(parts[1][0], "chan", 2)
        second_y = trade(parts[2][1], "chan", 4)
        first_y = trade(add_low(parts[2][0], from_x), "chan", 4)
        second_x = trade(add_low(parts[1][1], from_y), "chan", 2)
        return (parts[0][0], first_x, first_y), (parts[0][1], second_x, second_y)
    got = [(trade(parts[j][0], "chan", 2 * j), trade(parts[j][1], "chan", 2 * j)) for j in range(1, chips)]
    return (
        (parts[0][0],) + tuple(pair[0] for pair in got),
        (parts[0][1],) + tuple(pair[1] for pair in got),
    )


def total(values):
    out = values[0].astype(WIDE)
    for value in values[1:]:
        out = out + value.astype(WIDE)
    return out


def exchange_planes(parts):
    got = {k: trade(parts[k], "batch", k) for k in range(len(parts) - 1, 0, -1)}
    return [parts[0]] + [got[k] for k in range(1, len(parts))]


def gate_of(value):
    return 1.0 / (1.0 + jnp.exp(-value))


def silu_and_slope(value):
    gate = gate_of(value)
    act = value * gate
    return act, gate + act * (1.0 - gate)


def lane_place(width):
    return lax.broadcasted_iota(jnp.int32, (1, LANES), 1) // width


def shift_slots(value, width, source, target):
    if source == target:
        return value
    return pltpu.roll(value, ((target - source) * width) % LANES, 1)


def fc_prepare(fc_weight, core):
    towers, rows, units = fc_weight.shape
    width = rows // CELLS

    def kernel(core_ref, w_ref, o_ref):
        for cell in range(CELLS):
            o_ref[0, pl.ds(cell * width, width), :] = w_ref[
                0, pl.ds(cell, width, stride=CELLS), :
            ].astype(LOW)

    return pl.pallas_call(
        kernel,
        grid_spec=pltpu.PrefetchScalarGridSpec(
            num_scalar_prefetch=1,
            grid=(towers, units // LANES),
            in_specs=[pl.BlockSpec((1, rows, LANES), lambda i, j, core: (core[0] ^ i, 0, j))],
            out_specs=pl.BlockSpec((1, rows, LANES), lambda i, j, core: (i, 0, j)),
        ),
        out_shape=like(fc_weight.shape, LOW),
        compiler_params=pltpu.CompilerParams(vmem_limit_bytes=8 << 20),
        cost_estimate=pl.CostEstimate(flops=0, bytes_accessed=6 * fc_weight.size, transcendentals=0),
    )(core, fc_weight)


def conv_forward(images, parts, core, chip):
    high, wide, group, width_in = images.shape
    side = high - 2
    count = len(parts)
    shard = (parts[0].shape[0] - EXTRA) // TAPS
    full = shard * count
    slots = LANES // shard

    def kernel(core_ref, chip_ref, x_ref, *refs):
        pieces = refs[:count]
        pooled_ref, slope_ref, small_ref = refs[count : count + 3]
        joined, weights, acc, act = refs[count + 3 :]
        lane = lax.broadcasted_iota(jnp.int32, (EXTRA, LANES), 1) // shard
        smalls = [jnp.zeros((EXTRA, LANES), WIDE) for _ in range(full // LANES)]
        for j in range(count // 2):
            for r in range(2):
                piece = pieces[2 * j + r]
                where = (chip_ref[0] ^ j) * 2 + (core_ref[0] ^ r)
                at = pl.ds(pl.multiple_of(where * shard, shard), shard)
                for tap in range(TAPS):
                    weights[tap // 3, at, (tap % 3) * width_in : (tap % 3 + 1) * width_in] = piece[
                        tap * shard : (tap + 1) * shard, :
                    ]
                row = piece[TAPS * shard :, :LANES].astype(WIDE)
                copies = row
                for s in range(1, slots):
                    copies = copies + pltpu.roll(row, s * shard, 1)
                for v in range(len(smalls)):
                    smalls[v] = jnp.where(lane + v * slots == where, copies, smalls[v])
        for v, value in enumerate(smalls):
            small_ref[:, v * LANES : (v + 1) * LANES] = value
        for right in range(3):
            joined[:, :, :, right * width_in : (right + 1) * width_in] = x_ref[:, right : right + side]
        for down in range(3):
            part = dot(
                joined[down : down + side].reshape(side * side * group, 3 * width_in),
                weights[down],
                NT,
            )
            if down == 0:
                acc[...] = part
            else:
                acc[...] += part
        bias = small_ref[0:1, :]
        line = side * group
        for h in range(side):
            value, slope = silu_and_slope(acc[h * line : (h + 1) * line, :] + bias)
            slope_ref[h] = slope.reshape(side, group, full).astype(LOW)
            act[h] = value.reshape(side, group, full)
        for r in range(6):
            rows = act[2 * r] + act[2 * r + 1] + act[2 * r + 2]
            for c in range(6):
                pooled_ref[6 * r + c] = (rows[2 * c] + rows[2 * c + 1] + rows[2 * c + 2]) * (1.0 / 9.0)

    area = side * side * group
    return pl.pallas_call(
        kernel,
        in_specs=[SCALARS] * 2 + [WHOLE] * (1 + count),
        out_specs=[WHOLE] * 3,
        out_shape=[
            like((CELLS, group, full), WIDE),
            like((side, side, group, full), LOW),
            like((EXTRA, full), WIDE),
        ],
        scratch_shapes=[
            pltpu.VMEM((high, side, group, 3 * width_in), LOW),
            pltpu.VMEM((3, full, 3 * width_in), LOW),
            pltpu.VMEM((area, full), WIDE),
            pltpu.VMEM((side, side, group, full), WIDE),
        ],
        compiler_params=pltpu.CompilerParams(vmem_limit_bytes=28 << 20),
        cost_estimate=pl.CostEstimate(
            flops=2 * area * TAPS * width_in * full,
            bytes_accessed=2 * images.size + 2 * area * full,
            transcendentals=0,
        ),
    )(core, chip, images, *parts)


def mix_pieces(pooled, other, small, plane, planes):
    cells, group, full = pooled.shape
    width = full // planes
    per = LANES // width

    def kernel(plane_ref, a_ref, b_ref, small_ref, *refs):
        outs, held = refs[:planes], refs[planes]
        place = lane_place(width)
        one, two = small_ref[1:2, :], small_ref[2:3, :]
        for start in range(0, cells, per):
            mixed = [
                one * a_ref[start + i] + two * b_ref[start + i] for i in range(per)
            ]
            for p in range(planes):
                column, source = divmod(p * width, LANES)
                out = None
                for i in range(per):
                    moved = shift_slots(
                        mixed[i][:, column * LANES : (column + 1) * LANES], width, source // width, i
                    )
                    out = moved if out is None else jnp.where(place == i, moved, out)
                held[p, :, start * width : (start + per) * width] = out.astype(LOW)
        for k in range(planes):
            outs[k][...] = held[plane_ref[0] ^ k]

    rows = cells * width
    return pl.pallas_call(
        kernel,
        in_specs=[SCALARS] + [WHOLE] * 3,
        out_specs=[WHOLE] * planes,
        out_shape=[like((group, rows), LOW)] * planes,
        scratch_shapes=[pltpu.VMEM((planes, group, rows), LOW)],
        compiler_params=pltpu.CompilerParams(vmem_limit_bytes=8 << 20),
        cost_estimate=pl.CostEstimate(flops=4 * pooled.size, bytes_accessed=8 * pooled.size, transcendentals=0),
    )(plane, pooled, other, small)


def fc_forward(gathered, weights, chip, chips, planes):
    half, group, rows = gathered[0].shape
    units = weights[0].shape[-1]
    count = 2 * chips
    block = chips * group

    def kernel(chip_ref, *refs):
        pieces, (own, cross) = refs[:count], refs[count : count + 2]
        rows_ref, outs = refs[count + 2], refs[count + 3 :]
        for j in range(chips):
            for h in range(2):
                for i in range(half):
                    start = ((h * half + i) * chips + (chip_ref[0] ^ j)) * group
                    rows_ref[pl.ds(pl.multiple_of(start, group), group), :] = pieces[2 * j + h][i]
        for n, weight in enumerate((own, cross)):
            part = dot(rows_ref[...], weight[...], NN)
            for k in range(planes):
                outs[k][:, n * units : (n + 1) * units] = part[k * block : (k + 1) * block].astype(
                    outs[k].dtype
                )

    n_images = planes * block
    return pl.pallas_call(
        kernel,
        in_specs=[SCALARS] + [WHOLE] * (count + 2),
        out_specs=[WHOLE] * (1 + planes),
        out_shape=[like((n_images, rows), LOW)]
        + [like((block, 2 * units), LOW if k else WIDE) for k in range(planes)],
        compiler_params=pltpu.CompilerParams(vmem_limit_bytes=16 << 20),
        cost_estimate=pl.CostEstimate(
            flops=4 * n_images * rows * units, bytes_accessed=4 * rows * units, transcendentals=0
        ),
    )(chip, *gathered, *weights)


def fc_backward(grads, crossed, weights, chip, chips, planes):
    _, block, units = grads[0].shape
    rows = weights[0].shape[0]
    group = block // chips
    half = planes // 2
    n_images = planes * block

    def kernel(chip_ref, *refs):
        pieces, got = refs[:planes], refs[planes]
        own, cross = refs[planes + 1 : planes + 3]
        outs = refs[planes + 3 : planes + 3 + 2 * chips]
        held_own, held_cross, held = refs[planes + 3 + 2 * chips :]
        for k in range(planes):
            held_own[pl.ds(k * block, block), :] = pieces[k][0]
            held_cross[pl.ds(k * block, block), :] = got[k]
        step = rows // 3
        for s in range(3):
            at = pl.ds(s * step, step)
            value = dot(held_own[...], own[at, :], NT) + dot(held_cross[...], cross[at, :], NT)
            held[:, at] = value.astype(LOW)
        for j in range(chips):
            for h in range(2):
                for i in range(half):
                    start = ((h * half + i) * chips + (chip_ref[0] ^ j)) * group
                    outs[2 * j + h][i] = held[pl.ds(pl.multiple_of(start, group), group), :]

    return pl.pallas_call(
        kernel,
        in_specs=[SCALARS] + [WHOLE] * (planes + 3),
        out_specs=[WHOLE] * (2 * chips),
        out_shape=[like((half, group, rows), LOW)] * (2 * chips),
        scratch_shapes=[
            pltpu.VMEM((n_images, units), LOW),
            pltpu.VMEM((n_images, units), LOW),
            pltpu.VMEM((n_images, rows), LOW),
        ],
        compiler_params=pltpu.CompilerParams(vmem_limit_bytes=20 << 20),
        cost_estimate=pl.CostEstimate(
            flops=4 * n_images * rows * units, bytes_accessed=4 * rows * units, transcendentals=0
        ),
    )(chip, *grads, crossed, *weights)


def conv_backward(own, other, pooled, pooled_other, slope, images, small, core, chip, plane):
    planes = len(own)
    cells, group, full = pooled.shape
    high, _, _, width_in = images.shape
    side = high - 2
    width = full // planes
    per = LANES // width
    columns = full // LANES
    shards = lax.axis_size("chan")
    shard = full // shards
    slots = LANES // shard
    area = side * side * group

    def covering(h):
        return [r for r in range(6) if 2 * r <= h <= 2 * r + 2]

    def kernel(core_ref, chip_ref, plane_ref, *refs):
        own_refs, other_ref = refs[:planes], refs[planes]
        a_ref, b_ref, slope_ref, x_ref, small_ref = refs[planes + 1 : planes + 6]
        outs = refs[planes + 6 : planes + 6 + shards]
        grad_ref = refs[planes + 6 + shards]
        flat, pool_grad, turned, taps, smalls = refs[planes + 7 + shards :]
        place = lane_place(width)
        for k in range(planes):
            flat[0, plane_ref[0] ^ k] = own_refs[k][...].astype(WIDE)
            flat[1, plane_ref[0] ^ k] = other_ref[k].astype(WIDE)
        one, back = small_ref[1:2, :] * (1.0 / 9.0), small_ref[3:4, :] * (1.0 / 9.0)
        sum_one = jnp.zeros((group, full), WIDE)
        sum_two = jnp.zeros((group, full), WIDE)
        for cell in range(cells):
            column, source = divmod(cell * width, LANES)
            both = []
            for t in range(2):
                blocks = []
                for v in range(columns):
                    out = None
                    for i in range(per):
                        piece = flat[t, v * per + i, :, column * LANES : (column + 1) * LANES]
                        moved = shift_slots(piece, width, source // width, i)
                        out = moved if out is None else jnp.where(place == i, moved, out)
                    blocks.append(out)
                both.append(jnp.concatenate(blocks, axis=1))
            sum_one += both[0] * a_ref[cell]
            sum_two += both[0] * b_ref[cell]
            pool_grad[cell] = one * both[0] + back * both[1]
        sum_bias = jnp.zeros((group, full), WIDE)
        for h in range(side):
            line = [sum(pool_grad[6 * r + c] for r in covering(h)) for c in range(6)]
            for w in range(side):
                value = sum(line[c] for c in covering(w))
                value = (value * slope_ref[h, w].astype(WIDE)).astype(LOW)
                grad_ref[h, w] = value
                sum_bias += value.astype(WIDE)
        turned[...] = grad_ref[...].reshape(area, full).T
        for tap in range(TAPS):
            window = x_ref[tap // 3 : tap // 3 + side, tap % 3 : tap % 3 + side]
            taps[tap] = dot(turned[...], window.reshape(area, width_in), NN).astype(LOW)
        sums = [jnp.sum(value, axis=0, keepdims=True) for value in (sum_bias, sum_one, sum_two)]
        sums = jnp.concatenate(sums + [jnp.zeros((EXTRA - 3, full), WIDE)], axis=0)
        for v in range(columns):
            smalls[v] = sums[:, v * LANES : (v + 1) * LANES]
        lane = lax.broadcasted_iota(jnp.int32, (EXTRA, LANES), 1)
        for j in range(shards // 2):
            for r in range(2):
                where = (chip_ref[0] ^ j) * 2 + (core_ref[0] ^ r)
                at = pl.ds(pl.multiple_of(where * shard, shard), shard)
                out = outs[2 * j + r]
                for tap in range(TAPS):
                    out[tap * shard : (tap + 1) * shard, :] = taps[tap, at, :]
                row = smalls[where // slots]
                value = jnp.zeros((EXTRA, LANES), WIDE)
                for s in range(slots):
                    moved = row if s == 0 else pltpu.roll(row, LANES - s * shard, 1)
                    value = jnp.where(where % slots == s, moved, value)
                out[TAPS * shard :, :] = jnp.zeros((EXTRA, width_in), LOW)
                out[TAPS * shard :, :LANES] = jnp.where(lane < shard, value, 0.0).astype(LOW)

    return pl.pallas_call(
        kernel,
        in_specs=[SCALARS] * 3 + [WHOLE] * (planes + 6),
        out_specs=[WHOLE] * (shards + 1),
        out_shape=[like((TAPS * shard + EXTRA, width_in), LOW)] * shards
        + [like((side, side, group, full), LOW)],
        scratch_shapes=[
            pltpu.VMEM((2, planes, group, cells * width), WIDE),
            pltpu.VMEM((cells, group, full), WIDE),
            pltpu.VMEM((full, area), LOW),
            pltpu.VMEM((TAPS, full, width_in), LOW),
            pltpu.VMEM((columns, EXTRA, LANES), WIDE),
        ],
        compiler_params=pltpu.CompilerParams(vmem_limit_bytes=28 << 20),
        cost_estimate=pl.CostEstimate(
            flops=2 * area * TAPS * width_in * full,
            bytes_accessed=2 * images.size + 6 * area * full,
            transcendentals=0,
        ),
    )(core, chip, plane, *own, other, pooled, pooled_other, slope, images, small)


def fc_update(weight, moment, rows, grads, core, which, previous):
    towers, depth, units = weight.shape
    width = depth // CELLS
    n_images = rows.shape[0]
    planes = len(grads)
    block = n_images // planes

    def kernel(core_ref, w_ref, m_ref, rows_ref, *refs):
        grad_refs = refs[:planes]
        new_w, new_m, product, joined = refs[-4:]
        for k in range(planes):
            joined[pl.ds(k * block, block), :] = grad_refs[k][0]
        product[...] = dot(rows_ref[...], joined[...], TN)
        for cell in range(CELLS):
            at = pl.ds(cell, width, stride=CELLS)
            fresh = MOMENTUM * m_ref[0, at, :] + product[pl.ds(cell * width, width), :]
            new_m[0, at, :] = fresh
            new_w[0, at, :] = w_ref[0, at, :] - LEARN_RATE * fresh

    big = pl.BlockSpec((1, depth, LANES), lambda j, core: (core[0] ^ which, 0, j))
    grad_spec = pl.BlockSpec((1, block, LANES), lambda j, core: (which, 0, j))
    extra = [] if previous is None else list(previous)
    return pl.pallas_call(
        kernel,
        grid_spec=pltpu.PrefetchScalarGridSpec(
            num_scalar_prefetch=1,
            grid=(units // LANES,),
            in_specs=[big, big, pl.BlockSpec((n_images, depth), lambda j, core: (0, 0))]
            + [grad_spec] * planes
            + [pl.BlockSpec(memory_space=pl.ANY)] * len(extra),
            out_specs=[big, big],
            scratch_shapes=[pltpu.VMEM((depth, LANES), WIDE), pltpu.VMEM((n_images, LANES), LOW)],
        ),
        out_shape=[like(weight.shape, WIDE)] * 2,
        input_output_aliases={} if previous is None else {4 + planes: 0, 5 + planes: 1},
        compiler_params=pltpu.CompilerParams(vmem_limit_bytes=20 << 20),
        cost_estimate=pl.CostEstimate(
            flops=2 * n_images * depth * units, bytes_accessed=16 * depth * units, transcendentals=0
        ),
    )(core, weight, moment, rows, *grads, *extra)


def reorder(parts, place):
    bit = 1
    while bit < len(parts):
        flip = (place & bit) != 0
        parts = [
            jax.tree.map(lambda a, b: jnp.where(flip, b, a), parts[j], parts[j ^ bit])
            for j in range(len(parts))
        ]
        bit *= 2
    return parts


def pick(stacked, place, count):
    return [lax.dynamic_index_in_dim(stacked, place ^ j, 0, keepdims=False) for j in range(count)]


def pool(values):
    rows = values[0:11:2] + values[1:12:2] + values[2:13:2]
    return (rows[:, 0:11:2] + rows[:, 1:12:2] + rows[:, 2:13:2]) * (1.0 / 9.0)


def spread(values, axis):
    values = jnp.moveaxis(values, axis, 0)
    zero = jnp.zeros_like(values[:1])
    even = jnp.concatenate([values, zero]) + jnp.concatenate([zero, values])
    inter = jnp.stack([even[:-1], values], axis=1).reshape((12,) + values.shape[1:])
    return jnp.moveaxis(jnp.concatenate([inter, even[-1:]]), 0, axis)


def any_mesh(
    images,
    conv_weight,
    conv_bias,
    stitch_conv,
    fc_weight,
    fc_bias,
    stitch_fc,
    conv_moment,
    bias_moment,
    stitch_conv_moment,
    fc_moment,
    fc_bias_moment,
    stitch_fc_moment,
    cotangent,
    task_mask,
):
    chan_size, planes = lax.axis_size("chan"), lax.axis_size("batch")
    chips = chan_size // 2
    me, plane = lax.axis_index("chan"), lax.axis_index("batch")
    core, chip = me % 2, me // 2
    swap = lambda value: trade(value, "chan", 1)
    mine = lambda a, b: jnp.where(core == 0, a, b)
    per_core, side, width_in = images.shape[0], images.shape[2], images.shape[-1]
    chan_width = conv_weight.shape[-1]
    full_chan = chan_width * chan_size
    units = fc_weight.shape[-1]
    rows = fc_weight.shape[1]
    cells = 36
    plane_chan = rows // cells
    group = 2 * per_core

    kernel_rows = jnp.transpose(conv_weight, (0, 1, 2, 4, 3)).astype(LOW)
    kernel_rows = kernel_rows.reshape(2, 9 * chan_width, width_in)
    cross = stitch_conv[:, ::-1]
    small = jnp.stack(
        [
            conv_bias,
            jnp.stack([stitch_conv[0, 0], stitch_conv[1, 1]]),
            jnp.stack([stitch_conv[0, 1], stitch_conv[1, 0]]),
            jnp.stack([stitch_conv[1, 0], stitch_conv[0, 1]]),
        ],
        axis=1,
    ).astype(LOW)
    small = jnp.pad(small, ((0, 0), (0, 12), (0, width_in - chan_width)))
    kernel_rows = jnp.concatenate([kernel_rows, small], axis=1)
    keep = mine(kernel_rows[0], kernel_rows[1])
    got = swap(mine(kernel_rows[1], kernel_rows[0]))
    halves = mine(keep, got), mine(got, keep)
    kernel_parts = gather_chips(halves[0], halves[1], chips)

    keep = mine(images[:, 0], images[:, 1])
    got = swap(mine(images[:, 1], images[:, 0]))
    tower_images = jnp.concatenate([mine(keep, got), mine(got, keep)], axis=0)
    tower_images = jnp.transpose(tower_images, (1, 2, 0, 3))

    fc_low = fc_weight.astype(LOW).reshape(2, plane_chan, cells, units)
    fc_low = jnp.swapaxes(fc_low, 1, 2).reshape(2, rows, units)
    fc_keep = mine(fc_low[0], fc_low[1])
    fc_got = swap(mine(fc_low[1], fc_low[0]))
    fc_halves = mine(fc_keep, fc_got), mine(fc_got, fc_keep)

    ordered = reorder(kernel_parts, chip)
    kernel = jnp.concatenate(
        [half[: 9 * chan_width].reshape(9, chan_width, width_in) for pair in ordered for half in pair],
        axis=1,
    )
    small_all = jnp.concatenate(
        [half[9 * chan_width :, :chan_width] for pair in ordered for half in pair], axis=1
    ).astype(WIDE)
    bias_all, self_mix, cross_mix, back_mix = (small_all[i] for i in range(4))

    conv_out = lax.conv_general_dilated(
        tower_images,
        kernel.reshape(3, 3, full_chan, width_in),
        (1, 1),
        "SAME",
        dimension_numbers=("HWNC", "HWOI", "HWNC"),
        preferred_element_type=WIDE,
    )
    act, slope = silu_and_slope(conv_out + bias_all)
    pooled = pool(act)
    pooled_other = swap(pooled)
    mixed = (self_mix * pooled + cross_mix * pooled_other).astype(LOW)
    mixed = mixed.reshape(cells, group, planes, plane_chan)
    pieces = jnp.transpose(mixed, (2, 1, 0, 3)).reshape(planes, group, rows)
    got = exchange_planes(pick(pieces, plane, planes))
    half = planes // 2
    gathered = reorder(
        gather_chips(jnp.stack(got[:half]), jnp.stack(got[half:]), chips), chip
    )
    tower_rows = jnp.concatenate(
        [jnp.stack([pair[h] for pair in gathered], axis=1) for h in range(2)], axis=0
    )
    tower_rows = tower_rows.reshape(planes * chips * group, rows)
    other_rows = swap(tower_rows)

    fc_tower = jnp.concatenate(fc_halves, axis=1)
    partial = jnp.dot(tower_rows, fc_tower, preferred_element_type=WIDE).astype(LOW)
    partial = partial.reshape(planes, chips * group, 2 * units)
    fc_sum = total(exchange_planes([partial[k] for k in range(planes)]))
    fc_keep = mine(fc_sum[:, :units], fc_sum[:, units:])
    fc_got = swap(mine(fc_sum[:, units:], fc_sum[:, :units]))
    fc_out = [mine(fc_keep, fc_got) + fc_bias[0], mine(fc_got, fc_keep) + fc_bias[1]]

    acts, slopes = zip(*[silu_and_slope(value) for value in fc_out])
    features_out = jnp.stack(
        [stitch_fc[t, 0] * acts[0] + stitch_fc[t, 1] * acts[1] for t in range(2)], axis=1
    ).astype(LOW)
    out_grad = [
        cotangent[:, t].astype(WIDE) * task_mask[:, t].astype(WIDE)[:, None] for t in range(2)
    ]
    stitch_fc_grad = jnp.stack(
        [jnp.stack([jnp.sum(out_grad[t] * acts[s], axis=0) for s in range(2)]) for t in range(2)]
    )
    grad_low = jnp.stack(
        [
            (slopes[s] * (stitch_fc[0, s] * out_grad[0] + stitch_fc[1, s] * out_grad[1])).astype(LOW)
            for s in range(2)
        ]
    )
    grad_all = exchange_planes([grad_low] * planes)
    grad_all = jnp.stack(grad_all, axis=1).reshape(2, planes * chips * group, units)
    grad_keep = mine(grad_all[0], grad_all[1])
    grad_got = swap(mine(grad_all[1], grad_all[0]))
    grad_tower = jnp.concatenate([mine(grad_keep, grad_got), mine(grad_got, grad_keep)], axis=1)

    flat_grad = lax.dot_general(
        grad_tower, fc_tower, (((1,), (1,)), ((), ())), preferred_element_type=WIDE
    ).astype(LOW)
    flat_grad = flat_grad.reshape(2, half, chips, group, rows)
    by_chip = reorder([(flat_grad[0, :, m], flat_grad[1, :, m]) for m in range(chips)], chip)
    first, second = scatter_chips(by_chip, chips)
    sums = jnp.concatenate([total(first), total(second)]).astype(LOW)
    got = reorder(exchange_planes([sums[k] for k in range(planes)]), plane)
    mixed_grad = jnp.stack(got)
    mixed_grad_other = swap(mixed_grad)

    def unflatten(value):
        value = value.astype(WIDE).reshape(planes, group, cells, plane_chan)
        return jnp.transpose(value, (2, 1, 0, 3)).reshape(6, 6, group, full_chan)

    own_grad, other_grad = unflatten(mixed_grad), unflatten(mixed_grad_other)
    self_stitch = jnp.sum(own_grad * pooled, axis=(0, 1, 2))
    cross_stitch = jnp.sum(own_grad * pooled_other, axis=(0, 1, 2))
    pooled_grad = (self_mix * own_grad + back_mix * other_grad) * (1.0 / 9.0)
    conv_grad = (slope * spread(spread(pooled_grad, 0), 1)).astype(LOW)
    bias_grad = jnp.sum(conv_grad.astype(WIDE), axis=(0, 1, 2))

    padded = jnp.pad(tower_images, ((1, 1), (1, 1), (0, 0), (0, 0)))
    taps = []
    for down in range(3):
        for right in range(3):
            window = padded[down : down + side, right : right + side]
            taps.append(
                lax.dot_general(
                    conv_grad.reshape(-1, full_chan),
                    window.reshape(-1, width_in),
                    (((0,), (0,)), ((), ())),
                    preferred_element_type=WIDE,
                ).astype(LOW)
            )
    kernel_grad = jnp.stack(taps).reshape(9, chips, 2, chan_width, width_in)
    smalls = jnp.stack([bias_grad, self_stitch, cross_stitch]).astype(LOW)
    smalls = jnp.pad(
        smalls.reshape(3, chips, 2, chan_width), ((0, 13), (0, 0), (0, 0), (0, width_in - chan_width))
    )
    blocks = [
        tuple(
            jnp.concatenate([kernel_grad[:, m, c].reshape(9 * chan_width, width_in), smalls[:, m, c]])
            for c in range(2)
        )
        for m in range(chips)
    ]
    first, second = scatter_chips(reorder(blocks, chip), chips)
    sums = [total(first).astype(LOW), total(second).astype(LOW)]
    keep = mine(sums[0], sums[1])
    got = swap(mine(sums[1], sums[0]))
    towers = jnp.stack([mine(keep, got), mine(got, keep)])
    towers = lax.psum(towers, "batch").astype(WIDE)
    stitch_fc_grad = lax.psum(stitch_fc_grad.astype(LOW), "batch").astype(WIDE)

    images_grad = lax.conv_general_dilated(
        conv_grad,
        kernel.reshape(3, 3, full_chan, width_in)[::-1, ::-1],
        (1, 1),
        "SAME",
        dimension_numbers=("HWNC", "HWIO", "HWNC"),
        preferred_element_type=WIDE,
    ).astype(LOW)
    images_grad = jnp.transpose(images_grad, (2, 0, 1, 3))
    keep = mine(images_grad[:per_core], images_grad[per_core:])
    got = swap(mine(images_grad[per_core:], images_grad[:per_core]))
    images_grad = jnp.stack([mine(keep, got), mine(got, keep)], axis=1)

    both_rows = [mine(tower_rows, other_rows), mine(other_rows, tower_rows)]
    fc_weight_grad = jnp.stack(
        [
            lax.dot_general(
                jnp.swapaxes(both_rows[t].reshape(-1, cells, plane_chan), 1, 2).reshape(-1, rows),
                grad_all[t],
                (((0,), (0,)), ((), ())),
                preferred_element_type=WIDE,
            )
            for t in range(2)
        ]
    )
    fc_bias_grad = jnp.sum(grad_all.astype(WIDE), axis=1)

    conv_weight_grad = jnp.swapaxes(
        towers[:, : 9 * chan_width].reshape(2, 3, 3, chan_width, width_in), 3, 4
    )
    conv_bias_grad = towers[:, 9 * chan_width, :chan_width]
    straight = towers[:, 9 * chan_width + 1, :chan_width]
    crossed = towers[:, 9 * chan_width + 2, :chan_width]
    stitch_conv_grad = jnp.stack(
        [jnp.stack([straight[0], crossed[0]]), jnp.stack([crossed[1], straight[1]])]
    )
    grads = (
        conv_weight_grad,
        conv_bias_grad,
        stitch_conv_grad,
        fc_weight_grad,
        fc_bias_grad,
        stitch_fc_grad,
    )
    params = (conv_weight, conv_bias, stitch_conv, fc_weight, fc_bias, stitch_fc)
    moments = (
        conv_moment,
        bias_moment,
        stitch_conv_moment,
        fc_moment,
        fc_bias_moment,
        stitch_fc_moment,
    )
    rates = (LEARN_RATE, BIAS_RATE, STITCH_RATE, LEARN_RATE, BIAS_RATE, STITCH_RATE)
    fresh = [MOMENTUM * moments[place] + grads[place] for place in range(6)]
    updated = [params[place] - rates[place] * fresh[place] for place in range(6)]
    return (features_out, images_grad, *updated, *fresh)


def four_by_four(
    images,
    conv_weight,
    conv_bias,
    stitch_conv,
    fc_weight,
    fc_bias,
    stitch_fc,
    conv_moment,
    bias_moment,
    stitch_conv_moment,
    fc_moment,
    fc_bias_moment,
    stitch_fc_moment,
    cotangent,
    task_mask,
):
    chips, planes = lax.axis_size("chan") // 2, lax.axis_size("batch")
    me, plane = lax.axis_index("chan"), lax.axis_index("batch")
    core, chip = me % 2, me // 2
    as_scalar = lambda value: value.reshape(1).astype(jnp.int32)
    core_at, chip_at, plane_at = as_scalar(core), as_scalar(chip), as_scalar(plane)
    swap = lambda value: trade(value, "chan", 1)
    mine = lambda a, b: jnp.where(core == 0, a, b)
    per_core, side, width_in = images.shape[0], images.shape[2], images.shape[-1]
    shard = conv_weight.shape[-1]
    units = fc_weight.shape[-1]
    half = planes // 2

    kernel_rows = jnp.transpose(conv_weight, (0, 1, 2, 4, 3)).astype(LOW)
    kernel_rows = kernel_rows.reshape(2, TAPS * shard, width_in)
    straight = jnp.stack([stitch_conv[0, 0], stitch_conv[1, 1]])
    crossed = jnp.stack([stitch_conv[0, 1], stitch_conv[1, 0]])
    small = jnp.stack([conv_bias, straight, crossed, crossed[::-1]], axis=1).astype(LOW)
    small = jnp.pad(small, ((0, 0), (0, EXTRA - 4), (0, width_in - shard)))
    kernel_rows = jnp.concatenate([kernel_rows, small], axis=1)
    keep = mine(kernel_rows[0], kernel_rows[1])
    got = swap(mine(kernel_rows[1], kernel_rows[0]))
    kernel_parts = [part for pair in gather_chips(keep, got, chips) for part in pair]

    keep = mine(images[:, 0], images[:, 1])
    got = swap(mine(images[:, 1], images[:, 0]))
    tower_images = jnp.concatenate([mine(keep, got), mine(got, keep)], axis=0)
    tower_images = jnp.transpose(tower_images, (1, 2, 0, 3))
    tower_images = jnp.pad(tower_images, ((1, 1), (1, 1), (0, 0), (0, 0)))

    fc_low = fc_prepare(fc_weight, core_at)
    fc_own, fc_cross = fc_low[0], swap(fc_low[1])

    pooled, slope, small_all = conv_forward(tower_images, kernel_parts, core_at, chip_at)
    pooled_other = swap(pooled)
    got = exchange_planes(mix_pieces(pooled, pooled_other, small_all, plane_at, planes))
    gathered = gather_chips(jnp.stack(got[:half]), jnp.stack(got[half:]), chips)
    tower_rows, *partial = fc_forward(
        [part for pair in gathered for part in pair], (fc_own, fc_cross), chip_at, chips, planes
    )
    other_rows = swap(tower_rows)

    fc_sum = total(exchange_planes(partial))
    fc_out = [fc_sum[:, :units], swap(fc_sum[:, units:])]
    fc_out = [fc_out[a] + mine(fc_bias[a], fc_bias[1 - a]) for a in range(2)]
    acts, slopes = zip(*[silu_and_slope(value) for value in fc_out])
    mix = [[mine(stitch_fc[a, b], stitch_fc[1 - a, 1 - b]) for b in range(2)] for a in range(2)]
    features = [mix[a][0] * acts[0] + mix[a][1] * acts[1] for a in range(2)]
    features_out = jnp.stack([mine(features[0], features[1]), mine(features[1], features[0])], axis=1)
    masked = [cotangent[:, t].astype(WIDE) * task_mask[:, t].astype(WIDE)[:, None] for t in range(2)]
    out_grad = [mine(masked[a], masked[1 - a]) for a in range(2)]
    grad_low = jnp.stack(
        [(slopes[b] * (mix[0][b] * out_grad[0] + mix[1][b] * out_grad[1])).astype(LOW) for b in range(2)]
    )
    stitch_fc_grad = jnp.stack(
        [jnp.stack([jnp.sum(out_grad[a] * acts[b], axis=0) for b in range(2)]) for a in range(2)]
    )
    grads = exchange_planes([grad_low] * planes)
    grads_cross = swap(jnp.stack([value[1] for value in grads]))

    blocks = fc_backward(grads, grads_cross, (fc_own, fc_cross), chip_at, chips, planes)
    first, second = scatter_chips([blocks[2 * j : 2 * j + 2] for j in range(chips)], chips)
    sums = [total([value[i] for value in part]).astype(LOW) for part in (first, second) for i in range(half)]
    mixed_grad = exchange_planes(sums)
    mixed_grad_other = swap(jnp.stack(mixed_grad))

    *blocks, conv_grad = conv_backward(
        mixed_grad, mixed_grad_other, pooled, pooled_other, slope, tower_images, small_all, core_at, chip_at, plane_at
    )
    first, second = scatter_chips([blocks[2 * j : 2 * j + 2] for j in range(chips)], chips)
    towers = jnp.stack([total(first).astype(LOW), swap(total(second).astype(LOW))])
    lines = towers.shape[1]

    packed = jnp.concatenate([stitch_fc_grad.reshape(-1), jnp.zeros((-4 * units) % width_in)])
    packed = packed.astype(LOW).reshape(-1, width_in)
    tail = (-(2 * lines + packed.shape[0])) % (planes * 16)
    flat = jnp.concatenate([towers.reshape(-1, width_in), jnp.pad(packed, ((0, tail), (0, 0)))])
    flat = flat.reshape(planes, -1, width_in)
    quarters = [lax.dynamic_index_in_dim(flat, plane ^ k, 0, keepdims=False) for k in range(planes)]
    quarter = total(exchange_planes(quarters)).astype(LOW)
    whole = exchange_planes([quarter] * planes)
    whole = jnp.concatenate(reorder(whole, plane)).astype(WIDE)
    towers = whole[: 2 * lines].reshape(2, lines, width_in)
    stitch_fc_grad = whole[2 * lines :].reshape(-1)[: 4 * units].reshape(2, 2, units)
    stitch_fc_grad = mine(stitch_fc_grad, stitch_fc_grad[::-1, ::-1])
    towers = mine(towers, towers[::-1])

    full_chan = conv_grad.shape[-1]
    ordered = reorder([(kernel_parts[2 * j], kernel_parts[2 * j + 1]) for j in range(chips)], chip)
    ordered = [part for a, b in ordered for part in (mine(a, b), mine(b, a))]
    kernel = jnp.concatenate(
        [part[: TAPS * shard].reshape(3, 3, shard, width_in) for part in ordered], axis=2
    )
    images_grad = lax.conv_general_dilated(
        conv_grad,
        kernel[::-1, ::-1],
        (1, 1),
        "SAME",
        dimension_numbers=("HWNC", "HWIO", "HWNC"),
        preferred_element_type=WIDE,
    ).astype(LOW)
    images_grad = jnp.transpose(images_grad, (2, 0, 1, 3))
    keep = mine(images_grad[:per_core], images_grad[per_core:])
    got = swap(mine(images_grad[per_core:], images_grad[:per_core]))
    images_grad = jnp.stack([mine(keep, got), mine(got, keep)], axis=1)

    step = fc_update(fc_weight, fc_moment, tower_rows, grads, core_at, 0, None)
    new_fc_weight, new_fc_moment = fc_update(fc_weight, fc_moment, other_rows, grads, core_at, 1, step)
    fc_bias_grad = sum(jnp.sum(value.astype(WIDE), axis=1) for value in grads)
    fc_bias_grad = mine(fc_bias_grad, fc_bias_grad[::-1])

    conv_weight_grad = towers[:, : TAPS * shard].reshape(2, 3, 3, shard, width_in)
    conv_weight_grad = jnp.swapaxes(conv_weight_grad, 3, 4)
    conv_bias_grad = towers[:, TAPS * shard, :shard]
    straight = towers[:, TAPS * shard + 1, :shard]
    crossed = towers[:, TAPS * shard + 2, :shard]
    stitch_conv_grad = jnp.stack(
        [jnp.stack([straight[0], crossed[0]]), jnp.stack([crossed[1], straight[1]])]
    )

    def step_of(param, moment, grad, rate):
        fresh = MOMENTUM * moment + grad
        return param - rate * fresh, fresh

    kernel_step = step_of(conv_weight, conv_moment, conv_weight_grad, LEARN_RATE)
    bias_step = step_of(conv_bias, bias_moment, conv_bias_grad, BIAS_RATE)
    stitch_step = step_of(stitch_conv, stitch_conv_moment, stitch_conv_grad, STITCH_RATE)
    fc_bias_step = step_of(fc_bias, fc_bias_moment, fc_bias_grad, BIAS_RATE)
    fc_stitch_step = step_of(stitch_fc, stitch_fc_moment, stitch_fc_grad, STITCH_RATE)
    params, fresh = zip(
        kernel_step, bias_step, stitch_step, (new_fc_weight, new_fc_moment), fc_bias_step, fc_stitch_step
    )
    return (features_out.astype(LOW), images_grad, *params, *fresh)


def solution(mesh):
    chan_last = P(None, None, None, None, "chan")
    fc_spec = P(None, "batch", "chan")
    params = (chan_last, P(None, "chan"), P(None, None, "chan"), fc_spec, P(None, "chan"), P(None, None, "chan"))
    image_spec = P(("batch", "chan"), None, None, None, None)
    feature_spec = P("batch", None, "chan")
    in_specs = (image_spec, *params, *params, feature_spec, P("batch", None))
    out_specs = (feature_spec, image_spec, *params, *params)
    body = four_by_four if dict(mesh.shape) == {"chan": 8, "batch": 4} else any_mesh
    return jax.shard_map(body, mesh=mesh, in_specs=in_specs, out_specs=out_specs, check_vma=False)
```

profile of v0, /device:TPU:0, one launch (start us, length us, event | category | flops | bytes accessed | tf_op | source)
XLA Modules:
  0.0 235.6 jit_solution(2690374955689068315)
XLA Ops:
  4.3 3.0 %collective-permute-start.4 = (bf16[304,384]{1,0:T(8,128)(2,1)S(1)}, bf16[304,384]{1,0:T(8,128)(2,1)S(1)}, u32[]{:S(2)}, u32[]{:S(2)}) collective-permute-start(bf16[304,384]{1,0:T(8,128)(2,1)S(1)} %get-tuple-element.148.refs_0_), channel_id=1, source_target_pairs={{0,16},{4,20},{8,24},{12,28},{16,0},{20,4},{24,8},{28,12},{1,17},{... | collective-permute-start | bytes 700424 | tf_op jit(solution)/shard_map/ppermute | solution.py:37
  7.3 1.5 collective-permute-start.2
  8.8 2.9 %fusion.31 = (bf16[8,1,13,13,384]{4,1,3,2,0:T(2,128)(2,1)S(1)}, bf16[8,1,13,13,384]{4,1,3,2,0:T(2,128)(2,1)S(1)}) fusion(bf16[8,2,13,13,384]{4,1,3,2,0:T(2,128)(2,1)S(1)} %copy-done.34), kind=kLoop, calls=%fused_computation.174 | loop fusion | bytes 4153344 | tf_op jit(solution)/shard_map/slice | solution.py:775
  11.8 1.5 select_bitcast_fusion.2
  14.6 2.8 %shard_map.256 = bf16[2,2304,512]{2,1,0:T(8,128)(2,1)S(1)} custom-call(s32[1]{0:T(128)} %bitcast.3.core_ref, f32[2,2304,512]{2,1,0:T(8,128)S(1)} %copy-done), custom_call_target="tpu_custom_call" | custom-call | bytes 14155776 | tf_op jit(solution)/shard_map/pallas_call | solution.py:116
  17.5 1.7 slice_bitcast_fusion
  20.0 7.4 %collective-permute-done.3.refs_3_ = bf16[304,384]{1,0:T(8,128)(2,1)} collective-permute-done((bf16[304,384]{1,0:T(8,128)(2,1)S(1)}, bf16[304,384]{1,0:T(8,128)(2,1)}, u32[]{:S(2)}, u32[]{:S(2)}) %collective-permute-start.3) | collective-permute-done | bytes 233504 | tf_op jit(solution)/shard_map/ppermute | solution.py:37
  28.2 2.5 %bitcast_select_fusion.1 = (bf16[8,13,13,384]{3,0,2,1:T(8,128)(2,1)S(1)}, bf16[8,1,13,13,384]{4,0,3,2,1:T(8,128)(2,1)S(1)}) fusion(bf16[8,13,13,384]{3,0,2,1:T(8,128)(2,1)} %collective-permute-done, pred[]{:T(512)S(6)} %eq.4, bf16[8,1,13,13,384]{4,1,3,2,0:T(2,128)(2,1)} %copy-done.33, bf16[8,1,13,13,384]{4,1,3,2,0:T(2,128)(2,1)} %copy-done.32), kind=kLoop, calls=%fused_computation.7 | loop fusion | flops 1038336 | bytes 5191681 | tf_op jit(solution)/shard_map/jit(_where)/select_n | solution.py:758
  36.2 7.8 %shard_map.254 = (f32[36,16,256]{2,1,0:T(8,128)S(1)}, bf16[13,13,16,256]{3,2,1,0:T(8,128)(2,1)S(1)}, f32[16,256]{1,0:T(8,128)S(1)}) custom-call(s32[1]{0:T(128)} %bitcast.3.core_ref, s32[1]{0:T(128)} %bitcast.1.chip_ref, bf16[15,15,16,384]{3,2,1,0:T(8,128)(2,1)S(1)} %pad.14.x_ref.refs_8_, bf16[304,384]{1,0:T(8,128)(2,1)S(1)} %get-tuple-element.148.refs_0_, ...), custom_call_target="tpu_custom_call" | custom-call | flops 4784652288 | bytes 4149248 | tf_op jit(solution)/shard_map/pallas_call | solution.py:185
  49.1 2.7 %collective-permute-start.10 = (bf16[16,2304]{1,0:T(8,128)(2,1)S(1)}, bf16[16,2304]{1,0:T(8,128)(2,1)S(1)}, u32[]{:S(2)}, u32[]{:S(2)}) collective-permute-start(bf16[16,2304]{1,0:T(8,128)(2,1)S(1)} %get-tuple-element.51), channel_id=1, source_target_pairs={{0,2},{1,3},{2,0},{3,1},{4,6},{5,7},{6,4},{7,5},{8,10},{9,11},{10,... | collective-permute-start | bytes 221192 | tf_op jit(solution)/shard_map/ppermute | solution.py:37
  54.5 3.8 %collective-permute-done.10 = bf16[16,2304]{1,0:T(8,128)(2,1)S(1)} collective-permute-done((bf16[16,2304]{1,0:T(8,128)(2,1)S(1)}, bf16[16,2304]{1,0:T(8,128)(2,1)S(1)}, u32[]{:S(2)}, u32[]{:S(2)}) %collective-permute-start.10) | collective-permute-done | bytes 73760 | tf_op jit(solution)/shard_map/ppermute | solution.py:37
  58.3 1.6 collective-permute-start.13
  60.5 1.6 collective-permute-start.15
  64.0 2.7 %collective-permute-done.14.refs_4_ = bf16[2,16,2304]{2,1,0:T(8,128)(2,1)S(1)} collective-permute-done((bf16[2,16,2304]{2,1,0:T(8,128)(2,1)S(1)}, bf16[2,16,2304]{2,1,0:T(8,128)(2,1)S(1)}, u32[]{:S(2)}, u32[]{:S(2)}) %collective-permute-start.14) | collective-permute-done | bytes 147488 | tf_op jit(solution)/shard_map/ppermute | solution.py:37
  68.1 1.7 collective-permute-done.15.refs_5_
  69.8 2.1 collective-permute-done.17.refs_7_
  71.9 3.1 %shard_map.257 = (bf16[256,2304]{1,0:T(8,128)(2,1)}, f32[64,1024]{1,0:T(8,128)S(1)}, bf16[64,1024]{1,0:T(8,128)(2,1)S(1)}, bf16[64,1024]{1,0:T(8,128)(2,1)S(1)}, bf16[64,1024]{1,0:T(8,128)(2,1)S(1)}) custom-call(s32[1]{0:T(128)} %bitcast.1.chip_ref, bf16[2,16,2304]{2,1,0:T(8,128)(2,1)S(1)} %pad_maximum_fusion.5.refs_0_, ...), custom_call_target="tpu_custom_call" | custom-call | flops 1207959552 | bytes 4718592 | tf_op jit(solution)/shard_map/pallas_call | solution.py:268
  75.0 1.9 collective-permute-start.19
  76.9 2.0 collective-permute-start.20
  81.4 8.1 %collective-permute-done.20 = bf16[64,1024]{1,0:T(8,128)(2,1)S(1)} collective-permute-done((bf16[64,1024]{1,0:T(8,128)(2,1)S(1)}, bf16[64,1024]{1,0:T(8,128)(2,1)S(1)}, u32[]{:S(2)}, u32[]{:S(2)}) %collective-permute-start.20) | collective-permute-done | bytes 131104 | tf_op jit(solution)/shard_map/ppermute | solution.py:37
  92.7 2.0 collective-permute-start.23
  97.3 3.1 %collective-permute-done.23.refs_1_ = bf16[2,64,512]{2,1,0:T(8,128)(2,1)S(1)} collective-permute-done((bf16[2,64,512]{2,1,0:T(8,128)(2,1)S(1)}, bf16[2,64,512]{2,1,0:T(8,128)(2,1)S(1)}, u32[]{:S(2)}, u32[]{:S(2)}) %collective-permute-start.23) | collective-permute-done | bytes 131104 | tf_op jit(solution)/shard_map/ppermute | solution.py:37
  100.4 7.2 %collective-permute-done.24.refs_2_ = bf16[2,64,512]{2,1,0:T(8,128)(2,1)S(1)} collective-permute-done((bf16[2,64,512]{2,1,0:T(8,128)(2,1)S(1)}, bf16[2,64,512]{2,1,0:T(8,128)(2,1)S(1)}, u32[]{:S(2)}, u32[]{:S(2)}) %collective-permute-start.24) | collective-permute-done | bytes 131104 | tf_op jit(solution)/shard_map/ppermute | solution.py:37
  109.3 3.8 %shard_map.258 = (bf16[2,16,2304]{2,1,0:T(8,128)(2,1)S(1)}, bf16[2,16,2304]{2,1,0:T(8,128)(2,1)S(1)}, bf16[2,16,2304]{2,1,0:T(8,128)(2,1)S(1)}, bf16[2,16,2304]{...) custom-call(s32[1]{0:T(128)} %bitcast.1.chip_ref, ...), custom_call_target="tpu_custom_call" | custom-call | flops 1207959552 | bytes 4718592 | tf_op jit(solution)/shard_map/pallas_call | solution.py:307
  118.3 1.7 copy.39
  120.9 1.6 collective-permute-start.33
  126.1 3.4 %collective-permute-done.28 = bf16[2,16,2304]{2,1,0:T(8,128)(2,1)S(1)} collective-permute-done((bf16[2,16,2304]{2,1,0:T(8,128)(2,1)}, bf16[2,16,2304]{2,1,0:T(8,128)(2,1)S(1)}, u32[]{:S(2)}, u32[]{:S(2)}) %collective-permute-start.28) | collective-permute-done | bytes 147488 | tf_op jit(solution)/shard_map/ppermute | solution.py:37
  131.0 3.5 %collective-permute-done.32 = bf16[2,16,2304]{2,1,0:T(8,128)(2,1)S(1)} collective-permute-done((bf16[2,16,2304]{2,1,0:T(8,128)(2,1)S(1)}, bf16[2,16,2304]{2,1,0:T(8,128)(2,1)S(1)}, u32[]{:S(2)}, u32[]{:S(2)}) %collective-permute-start.32) | collective-permute-done | bytes 147488 | tf_op jit(solution)/shard_map/ppermute | solution.py:37
  135.5 3.3 %collective-permute-start.34 = (bf16[16,2304]{1,0:T(8,128)(2,1)S(1)}, bf16[16,2304]{1,0:T(8,128)(2,1)S(1)}, u32[]{:S(2)}, u32[]{:S(2)}) collective-permute-start(bf16[16,2304]{1,0:T(8,128)(2,1)S(1)} %get-tuple-element.150), channel_id=1, source_target_pairs={{0,2},{1,3},{2,0},{3,1},{4,6},{5,7},{6,4},{7,5},{8,10},{9,11},{10,... | collective-permute-start | bytes 221192 | tf_op jit(solution)/shard_map/ppermute | solution.py:37
  141.7 3.4 %collective-permute-done.35.refs_3_ = bf16[16,2304]{1,0:T(8,128)(2,1)S(1)} collective-permute-done((bf16[16,2304]{1,0:T(8,128)(2,1)S(1)}, bf16[16,2304]{1,0:T(8,128)(2,1)S(1)}, u32[]{:S(2)}, u32[]{:S(2)}) %collective-permute-start.35) | collective-permute-done | bytes 73760 | tf_op jit(solution)/shard_map/ppermute | solution.py:37
  146.2 3.7 %copy-done.1 = f32[2,2304,512]{2,1,0:T(8,128)S(1)} copy-done((f32[2,2304,512]{2,1,0:T(8,128)S(1)}, f32[2,2304,512]{2,1,0:T(8,128)}, u32[]{:S(2)}) %copy-start.1) | copy-done | bytes 9437208
  149.9 3.7 %copy-done.2 = f32[2,2304,512]{2,1,0:T(8,128)S(1)} copy-done((f32[2,2304,512]{2,1,0:T(8,128)S(1)}, f32[2,2304,512]{2,1,0:T(8,128)}, u32[]{:S(2)}) %copy-start.2) | copy-done | bytes 9437208
  153.6 7.2 %shard_map.260 = (f32[2,2304,512]{2,1,0:T(8,128)}, f32[2,2304,512]{2,1,0:T(8,128)}) custom-call(s32[1]{0:T(128)} %bitcast.3.core_ref, f32[2,2304,512]{2,1,0:T(8,128)S(1)} %copy-done.1, f32[2,2304,512]{2,1,0:T(8,128)S(1)} %copy-done.2, bf16[256,2304]{1,0:T(8,128)(2,1)} %get-tuple-element.75.rows_ref, bf16[2,64,512]{2,1,0:T(8,128)(2,1)S(1)} %pad_maximum_fusion.8.refs_0_, ...), custom_call_target="tpu_custom_call" | custom-call | flops 603979776 | bytes 18874368 | tf_op jit(solution)/shard_map/pallas_call | solution.py:445
  162.7 9.6 %shard_map.259 = (bf16[304,384]{1,0:T(8,128)(2,1)S(1)}, bf16[304,384]{1,0:T(8,128)(2,1)S(1)}, bf16[304,384]{1,0:T(8,128)(2,1)S(1)}, bf16[304,384]{1,0:T(8,128)(2...) custom-call(s32[1]{0:T(128)} %bitcast.3.core_ref, ...), custom_call_target="tpu_custom_call" | custom-call | flops 4784652288 | bytes 6918144 | tf_op jit(solution)/shard_map/pallas_call | solution.py:401
  173.5 6.7 %shard_map.261 = (f32[2,2304,512]{2,1,0:T(8,128)}, f32[2,2304,512]{2,1,0:T(8,128)}) custom-call(s32[1]{0:T(128)} %bitcast.3.core_ref, f32[2,2304,512]{2,1,0:T(8,128)S(1)} %bitcast.141, f32[2,2304,512]{2,1,0:T(8,128)S(1)} %bitcast.143, bf16[256,2304]{1,0:T(8,128)(2,1)} %collective-permute-done.51.rows_ref, ...), custom_call_target="tpu_custom_call", output_to_operand_aliasing={{0}: (8, {}), {1}: (9, {})} | custom-call | flops 603979776 | bytes 18874368 | tf_op jit(solution)/shard_map/pallas_call | solution.py:445
  182.3 1.5 collective-permute-start.43
  184.5 4.4 %collective-permute-done.39 = bf16[304,384]{1,0:T(8,128)(2,1)S(1)} collective-permute-done((bf16[304,384]{1,0:T(8,128)(2,1)S(1)}, bf16[304,384]{1,0:T(8,128)(2,1)S(1)}, u32[]{:S(2)}, u32[]{:S(2)}) %collective-permute-start.39) | collective-permute-done | bytes 233504 | tf_op jit(solution)/shard_map/ppermute | solution.py:37
  188.9 1.6 collective-permute-start.40
  190.5 7.2 %collective-permute-done.42 = bf16[304,384]{1,0:T(8,128)(2,1)S(1)} collective-permute-done((bf16[304,384]{1,0:T(8,128)(2,1)S(1)}, bf16[304,384]{1,0:T(8,128)(2,1)S(1)}, u32[]{:S(2)}, u32[]{:S(2)}) %collective-permute-start.42) | collective-permute-done | bytes 233504 | tf_op jit(solution)/shard_map/ppermute | solution.py:37
  199.6 2.3 collective-permute-start.46
  201.8 2.1 collective-permute-start.47
  204.0 6.8 %convolution_convert_fusion = bf16[16,13,13,384]{3,0,2,1:T(8,128)(2,1)S(1)} fusion(bf16[13,13,16,256]{3,2,1,0:T(8,128)(2,1)S(1)} %get-tuple-element.66, bf16[3,3,256,384]{3,2,1,0:T(8,128)(2,1)S(1)} %copy-done.40), kind=kOutput, calls=%fused_computation.4 | convolution fusion | flops 4307539968 | bytes 5230592 | tf_op jit(solution)/shard_map/conv_general_dilated | solution.py:844
  212.1 2.3 collective-permute-start.48
  214.4 1.6 collective-permute-start.49
  217.7 2.5 %collective-permute-done.48 = bf16[160,384]{1,0:T(8,128)(2,1)S(1)} collective-permute-done((bf16[160,384]{1,0:T(8,128)(2,1)S(1)}, bf16[160,384]{1,0:T(8,128)(2,1)S(1)}, u32[]{:S(2)}, u32[]{:S(2)}) %collective-permute-start.48) | collective-permute-done | bytes 122912 | tf_op jit(solution)/shard_map/ppermute | solution.py:37
  220.2 5.0 %collective-permute-done.49 = bf16[160,384]{1,0:T(8,128)(2,1)S(1)} collective-permute-done((bf16[160,384]{1,0:T(8,128)(2,1)S(1)}, bf16[160,384]{1,0:T(8,128)(2,1)S(1)}, u32[]{:S(2)}, u32[]{:S(2)}) %collective-permute-start.49) | collective-permute-done | bytes 122912 | tf_op jit(solution)/shard_map/ppermute | solution.py:37
  227.9 3.0 %multiply_subtract_fusion = (f32[2,3,3,384,32]{3,4,2,1,0:T(8,128)}, f32[2,3,3,384,32]{3,4,2,1,0:T(8,128)}) fusion(f32[2,3,3,384,32]{3,4,2,1,0:T(8,128)} %param.16, f32[2,3,3,384,32]{3,4,2,1,0:T(8,128)S(1)} %bitcast.150, f32[2,3,3,384,32]{3,4,2,1,0:T(8,128)} %param.22), kind=kLoop, calls=%fused_computation.16 | loop fusion | flops 884736 | bytes 4423680 | tf_op jit(solution)/shard_map/sub | solution.py:873
  232.7 2.9 %copy.40 = bf16[8,2,13,13,384]{4,1,3,2,0:T(2,128)(2,1)} copy(bf16[8,2,13,13,384]{4,0,3,2,1:T(8,128)(2,1)S(1)} %pad_maximum_fusion) | data formatting | bytes 4153344
  (287 shorter events, 64.6 us)
Async XLA Ops:
  4.3 15.5 %collective-permute-start.4 = (bf16[304,384]{1,0:T(8,128)(2,1)S(1)}, bf16[304,384]{1,0:T(8,128)(2,1)S(1)}, u32[]{:S(2)}, u32[]{:S(2)}) collective-permute-start(bf16[304,384]{1,0:T(8,128)(2,1)S(1)} %get-tuple-element.148.refs_0_), channel_id=1, source_target_pairs={{0,16},{4,20},{8,24},{12,28},{16,0},{20,4},{24,8},{28,12},{1,17},{... | collective-permute-start | bytes 700424 | tf_op jit(solution)/shard_map/ppermute | solution.py:37
  7.3 25.3 %collective-permute-start.2 = (bf16[304,384]{1,0:T(8,128)(2,1)S(1)}, bf16[304,384]{1,0:T(8,128)(2,1)S(1)}, u32[]{:S(2)}, u32[]{:S(2)}) collective-permute-start(bf16[304,384]{1,0:T(8,128)(2,1)S(1)} %get-tuple-element.148.refs_0_), channel_id=1, source_target_pairs={{0,8},{4,12},{8,0},{12,4},{16,24},{20,28},{24,16},{28,20},{1,9},{5... | collective-permute-start | bytes 700424 | tf_op jit(solution)/shard_map/ppermute | solution.py:37
  14.1 13.8 %collective-permute-start = (bf16[8,13,13,384]{3,0,2,1:T(8,128)(2,1)}, bf16[8,13,13,384]{3,0,2,1:T(8,128)(2,1)}, u32[]{:S(2)}, u32[]{:S(2)}) collective-permute-start(bf16[8,13,13,384]{3,0,2,1:T(8,128)(2,1)} %select_bitcast_fusion.2), channel_id=1, source_target_pairs={{0,4},{4,0},{8,12},{12,8},{16,20},{20,16},{24,28},{28,24},{1,5},{5... | collective-permute-start | bytes 3115016 | tf_op jit(solution)/shard_map/ppermute | solution.py:37
  14.1 5.1 %collective-permute-start.1 = (bf16[304,384]{1,0:T(8,128)(2,1)S(1)}, bf16[304,384]{1,0:T(8,128)(2,1)S(1)}, u32[]{:S(2)}, u32[]{:S(2)}) collective-permute-start(bf16[304,384]{1,0:T(8,128)(2,1)S(1)} %get-tuple-element.147), channel_id=1, source_target_pairs={{0,4},{4,0},{8,12},{12,8},{16,20},{20,16},{24,28},{28,24},{1,5},{5... | collective-permute-start | bytes 700424 | tf_op jit(solution)/shard_map/ppermute | solution.py:37
  19.2 52.7 %collective-permute-start.18 = (bf16[2304,512]{1,0:T(8,128)(2,1)}, bf16[2304,512]{1,0:T(8,128)(2,1)}, u32[]{:S(2)}, u32[]{:S(2)}) collective-permute-start(bf16[2304,512]{1,0:T(8,128)(2,1)} %get-tuple-element.114), channel_id=1, source_target_pairs={{0,4},{4,0},{8,12},{12,8},{16,20},{20,16},{24,28},{28,24},{1,5},{5... | collective-permute-start | bytes 7077896 | tf_op jit(solution)/shard_map/ppermute | solution.py:37
  19.2 8.2 %collective-permute-start.3 = (bf16[304,384]{1,0:T(8,128)(2,1)S(1)}, bf16[304,384]{1,0:T(8,128)(2,1)}, u32[]{:S(2)}, u32[]{:S(2)}) collective-permute-start(bf16[304,384]{1,0:T(8,128)(2,1)S(1)} %collective-permute-done.1.refs_1_), channel_id=1, source_target_pairs={{0,8},{4,12},{8,0},{12,4},{16,24},{20,28},{24,16},{28,20},{1,9},{5... | collective-permute-start | bytes 700424 | tf_op jit(solution)/shard_map/ppermute | solution.py:37
  19.8 14.9 %collective-permute-start.5 = (bf16[304,384]{1,0:T(8,128)(2,1)S(1)}, bf16[304,384]{1,0:T(8,128)(2,1)S(1)}, u32[]{:S(2)}, u32[]{:S(2)}) collective-permute-start(bf16[304,384]{1,0:T(8,128)(2,1)S(1)} %collective-permute-done.1.refs_1_), channel_id=1, source_target_pairs={{0,16},{4,20},{8,24},{12,28},{16,0},{20,4},{24,8},{28,12},{1,17},{... | collective-permute-start | bytes 700424 | tf_op jit(solution)/shard_map/ppermute | solution.py:37
  27.4 7.3 %collective-permute-start.6 = (bf16[304,384]{1,0:T(8,128)(2,1)S(1)}, bf16[304,384]{1,0:T(8,128)(2,1)S(1)}, u32[]{:S(2)}, u32[]{:S(2)}) collective-permute-start(bf16[304,384]{1,0:T(8,128)(2,1)S(1)} %collective-permute-done.4.refs_4_), channel_id=1, source_target_pairs={{0,8},{4,12},{8,0},{12,4},{16,24},{20,28},{24,16},{28,20},{1,9},{5... | collective-permute-start | bytes 700424 | tf_op jit(solution)/shard_map/ppermute | solution.py:37
  27.9 7.3 %collective-permute-start.7 = (bf16[304,384]{1,0:T(8,128)(2,1)}, bf16[304,384]{1,0:T(8,128)(2,1)S(1)}, u32[]{:S(2)}, u32[]{:S(2)}) collective-permute-start(bf16[304,384]{1,0:T(8,128)(2,1)} %collective-permute-done.3.refs_3_), channel_id=1, source_target_pairs={{0,16},{4,20},{8,24},{12,28},{16,0},{20,4},{24,8},{28,12},{1,17},{... | collective-permute-start | bytes 700424 | tf_op jit(solution)/shard_map/ppermute | solution.py:37
  49.1 9.2 %collective-permute-start.10 = (bf16[16,2304]{1,0:T(8,128)(2,1)S(1)}, bf16[16,2304]{1,0:T(8,128)(2,1)S(1)}, u32[]{:S(2)}, u32[]{:S(2)}) collective-permute-start(bf16[16,2304]{1,0:T(8,128)(2,1)S(1)} %get-tuple-element.51), channel_id=1, source_target_pairs={{0,2},{1,3},{2,0},{3,1},{4,6},{5,7},{6,4},{7,5},{8,10},{9,11},{10,... | collective-permute-start | bytes 221192 | tf_op jit(solution)/shard_map/ppermute | solution.py:37
  51.7 6.5 %collective-permute-start.11 = (bf16[16,2304]{1,0:T(8,128)(2,1)S(1)}, bf16[16,2304]{1,0:T(8,128)(2,1)S(1)}, u32[]{:S(2)}, u32[]{:S(2)}) collective-permute-start(bf16[16,2304]{1,0:T(8,128)(2,1)S(1)} %get-tuple-element.52), channel_id=1, source_target_pairs={{0,3},{1,2},{2,1},{3,0},{4,7},{5,6},{6,5},{7,4},{8,11},{9,10},{10,... | collective-permute-start | bytes 221192 | tf_op jit(solution)/shard_map/ppermute | solution.py:37
  54.2 5.7 %collective-permute-start.9 = (bf16[16,2304]{1,0:T(8,128)(2,1)S(1)}, bf16[16,2304]{1,0:T(8,128)(2,1)S(1)}, u32[]{:S(2)}, u32[]{:S(2)}) collective-permute-start(bf16[16,2304]{1,0:T(8,128)(2,1)S(1)} %get-tuple-element.50), channel_id=1, source_target_pairs={{0,1},{1,0},{2,3},{3,2},{4,5},{5,4},{6,7},{7,6},{8,9},{9,8},{10,11... | collective-permute-start | bytes 221192 | tf_op jit(solution)/shard_map/ppermute | solution.py:37
  58.3 5.2 %collective-permute-start.13 = (bf16[2,16,2304]{2,1,0:T(8,128)(2,1)S(1)}, bf16[2,16,2304]{2,1,0:T(8,128)(2,1)S(1)}, u32[]{:S(2)}, u32[]{:S(2)}) collective-permute-start(bf16[2,16,2304]{2,1,0:T(8,128)(2,1)S(1)} %pad_maximum_fusion.6.refs_1_), channel_id=1, source_target_pairs={{0,8},{4,12},{8,0},{12,4},{16,24},{20,28},{24,16},{28,20},{1,9},{5... | collective-permute-start | bytes 442376 | tf_op jit(solution)/shard_map/ppermute | solution.py:37
  59.9 6.8 %collective-permute-start.14 = (bf16[2,16,2304]{2,1,0:T(8,128)(2,1)S(1)}, bf16[2,16,2304]{2,1,0:T(8,128)(2,1)S(1)}, u32[]{:S(2)}, u32[]{:S(2)}) collective-permute-start(bf16[2,16,2304]{2,1,0:T(8,128)(2,1)S(1)} %pad_maximum_fusion.5.refs_0_), channel_id=1, source_target_pairs={{0,16},{4,20},{8,24},{12,28},{16,0},{20,4},{24,8},{28,12},{1,17},{... | collective-permute-start | bytes 442376 | tf_op jit(solution)/shard_map/ppermute | solution.py:37
  60.5 9.3 %collective-permute-start.15 = (bf16[2,16,2304]{2,1,0:T(8,128)(2,1)S(1)}, bf16[2,16,2304]{2,1,0:T(8,128)(2,1)S(1)}, u32[]{:S(2)}, u32[]{:S(2)}) collective-permute-start(bf16[2,16,2304]{2,1,0:T(8,128)(2,1)S(1)} %pad_maximum_fusion.6.refs_1_), channel_id=1, source_target_pairs={{0,16},{4,20},{8,24},{12,28},{16,0},{20,4},{24,8},{28,12},{1,17},{... | collective-permute-start | bytes 442376 | tf_op jit(solution)/shard_map/ppermute | solution.py:37
  62.1 7.7 %collective-permute-start.12 = (bf16[2,16,2304]{2,1,0:T(8,128)(2,1)S(1)}, bf16[2,16,2304]{2,1,0:T(8,128)(2,1)S(1)}, u32[]{:S(2)}, u32[]{:S(2)}) collective-permute-start(bf16[2,16,2304]{2,1,0:T(8,128)(2,1)S(1)} %pad_maximum_fusion.5.refs_0_), channel_id=1, source_target_pairs={{0,8},{4,12},{8,0},{12,4},{16,24},{20,28},{24,16},{28,20},{1,9},{5... | collective-permute-start | bytes 442376 | tf_op jit(solution)/shard_map/ppermute | solution.py:37
  63.5 8.4 %collective-permute-start.17 = (bf16[2,16,2304]{2,1,0:T(8,128)(2,1)S(1)}, bf16[2,16,2304]{2,1,0:T(8,128)(2,1)S(1)}, u32[]{:S(2)}, u32[]{:S(2)}) collective-permute-start(bf16[2,16,2304]{2,1,0:T(8,128)(2,1)S(1)} %collective-permute-done.13.refs_3_), channel_id=1, source_target_pairs={{0,16},{4,20},{8,24},{12,28},{16,0},{20,4},{24,8},{28,12},{1,17},{... | collective-permute-start | bytes 442376 | tf_op jit(solution)/shard_map/ppermute | solution.py:37
  66.7 5.2 %collective-permute-start.16 = (bf16[2,16,2304]{2,1,0:T(8,128)(2,1)S(1)}, bf16[2,16,2304]{2,1,0:T(8,128)(2,1)S(1)}, u32[]{:S(2)}, u32[]{:S(2)}) collective-permute-start(bf16[2,16,2304]{2,1,0:T(8,128)(2,1)S(1)} %collective-permute-done.14.refs_4_), channel_id=1, source_target_pairs={{0,8},{4,12},{8,0},{12,4},{16,24},{20,28},{24,16},{28,20},{1,9},{5... | collective-permute-start | bytes 442376 | tf_op jit(solution)/shard_map/ppermute | solution.py:37
  75.0 6.4 %collective-permute-start.19 = (bf16[64,1024]{1,0:T(8,128)(2,1)S(1)}, bf16[64,1024]{1,0:T(8,128)(2,1)S(1)}, u32[]{:S(2)}, u32[]{:S(2)}) collective-permute-start(bf16[64,1024]{1,0:T(8,128)(2,1)S(1)} %get-tuple-element.54), channel_id=1, source_target_pairs={{0,1},{1,0},{2,3},{3,2},{4,5},{5,4},{6,7},{7,6},{8,9},{9,8},{10,11... | collective-permute-start | bytes 393224 | tf_op jit(solution)/shard_map/ppermute | solution.py:37
  76.9 12.6 %collective-permute-start.20 = (bf16[64,1024]{1,0:T(8,128)(2,1)S(1)}, bf16[64,1024]{1,0:T(8,128)(2,1)S(1)}, u32[]{:S(2)}, u32[]{:S(2)}) collective-permute-start(bf16[64,1024]{1,0:T(8,128)(2,1)S(1)} %get-tuple-element.55), channel_id=1, source_target_pairs={{0,2},{1,3},{2,0},{3,1},{4,6},{5,7},{6,4},{7,5},{8,10},{9,11},{10,... | collective-permute-start | bytes 393224 | tf_op jit(solution)/shard_map/ppermute | solution.py:37
  78.9 10.7 %collective-permute-start.21 = (bf16[64,1024]{1,0:T(8,128)(2,1)S(1)}, bf16[64,1024]{1,0:T(8,128)(2,1)S(1)}, u32[]{:S(2)}, u32[]{:S(2)}) collective-permute-start(bf16[64,1024]{1,0:T(8,128)(2,1)S(1)} %get-tuple-element.56), channel_id=1, source_target_pairs={{0,3},{1,2},{2,1},{3,0},{4,7},{5,6},{6,5},{7,4},{8,11},{9,10},{10,... | collective-permute-start | bytes 393224 | tf_op jit(solution)/shard_map/ppermute | solution.py:37
  92.7 7.7 %collective-permute-start.23 = (bf16[2,64,512]{2,1,0:T(8,128)(2,1)S(1)}, bf16[2,64,512]{2,1,0:T(8,128)(2,1)S(1)}, u32[]{:S(2)}, u32[]{:S(2)}) collective-permute-start(bf16[2,64,512]{2,1,0:T(8,128)(2,1)S(1)} %pad_maximum_fusion.8.refs_0_), channel_id=1, source_target_pairs={{0,1},{1,0},{2,3},{3,2},{4,5},{5,4},{6,7},{7,6},{8,9},{9,8},{10,11... | collective-permute-start | bytes 393224 | tf_op jit(solution)/shard_map/ppermute | solution.py:37
  94.7 12.9 %collective-permute-start.24 = (bf16[2,64,512]{2,1,0:T(8,128)(2,1)S(1)}, bf16[2,64,512]{2,1,0:T(8,128)(2,1)S(1)}, u32[]{:S(2)}, u32[]{:S(2)}) collective-permute-start(bf16[2,64,512]{2,1,0:T(8,128)(2,1)S(1)} %pad_maximum_fusion.8.refs_0_), channel_id=1, source_target_pairs={{0,2},{1,3},{2,0},{3,1},{4,6},{5,7},{6,4},{7,5},{8,10},{9,11},{10,... | collective-permute-start | bytes 393224 | tf_op jit(solution)/shard_map/ppermute | solution.py:37
  95.7 11.9 %collective-permute-start.25 = (bf16[2,64,512]{2,1,0:T(8,128)(2,1)S(1)}, bf16[2,64,512]{2,1,0:T(8,128)(2,1)S(1)}, u32[]{:S(2)}, u32[]{:S(2)}) collective-permute-start(bf16[2,64,512]{2,1,0:T(8,128)(2,1)S(1)} %pad_maximum_fusion.8.refs_0_), channel_id=1, source_target_pairs={{0,3},{1,2},{2,1},{3,0},{4,7},{5,6},{6,5},{7,4},{8,11},{9,10},{10,... | collective-permute-start | bytes 393224 | tf_op jit(solution)/shard_map/ppermute | solution.py:37
  107.8 65.7 %collective-permute-start.51 = (bf16[256,2304]{1,0:T(8,128)(2,1)}, bf16[256,2304]{1,0:T(8,128)(2,1)}, u32[]{:S(2)}, u32[]{:S(2)}) collective-permute-start(bf16[256,2304]{1,0:T(8,128)(2,1)} %get-tuple-element.75.rows_ref), channel_id=1, source_target_pairs={{0,4},{4,0},{8,12},{12,8},{16,20},{20,16},{24,28},{28,24},{1,5},{5... | collective-permute-start | bytes 3538952 | tf_op jit(solution)/shard_map/ppermute | solution.py:37
  117.8 6.8 %collective-permute-start.31 = (bf16[2,16,2304]{2,1,0:T(8,128)(2,1)}, bf16[2,16,2304]{2,1,0:T(8,128)(2,1)S(1)}, u32[]{:S(2)}, u32[]{:S(2)}) collective-permute-start(bf16[2,16,2304]{2,1,0:T(8,128)(2,1)} %get-tuple-element.63), channel_id=1, source_target_pairs={{0,16},{4,20},{8,24},{12,28},{16,0},{20,4},{24,8},{28,12},{1,17},{... | collective-permute-start | bytes 442376 | tf_op jit(solution)/shard_map/ppermute | solution.py:37
  120.9 10.1 %collective-permute-start.33 = (bf16[2,16,2304]{2,1,0:T(8,128)(2,1)}, bf16[2,16,2304]{2,1,0:T(8,128)(2,1)S(1)}, u32[]{:S(2)}, u32[]{:S(2)}) collective-permute-start(bf16[2,16,2304]{2,1,0:T(8,128)(2,1)} %copy-done.28), channel_id=1, source_target_pairs={{0,16},{4,20},{8,24},{12,28},{16,0},{20,4},{24,8},{28,12},{1,17},{... | collective-permute-start | bytes 442376 | tf_op jit(solution)/shard_map/ppermute | solution.py:37
  122.5 7.0 %collective-permute-start.28 = (bf16[2,16,2304]{2,1,0:T(8,128)(2,1)}, bf16[2,16,2304]{2,1,0:T(8,128)(2,1)S(1)}, u32[]{:S(2)}, u32[]{:S(2)}) collective-permute-start(bf16[2,16,2304]{2,1,0:T(8,128)(2,1)} %copy-done.29), channel_id=1, source_target_pairs={{0,8},{4,12},{8,0},{12,4},{16,24},{20,28},{24,16},{28,20},{1,9},{5... | collective-permute-start | bytes 442376 | tf_op jit(solution)/shard_map/ppermute | solution.py:37
  123.0 17.1 %collective-permute-start.27 = (bf16[2,16,2304]{2,1,0:T(8,128)(2,1)}, bf16[2,16,2304]{2,1,0:T(8,128)(2,1)S(1)}, u32[]{:S(2)}, u32[]{:S(2)}) collective-permute-start(bf16[2,16,2304]{2,1,0:T(8,128)(2,1)} %copy-done.27), channel_id=1, source_target_pairs={{0,8},{4,12},{8,0},{12,4},{16,24},{20,28},{24,16},{28,20},{1,9},{5... | collective-permute-start | bytes 442376 | tf_op jit(solution)/shard_map/ppermute | solution.py:37
  125.5 9.0 %collective-permute-start.32 = (bf16[2,16,2304]{2,1,0:T(8,128)(2,1)S(1)}, bf16[2,16,2304]{2,1,0:T(8,128)(2,1)S(1)}, u32[]{:S(2)}, u32[]{:S(2)}) collective-permute-start(bf16[2,16,2304]{2,1,0:T(8,128)(2,1)S(1)} %add_convert_fusion.4), channel_id=1, source_target_pairs={{0,8},{4,12},{8,0},{12,4},{16,24},{20,28},{24,16},{28,20},{1,9},{5... | collective-permute-start | bytes 442376 | tf_op jit(solution)/shard_map/ppermute | solution.py:37
  130.4 9.8 %collective-permute-start.29 = (bf16[2,16,2304]{2,1,0:T(8,128)(2,1)S(1)}, bf16[2,16,2304]{2,1,0:T(8,128)(2,1)S(1)}, u32[]{:S(2)}, u32[]{:S(2)}) collective-permute-start(bf16[2,16,2304]{2,1,0:T(8,128)(2,1)S(1)} %add_convert_fusion.5), channel_id=1, source_target_pairs={{0,16},{4,20},{8,24},{12,28},{16,0},{20,4},{24,8},{28,12},{1,17},{... | collective-permute-start | bytes 442376 | tf_op jit(solution)/shard_map/ppermute | solution.py:37
  135.5 6.2 %collective-permute-start.34 = (bf16[16,2304]{1,0:T(8,128)(2,1)S(1)}, bf16[16,2304]{1,0:T(8,128)(2,1)S(1)}, u32[]{:S(2)}, u32[]{:S(2)}) collective-permute-start(bf16[16,2304]{1,0:T(8,128)(2,1)S(1)} %get-tuple-element.150), channel_id=1, source_target_pairs={{0,2},{1,3},{2,0},{3,1},{4,6},{5,7},{6,4},{7,5},{8,10},{9,11},{10,... | collective-permute-start | bytes 221192 | tf_op jit(solution)/shard_map/ppermute | solution.py:37
  138.8 6.3 %collective-permute-start.35 = (bf16[16,2304]{1,0:T(8,128)(2,1)S(1)}, bf16[16,2304]{1,0:T(8,128)(2,1)S(1)}, u32[]{:S(2)}, u32[]{:S(2)}) collective-permute-start(bf16[16,2304]{1,0:T(8,128)(2,1)S(1)} %get-tuple-element.149), channel_id=1, source_target_pairs={{0,3},{1,2},{2,1},{3,0},{4,7},{5,6},{6,5},{7,4},{8,11},{9,10},{10,... | collective-permute-start | bytes 221192 | tf_op jit(solution)/shard_map/ppermute | solution.py:37
  140.3 5.2 %collective-permute-start.30 = (bf16[16,2304]{1,0:T(8,128)(2,1)S(1)}, bf16[16,2304]{1,0:T(8,128)(2,1)S(1)}, u32[]{:S(2)}, u32[]{:S(2)}) collective-permute-start(bf16[16,2304]{1,0:T(8,128)(2,1)S(1)} %get-tuple-element.151), channel_id=1, source_target_pairs={{0,1},{1,0},{2,3},{3,2},{4,5},{5,4},{6,7},{7,6},{8,9},{9,8},{10,11... | collective-permute-start | bytes 221192 | tf_op jit(solution)/shard_map/ppermute | solution.py:37
  145.5 15.3 %collective-permute-start.36 = (bf16[4,16,2304]{2,1,0:T(8,128)(2,1)S(1)}, bf16[4,16,2304]{2,1,0:T(8,128)(2,1)S(1)}, u32[]{:S(2)}, u32[]{:S(2)}) collective-permute-start(bf16[4,16,2304]{2,1,0:T(8,128)(2,1)S(1)} %pad_maximum_fusion.2), channel_id=1, source_target_pairs={{0,4},{4,0},{8,12},{12,8},{16,20},{20,16},{24,28},{28,24},{1,5},{5... | collective-permute-start | bytes 884744 | tf_op jit(solution)/shard_map/ppermute | solution.py:37
  172.3 11.5 %collective-permute-start.41 = (bf16[304,384]{1,0:T(8,128)(2,1)S(1)}, bf16[304,384]{1,0:T(8,128)(2,1)S(1)}, u32[]{:S(2)}, u32[]{:S(2)}) collective-permute-start(bf16[304,384]{1,0:T(8,128)(2,1)S(1)} %get-tuple-element.73), channel_id=1, source_target_pairs={{0,16},{4,20},{8,24},{12,28},{16,0},{20,4},{24,8},{28,12},{1,17},{... | collective-permute-start | bytes 700424 | tf_op jit(solution)/shard_map/ppermute | solution.py:37
  180.3 8.6 %collective-permute-start.39 = (bf16[304,384]{1,0:T(8,128)(2,1)S(1)}, bf16[304,384]{1,0:T(8,128)(2,1)S(1)}, u32[]{:S(2)}, u32[]{:S(2)}) collective-permute-start(bf16[304,384]{1,0:T(8,128)(2,1)S(1)} %get-tuple-element.70), channel_id=1, source_target_pairs={{0,8},{4,12},{8,0},{12,4},{16,24},{20,28},{24,16},{28,20},{1,9},{5... | collective-permute-start | bytes 700424 | tf_op jit(solution)/shard_map/ppermute | solution.py:37
  180.8 17.0 %collective-permute-start.38 = (bf16[304,384]{1,0:T(8,128)(2,1)S(1)}, bf16[304,384]{1,0:T(8,128)(2,1)S(1)}, u32[]{:S(2)}, u32[]{:S(2)}) collective-permute-start(bf16[304,384]{1,0:T(8,128)(2,1)S(1)} %get-tuple-element.68), channel_id=1, source_target_pairs={{0,8},{4,12},{8,0},{12,4},{16,24},{20,28},{24,16},{28,20},{1,9},{5... | collective-permute-start | bytes 700424 | tf_op jit(solution)/shard_map/ppermute | solution.py:37
  182.3 8.2 %collective-permute-start.43 = (bf16[304,384]{1,0:T(8,128)(2,1)S(1)}, bf16[304,384]{1,0:T(8,128)(2,1)S(1)}, u32[]{:S(2)}, u32[]{:S(2)}) collective-permute-start(bf16[304,384]{1,0:T(8,128)(2,1)S(1)} %get-tuple-element.74), channel_id=1, source_target_pairs={{0,16},{4,20},{8,24},{12,28},{16,0},{20,4},{24,8},{28,12},{1,17},{... | collective-permute-start | bytes 700424 | tf_op jit(solution)/shard_map/ppermute | solution.py:37
  183.9 13.8 %collective-permute-start.42 = (bf16[304,384]{1,0:T(8,128)(2,1)S(1)}, bf16[304,384]{1,0:T(8,128)(2,1)S(1)}, u32[]{:S(2)}, u32[]{:S(2)}) collective-permute-start(bf16[304,384]{1,0:T(8,128)(2,1)S(1)} %add_convert_fusion.1), channel_id=1, source_target_pairs={{0,8},{4,12},{8,0},{12,4},{16,24},{20,28},{24,16},{28,20},{1,9},{5... | collective-permute-start | bytes 700424 | tf_op jit(solution)/shard_map/ppermute | solution.py:37
  188.9 8.9 %collective-permute-start.40 = (bf16[304,384]{1,0:T(8,128)(2,1)S(1)}, bf16[304,384]{1,0:T(8,128)(2,1)S(1)}, u32[]{:S(2)}, u32[]{:S(2)}) collective-permute-start(bf16[304,384]{1,0:T(8,128)(2,1)S(1)} %add_convert_fusion.3), channel_id=1, source_target_pairs={{0,16},{4,20},{8,24},{12,28},{16,0},{20,4},{24,8},{28,12},{1,17},{... | collective-permute-start | bytes 700424 | tf_op jit(solution)/shard_map/ppermute | solution.py:37
  199.5 11.3 %collective-permute-start.45 = (bf16[160,384]{1,0:T(8,128)(2,1)S(1)}, bf16[160,384]{1,0:T(8,128)(2,1)S(1)}, u32[]{:S(2)}, u32[]{:S(2)}) collective-permute-start(bf16[160,384]{1,0:T(8,128)(2,1)S(1)} %get-tuple-element.136), channel_id=1, source_target_pairs={{0,1},{1,0},{2,3},{3,2},{4,5},{5,4},{6,7},{7,6},{8,9},{9,8},{10,11... | collective-permute-start | bytes 368648 | tf_op jit(solution)/shard_map/ppermute | solution.py:37
  199.6 12.4 %collective-permute-start.46 = (bf16[160,384]{1,0:T(8,128)(2,1)S(1)}, bf16[160,384]{1,0:T(8,128)(2,1)S(1)}, u32[]{:S(2)}, u32[]{:S(2)}) collective-permute-start(bf16[160,384]{1,0:T(8,128)(2,1)S(1)} %get-tuple-element.138), channel_id=1, source_target_pairs={{0,2},{1,3},{2,0},{3,1},{4,6},{5,7},{6,4},{7,5},{8,10},{9,11},{10,... | collective-permute-start | bytes 368648 | tf_op jit(solution)/shard_map/ppermute | solution.py:37
  201.8 10.2 %collective-permute-start.47 = (bf16[160,384]{1,0:T(8,128)(2,1)S(1)}, bf16[160,384]{1,0:T(8,128)(2,1)S(1)}, u32[]{:S(2)}, u32[]{:S(2)}) collective-permute-start(bf16[160,384]{1,0:T(8,128)(2,1)S(1)} %get-tuple-element.137), channel_id=1, source_target_pairs={{0,3},{1,2},{2,1},{3,0},{4,7},{5,6},{6,5},{7,4},{8,11},{9,10},{10,... | collective-permute-start | bytes 368648 | tf_op jit(solution)/shard_map/ppermute | solution.py:37
  212.1 8.1 %collective-permute-start.48 = (bf16[160,384]{1,0:T(8,128)(2,1)S(1)}, bf16[160,384]{1,0:T(8,128)(2,1)S(1)}, u32[]{:S(2)}, u32[]{:S(2)}) collective-permute-start(bf16[160,384]{1,0:T(8,128)(2,1)S(1)} %fusion.4), channel_id=1, source_target_pairs={{0,3},{1,2},{2,1},{3,0},{4,7},{5,6},{6,5},{7,4},{8,11},{9,10},{10,... | collective-permute-start | bytes 368648 | tf_op jit(solution)/shard_map/ppermute | solution.py:37
  214.4 10.8 %collective-permute-start.49 = (bf16[160,384]{1,0:T(8,128)(2,1)S(1)}, bf16[160,384]{1,0:T(8,128)(2,1)S(1)}, u32[]{:S(2)}, u32[]{:S(2)}) collective-permute-start(bf16[160,384]{1,0:T(8,128)(2,1)S(1)} %fusion.4), channel_id=1, source_target_pairs={{0,2},{1,3},{2,0},{3,1},{4,6},{5,7},{6,4},{7,5},{8,10},{9,11},{10,... | collective-permute-start | bytes 368648 | tf_op jit(solution)/shard_map/ppermute | solution.py:37
  216.0 9.2 %collective-permute-start.50 = (bf16[160,384]{1,0:T(8,128)(2,1)S(1)}, bf16[160,384]{1,0:T(8,128)(2,1)S(1)}, u32[]{:S(2)}, u32[]{:S(2)}) collective-permute-start(bf16[160,384]{1,0:T(8,128)(2,1)S(1)} %fusion.4), channel_id=1, source_target_pairs={{0,1},{1,0},{2,3},{3,2},{4,5},{5,4},{6,7},{7,6},{8,9},{9,8},{10,11... | collective-permute-start | bytes 368648 | tf_op jit(solution)/shard_map/ppermute | solution.py:37
  217.7 13.3 %collective-permute-start.37 = (bf16[8,13,13,384]{3,0,2,1:T(8,128)(2,1)}, bf16[8,13,13,384]{3,0,2,1:T(8,128)(2,1)}, u32[]{:S(2)}, u32[]{:S(2)}) collective-permute-start(bf16[8,13,13,384]{3,0,2,1:T(8,128)(2,1)} %broadcast_select_fusion.1), channel_id=1, source_target_pairs={{0,4},{4,0},{8,12},{12,8},{16,20},{20,16},{24,28},{28,24},{1,5},{5... | collective-permute-start | bytes 3115016 | tf_op jit(solution)/shard_map/ppermute | solution.py:37
  (64 other events, 615.8 us)
where the time goes:
time: 236 us
  waiting for transfers between devices  74 us (31%)
  starting transfers between devices  53.5 us (23%)
  Pallas kernels  42.3 us (18%)
  local copies, waits for them, and re-layouts  31.3 us (13%)
  other arithmetic  25.9 us (11%)
  matrix products  6.82 us (3%)
    ppermute x52, waiting for transfers between devices, trade(): return lax.ppermute(value, axis, [(i, i ^ bit) for i in range(size)])  74 us
    ppermute x52, starting transfers between devices, trade(): return lax.ppermute(value, axis, [(i, i ^ bit) for i in range(size)])  53.5 us
    unnamed x130, local copies, waits for them, and re-layouts  23.9 us
    pallas_call x2, Pallas kernels, fc_update(): pl.pallas_call(kernel, grid_spec=pltpu.PrefetchScalarGridSpec(num_scalar_...  13.9 us
    pallas_call x1, Pallas kernels, conv_backward(): pl.pallas_call(kernel, in_specs=[SCALARS] * 3 + [WHOLE] * (planes + 6), o...  9.62 us
    pallas_call x1, Pallas kernels, conv_forward(): pl.pallas_call(kernel, in_specs=[SCALARS] * 2 + [WHOLE] * (1 + count), ou...  7.79 us
    select_n x10, other arithmetic, four_by_four(): mine = lambda a, b: jnp.where(core == 0, a, b)  6.91 us
    conv_general_dilated x1, matrix products, four_by_four(): lax.conv_general_dilated(conv_grad, kernel[::-1, ::-1], (1, 1), 'SAME', d...  6.82 us
  transfers between devices with their start and end apart: 52, of which 24 were waited for; matrix products, arithmetic and copies ran while one was open for 15% of the time, Pallas kernels for 17%

commit v1 on v0

--- a/solution.py
+++ b/solution.py
@@ -37,10 +37,14 @@
     return lax.ppermute(value, axis, [(i, i ^ bit) for i in range(size)])
 
 
+def tie(*values):
+    return lax.optimization_barrier(values)
+
+
 def gather_chips(first, second, chips):
     if chips == 4:
+        first_y = trade(first, "chan", 4)
         second_x = trade(second, "chan", 2)
-        first_y = trade(first, "chan", 4)
         first_x = trade(first, "chan", 2)
         second_y = trade(second, "chan", 4)
         first_d = trade(first_y, "chan", 2)
@@ -55,14 +59,17 @@
     return (a.astype(WIDE) + b.astype(WIDE)).astype(LOW)
 
 
-def scatter_chips(parts, chips):
+def scatter_chips(parts, chips, later=lambda gate, value: (gate, value)):
     if chips == 4:
         from_x = trade(parts[3][0], "chan", 2)
         from_y = trade(parts[3][1], "chan", 4)
         first_x = trade(parts[1][0], "chan", 2)
         second_y = trade(parts[2][1], "chan", 4)
-        first_y = trade(add_low(parts[2][0], from_x), "chan", 4)
-        second_x = trade(add_low(parts[1][1], from_y), "chan", 2)
+        to_y = add_low(parts[2][0], from_x)
+        first_y = trade(to_y, "chan", 4)
+        to_x = add_low(parts[1][1], from_y)
+        to_x, first_y = later(to_x, first_y)
+        second_x = trade(to_x, "chan", 2)
         return (parts[0][0], first_x, first_y), (parts[0][1], second_x, second_y)
     got = [(trade(parts[j][0], "chan", 2 * j), trade(parts[j][1], "chan", 2 * j)) for j in range(1, chips)]
     return (
@@ -103,28 +110,63 @@
     return pltpu.roll(value, ((target - source) * width) % LANES, 1)
 
 
-def fc_prepare(fc_weight, core):
-    towers, rows, units = fc_weight.shape
+def pack_kernels(conv_weight, conv_bias, stitch_conv, core):
+    _, lines, width_in = conv_weight.shape
+    shard = conv_bias.shape[-1]
+
+    def kernel(core_ref, w_ref, bias_ref, mix_ref, keep_ref, give_ref):
+        first = core_ref[0] == 0
+        for a, out in enumerate((keep_ref, give_ref)):
+            out[:lines, :] = w_ref[core_ref[0] ^ a].astype(LOW)
+            choose = lambda p, q: jnp.where(first, *((q, p) if a else (p, q)))
+            rows = [
+                choose(bias_ref[0:1, :], bias_ref[1:2, :]),
+                choose(mix_ref[0, 0:1, :], mix_ref[1, 1:2, :]),
+                choose(mix_ref[0, 1:2, :], mix_ref[1, 0:1, :]),
+                choose(mix_ref[1, 0:1, :], mix_ref[0, 1:2, :]),
+                jnp.zeros((EXTRA - 4, shard), WIDE),
+            ]
+            out[lines:, :] = jnp.zeros((EXTRA, width_in), LOW)
+            out[lines:, :shard] = jnp.concatenate(rows, axis=0).astype(LOW)
+
+    return pl.pallas_call(
+        kernel,
+        in_specs=[SCALARS] + [WHOLE] * 3,
+        out_specs=[WHOLE] * 2,
+        out_shape=[like((lines + EXTRA, width_in), LOW)] * 2,
+        compiler_params=pltpu.CompilerParams(vmem_limit_bytes=8 << 20),
+        cost_estimate=pl.CostEstimate(flops=0, bytes_accessed=8 * lines * width_in, transcendentals=0),
+    )(core, conv_weight, conv_bias, stitch_conv)
+
+
+def fc_prepare(fc_weight, core, gate):
+    _, rows, units = fc_weight.shape
     width = rows // CELLS
-
-    def kernel(core_ref, w_ref, o_ref):
-        for cell in range(CELLS):
-            o_ref[0, pl.ds(cell * width, width), :] = w_ref[
-                0, pl.ds(cell, width, stride=CELLS), :
-            ].astype(LOW)
+    fc_weight = pltpu.with_memory_space_constraint(fc_weight, pltpu.HBM)
+
+    def kernel(core_ref, own_ref, other_ref, _, keep_ref, give_ref):
+        for source, out in ((own_ref, keep_ref), (other_ref, give_ref)):
+            for cell in range(CELLS):
+                out[pl.ds(cell * width, width), :] = source[
+                    0, pl.ds(cell, width, stride=CELLS), :
+                ].astype(LOW)
 
     return pl.pallas_call(
         kernel,
         grid_spec=pltpu.PrefetchScalarGridSpec(
             num_scalar_prefetch=1,
-            grid=(towers, units // LANES),
-            in_specs=[pl.BlockSpec((1, rows, LANES), lambda i, j, core: (core[0] ^ i, 0, j))],
-            out_specs=pl.BlockSpec((1, rows, LANES), lambda i, j, core: (i, 0, j)),
+            grid=(units // LANES,),
+            in_specs=[
+                pl.BlockSpec((1, rows, LANES), lambda j, core: (core[0], 0, j)),
+                pl.BlockSpec((1, rows, LANES), lambda j, core: (core[0] ^ 1, 0, j)),
+                pl.BlockSpec(memory_space=pl.ANY),
+            ],
+            out_specs=[pl.BlockSpec((rows, LANES), lambda j, core: (0, j))] * 2,
         ),
-        out_shape=like(fc_weight.shape, LOW),
-        compiler_params=pltpu.CompilerParams(vmem_limit_bytes=8 << 20),
+        out_shape=[like((rows, units), LOW)] * 2,
+        compiler_params=pltpu.CompilerParams(vmem_limit_bytes=12 << 20),
         cost_estimate=pl.CostEstimate(flops=0, bytes_accessed=6 * fc_weight.size, transcendentals=0),
-    )(core, fc_weight)
+    )(core, fc_weight, fc_weight, gate)
 
 
 def conv_forward(images, parts, core, chip):
@@ -137,8 +179,9 @@
 
     def kernel(core_ref, chip_ref, x_ref, *refs):
         pieces = refs[:count]
-        pooled_ref, slope_ref, small_ref = refs[count : count + 3]
-        joined, weights, acc, act = refs[count + 3 :]
+        pooled_ref, slope_out, small_ref = refs[count : count + 3]
+        weights, acc, slope_ref, sems = refs[count + 3 :]
+        copies = [pltpu.make_async_copy(slope_ref.at[h], slope_out.at[h], sems.at[h]) for h in range(side)]
         lane = lax.broadcasted_iota(jnp.int32, (EXTRA, LANES), 1) // shard
         smalls = [jnp.zeros((EXTRA, LANES), WIDE) for _ in range(full // LANES)]
         for j in range(count // 2):
@@ -147,57 +190,54 @@
                 where = (chip_ref[0] ^ j) * 2 + (core_ref[0] ^ r)
                 at = pl.ds(pl.multiple_of(where * shard, shard), shard)
                 for tap in range(TAPS):
-                    weights[tap // 3, at, (tap % 3) * width_in : (tap % 3 + 1) * width_in] = piece[
-                        tap * shard : (tap + 1) * shard, :
-                    ]
+                    weights[at, tap * width_in : (tap + 1) * width_in] = piece[tap * shard : (tap + 1) * shard, :]
                 row = piece[TAPS * shard :, :LANES].astype(WIDE)
-                copies = row
+                spread = row
                 for s in range(1, slots):
-                    copies = copies + pltpu.roll(row, s * shard, 1)
+                    spread = spread + pltpu.roll(row, s * shard, 1)
                 for v in range(len(smalls)):
-                    smalls[v] = jnp.where(lane + v * slots == where, copies, smalls[v])
+                    smalls[v] = jnp.where(lane + v * slots == where, spread, smalls[v])
         for v, value in enumerate(smalls):
             small_ref[:, v * LANES : (v + 1) * LANES] = value
-        for right in range(3):
-            joined[:, :, :, right * width_in : (right + 1) * width_in] = x_ref[:, right : right + side]
-        for down in range(3):
-            part = dot(
-                joined[down : down + side].reshape(side * side * group, 3 * width_in),
-                weights[down],
-                NT,
-            )
-            if down == 0:
-                acc[...] = part
-            else:
-                acc[...] += part
+        line = side * group
         bias = small_ref[0:1, :]
-        line = side * group
+        for low, high_row in ((0, (side + 1) // 2), ((side + 1) // 2, side)):
+            tall = high_row - low
+            windows = [
+                x_ref[tap // 3 + low : tap // 3 + high_row, tap % 3 : tap % 3 + side].reshape(tall * line, width_in)
+                for tap in range(TAPS)
+            ]
+            acc[low * line : high_row * line, :] = dot(jnp.concatenate(windows, axis=1), weights[...], NT)
         for h in range(side):
             value, slope = silu_and_slope(acc[h * line : (h + 1) * line, :] + bias)
             slope_ref[h] = slope.reshape(side, group, full).astype(LOW)
-            act[h] = value.reshape(side, group, full)
+            acc[h * line : (h + 1) * line, :] = value
+            copies[h].start()
+        cell = lambda h, w: acc[(h * side + w) * group : (h * side + w + 1) * group, :]
         for r in range(6):
-            rows = act[2 * r] + act[2 * r + 1] + act[2 * r + 2]
+            rows = [cell(2 * r, w) + cell(2 * r + 1, w) + cell(2 * r + 2, w) for w in range(side)]
             for c in range(6):
                 pooled_ref[6 * r + c] = (rows[2 * c] + rows[2 * c + 1] + rows[2 * c + 2]) * (1.0 / 9.0)
+        for copy in copies:
+            copy.wait()
 
     area = side * side * group
     return pl.pallas_call(
         kernel,
         in_specs=[SCALARS] * 2 + [WHOLE] * (1 + count),
-        out_specs=[WHOLE] * 3,
+        out_specs=[WHOLE, pl.BlockSpec(memory_space=pltpu.HBM), WHOLE],
         out_shape=[
             like((CELLS, group, full), WIDE),
             like((side, side, group, full), LOW),
             like((EXTRA, full), WIDE),
         ],
         scratch_shapes=[
-            pltpu.VMEM((high, side, group, 3 * width_in), LOW),
-            pltpu.VMEM((3, full, 3 * width_in), LOW),
+            pltpu.VMEM((full, TAPS * width_in), LOW),
             pltpu.VMEM((area, full), WIDE),
-            pltpu.VMEM((side, side, group, full), WIDE),
+            pltpu.VMEM((side, side, group, full), LOW),
+            pltpu.SemaphoreType.DMA((side,)),
         ],
-        compiler_params=pltpu.CompilerParams(vmem_limit_bytes=28 << 20),
+        compiler_params=pltpu.CompilerParams(vmem_limit_bytes=16 << 20),
         cost_estimate=pl.CostEstimate(
             flops=2 * area * TAPS * width_in * full,
             bytes_accessed=2 * images.size + 2 * area * full,
@@ -206,19 +246,26 @@
     )(core, chip, images, *parts)
 
 
-def mix_pieces(pooled, other, small, plane, planes):
+def turn(value):
+    half = value.shape[0] // 2
+    return jnp.concatenate([value[half:], value[:half]], axis=0)
+
+
+def mix_pieces(pooled, other, small, core, plane, planes):
     cells, group, full = pooled.shape
     width = full // planes
     per = LANES // width
 
-    def kernel(plane_ref, a_ref, b_ref, small_ref, *refs):
+    def kernel(core_ref, plane_ref, a_ref, b_ref, small_ref, *refs):
         outs, held = refs[:planes], refs[planes]
+        first = core_ref[0] == 0
         place = lane_place(width)
         one, two = small_ref[1:2, :], small_ref[2:3, :]
         for start in range(0, cells, per):
             mixed = [
-                one * a_ref[start + i] + two * b_ref[start + i] for i in range(per)
+                one * a_ref[start + i] + two * turn(b_ref[start + i]) for i in range(per)
             ]
+            mixed = [jnp.where(first, value, turn(value)) for value in mixed]
             for p in range(planes):
                 column, source = divmod(p * width, LANES)
                 out = None
@@ -234,13 +281,13 @@
     rows = cells * width
     return pl.pallas_call(
         kernel,
-        in_specs=[SCALARS] + [WHOLE] * 3,
+        in_specs=[SCALARS] * 2 + [WHOLE] * 3,
         out_specs=[WHOLE] * planes,
         out_shape=[like((group, rows), LOW)] * planes,
         scratch_shapes=[pltpu.VMEM((planes, group, rows), LOW)],
         compiler_params=pltpu.CompilerParams(vmem_limit_bytes=8 << 20),
         cost_estimate=pl.CostEstimate(flops=4 * pooled.size, bytes_accessed=8 * pooled.size, transcendentals=0),
-    )(plane, pooled, other, small)
+    )(core, plane, pooled, other, small)
 
 
 def fc_forward(gathered, weights, chip, chips, planes):
@@ -321,7 +368,7 @@
     )(chip, *grads, crossed, *weights)
 
 
-def conv_backward(own, other, pooled, pooled_other, slope, images, small, core, chip, plane):
+def conv_backward(gate, own, other, pooled, pooled_other, slope, images, small, core, chip, plane):
     planes = len(own)
     cells, group, full = pooled.shape
     high, _, _, width_in = images.shape
@@ -337,16 +384,18 @@
     def covering(h):
         return [r for r in range(6) if 2 * r <= h <= 2 * r + 2]
 
-    def kernel(core_ref, chip_ref, plane_ref, *refs):
+    def kernel(core_ref, chip_ref, plane_ref, gate_ref, *refs):
         own_refs, other_ref = refs[:planes], refs[planes]
         a_ref, b_ref, slope_ref, x_ref, small_ref = refs[planes + 1 : planes + 6]
         outs = refs[planes + 6 : planes + 6 + shards]
         grad_ref = refs[planes + 6 + shards]
         flat, pool_grad, turned, taps, smalls = refs[planes + 7 + shards :]
         place = lane_place(width)
+        first = core_ref[0] == 0
         for k in range(planes):
-            flat[0, plane_ref[0] ^ k] = own_refs[k][...].astype(WIDE)
-            flat[1, plane_ref[0] ^ k] = other_ref[k].astype(WIDE)
+            for t, value in enumerate((own_refs[k][...], other_ref[k])):
+                value = value.astype(WIDE)
+                flat[t, plane_ref[0] ^ k] = jnp.where(first, value, turn(value))
         one, back = small_ref[1:2, :] * (1.0 / 9.0), small_ref[3:4, :] * (1.0 / 9.0)
         sum_one = jnp.zeros((group, full), WIDE)
         sum_two = jnp.zeros((group, full), WIDE)
@@ -364,7 +413,7 @@
                     blocks.append(out)
                 both.append(jnp.concatenate(blocks, axis=1))
             sum_one += both[0] * a_ref[cell]
-            sum_two += both[0] * b_ref[cell]
+            sum_two += both[0] * turn(b_ref[cell])
             pool_grad[cell] = one * both[0] + back * both[1]
         sum_bias = jnp.zeros((group, full), WIDE)
         for h in range(side):
@@ -375,9 +424,14 @@
                 grad_ref[h, w] = value
                 sum_bias += value.astype(WIDE)
         turned[...] = grad_ref[...].reshape(area, full).T
-        for tap in range(TAPS):
-            window = x_ref[tap // 3 : tap // 3 + side, tap % 3 : tap % 3 + side]
-            taps[tap] = dot(turned[...], window.reshape(area, width_in), NN).astype(LOW)
+        for start in range(0, TAPS, 2):
+            some = range(start, min(start + 2, TAPS))
+            windows = [
+                x_ref[tap // 3 : tap // 3 + side, tap % 3 : tap % 3 + side].reshape(area, width_in) for tap in some
+            ]
+            part = dot(turned[...], jnp.concatenate(windows, axis=1), NN)
+            for n, tap in enumerate(some):
+                taps[tap] = part[:, n * width_in : (n + 1) * width_in].astype(LOW)
         sums = [jnp.sum(value, axis=0, keepdims=True) for value in (sum_bias, sum_one, sum_two)]
         sums = jnp.concatenate(sums + [jnp.zeros((EXTRA - 3, full), WIDE)], axis=0)
         for v in range(columns):
@@ -400,7 +454,7 @@
 
     return pl.pallas_call(
         kernel,
-        in_specs=[SCALARS] * 3 + [WHOLE] * (planes + 6),
+        in_specs=[SCALARS] * 3 + [pl.BlockSpec(memory_space=pl.ANY)] + [WHOLE] * (planes + 6),
         out_specs=[WHOLE] * (shards + 1),
         out_shape=[like((TAPS * shard + EXTRA, width_in), LOW)] * shards
         + [like((side, side, group, full), LOW)],
@@ -411,55 +465,144 @@
             pltpu.VMEM((TAPS, full, width_in), LOW),
             pltpu.VMEM((columns, EXTRA, LANES), WIDE),
         ],
-        compiler_params=pltpu.CompilerParams(vmem_limit_bytes=28 << 20),
+        compiler_params=pltpu.CompilerParams(vmem_limit_bytes=14 << 20),
         cost_estimate=pl.CostEstimate(
             flops=2 * area * TAPS * width_in * full,
             bytes_accessed=2 * images.size + 6 * area * full,
             transcendentals=0,
         ),
-    )(core, chip, plane, *own, other, pooled, pooled_other, slope, images, small)
-
-
-def fc_update(weight, moment, rows, grads, core, which, previous):
-    towers, depth, units = weight.shape
+    )(core, chip, plane, gate, *own, other, pooled, pooled_other, slope, images, small)
+
+
+def fc_update(weight, moment, rows, grads, core, which, part, previous, gate):
+    _, depth, units = weight.shape
     width = depth // CELLS
     n_images = rows.shape[0]
     planes = len(grads)
     block = n_images // planes
+    columns = units // LANES
+    steps = 4
+    few = width // 2
+    tall = depth // 2 // steps
+    weight, moment = (pltpu.with_memory_space_constraint(value, pltpu.HBM) for value in (weight, moment))
 
     def kernel(core_ref, w_ref, m_ref, rows_ref, *refs):
         grad_refs = refs[:planes]
-        new_w, new_m, product, joined = refs[-4:]
-        for k in range(planes):
-            joined[pl.ds(k * block, block), :] = grad_refs[k][0]
-        product[...] = dot(rows_ref[...], joined[...], TN)
-        for cell in range(CELLS):
-            at = pl.ds(cell, width, stride=CELLS)
-            fresh = MOMENTUM * m_ref[0, at, :] + product[pl.ds(cell * width, width), :]
-            new_m[0, at, :] = fresh
-            new_w[0, at, :] = w_ref[0, at, :] - LEARN_RATE * fresh
-
-    big = pl.BlockSpec((1, depth, LANES), lambda j, core: (core[0] ^ which, 0, j))
-    grad_spec = pl.BlockSpec((1, block, LANES), lambda j, core: (which, 0, j))
+        new_w, new_m, token, joined, product = refs[-5:]
+        step = pl.program_id(0)
+
+        @pl.when(step == 0)
+        def _():
+            token[...] = jnp.zeros_like(token)
+            for k in range(planes):
+                joined[pl.ds(k * block, block), :] = grad_refs[k][which]
+            for v in range(columns):
+                grad = dot(rows_ref[...], joined[:, v * LANES : (v + 1) * LANES], TN)
+                for cell in range(CELLS):
+                    start = cell * width + part * few
+                    product[v, pl.ds(cell, few, stride=CELLS), :] = grad[start : start + few]
+
+        at = pl.ds(pl.multiple_of(step * tall, tall), tall)
+        for v in range(columns):
+            lanes = slice(v * LANES, (v + 1) * LANES)
+            fresh = MOMENTUM * m_ref[0, :, lanes] + product[v, at, :]
+            new_m[0, :, lanes] = fresh
+            new_w[0, :, lanes] = w_ref[0, :, lanes] - LEARN_RATE * fresh
+
+    big = pl.BlockSpec((1, tall, units), lambda s, core: (core[0] ^ which, part * steps + s, 0))
+    fixed = lambda shape: pl.BlockSpec(shape, lambda s, core: (0,) * len(shape))
+    anywhere = pl.BlockSpec(memory_space=pl.ANY)
     extra = [] if previous is None else list(previous)
     return pl.pallas_call(
         kernel,
         grid_spec=pltpu.PrefetchScalarGridSpec(
             num_scalar_prefetch=1,
-            grid=(units // LANES,),
-            in_specs=[big, big, pl.BlockSpec((n_images, depth), lambda j, core: (0, 0))]
-            + [grad_spec] * planes
-            + [pl.BlockSpec(memory_space=pl.ANY)] * len(extra),
-            out_specs=[big, big],
-            scratch_shapes=[pltpu.VMEM((depth, LANES), WIDE), pltpu.VMEM((n_images, LANES), LOW)],
+            grid=(steps,),
+            in_specs=[big, big, fixed(rows.shape)]
+            + [fixed(value.shape) for value in grads]
+            + [anywhere] * (len(extra) + 1),
+            out_specs=[big, big, fixed((8, LANES))],
+            scratch_shapes=[
+                pltpu.VMEM((n_images, units), LOW),
+                pltpu.VMEM((columns, depth // 2, LANES), WIDE),
+            ],
         ),
-        out_shape=[like(weight.shape, WIDE)] * 2,
+        out_shape=[like(weight.shape, WIDE)] * 2 + [like((8, LANES), WIDE)],
         input_output_aliases={} if previous is None else {4 + planes: 0, 5 + planes: 1},
-        compiler_params=pltpu.CompilerParams(vmem_limit_bytes=20 << 20),
+        compiler_params=pltpu.CompilerParams(vmem_limit_bytes=14 << 20),
         cost_estimate=pl.CostEstimate(
-            flops=2 * n_images * depth * units, bytes_accessed=16 * depth * units, transcendentals=0
+            flops=2 * n_images * depth * units, bytes_accessed=8 * depth * units, transcendentals=0
         ),
-    )(core, weight, moment, rows, *grads, *extra)
+    )(core, weight, moment, rows, *grads, *extra, gate)
+
+
+def order_towers(own, other, core):
+    def kernel(core_ref, own_ref, other_ref, out_ref):
+        out_ref[core_ref[0]] = own_ref[...]
+        out_ref[1 - core_ref[0]] = other_ref[...]
+
+    return pl.pallas_call(
+        kernel,
+        in_specs=[SCALARS, WHOLE, WHOLE],
+        out_specs=WHOLE,
+        out_shape=like((2, *own.shape), own.dtype),
+        compiler_params=pltpu.CompilerParams(vmem_limit_bytes=8 << 20),
+        cost_estimate=pl.CostEstimate(flops=0, bytes_accessed=8 * own.size, transcendentals=0),
+    )(core, own, other)
+
+
+def small_update(gates, pieces, lines, params, moments, core, plane):
+    planes = len(pieces)
+    height, width_in = pieces[0].shape
+    shard = params[1].shape[-1]
+    units = params[3].shape[-1]
+    count = lines - EXTRA
+    rates = (LEARN_RATE, BIAS_RATE, STITCH_RATE, STITCH_RATE)
+
+    def kernel(core_ref, plane_ref, done_ref, ready_ref, *refs):
+        piece_refs = refs[:planes]
+        p_refs, m_refs = refs[planes : planes + 4], refs[planes + 4 : planes + 8]
+        new_p, new_m = refs[planes + 8 : planes + 12], refs[planes + 12 : planes + 16]
+        whole = refs[planes + 16]
+        for k in range(planes):
+            at = pl.ds(pl.multiple_of((plane_ref[0] ^ k) * height, height), height)
+            whole[at, :] = piece_refs[k][...].astype(WIDE)
+
+        def advance(which, at, grad):
+            fresh = MOMENTUM * m_refs[which][at] + grad
+            new_m[which][at] = fresh
+            new_p[which][at] = p_refs[which][at] - rates[which] * fresh
+
+        first = core_ref[0] == 0
+        for a in range(2):
+            advance(0, core_ref[0] ^ a, whole[a * lines : a * lines + count, :])
+        rows = [[whole[a * lines + count + i : a * lines + count + i + 1, :shard] for i in range(3)] for a in range(2)]
+        rows = [[jnp.where(first, rows[a][i], rows[1 - a][i]) for i in range(3)] for a in range(2)]
+        for t in range(2):
+            advance(1, (slice(t, t + 1), slice(None)), rows[t][0])
+            advance(2, (t, slice(t, t + 1), slice(None)), rows[t][1])
+            advance(2, (t, slice(1 - t, 2 - t), slice(None)), rows[t][2])
+        base = 2 * lines
+        parts, start = [], 0
+        while start < units:
+            step = min(width_in, units - start)
+            parts.append(whole[base : base + 4, :step])
+            base, start = base + 4, start + step
+        packed = jnp.concatenate(parts, axis=1) if len(parts) > 1 else parts[0]
+        for i in range(4):
+            row = jnp.where(first, packed[i : i + 1, :], packed[3 - i : 4 - i, :])
+            advance(3, (i // 2, slice(i % 2, i % 2 + 1), slice(None)), row)
+
+    out_shape = [like(value.shape, WIDE) for value in (*params, *moments)]
+    return pl.pallas_call(
+        kernel,
+        in_specs=[SCALARS] * 2 + [pl.BlockSpec(memory_space=pl.ANY)] * 2 + [WHOLE] * (planes + 8),
+        out_specs=[WHOLE] * 8,
+        out_shape=out_shape,
+        scratch_shapes=[pltpu.VMEM((planes * height, width_in), WIDE)],
+        compiler_params=pltpu.CompilerParams(vmem_limit_bytes=12 << 20),
+        cost_estimate=pl.CostEstimate(flops=0, bytes_accessed=24 * 2 * lines * width_in, transcendentals=0),
+    )(core, plane, *gates, *pieces, *params, *moments)
 
 
 def reorder(parts, place):
@@ -761,29 +904,23 @@
     units = fc_weight.shape[-1]
     half = planes // 2
 
-    kernel_rows = jnp.transpose(conv_weight, (0, 1, 2, 4, 3)).astype(LOW)
-    kernel_rows = kernel_rows.reshape(2, TAPS * shard, width_in)
-    straight = jnp.stack([stitch_conv[0, 0], stitch_conv[1, 1]])
-    crossed = jnp.stack([stitch_conv[0, 1], stitch_conv[1, 0]])
-    small = jnp.stack([conv_bias, straight, crossed, crossed[::-1]], axis=1).astype(LOW)
-    small = jnp.pad(small, ((0, 0), (0, EXTRA - 4), (0, width_in - shard)))
-    kernel_rows = jnp.concatenate([kernel_rows, small], axis=1)
-    keep = mine(kernel_rows[0], kernel_rows[1])
-    got = swap(mine(kernel_rows[1], kernel_rows[0]))
+    as_rows = lambda value: jnp.transpose(value, (0, 1, 2, 4, 3)).reshape(2, TAPS * shard, width_in)
+    keep, give = pack_kernels(as_rows(conv_weight), conv_bias, stitch_conv, core_at)
+    got = swap(give)
     kernel_parts = [part for pair in gather_chips(keep, got, chips) for part in pair]
-
-    keep = mine(images[:, 0], images[:, 1])
-    got = swap(mine(images[:, 1], images[:, 0]))
-    tower_images = jnp.concatenate([mine(keep, got), mine(got, keep)], axis=0)
-    tower_images = jnp.transpose(tower_images, (1, 2, 0, 3))
+    fc_own, fc_give = fc_prepare(fc_weight, core_at, kernel_parts[3])
+    fc_cross = swap(fc_give)
+
+    late_core, kernel_parts[3] = tie(core, kernel_parts[3])
+    towers = lax.optimization_barrier(jnp.transpose(images, (1, 2, 3, 0, 4)))
+    keep, give = (jnp.where(late_core == 0, towers[a], towers[1 - a]) for a in range(2))
+    tower_images = jnp.concatenate([keep, swap(give)], axis=2)
     tower_images = jnp.pad(tower_images, ((1, 1), (1, 1), (0, 0), (0, 0)))
-
-    fc_low = fc_prepare(fc_weight, core_at)
-    fc_own, fc_cross = fc_low[0], swap(fc_low[1])
 
     pooled, slope, small_all = conv_forward(tower_images, kernel_parts, core_at, chip_at)
     pooled_other = swap(pooled)
-    got = exchange_planes(mix_pieces(pooled, pooled_other, small_all, plane_at, planes))
+    pieces = mix_pieces(pooled, pooled_other, small_all, core_at, plane_at, planes)
+    got = exchange_planes(pieces)
     gathered = gather_chips(jnp.stack(got[:half]), jnp.stack(got[half:]), chips)
     tower_rows, *partial = fc_forward(
         [part for pair in gathered for part in pair], (fc_own, fc_cross), chip_at, chips, planes
@@ -808,32 +945,38 @@
     grads = exchange_planes([grad_low] * planes)
     grads_cross = swap(jnp.stack([value[1] for value in grads]))
 
+    step = done = None
+
+    def update_own(gate, value):
+        nonlocal step, done
+        *step, done = fc_update(fc_weight, fc_moment, tower_rows, grads, core_at, 0, 0, None, gate)
+        value, done = tie(value, done)
+        return gate, value
+
     blocks = fc_backward(grads, grads_cross, (fc_own, fc_cross), chip_at, chips, planes)
-    first, second = scatter_chips([blocks[2 * j : 2 * j + 2] for j in range(chips)], chips)
+    first, second = scatter_chips(
+        [blocks[2 * j : 2 * j + 2] for j in range(chips)], chips, later=update_own
+    )
     sums = [total([value[i] for value in part]).astype(LOW) for part in (first, second) for i in range(half)]
     mixed_grad = exchange_planes(sums)
+    *step, token = fc_update(fc_weight, fc_moment, tower_rows, grads, core_at, 0, 1, step, sums[-1])
+    mixed_grad[1], done, token = tie(mixed_grad[1], done, token)
+    done = done + token
     mixed_grad_other = swap(jnp.stack(mixed_grad))
 
     *blocks, conv_grad = conv_backward(
-        mixed_grad, mixed_grad_other, pooled, pooled_other, slope, tower_images, small_all, core_at, chip_at, plane_at
-    )
-    first, second = scatter_chips([blocks[2 * j : 2 * j + 2] for j in range(chips)], chips)
-    towers = jnp.stack([total(first).astype(LOW), swap(total(second).astype(LOW))])
-    lines = towers.shape[1]
-
-    packed = jnp.concatenate([stitch_fc_grad.reshape(-1), jnp.zeros((-4 * units) % width_in)])
-    packed = packed.astype(LOW).reshape(-1, width_in)
-    tail = (-(2 * lines + packed.shape[0])) % (planes * 16)
-    flat = jnp.concatenate([towers.reshape(-1, width_in), jnp.pad(packed, ((0, tail), (0, 0)))])
-    flat = flat.reshape(planes, -1, width_in)
-    quarters = [lax.dynamic_index_in_dim(flat, plane ^ k, 0, keepdims=False) for k in range(planes)]
-    quarter = total(exchange_planes(quarters)).astype(LOW)
-    whole = exchange_planes([quarter] * planes)
-    whole = jnp.concatenate(reorder(whole, plane)).astype(WIDE)
-    towers = whole[: 2 * lines].reshape(2, lines, width_in)
-    stitch_fc_grad = whole[2 * lines :].reshape(-1)[: 4 * units].reshape(2, 2, units)
-    stitch_fc_grad = mine(stitch_fc_grad, stitch_fc_grad[::-1, ::-1])
-    towers = mine(towers, towers[::-1])
+        done, mixed_grad, mixed_grad_other, pooled, pooled_other, slope, tower_images, small_all, core_at, chip_at, plane_at
+    )
+
+    def turned_conv(grad):
+        return lax.conv_general_dilated(
+            grad,
+            kernel[::-1, ::-1],
+            (1, 1),
+            "SAME",
+            dimension_numbers=("HWNC", "HWIO", "HWNC"),
+            preferred_element_type=WIDE,
+        ).astype(LOW)
 
     full_chan = conv_grad.shape[-1]
     ordered = reorder([(kernel_parts[2 * j], kernel_parts[2 * j + 1]) for j in range(chips)], chip)
@@ -841,45 +984,63 @@
     kernel = jnp.concatenate(
         [part[: TAPS * shard].reshape(3, 3, shard, width_in) for part in ordered], axis=2
     )
-    images_grad = lax.conv_general_dilated(
-        conv_grad,
-        kernel[::-1, ::-1],
-        (1, 1),
-        "SAME",
-        dimension_numbers=("HWNC", "HWIO", "HWNC"),
-        preferred_element_type=WIDE,
+    images_grad = None
+
+    def after_sums(gate, value):
+        nonlocal images_grad
+        gate, grad = tie(gate, conv_grad)
+        value, images_grad = tie(value, turned_conv(grad))
+        return gate, value
+
+    first, second = scatter_chips(
+        [blocks[2 * j : 2 * j + 2] for j in range(chips)],
+        chips,
+        later=after_sums,
+    )
+    towers = jnp.stack([total(first).astype(LOW), swap(total(second).astype(LOW))])
+    lines = towers.shape[1]
+
+    vectors = stitch_fc_grad.reshape(4, units)
+    packed = [vectors[:, at : at + width_in] for at in range(0, units, width_in)]
+    packed = jnp.concatenate(
+        [jnp.pad(value, ((0, 0), (0, width_in - value.shape[1]))) for value in packed]
     ).astype(LOW)
-    images_grad = jnp.transpose(images_grad, (2, 0, 1, 3))
-    keep = mine(images_grad[:per_core], images_grad[per_core:])
-    got = swap(mine(images_grad[per_core:], images_grad[:per_core]))
-    images_grad = jnp.stack([mine(keep, got), mine(got, keep)], axis=1)
-
-    step = fc_update(fc_weight, fc_moment, tower_rows, grads, core_at, 0, None)
-    new_fc_weight, new_fc_moment = fc_update(fc_weight, fc_moment, other_rows, grads, core_at, 1, step)
+    tail = (-(2 * lines + packed.shape[0])) % (planes * EXTRA)
+    flat = jnp.concatenate([towers.reshape(-1, width_in), jnp.pad(packed, ((0, tail), (0, 0)))])
+    flat = flat.reshape(planes, -1, width_in)
+    quarters = [lax.dynamic_index_in_dim(flat, plane ^ k, 0, keepdims=False) for k in range(planes)]
+    quarters = exchange_planes(quarters)
+    *step, done = fc_update(fc_weight, fc_moment, other_rows, grads, core_at, 1, 0, step, quarters[0])
+    quarters[1], done = tie(quarters[1], done)
+    quarter = total(quarters).astype(LOW)
+    quarters = exchange_planes([quarter] * planes)
+    *step, done = fc_update(fc_weight, fc_moment, other_rows, grads, core_at, 1, 1, step, done)
+
+    images_grad, quarters[0] = tie(images_grad, quarters[0])
+    keep, got = images_grad[:, :, :per_core], swap(images_grad[:, :, per_core:])
+    images_grad = order_towers(keep, got, core_at)
+    images_grad = jnp.transpose(images_grad, (3, 1, 2, 0, 4))
+
+    new_small = small_update(
+        (done, images_grad),
+        quarters,
+        lines,
+        (as_rows(conv_weight), conv_bias, stitch_conv, stitch_fc),
+        (as_rows(conv_moment), bias_moment, stitch_conv_moment, stitch_fc_moment),
+        core_at,
+        plane_at,
+    )
+
     fc_bias_grad = sum(jnp.sum(value.astype(WIDE), axis=1) for value in grads)
     fc_bias_grad = mine(fc_bias_grad, fc_bias_grad[::-1])
-
-    conv_weight_grad = towers[:, : TAPS * shard].reshape(2, 3, 3, shard, width_in)
-    conv_weight_grad = jnp.swapaxes(conv_weight_grad, 3, 4)
-    conv_bias_grad = towers[:, TAPS * shard, :shard]
-    straight = towers[:, TAPS * shard + 1, :shard]
-    crossed = towers[:, TAPS * shard + 2, :shard]
-    stitch_conv_grad = jnp.stack(
-        [jnp.stack([straight[0], crossed[0]]), jnp.stack([crossed[1], straight[1]])]
-    )
-
-    def step_of(param, moment, grad, rate):
-        fresh = MOMENTUM * moment + grad
-        return param - rate * fresh, fresh
-
-    kernel_step = step_of(conv_weight, conv_moment, conv_weight_grad, LEARN_RATE)
-    bias_step = step_of(conv_bias, bias_moment, conv_bias_grad, BIAS_RATE)
-    stitch_step = step_of(stitch_conv, stitch_conv_moment, stitch_conv_grad, STITCH_RATE)
-    fc_bias_step = step_of(fc_bias, fc_bias_moment, fc_bias_grad, BIAS_RATE)
-    fc_stitch_step = step_of(stitch_fc, stitch_fc_moment, stitch_fc_grad, STITCH_RATE)
-    params, fresh = zip(
-        kernel_step, bias_step, stitch_step, (new_fc_weight, new_fc_moment), fc_bias_step, fc_stitch_step
-    )
+    new_fc_bias_moment = MOMENTUM * fc_bias_moment + fc_bias_grad
+    new_fc_bias = fc_bias - BIAS_RATE * new_fc_bias_moment
+
+    as_given = lambda value: jnp.swapaxes(value.reshape(2, 3, 3, shard, width_in), 3, 4)
+    params, fresh = list(new_small[:4]), list(new_small[4:])
+    params[0], fresh[0] = as_given(params[0]), as_given(fresh[0])
+    params[3:3], fresh[3:3] = (step[0], new_fc_bias), (step[1], new_fc_bias_moment)
+    images_grad = jnp.transpose(images_grad, (0, 3, 1, 2, 4))
     return (features_out.astype(LOW), images_grad, *params, *fresh)
 
 

time: 236 us -> 218 us (0.924)
  Pallas kernels: 42.3 us -> 62.9 us
  other arithmetic: 25.9 us -> 9.18 us
  waiting for transfers between devices: 74 us -> 57.4 us
  local copies, waits for them, and re-layouts: 31.3 us -> 18.9 us
  starting transfers between devices: 53.5 us -> 58.6 us
    ppermute x52, waiting for transfers between devices: 74 us -> 57.4 us  [trade(): return lax.ppermute(value, axis, [(i, i ^ bit) for i in range(size)])]
    pallas_call x2 -> x4, Pallas kernels: 13.9 us -> 27.2 us  [fc_update(): pl.pallas_call(kernel, grid_spec=pltpu.PrefetchScalarGridSpec(num_scalar_...]
    unnamed x130 -> x96, local copies, waits for them, and re-layouts: 23.9 us -> 14 us
    select_n x10 -> x4, other arithmetic: 6.91 us -> 0.22 us  [four_by_four(): mine = lambda a, b: jnp.where(core == 0, a, b)]
    ppermute x52, starting transfers between devices: 53.5 us -> 58.6 us  [trade(): return lax.ppermute(value, axis, [(i, i ^ bit) for i in range(size)])]
    sub x5 -> x1, other arithmetic: 5.41 us -> 0.6 us  [four_by_four(): new_fc_bias = fc_bias - BIAS_RATE * new_fc_bias_moment]
    another operation x9 -> x1, other arithmetic: 3.27 us -> 0.01 us  [the longest x2 1.71 us: four_by_four(): images_grad = jnp.stack([mine(keep, got), mine(got, keep)], axis=1)]
    pallas_call x1, Pallas kernels: 2.8 us -> 5.85 us  [fc_prepare(): pl.pallas_call(kernel, grid_spec=pltpu.PrefetchScalarGridSpec(num_scalar_...]
  transfers between devices with their start and end apart: 52 -> 52, of which waited for: 24 -> 23; matrix products, arithmetic and copies ran while one was open for 15% -> 11% of each run, Pallas kernels for 17% -> 25%
where the time goes in v1:
time: 218 us; the launch traced here: 217 us
  Pallas kernels  62.9 us (29%)
  starting transfers between devices  58.6 us (27%)
  waiting for transfers between devices  57.4 us (26%)
  local copies, waits for them, and re-layouts  18.9 us (9%)
  other arithmetic  9.18 us (4%)
  matrix products  8.49 us (4%)
    ppermute x52, starting transfers between devices, trade(): return lax.ppermute(value, axis, [(i, i ^ bit) for i in range(size)])  58.6 us
    ppermute x52, waiting for transfers between devices, trade(): return lax.ppermute(value, axis, [(i, i ^ bit) for i in range(size)])  57.4 us
    pallas_call x4, Pallas kernels, fc_update(): pl.pallas_call(kernel, grid_spec=pltpu.PrefetchScalarGridSpec(num_scalar_...  27.2 us
    unnamed x96, local copies, waits for them, and re-layouts  14 us
    pallas_call x1, Pallas kernels, conv_forward(): pl.pallas_call(kernel, in_specs=[SCALARS] * 2 + [WHOLE] * (1 + count), ou...  10.1 us
    pallas_call x1, Pallas kernels, conv_backward(): pl.pallas_call(kernel, in_specs=[SCALARS] * 3 + [pl.BlockSpec(memory_spac...  8.52 us
    conv_general_dilated x1, matrix products, turned_conv(): lax.conv_general_dilated(grad, kernel[::-1, ::-1], (1, 1), 'SAME', dimens...  8.49 us
    pallas_call x1, Pallas kernels, fc_prepare(): pl.pallas_call(kernel, grid_spec=pltpu.PrefetchScalarGridSpec(num_scalar_...  5.85 us
  transfers between devices with their start and end apart: 52, of which 23 were waited for; matrix products, arithmetic and copies ran while one was open for 11% of the time, Pallas kernels for 25%

profile of v1, /device:TPU:0, one launch (start us, length us, event | category | flops | bytes accessed | tf_op | source)
XLA Modules:
  0.0 217.1 jit_solution(13289742902437279955)
XLA Ops:
  4.9 2.9 %collective-permute-start.1 = (bf16[304,384]{1,0:T(8,128)(2,1)S(1)}, bf16[304,384]{1,0:T(8,128)(2,1)S(1)}, u32[]{:S(2)}, u32[]{:S(2)}) collective-permute-start(bf16[304,384]{1,0:T(8,128)(2,1)S(1)} %collective-permute-done.refs_1_), channel_id=1, source_target_pairs={{0,8},{4,12},{8,0},{12,4},{16,24},{20,28},{24,16},{28,20},{1,9},{5... | collective-permute-start | bytes 700424 | tf_op jit(solution)/shard_map/ppermute | solution.py:37
  7.8 1.8 copy.60
  9.6 4.1 %collective-permute-done.1.refs_3_._ = bf16[304,384]{1,0:T(8,128)(2,1)S(1)} collective-permute-done((bf16[304,384]{1,0:T(8,128)(2,1)S(1)}, bf16[304,384]{1,0:T(8,128)(2,1)S(1)}, u32[]{:S(2)}, u32[]{:S(2)}) %collective-permute-start.1) | collective-permute-done | bytes 233504 | tf_op jit(solution)/shard_map/ppermute | solution.py:37
  15.2 1.8 collective-permute-start.4
  17.0 1.5 collective-permute-start.3
  19.0 4.7 %collective-permute-done.4.refs_4_ = bf16[304,384]{1,0:T(8,128)(2,1)S(1)} collective-permute-done((bf16[304,384]{1,0:T(8,128)(2,1)S(1)}, bf16[304,384]{1,0:T(8,128)(2,1)S(1)}, u32[]{:S(2)}, u32[]{:S(2)}) %collective-permute-start.4) | collective-permute-done | bytes 233504 | tf_op jit(solution)/shard_map/ppermute | solution.py:37
  23.7 1.7 collective-permute-start.6
  25.5 5.8 %shard_map.257 = (bf16[2304,512]{1,0:T(8,128)(2,1)S(1)}, bf16[2304,512]{1,0:T(8,128)(2,1)}) custom-call(s32[1]{0:T(128)} %bitcast.2.core_ref, f32[2,2304,512]{2,1,0:T(8,128)} %w_ref.7, f32[2,2304,512]{2,1,0:T(8,128)} %w_ref.7, bf16[304,384]{1,0:T(8,128)(2,1)S(1)} %collective-permute-done.1.refs_3_._), custom_call_target="tpu_custom_call" | custom-call | bytes 14155776 | tf_op jit(solution)/shard_map/pallas_call | solution.py:154
  31.3 1.6 collective-permute-start.7
  32.9 2.3 %fusion.6.x_ref.refs_8_ = bf16[15,15,16,384]{3,2,1,0:T(8,128)(2,1)S(1)} fusion(bf16[13,13,8,384]{3,2,1,0:T(8,128)(2,1)} %collective-permute-done.2, bf16[13,13,8,384]{3,2,1,0:T(8,128)(2,1)S(1)} %copy-done.31), kind=kLoop, calls=%fused_computation.10 | loop fusion | flops 20736000 | bytes 4841472 | tf_op jit(solution)/shard_map/concatenate | solution.py:917
  35.4 4.1 %collective-permute-done.7.refs_7_ = bf16[304,384]{1,0:T(8,128)(2,1)S(1)} collective-permute-done((bf16[304,384]{1,0:T(8,128)(2,1)S(1)}, bf16[304,384]{1,0:T(8,128)(2,1)S(1)}, u32[]{:S(2)}, u32[]{:S(2)}) %collective-permute-start.7) | collective-permute-done | bytes 233504 | tf_op jit(solution)/shard_map/ppermute | solution.py:37
  39.5 10.1 %shard_map.255 = (f32[36,16,256]{2,1,0:T(8,128)S(1)}, bf16[13,13,16,256]{3,2,1,0:T(8,128)(2,1)S(1)}, f32[16,256]{1,0:T(8,128)S(1)}) custom-call(s32[1]{0:T(128)} %bitcast.2.core_ref, s32[1]{0:T(128)} %bitcast.1.chip_ref, bf16[15,15,16,384]{3,2,1,0:T(8,128)(2,1)S(1)} %fusion.6.x_ref.refs_8_, bf16[304,384]{1,0:T(8,128)(2,1)S(1)} %copy-done.6, ...), custom_call_target="tpu_custom_call" | custom-call | flops 4784652288 | bytes 4149248 | tf_op jit(solution)/shard_map/pallas_call | solution.py:225
  50.7 1.9 fusion.26
  52.8 1.9 shard_map.256
  55.4 3.6 %collective-permute-start.11 = (bf16[16,2304]{1,0:T(8,128)(2,1)}, bf16[16,2304]{1,0:T(8,128)(2,1)}, u32[]{:S(2)}, u32[]{:S(2)}) collective-permute-start(bf16[16,2304]{1,0:T(8,128)(2,1)} %get-tuple-element.91), channel_id=1, source_target_pairs={{0,3},{1,2},{2,1},{3,0},{4,7},{5,6},{6,5},{7,4},{8,11},{9,10},{10,... | collective-permute-start | bytes 221192 | tf_op jit(solution)/shard_map/ppermute | solution.py:37
  59.9 2.6 %collective-permute-done.11 = bf16[16,2304]{1,0:T(8,128)(2,1)} collective-permute-done((bf16[16,2304]{1,0:T(8,128)(2,1)}, bf16[16,2304]{1,0:T(8,128)(2,1)}, u32[]{:S(2)}, u32[]{:S(2)}) %collective-permute-start.11) | collective-permute-done | bytes 73760 | tf_op jit(solution)/shard_map/ppermute | solution.py:37
  62.5 3.5 %collective-permute-done.10 = bf16[16,2304]{1,0:T(8,128)(2,1)} collective-permute-done((bf16[16,2304]{1,0:T(8,128)(2,1)}, bf16[16,2304]{1,0:T(8,128)(2,1)}, u32[]{:S(2)}, u32[]{:S(2)}) %collective-permute-start.10) | collective-permute-done | bytes 73760 | tf_op jit(solution)/shard_map/ppermute | solution.py:37
  67.5 1.6 collective-permute-start.14
  71.1 2.6 %collective-permute-done.14.refs_4_ = bf16[2,16,2304]{2,1,0:T(8,128)(2,1)S(1)} collective-permute-done((bf16[2,16,2304]{2,1,0:T(8,128)(2,1)S(1)}, bf16[2,16,2304]{2,1,0:T(8,128)(2,1)S(1)}, u32[]{:S(2)}, u32[]{:S(2)}) %collective-permute-start.14) | collective-permute-done | bytes 147488 | tf_op jit(solution)/shard_map/ppermute | solution.py:37
  73.6 2.1 collective-permute-start.16
  75.7 1.5 collective-permute-start.17
  78.8 2.0 collective-permute-done.17.refs_7_
  80.9 3.2 %shard_map.258 = (bf16[256,2304]{1,0:T(8,128)(2,1)}, f32[64,1024]{1,0:T(8,128)S(1)}, bf16[64,1024]{1,0:T(8,128)(2,1)S(1)}, bf16[64,1024]{1,0:T(8,128)(2,1)S(1)}, bf16[64,1024]{1,0:T(8,128)(2,1)S(1)}) custom-call(s32[1]{0:T(128)} %bitcast.1.chip_ref, bf16[2,16,2304]{2,1,0:T(8,128)(2,1)S(1)} %pad_maximum_fusion.3.refs_0_, ...), custom_call_target="tpu_custom_call" | custom-call | flops 1207959552 | bytes 4718592 | tf_op jit(solution)/shard_map/pallas_call | solution.py:315
  84.0 2.7 %collective-permute-start.21 = (bf16[64,1024]{1,0:T(8,128)(2,1)S(1)}, bf16[64,1024]{1,0:T(8,128)(2,1)S(1)}, u32[]{:S(2)}, u32[]{:S(2)}) collective-permute-start(bf16[64,1024]{1,0:T(8,128)(2,1)S(1)} %get-tuple-element.97), channel_id=1, source_target_pairs={{0,3},{1,2},{2,1},{3,0},{4,7},{5,6},{6,5},{7,4},{8,11},{9,10},{10,... | collective-permute-start | bytes 393224 | tf_op jit(solution)/shard_map/ppermute | solution.py:37
  86.7 1.8 collective-permute-start.19
  88.6 2.4 %collective-permute-done.21 = bf16[64,1024]{1,0:T(8,128)(2,1)S(1)} collective-permute-done((bf16[64,1024]{1,0:T(8,128)(2,1)S(1)}, bf16[64,1024]{1,0:T(8,128)(2,1)S(1)}, u32[]{:S(2)}, u32[]{:S(2)}) %collective-permute-start.21) | collective-permute-done | bytes 131104 | tf_op jit(solution)/shard_map/ppermute | solution.py:37
  91.0 4.0 %collective-permute-done.20 = bf16[64,1024]{1,0:T(8,128)(2,1)S(1)} collective-permute-done((bf16[64,1024]{1,0:T(8,128)(2,1)S(1)}, bf16[64,1024]{1,0:T(8,128)(2,1)S(1)}, u32[]{:S(2)}, u32[]{:S(2)}) %collective-permute-start.20) | collective-permute-done | bytes 131104 | tf_op jit(solution)/shard_map/ppermute | solution.py:37
  98.2 3.0 %collective-permute-start.24 = (bf16[2,64,512]{2,1,0:T(8,128)(2,1)S(1)}, bf16[2,64,512]{2,1,0:T(8,128)(2,1)S(1)}, u32[]{:S(2)}, u32[]{:S(2)}) collective-permute-start(bf16[2,64,512]{2,1,0:T(8,128)(2,1)S(1)} %pad_maximum_fusion.6.refs_0_), channel_id=1, source_target_pairs={{0,2},{1,3},{2,0},{3,1},{4,6},{5,7},{6,4},{7,5},{8,10},{9,11},{10,... | collective-permute-start | bytes 393224 | tf_op jit(solution)/shard_map/ppermute | solution.py:37
  102.7 7.5 %collective-permute-done.25.refs_3_ = bf16[2,64,512]{2,1,0:T(8,128)(2,1)S(1)} collective-permute-done((bf16[2,64,512]{2,1,0:T(8,128)(2,1)S(1)}, bf16[2,64,512]{2,1,0:T(8,128)(2,1)S(1)}, u32[]{:S(2)}, u32[]{:S(2)}) %collective-permute-start.25) | collective-permute-done | bytes 131104 | tf_op jit(solution)/shard_map/ppermute | solution.py:37
  112.9 3.2 %shard_map.259 = (bf16[2,16,2304]{2,1,0:T(8,128)(2,1)S(1)}, bf16[2,16,2304]{2,1,0:T(8,128)(2,1)S(1)}, bf16[2,16,2304]{2,1,0:T(8,128)(2,1)S(1)}, bf16[2,16,2304]{...) custom-call(s32[1]{0:T(128)} %bitcast.1.chip_ref, ...), custom_call_target="tpu_custom_call" | custom-call | flops 1207959552 | bytes 4718592 | tf_op jit(solution)/shard_map/pallas_call | solution.py:354
  120.3 2.5 %collective-permute-done.28 = bf16[2,16,2304]{2,1,0:T(8,128)(2,1)S(1)} collective-permute-done((bf16[2,16,2304]{2,1,0:T(8,128)(2,1)S(1)}, bf16[2,16,2304]{2,1,0:T(8,128)(2,1)S(1)}, u32[]{:S(2)}, u32[]{:S(2)}) %collective-permute-start.28) | collective-permute-done | bytes 147488 | tf_op jit(solution)/shard_map/ppermute | solution.py:37
  126.4 7.0 %shard_map.260 = (f32[2,2304,512]{2,1,0:T(8,128)}, f32[2,2304,512]{2,1,0:T(8,128)}, f32[8,128]{1,0:T(8,128)S(1)}) custom-call(s32[1]{0:T(128)} %bitcast.2.core_ref, f32[2,2304,512]{2,1,0:T(8,128)} %w_ref.7, f32[2,2304,512]{2,1,0:T(8,128)} %m_ref.7, bf16[256,2304]{1,0:T(8,128)(2,1)} %get-tuple-element.102.rows_ref, ...), custom_call_target="tpu_custom_call" | custom-call | flops 603979776 | bytes 9437184 | tf_op jit(solution)/shard_map/pallas_call | solution.py:516
  133.4 2.7 %collective-permute-start.31 = (bf16[16,2304]{1,0:T(8,128)(2,1)S(1)}, bf16[16,2304]{1,0:T(8,128)(2,1)S(1)}, u32[]{:S(2)}, u32[]{:S(2)}) collective-permute-start(bf16[16,2304]{1,0:T(8,128)(2,1)S(1)} %get-tuple-element.201), channel_id=1, source_target_pairs={{0,1},{1,0},{2,3},{3,2},{4,5},{5,4},{6,7},{7,6},{8,9},{9,8},{10,11... | collective-permute-start | bytes 221192 | tf_op jit(solution)/shard_map/ppermute | solution.py:37
  137.2 1.5 collective-permute-start.35
  138.8 7.1 %shard_map.261 = (f32[2,2304,512]{2,1,0:T(8,128)}, f32[2,2304,512]{2,1,0:T(8,128)}, f32[8,128]{1,0:T(8,128)S(1)}) custom-call(s32[1]{0:T(128)} %bitcast.2.core_ref, f32[2,2304,512]{2,1,0:T(8,128)} %w_ref.7, f32[2,2304,512]{2,1,0:T(8,128)} %m_ref.7, bf16[256,2304]{1,0:T(8,128)(2,1)} %get-tuple-element.102.rows_ref, ...), custom_call_target="tpu_custom_call", output_to_operand_aliasing={{0}: (8, {}), {1}: (9, {})} | custom-call | flops 603979776 | bytes 9437184 | tf_op jit(solution)/shard_map/pallas_call | solution.py:516
  147.7 8.5 %shard_map.262 = (bf16[304,384]{1,0:T(8,128)(2,1)S(1)}, bf16[304,384]{1,0:T(8,128)(2,1)S(1)}, bf16[304,384]{1,0:T(8,128)(2,1)S(1)}, bf16[304,384]{1,0:T(8,128)(2...) custom-call(s32[1]{0:T(128)} %bitcast.2.core_ref, ...), custom_call_target="tpu_custom_call" | custom-call | flops 4784652288 | bytes 6918144 | tf_op jit(solution)/shard_map/pallas_call | solution.py:455
  163.6 4.5 %collective-permute-done.37 = bf16[304,384]{1,0:T(8,128)(2,1)S(1)} collective-permute-done((bf16[304,384]{1,0:T(8,128)(2,1)}, bf16[304,384]{1,0:T(8,128)(2,1)S(1)}, u32[]{:S(2)}, u32[]{:S(2)}) %collective-permute-start.37) | collective-permute-done | bytes 233504 | tf_op jit(solution)/shard_map/ppermute | solution.py:37
  168.2 1.6 collective-permute-start.38
  170.5 8.5 %convolution_convert_fusion = bf16[13,13,16,384]{3,2,1,0:T(8,128)(2,1)S(1)} fusion(bf16[13,13,16,256]{3,2,1,0:T(8,128)(2,1)} %copy-done.30, bf16[3,3,256,384]{3,2,1,0:T(8,128)(2,1)} %copy-done.38), kind=kOutput, calls=%fused_computation.14 | convolution fusion | flops 4307539968 | bytes 5230592 | tf_op jit(solution)/shard_map/conv_general_dilated | solution.py:972
  181.8 2.5 %collective-permute-start.47 = (bf16[160,384]{1,0:T(8,128)(2,1)S(1)}, bf16[160,384]{1,0:T(8,128)(2,1)S(1)}, u32[]{:S(2)}, u32[]{:S(2)}) collective-permute-start(bf16[160,384]{1,0:T(8,128)(2,1)S(1)} %get-tuple-element.187), channel_id=1, source_target_pairs={{0,3},{1,2},{2,1},{3,0},{4,7},{5,6},{6,5},{7,4},{8,11},{9,10},{10,... | collective-permute-start | bytes 368648 | tf_op jit(solution)/shard_map/ppermute | solution.py:37
  184.4 6.6 %shard_map.263 = (f32[2,2304,512]{2,1,0:T(8,128)}, f32[2,2304,512]{2,1,0:T(8,128)}, f32[8,128]{1,0:T(8,128)S(1)}) custom-call(s32[1]{0:T(128)} %bitcast.2.core_ref, f32[2,2304,512]{2,1,0:T(8,128)} %w_ref.7, f32[2,2304,512]{2,1,0:T(8,128)} %m_ref.7, ...), custom_call_target="tpu_custom_call", output_to_operand_aliasing={{0}: (8, {}), {1}: (9, {})} | custom-call | flops 603979776 | bytes 9437184 | tf_op jit(solution)/shard_map/pallas_call | solution.py:516
  191.2 4.2 %collective-permute-done.46 = bf16[160,384]{1,0:T(8,128)(2,1)S(1)} collective-permute-done((bf16[160,384]{1,0:T(8,128)(2,1)S(1)}, bf16[160,384]{1,0:T(8,128)(2,1)S(1)}, u32[]{:S(2)}, u32[]{:S(2)}) %collective-permute-start.46) | collective-permute-done | bytes 122912 | tf_op jit(solution)/shard_map/ppermute | solution.py:37
  197.9 2.9 %collective-permute-start.50 = (bf16[160,384]{1,0:T(8,128)(2,1)S(1)}, bf16[160,384]{1,0:T(8,128)(2,1)S(1)}, u32[]{:S(2)}, u32[]{:S(2)}) collective-permute-start(bf16[160,384]{1,0:T(8,128)(2,1)S(1)} %add_convert_fusion.6.refs_0_), channel_id=1, source_target_pairs={{0,2},{1,3},{2,0},{3,1},{4,6},{5,7},{6,4},{7,5},{8,10},{9,11},{10,... | collective-permute-start | bytes 368648 | tf_op jit(solution)/shard_map/ppermute | solution.py:37
  200.7 1.5 collective-permute-start.51
  202.9 6.6 %shard_map.265 = (f32[2,2304,512]{2,1,0:T(8,128)}, f32[2,2304,512]{2,1,0:T(8,128)}, f32[8,128]{1,0:T(8,128)S(1)}) custom-call(s32[1]{0:T(128)} %bitcast.2.core_ref, f32[2,2304,512]{2,1,0:T(8,128)} %w_ref.7, f32[2,2304,512]{2,1,0:T(8,128)} %m_ref.7, ...), custom_call_target="tpu_custom_call", output_to_operand_aliasing={{0}: (8, {}), {1}: (9, {})} | custom-call | flops 603979776 | bytes 9437184 | tf_op jit(solution)/shard_map/pallas_call | solution.py:516
  210.8 1.6 copy.59
  212.5 2.9 %copy.40 = bf16[8,2,13,13,384]{4,1,3,2,0:T(2,128)(2,1)} copy(bf16[8,2,13,13,384]{4,0,3,2,1:T(8,128)(2,1)S(1)} %bitcast.107) | data formatting | bytes 4153344
  215.5 1.6 shard_map.266
  (218 shorter events, 48.0 us)
Async XLA Ops:
  4.9 8.8 %collective-permute-start.1 = (bf16[304,384]{1,0:T(8,128)(2,1)S(1)}, bf16[304,384]{1,0:T(8,128)(2,1)S(1)}, u32[]{:S(2)}, u32[]{:S(2)}) collective-permute-start(bf16[304,384]{1,0:T(8,128)(2,1)S(1)} %collective-permute-done.refs_1_), channel_id=1, source_target_pairs={{0,8},{4,12},{8,0},{12,4},{16,24},{20,28},{24,16},{28,20},{1,9},{5... | collective-permute-start | bytes 700424 | tf_op jit(solution)/shard_map/ppermute | solution.py:37
  15.2 16.1 %collective-permute-start.2 = (bf16[13,13,8,384]{3,2,1,0:T(8,128)(2,1)}, bf16[13,13,8,384]{3,2,1,0:T(8,128)(2,1)}, u32[]{:S(2)}, u32[]{:S(2)}) collective-permute-start(bf16[13,13,8,384]{3,2,1,0:T(8,128)(2,1)} %get-tuple-element.177), channel_id=1, source_target_pairs={{0,4},{4,0},{8,12},{12,8},{16,20},{20,16},{24,28},{28,24},{1,5},{5... | collective-permute-start | bytes 3115016 | tf_op jit(solution)/shard_map/ppermute | solution.py:37
  15.2 8.5 %collective-permute-start.4 = (bf16[304,384]{1,0:T(8,128)(2,1)S(1)}, bf16[304,384]{1,0:T(8,128)(2,1)S(1)}, u32[]{:S(2)}, u32[]{:S(2)}) collective-permute-start(bf16[304,384]{1,0:T(8,128)(2,1)S(1)} %get-tuple-element.84.refs_0_), channel_id=1, source_target_pairs={{0,16},{4,20},{8,24},{12,28},{16,0},{20,4},{24,8},{28,12},{1,17},{... | collective-permute-start | bytes 700424 | tf_op jit(solution)/shard_map/ppermute | solution.py:37
  17.0 18.3 %collective-permute-start.3 = (bf16[304,384]{1,0:T(8,128)(2,1)S(1)}, bf16[304,384]{1,0:T(8,128)(2,1)}, u32[]{:S(2)}, u32[]{:S(2)}) collective-permute-start(bf16[304,384]{1,0:T(8,128)(2,1)S(1)} %get-tuple-element.84.refs_0_), channel_id=1, source_target_pairs={{0,8},{4,12},{8,0},{12,4},{16,24},{20,28},{24,16},{28,20},{1,9},{5... | collective-permute-start | bytes 700424 | tf_op jit(solution)/shard_map/ppermute | solution.py:37
  18.5 16.8 %collective-permute-start.5 = (bf16[304,384]{1,0:T(8,128)(2,1)S(1)}, bf16[304,384]{1,0:T(8,128)(2,1)S(1)}, u32[]{:S(2)}, u32[]{:S(2)}) collective-permute-start(bf16[304,384]{1,0:T(8,128)(2,1)S(1)} %collective-permute-done.refs_1_), channel_id=1, source_target_pairs={{0,16},{4,20},{8,24},{12,28},{16,0},{20,4},{24,8},{28,12},{1,17},{... | collective-permute-start | bytes 700424 | tf_op jit(solution)/shard_map/ppermute | solution.py:37
  23.7 11.6 %collective-permute-start.6 = (bf16[304,384]{1,0:T(8,128)(2,1)S(1)}, bf16[304,384]{1,0:T(8,128)(2,1)S(1)}, u32[]{:S(2)}, u32[]{:S(2)}) collective-permute-start(bf16[304,384]{1,0:T(8,128)(2,1)S(1)} %collective-permute-done.4.refs_4_), channel_id=1, source_target_pairs={{0,8},{4,12},{8,0},{12,4},{16,24},{20,28},{24,16},{28,20},{1,9},{5... | collective-permute-start | bytes 700424 | tf_op jit(solution)/shard_map/ppermute | solution.py:37
  31.3 49.5 %collective-permute-start.18 = (bf16[2304,512]{1,0:T(8,128)(2,1)}, bf16[2304,512]{1,0:T(8,128)(2,1)}, u32[]{:S(2)}, u32[]{:S(2)}) collective-permute-start(bf16[2304,512]{1,0:T(8,128)(2,1)} %get-tuple-element.93), channel_id=1, source_target_pairs={{0,4},{4,0},{8,12},{12,8},{16,20},{20,16},{24,28},{28,24},{1,5},{5... | collective-permute-start | bytes 7077896 | tf_op jit(solution)/shard_map/ppermute | solution.py:37
  31.3 8.1 %collective-permute-start.7 = (bf16[304,384]{1,0:T(8,128)(2,1)S(1)}, bf16[304,384]{1,0:T(8,128)(2,1)S(1)}, u32[]{:S(2)}, u32[]{:S(2)}) collective-permute-start(bf16[304,384]{1,0:T(8,128)(2,1)S(1)} %collective-permute-done.1.refs_3_._), channel_id=1, source_target_pairs={{0,16},{4,20},{8,24},{12,28},{16,0},{20,4},{24,8},{28,12},{1,17},{... | collective-permute-start | bytes 700424 | tf_op jit(solution)/shard_map/ppermute | solution.py:37
  50.7 2.1 collective-permute-start.8
  55.4 7.1 %collective-permute-start.11 = (bf16[16,2304]{1,0:T(8,128)(2,1)}, bf16[16,2304]{1,0:T(8,128)(2,1)}, u32[]{:S(2)}, u32[]{:S(2)}) collective-permute-start(bf16[16,2304]{1,0:T(8,128)(2,1)} %get-tuple-element.91), channel_id=1, source_target_pairs={{0,3},{1,2},{2,1},{3,0},{4,7},{5,6},{6,5},{7,4},{8,11},{9,10},{10,... | collective-permute-start | bytes 221192 | tf_op jit(solution)/shard_map/ppermute | solution.py:37
  59.0 6.9 %collective-permute-start.10 = (bf16[16,2304]{1,0:T(8,128)(2,1)}, bf16[16,2304]{1,0:T(8,128)(2,1)}, u32[]{:S(2)}, u32[]{:S(2)}) collective-permute-start(bf16[16,2304]{1,0:T(8,128)(2,1)} %get-tuple-element.90), channel_id=1, source_target_pairs={{0,2},{1,3},{2,0},{3,1},{4,6},{5,7},{6,4},{7,5},{8,10},{9,11},{10,... | collective-permute-start | bytes 221192 | tf_op jit(solution)/shard_map/ppermute | solution.py:37
  59.0 8.4 %collective-permute-start.9 = (bf16[16,2304]{1,0:T(8,128)(2,1)}, bf16[16,2304]{1,0:T(8,128)(2,1)S(1)}, u32[]{:S(2)}, u32[]{:S(2)}) collective-permute-start(bf16[16,2304]{1,0:T(8,128)(2,1)} %copy-done.27), channel_id=1, source_target_pairs={{0,1},{1,0},{2,3},{3,2},{4,5},{5,4},{6,7},{7,6},{8,9},{9,8},{10,11... | collective-permute-start | bytes 221192 | tf_op jit(solution)/shard_map/ppermute | solution.py:37
  66.9 8.8 %collective-permute-start.13 = (bf16[2,16,2304]{2,1,0:T(8,128)(2,1)S(1)}, bf16[2,16,2304]{2,1,0:T(8,128)(2,1)S(1)}, u32[]{:S(2)}, u32[]{:S(2)}) collective-permute-start(bf16[2,16,2304]{2,1,0:T(8,128)(2,1)S(1)} %pad_maximum_fusion.4.refs_1_), channel_id=1, source_target_pairs={{0,8},{4,12},{8,0},{12,4},{16,24},{20,28},{24,16},{28,20},{1,9},{5... | collective-permute-start | bytes 442376 | tf_op jit(solution)/shard_map/ppermute | solution.py:37
  67.5 6.1 %collective-permute-start.14 = (bf16[2,16,2304]{2,1,0:T(8,128)(2,1)S(1)}, bf16[2,16,2304]{2,1,0:T(8,128)(2,1)S(1)}, u32[]{:S(2)}, u32[]{:S(2)}) collective-permute-start(bf16[2,16,2304]{2,1,0:T(8,128)(2,1)S(1)} %pad_maximum_fusion.3.refs_0_), channel_id=1, source_target_pairs={{0,16},{4,20},{8,24},{12,28},{16,0},{20,4},{24,8},{28,12},{1,17},{... | collective-permute-start | bytes 442376 | tf_op jit(solution)/shard_map/ppermute | solution.py:37
  69.1 9.6 %collective-permute-start.12 = (bf16[2,16,2304]{2,1,0:T(8,128)(2,1)S(1)}, bf16[2,16,2304]{2,1,0:T(8,128)(2,1)S(1)}, u32[]{:S(2)}, u32[]{:S(2)}) collective-permute-start(bf16[2,16,2304]{2,1,0:T(8,128)(2,1)S(1)} %pad_maximum_fusion.3.refs_0_), channel_id=1, source_target_pairs={{0,8},{4,12},{8,0},{12,4},{16,24},{20,28},{24,16},{28,20},{1,9},{5... | collective-permute-start | bytes 442376 | tf_op jit(solution)/shard_map/ppermute | solution.py:37
  70.6 8.1 %collective-permute-start.15 = (bf16[2,16,2304]{2,1,0:T(8,128)(2,1)S(1)}, bf16[2,16,2304]{2,1,0:T(8,128)(2,1)S(1)}, u32[]{:S(2)}, u32[]{:S(2)}) collective-permute-start(bf16[2,16,2304]{2,1,0:T(8,128)(2,1)S(1)} %pad_maximum_fusion.4.refs_1_), channel_id=1, source_target_pairs={{0,16},{4,20},{8,24},{12,28},{16,0},{20,4},{24,8},{28,12},{1,17},{... | collective-permute-start | bytes 442376 | tf_op jit(solution)/shard_map/ppermute | solution.py:37
  73.6 5.2 %collective-permute-start.16 = (bf16[2,16,2304]{2,1,0:T(8,128)(2,1)S(1)}, bf16[2,16,2304]{2,1,0:T(8,128)(2,1)S(1)}, u32[]{:S(2)}, u32[]{:S(2)}) collective-permute-start(bf16[2,16,2304]{2,1,0:T(8,128)(2,1)S(1)} %collective-permute-done.14.refs_4_), channel_id=1, source_target_pairs={{0,8},{4,12},{8,0},{12,4},{16,24},{20,28},{24,16},{28,20},{1,9},{5... | collective-permute-start | bytes 442376 | tf_op jit(solution)/shard_map/ppermute | solution.py:37
  75.7 5.1 %collective-permute-start.17 = (bf16[2,16,2304]{2,1,0:T(8,128)(2,1)S(1)}, bf16[2,16,2304]{2,1,0:T(8,128)(2,1)S(1)}, u32[]{:S(2)}, u32[]{:S(2)}) collective-permute-start(bf16[2,16,2304]{2,1,0:T(8,128)(2,1)S(1)} %collective-permute-done.13.refs_3_), channel_id=1, source_target_pairs={{0,16},{4,20},{8,24},{12,28},{16,0},{20,4},{24,8},{28,12},{1,17},{... | collective-permute-start | bytes 442376 | tf_op jit(solution)/shard_map/ppermute | solution.py:37
  84.0 7.0 %collective-permute-start.21 = (bf16[64,1024]{1,0:T(8,128)(2,1)S(1)}, bf16[64,1024]{1,0:T(8,128)(2,1)S(1)}, u32[]{:S(2)}, u32[]{:S(2)}) collective-permute-start(bf16[64,1024]{1,0:T(8,128)(2,1)S(1)} %get-tuple-element.97), channel_id=1, source_target_pairs={{0,3},{1,2},{2,1},{3,0},{4,7},{5,6},{6,5},{7,4},{8,11},{9,10},{10,... | collective-permute-start | bytes 393224 | tf_op jit(solution)/shard_map/ppermute | solution.py:37
  86.7 8.3 %collective-permute-start.20 = (bf16[64,1024]{1,0:T(8,128)(2,1)S(1)}, bf16[64,1024]{1,0:T(8,128)(2,1)S(1)}, u32[]{:S(2)}, u32[]{:S(2)}) collective-permute-start(bf16[64,1024]{1,0:T(8,128)(2,1)S(1)} %get-tuple-element.96), channel_id=1, source_target_pairs={{0,2},{1,3},{2,0},{3,1},{4,6},{5,7},{6,4},{7,5},{8,10},{9,11},{10,... | collective-permute-start | bytes 393224 | tf_op jit(solution)/shard_map/ppermute | solution.py:37
  86.7 8.3 %collective-permute-start.19 = (bf16[64,1024]{1,0:T(8,128)(2,1)S(1)}, bf16[64,1024]{1,0:T(8,128)(2,1)S(1)}, u32[]{:S(2)}, u32[]{:S(2)}) collective-permute-start(bf16[64,1024]{1,0:T(8,128)(2,1)S(1)} %get-tuple-element.95), channel_id=1, source_target_pairs={{0,1},{1,0},{2,3},{3,2},{4,5},{5,4},{6,7},{7,6},{8,9},{9,8},{10,11... | collective-permute-start | bytes 393224 | tf_op jit(solution)/shard_map/ppermute | solution.py:37
  98.1 13.1 %collective-permute-start.23 = (bf16[2,64,512]{2,1,0:T(8,128)(2,1)S(1)}, bf16[2,64,512]{2,1,0:T(8,128)(2,1)S(1)}, u32[]{:S(2)}, u32[]{:S(2)}) collective-permute-start(bf16[2,64,512]{2,1,0:T(8,128)(2,1)S(1)} %pad_maximum_fusion.6.refs_0_), channel_id=1, source_target_pairs={{0,1},{1,0},{2,3},{3,2},{4,5},{5,4},{6,7},{7,6},{8,9},{9,8},{10,11... | collective-permute-start | bytes 393224 | tf_op jit(solution)/shard_map/ppermute | solution.py:37
  98.2 13.0 %collective-permute-start.24 = (bf16[2,64,512]{2,1,0:T(8,128)(2,1)S(1)}, bf16[2,64,512]{2,1,0:T(8,128)(2,1)S(1)}, u32[]{:S(2)}, u32[]{:S(2)}) collective-permute-start(bf16[2,64,512]{2,1,0:T(8,128)(2,1)S(1)} %pad_maximum_fusion.6.refs_0_), channel_id=1, source_target_pairs={{0,2},{1,3},{2,0},{3,1},{4,6},{5,7},{6,4},{7,5},{8,10},{9,11},{10,... | collective-permute-start | bytes 393224 | tf_op jit(solution)/shard_map/ppermute | solution.py:37
  101.2 9.0 %collective-permute-start.25 = (bf16[2,64,512]{2,1,0:T(8,128)(2,1)S(1)}, bf16[2,64,512]{2,1,0:T(8,128)(2,1)S(1)}, u32[]{:S(2)}, u32[]{:S(2)}) collective-permute-start(bf16[2,64,512]{2,1,0:T(8,128)(2,1)S(1)} %pad_maximum_fusion.6.refs_0_), channel_id=1, source_target_pairs={{0,3},{1,2},{2,1},{3,0},{4,7},{5,6},{6,5},{7,4},{8,11},{9,10},{10,... | collective-permute-start | bytes 393224 | tf_op jit(solution)/shard_map/ppermute | solution.py:37
  116.1 6.8 %collective-permute-start.28 = (bf16[2,16,2304]{2,1,0:T(8,128)(2,1)S(1)}, bf16[2,16,2304]{2,1,0:T(8,128)(2,1)S(1)}, u32[]{:S(2)}, u32[]{:S(2)}) collective-permute-start(bf16[2,16,2304]{2,1,0:T(8,128)(2,1)S(1)} %get-tuple-element.101), channel_id=1, source_target_pairs={{0,8},{4,12},{8,0},{12,4},{16,24},{20,28},{24,16},{28,20},{1,9},{5... | collective-permute-start | bytes 442376 | tf_op jit(solution)/shard_map/ppermute | solution.py:37
  117.4 15.9 %collective-permute-start.27 = (bf16[2,16,2304]{2,1,0:T(8,128)(2,1)S(1)}, bf16[2,16,2304]{2,1,0:T(8,128)(2,1)S(1)}, u32[]{:S(2)}, u32[]{:S(2)}) collective-permute-start(bf16[2,16,2304]{2,1,0:T(8,128)(2,1)S(1)} %get-tuple-element.99), channel_id=1, source_target_pairs={{0,8},{4,12},{8,0},{12,4},{16,24},{20,28},{24,16},{28,20},{1,9},{5... | collective-permute-start | bytes 442376 | tf_op jit(solution)/shard_map/ppermute | solution.py:37
  118.3 6.8 %collective-permute-start.30 = (bf16[2,16,2304]{2,1,0:T(8,128)(2,1)S(1)}, bf16[2,16,2304]{2,1,0:T(8,128)(2,1)S(1)}, u32[]{:S(2)}, u32[]{:S(2)}) collective-permute-start(bf16[2,16,2304]{2,1,0:T(8,128)(2,1)S(1)} %get-tuple-element.104), channel_id=1, source_target_pairs={{0,16},{4,20},{8,24},{12,28},{16,0},{20,4},{24,8},{28,12},{1,17},{... | collective-permute-start | bytes 442376 | tf_op jit(solution)/shard_map/ppermute | solution.py:37
  119.4 16.7 %collective-permute-start.33 = (bf16[2,16,2304]{2,1,0:T(8,128)(2,1)S(1)}, bf16[2,16,2304]{2,1,0:T(8,128)(2,1)S(1)}, u32[]{:S(2)}, u32[]{:S(2)}) collective-permute-start(bf16[2,16,2304]{2,1,0:T(8,128)(2,1)S(1)} %get-tuple-element.111), channel_id=1, source_target_pairs={{0,16},{4,20},{8,24},{12,28},{16,0},{20,4},{24,8},{28,12},{1,17},{... | collective-permute-start | bytes 442376 | tf_op jit(solution)/shard_map/ppermute | solution.py:37
  122.9 10.5 %collective-permute-start.29 = (bf16[2,16,2304]{2,1,0:T(8,128)(2,1)S(1)}, bf16[2,16,2304]{2,1,0:T(8,128)(2,1)S(1)}, u32[]{:S(2)}, u32[]{:S(2)}) collective-permute-start(bf16[2,16,2304]{2,1,0:T(8,128)(2,1)S(1)} %add_convert_fusion.5), channel_id=1, source_target_pairs={{0,16},{4,20},{8,24},{12,28},{16,0},{20,4},{24,8},{28,12},{1,17},{... | collective-permute-start | bytes 442376 | tf_op jit(solution)/shard_map/ppermute | solution.py:37
  125.1 11.0 %collective-permute-start.32 = (bf16[2,16,2304]{2,1,0:T(8,128)(2,1)S(1)}, bf16[2,16,2304]{2,1,0:T(8,128)(2,1)S(1)}, u32[]{:S(2)}, u32[]{:S(2)}) collective-permute-start(bf16[2,16,2304]{2,1,0:T(8,128)(2,1)S(1)} %add_convert_fusion.4.refs_4_), channel_id=1, source_target_pairs={{0,8},{4,12},{8,0},{12,4},{16,24},{20,28},{24,16},{28,20},{1,9},{5... | collective-permute-start | bytes 442376 | tf_op jit(solution)/shard_map/ppermute | solution.py:37
  133.4 12.6 %collective-permute-start.31 = (bf16[16,2304]{1,0:T(8,128)(2,1)S(1)}, bf16[16,2304]{1,0:T(8,128)(2,1)S(1)}, u32[]{:S(2)}, u32[]{:S(2)}) collective-permute-start(bf16[16,2304]{1,0:T(8,128)(2,1)S(1)} %get-tuple-element.201), channel_id=1, source_target_pairs={{0,1},{1,0},{2,3},{3,2},{4,5},{5,4},{6,7},{7,6},{8,9},{9,8},{10,11... | collective-permute-start | bytes 221192 | tf_op jit(solution)/shard_map/ppermute | solution.py:37
  136.1 9.8 %collective-permute-start.34 = (bf16[16,2304]{1,0:T(8,128)(2,1)S(1)}, bf16[16,2304]{1,0:T(8,128)(2,1)S(1)}, u32[]{:S(2)}, u32[]{:S(2)}) collective-permute-start(bf16[16,2304]{1,0:T(8,128)(2,1)S(1)} %get-tuple-element.198), channel_id=1, source_target_pairs={{0,2},{1,3},{2,0},{3,1},{4,6},{5,7},{6,4},{7,5},{8,10},{9,11},{10,... | collective-permute-start | bytes 221192 | tf_op jit(solution)/shard_map/ppermute | solution.py:37
  137.2 8.7 %collective-permute-start.35 = (bf16[16,2304]{1,0:T(8,128)(2,1)S(1)}, bf16[16,2304]{1,0:T(8,128)(2,1)S(1)}, u32[]{:S(2)}, u32[]{:S(2)}) collective-permute-start(bf16[16,2304]{1,0:T(8,128)(2,1)S(1)} %get-tuple-element.199.refs_6_), channel_id=1, source_target_pairs={{0,3},{1,2},{2,1},{3,0},{4,7},{5,6},{6,5},{7,4},{8,11},{9,10},{10,... | collective-permute-start | bytes 221192 | tf_op jit(solution)/shard_map/ppermute | solution.py:37
  146.0 1.6 collective-permute-start.36
  146.2 38.2 %collective-permute-start.45 = (bf16[256,2304]{1,0:T(8,128)(2,1)}, bf16[256,2304]{1,0:T(8,128)(2,1)S(1)}, u32[]{:S(2)}, u32[]{:S(2)}) collective-permute-start(bf16[256,2304]{1,0:T(8,128)(2,1)} %get-tuple-element.102.rows_ref), channel_id=1, source_target_pairs={{0,4},{4,0},{8,12},{12,8},{16,20},{20,16},{24,28},{28,24},{1,5},{5... | collective-permute-start | bytes 3538952 | tf_op jit(solution)/shard_map/ppermute | solution.py:37
  159.4 8.8 %collective-permute-start.37 = (bf16[304,384]{1,0:T(8,128)(2,1)}, bf16[304,384]{1,0:T(8,128)(2,1)S(1)}, u32[]{:S(2)}, u32[]{:S(2)}) collective-permute-start(bf16[304,384]{1,0:T(8,128)(2,1)} %get-tuple-element.118), channel_id=1, source_target_pairs={{0,8},{4,12},{8,0},{12,4},{16,24},{20,28},{24,16},{28,20},{1,9},{5... | collective-permute-start | bytes 700424 | tf_op jit(solution)/shard_map/ppermute | solution.py:37
  160.3 9.5 %collective-permute-start.39 = (bf16[304,384]{1,0:T(8,128)(2,1)}, bf16[304,384]{1,0:T(8,128)(2,1)S(1)}, u32[]{:S(2)}, u32[]{:S(2)}) collective-permute-start(bf16[304,384]{1,0:T(8,128)(2,1)} %copy-done.26), channel_id=1, source_target_pairs={{0,16},{4,20},{8,24},{12,28},{16,0},{20,4},{24,8},{28,12},{1,17},{... | collective-permute-start | bytes 700424 | tf_op jit(solution)/shard_map/ppermute | solution.py:37
  161.4 17.5 %collective-permute-start.42 = (bf16[304,384]{1,0:T(8,128)(2,1)}, bf16[304,384]{1,0:T(8,128)(2,1)S(1)}, u32[]{:S(2)}, u32[]{:S(2)}) collective-permute-start(bf16[304,384]{1,0:T(8,128)(2,1)} %copy-done.25), channel_id=1, source_target_pairs={{0,16},{4,20},{8,24},{12,28},{16,0},{20,4},{24,8},{28,12},{1,17},{... | collective-permute-start | bytes 700424 | tf_op jit(solution)/shard_map/ppermute | solution.py:37
  162.4 16.8 %collective-permute-start.40 = (bf16[304,384]{1,0:T(8,128)(2,1)}, bf16[304,384]{1,0:T(8,128)(2,1)S(1)}, u32[]{:S(2)}, u32[]{:S(2)}) collective-permute-start(bf16[304,384]{1,0:T(8,128)(2,1)} %copy-done.24), channel_id=1, source_target_pairs={{0,8},{4,12},{8,0},{12,4},{16,24},{20,28},{24,16},{28,20},{1,9},{5... | collective-permute-start | bytes 700424 | tf_op jit(solution)/shard_map/ppermute | solution.py:37
  168.2 10.8 %collective-permute-start.38 = (bf16[304,384]{1,0:T(8,128)(2,1)S(1)}, bf16[304,384]{1,0:T(8,128)(2,1)S(1)}, u32[]{:S(2)}, u32[]{:S(2)}) collective-permute-start(bf16[304,384]{1,0:T(8,128)(2,1)S(1)} %add_convert_fusion.3), channel_id=1, source_target_pairs={{0,16},{4,20},{8,24},{12,28},{16,0},{20,4},{24,8},{28,12},{1,17},{... | collective-permute-start | bytes 700424 | tf_op jit(solution)/shard_map/ppermute | solution.py:37
  169.8 9.1 %collective-permute-start.41 = (bf16[304,384]{1,0:T(8,128)(2,1)S(1)}, bf16[304,384]{1,0:T(8,128)(2,1)S(1)}, u32[]{:S(2)}, u32[]{:S(2)}) collective-permute-start(bf16[304,384]{1,0:T(8,128)(2,1)S(1)} %add_convert_fusion.2), channel_id=1, source_target_pairs={{0,8},{4,12},{8,0},{12,4},{16,24},{20,28},{24,16},{28,20},{1,9},{5... | collective-permute-start | bytes 700424 | tf_op jit(solution)/shard_map/ppermute | solution.py:37
  180.8 10.1 %collective-permute-start.44 = (bf16[160,384]{1,0:T(8,128)(2,1)S(1)}, bf16[160,384]{1,0:T(8,128)(2,1)S(1)}, u32[]{:S(2)}, u32[]{:S(2)}) collective-permute-start(bf16[160,384]{1,0:T(8,128)(2,1)S(1)} %get-tuple-element.189), channel_id=1, source_target_pairs={{0,1},{1,0},{2,3},{3,2},{4,5},{5,4},{6,7},{7,6},{8,9},{9,8},{10,11... | collective-permute-start | bytes 368648 | tf_op jit(solution)/shard_map/ppermute | solution.py:37
  181.8 9.3 %collective-permute-start.47 = (bf16[160,384]{1,0:T(8,128)(2,1)S(1)}, bf16[160,384]{1,0:T(8,128)(2,1)S(1)}, u32[]{:S(2)}, u32[]{:S(2)}) collective-permute-start(bf16[160,384]{1,0:T(8,128)(2,1)S(1)} %get-tuple-element.187), channel_id=1, source_target_pairs={{0,3},{1,2},{2,1},{3,0},{4,7},{5,6},{6,5},{7,4},{8,11},{9,10},{10,... | collective-permute-start | bytes 368648 | tf_op jit(solution)/shard_map/ppermute | solution.py:37
  184.3 11.0 %collective-permute-start.46 = (bf16[160,384]{1,0:T(8,128)(2,1)S(1)}, bf16[160,384]{1,0:T(8,128)(2,1)S(1)}, u32[]{:S(2)}, u32[]{:S(2)}) collective-permute-start(bf16[160,384]{1,0:T(8,128)(2,1)S(1)} %get-tuple-element.188), channel_id=1, source_target_pairs={{0,2},{1,3},{2,0},{3,1},{4,6},{5,7},{6,4},{7,5},{8,10},{9,11},{10,... | collective-permute-start | bytes 368648 | tf_op jit(solution)/shard_map/ppermute | solution.py:37
  196.7 12.8 %collective-permute-start.48 = (bf16[13,13,8,384]{3,2,1,0:T(8,128)(2,1)}, bf16[13,13,8,384]{3,2,1,0:T(8,128)(2,1)}, u32[]{:S(2)}, u32[]{:S(2)}) collective-permute-start(bf16[13,13,8,384]{3,2,1,0:T(8,128)(2,1)} %get-tuple-element.174), channel_id=1, source_target_pairs={{0,4},{4,0},{8,12},{12,8},{16,20},{20,16},{24,28},{28,24},{1,5},{5... | collective-permute-start | bytes 3115016 | tf_op jit(solution)/shard_map/ppermute | solution.py:37
  197.8 17.7 %collective-permute-start.49 = (bf16[160,384]{1,0:T(8,128)(2,1)S(1)}, bf16[160,384]{1,0:T(8,128)(2,1)S(1)}, u32[]{:S(2)}, u32[]{:S(2)}) collective-permute-start(bf16[160,384]{1,0:T(8,128)(2,1)S(1)} %add_convert_fusion.6.refs_0_), channel_id=1, source_target_pairs={{0,1},{1,0},{2,3},{3,2},{4,5},{5,4},{6,7},{7,6},{8,9},{9,8},{10,11... | collective-permute-start | bytes 368648 | tf_op jit(solution)/shard_map/ppermute | solution.py:37
  197.9 17.6 %collective-permute-start.50 = (bf16[160,384]{1,0:T(8,128)(2,1)S(1)}, bf16[160,384]{1,0:T(8,128)(2,1)S(1)}, u32[]{:S(2)}, u32[]{:S(2)}) collective-permute-start(bf16[160,384]{1,0:T(8,128)(2,1)S(1)} %add_convert_fusion.6.refs_0_), channel_id=1, source_target_pairs={{0,2},{1,3},{2,0},{3,1},{4,6},{5,7},{6,4},{7,5},{8,10},{9,11},{10,... | collective-permute-start | bytes 368648 | tf_op jit(solution)/shard_map/ppermute | solution.py:37
  200.7 14.7 %collective-permute-start.51 = (bf16[160,384]{1,0:T(8,128)(2,1)S(1)}, bf16[160,384]{1,0:T(8,128)(2,1)S(1)}, u32[]{:S(2)}, u32[]{:S(2)}) collective-permute-start(bf16[160,384]{1,0:T(8,128)(2,1)S(1)} %add_convert_fusion.6.refs_0_), channel_id=1, source_target_pairs={{0,3},{1,2},{2,1},{3,0},{4,7},{5,6},{6,5},{7,4},{8,11},{9,10},{10,... | collective-permute-start | bytes 368648 | tf_op jit(solution)/shard_map/ppermute | solution.py:37
  (47 other events, 303.7 us)

commit v2 on v1

--- a/solution.py
+++ b/solution.py
@@ -16,9 +16,11 @@
 TAPS = 9
 CELLS = 36
 EXTRA = 16
+PORTION = 160
 LANES = 128
 WHOLE = pl.BlockSpec(memory_space=pltpu.VMEM)
 SCALARS = pl.BlockSpec(memory_space=pltpu.SMEM)
+BRIEF = pl.CostEstimate(flops=0, bytes_accessed=0, transcendentals=0)
 NN = (((1,), (0,)), ((), ()))
 NT = (((1,), (1,)), ((), ()))
 TN = (((0,), (0,)), ((), ()))
@@ -114,8 +116,14 @@
     _, lines, width_in = conv_weight.shape
     shard = conv_bias.shape[-1]
 
-    def kernel(core_ref, w_ref, bias_ref, mix_ref, keep_ref, give_ref):
+    def kernel(core_ref, w_hbm, bias_hbm, mix_hbm, keep_ref, give_ref, w_ref, bias_ref, mix_ref, sems):
+        pairs = ((bias_hbm, bias_ref), (mix_hbm, mix_ref), (w_hbm, w_ref))
+        copies = [pltpu.make_async_copy(source, held, sems.at[i]) for i, (source, held) in enumerate(pairs)]
+        for copy in copies:
+            copy.start()
         first = core_ref[0] == 0
+        for copy in copies:
+            copy.wait()
         for a, out in enumerate((keep_ref, give_ref)):
             out[:lines, :] = w_ref[core_ref[0] ^ a].astype(LOW)
             choose = lambda p, q: jnp.where(first, *((q, p) if a else (p, q)))
@@ -129,14 +137,16 @@
             out[lines:, :] = jnp.zeros((EXTRA, width_in), LOW)
             out[lines:, :shard] = jnp.concatenate(rows, axis=0).astype(LOW)
 
+    sources = (conv_weight, conv_bias, stitch_conv)
     return pl.pallas_call(
         kernel,
-        in_specs=[SCALARS] + [WHOLE] * 3,
+        in_specs=[SCALARS] + [pl.BlockSpec(memory_space=pltpu.HBM)] * 3,
         out_specs=[WHOLE] * 2,
         out_shape=[like((lines + EXTRA, width_in), LOW)] * 2,
+        scratch_shapes=[pltpu.VMEM(value.shape, WIDE) for value in sources] + [pltpu.SemaphoreType.DMA((3,))],
         compiler_params=pltpu.CompilerParams(vmem_limit_bytes=8 << 20),
-        cost_estimate=pl.CostEstimate(flops=0, bytes_accessed=8 * lines * width_in, transcendentals=0),
-    )(core, conv_weight, conv_bias, stitch_conv)
+        cost_estimate=BRIEF,
+    )(core, *(pltpu.with_memory_space_constraint(value, pltpu.HBM) for value in sources))
 
 
 def fc_prepare(fc_weight, core, gate):
@@ -165,7 +175,7 @@
         ),
         out_shape=[like((rows, units), LOW)] * 2,
         compiler_params=pltpu.CompilerParams(vmem_limit_bytes=12 << 20),
-        cost_estimate=pl.CostEstimate(flops=0, bytes_accessed=6 * fc_weight.size, transcendentals=0),
+        cost_estimate=BRIEF,
     )(core, fc_weight, fc_weight, gate)
 
 
@@ -179,9 +189,15 @@
 
     def kernel(core_ref, chip_ref, x_ref, *refs):
         pieces = refs[:count]
-        pooled_ref, slope_out, small_ref = refs[count : count + 3]
-        weights, acc, slope_ref, sems = refs[count + 3 :]
+        pooled_ref, slope_out, small_ref, weights_out = refs[count : count + 4]
+        weights, acc, slope_ref, sems = refs[count + 4 :]
         copies = [pltpu.make_async_copy(slope_ref.at[h], slope_out.at[h], sems.at[h]) for h in range(side)]
+        copies += [
+            pltpu.make_async_copy(
+                weights.at[:, pl.ds(tap * width_in, width_in)], weights_out.at[tap], sems.at[side + tap]
+            )
+            for tap in range(TAPS)
+        ]
         lane = lax.broadcasted_iota(jnp.int32, (EXTRA, LANES), 1) // shard
         smalls = [jnp.zeros((EXTRA, LANES), WIDE) for _ in range(full // LANES)]
         for j in range(count // 2):
@@ -199,6 +215,8 @@
                     smalls[v] = jnp.where(lane + v * slots == where, spread, smalls[v])
         for v, value in enumerate(smalls):
             small_ref[:, v * LANES : (v + 1) * LANES] = value
+        for copy in copies[side:]:
+            copy.start()
         line = side * group
         bias = small_ref[0:1, :]
         for low, high_row in ((0, (side + 1) // 2), ((side + 1) // 2, side)):
@@ -225,24 +243,21 @@
     return pl.pallas_call(
         kernel,
         in_specs=[SCALARS] * 2 + [WHOLE] * (1 + count),
-        out_specs=[WHOLE, pl.BlockSpec(memory_space=pltpu.HBM), WHOLE],
+        out_specs=[WHOLE, pl.BlockSpec(memory_space=pltpu.HBM), WHOLE, pl.BlockSpec(memory_space=pltpu.HBM)],
         out_shape=[
             like((CELLS, group, full), WIDE),
-            like((side, side, group, full), LOW),
+            pltpu.HBM((side, side, group, full), LOW),
             like((EXTRA, full), WIDE),
+            pltpu.HBM((TAPS, full, width_in), LOW),
         ],
         scratch_shapes=[
             pltpu.VMEM((full, TAPS * width_in), LOW),
             pltpu.VMEM((area, full), WIDE),
             pltpu.VMEM((side, side, group, full), LOW),
-            pltpu.SemaphoreType.DMA((side,)),
+            pltpu.SemaphoreType.DMA((side + TAPS,)),
         ],
         compiler_params=pltpu.CompilerParams(vmem_limit_bytes=16 << 20),
-        cost_estimate=pl.CostEstimate(
-            flops=2 * area * TAPS * width_in * full,
-            bytes_accessed=2 * images.size + 2 * area * full,
-            transcendentals=0,
-        ),
+        cost_estimate=BRIEF,
     )(core, chip, images, *parts)
 
 
@@ -286,7 +301,7 @@
         out_shape=[like((group, rows), LOW)] * planes,
         scratch_shapes=[pltpu.VMEM((planes, group, rows), LOW)],
         compiler_params=pltpu.CompilerParams(vmem_limit_bytes=8 << 20),
-        cost_estimate=pl.CostEstimate(flops=4 * pooled.size, bytes_accessed=8 * pooled.size, transcendentals=0),
+        cost_estimate=BRIEF,
     )(core, plane, pooled, other, small)
 
 
@@ -319,9 +334,7 @@
         out_shape=[like((n_images, rows), LOW)]
         + [like((block, 2 * units), LOW if k else WIDE) for k in range(planes)],
         compiler_params=pltpu.CompilerParams(vmem_limit_bytes=16 << 20),
-        cost_estimate=pl.CostEstimate(
-            flops=4 * n_images * rows * units, bytes_accessed=4 * rows * units, transcendentals=0
-        ),
+        cost_estimate=BRIEF,
     )(chip, *gathered, *weights)
 
 
@@ -362,9 +375,7 @@
             pltpu.VMEM((n_images, rows), LOW),
         ],
         compiler_params=pltpu.CompilerParams(vmem_limit_bytes=20 << 20),
-        cost_estimate=pl.CostEstimate(
-            flops=4 * n_images * rows * units, bytes_accessed=4 * rows * units, transcendentals=0
-        ),
+        cost_estimate=BRIEF,
     )(chip, *grads, crossed, *weights)
 
 
@@ -388,8 +399,9 @@
         own_refs, other_ref = refs[:planes], refs[planes]
         a_ref, b_ref, slope_ref, x_ref, small_ref = refs[planes + 1 : planes + 6]
         outs = refs[planes + 6 : planes + 6 + shards]
-        grad_ref = refs[planes + 6 + shards]
-        flat, pool_grad, turned, taps, smalls = refs[planes + 7 + shards :]
+        grad_out = refs[planes + 6 + shards]
+        flat, pool_grad, turned, taps, smalls, grad_ref, sem = refs[planes + 7 + shards :]
+        copy = pltpu.make_async_copy(grad_ref, grad_out, sem)
         place = lane_place(width)
         first = core_ref[0] == 0
         for k in range(planes):
@@ -423,6 +435,7 @@
                 value = (value * slope_ref[h, w].astype(WIDE)).astype(LOW)
                 grad_ref[h, w] = value
                 sum_bias += value.astype(WIDE)
+        copy.start()
         turned[...] = grad_ref[...].reshape(area, full).T
         for start in range(0, TAPS, 2):
             some = range(start, min(start + 2, TAPS))
@@ -451,26 +464,25 @@
                     value = jnp.where(where % slots == s, moved, value)
                 out[TAPS * shard :, :] = jnp.zeros((EXTRA, width_in), LOW)
                 out[TAPS * shard :, :LANES] = jnp.where(lane < shard, value, 0.0).astype(LOW)
+        copy.wait()
 
     return pl.pallas_call(
         kernel,
         in_specs=[SCALARS] * 3 + [pl.BlockSpec(memory_space=pl.ANY)] + [WHOLE] * (planes + 6),
-        out_specs=[WHOLE] * (shards + 1),
+        out_specs=[WHOLE] * shards + [pl.BlockSpec(memory_space=pltpu.HBM)],
         out_shape=[like((TAPS * shard + EXTRA, width_in), LOW)] * shards
-        + [like((side, side, group, full), LOW)],
+        + [pltpu.HBM((side, side, group, full), LOW)],
         scratch_shapes=[
             pltpu.VMEM((2, planes, group, cells * width), WIDE),
             pltpu.VMEM((cells, group, full), WIDE),
             pltpu.VMEM((full, area), LOW),
             pltpu.VMEM((TAPS, full, width_in), LOW),
             pltpu.VMEM((columns, EXTRA, LANES), WIDE),
+            pltpu.VMEM((side, side, group, full), LOW),
+            pltpu.SemaphoreType.DMA(()),
         ],
         compiler_params=pltpu.CompilerParams(vmem_limit_bytes=14 << 20),
-        cost_estimate=pl.CostEstimate(
-            flops=2 * area * TAPS * width_in * full,
-            bytes_accessed=2 * images.size + 6 * area * full,
-            transcendentals=0,
-        ),
+        cost_estimate=BRIEF,
     )(core, chip, plane, gate, *own, other, pooled, pooled_other, slope, images, small)
 
 
@@ -484,55 +496,67 @@
     steps = 4
     few = width // 2
     tall = depth // 2 // steps
+    hbm = pl.BlockSpec(memory_space=pltpu.HBM)
     weight, moment = (pltpu.with_memory_space_constraint(value, pltpu.HBM) for value in (weight, moment))
 
-    def kernel(core_ref, w_ref, m_ref, rows_ref, *refs):
+    def kernel(core_ref, w_hbm, m_hbm, rows_ref, *refs):
         grad_refs = refs[:planes]
-        new_w, new_m, token, joined, product = refs[-5:]
-        step = pl.program_id(0)
-
-        @pl.when(step == 0)
-        def _():
-            token[...] = jnp.zeros_like(token)
-            for k in range(planes):
-                joined[pl.ds(k * block, block), :] = grad_refs[k][which]
+        new_w, new_m, token, joined, product, held_w, held_m, sems = refs[-8:]
+        tower = core_ref[0] ^ which
+
+        def copies(pairs, s, first):
+            at = pl.ds((part * steps + s) * tall, tall)
+            return [
+                pltpu.make_async_copy(held.at[s], hbm_ref.at[tower, at, :], sems.at[s, first + i])
+                if first
+                else pltpu.make_async_copy(hbm_ref.at[tower, at, :], held.at[s], sems.at[s, i])
+                for i, (hbm_ref, held) in enumerate(pairs)
+            ]
+
+        loads = [copies(((w_hbm, held_w), (m_hbm, held_m)), s, 0) for s in range(steps)]
+        stores = [copies(((new_w, held_w), (new_m, held_m)), s, 2) for s in range(steps)]
+        for pair in loads:
+            for copy in pair:
+                copy.start()
+        token[...] = jnp.zeros_like(token)
+        for k in range(planes):
+            joined[pl.ds(k * block, block), :] = grad_refs[k][which]
+        for v in range(columns):
+            grad = dot(rows_ref[...], joined[:, v * LANES : (v + 1) * LANES], TN)
+            for cell in range(CELLS):
+                start = cell * width + part * few
+                product[v, pl.ds(cell, few, stride=CELLS), :] = grad[start : start + few]
+        for s in range(steps):
+            for copy in loads[s]:
+                copy.wait()
             for v in range(columns):
-                grad = dot(rows_ref[...], joined[:, v * LANES : (v + 1) * LANES], TN)
-                for cell in range(CELLS):
-                    start = cell * width + part * few
-                    product[v, pl.ds(cell, few, stride=CELLS), :] = grad[start : start + few]
-
-        at = pl.ds(pl.multiple_of(step * tall, tall), tall)
-        for v in range(columns):
-            lanes = slice(v * LANES, (v + 1) * LANES)
-            fresh = MOMENTUM * m_ref[0, :, lanes] + product[v, at, :]
-            new_m[0, :, lanes] = fresh
-            new_w[0, :, lanes] = w_ref[0, :, lanes] - LEARN_RATE * fresh
-
-    big = pl.BlockSpec((1, tall, units), lambda s, core: (core[0] ^ which, part * steps + s, 0))
-    fixed = lambda shape: pl.BlockSpec(shape, lambda s, core: (0,) * len(shape))
+                at = (s, slice(None), slice(v * LANES, (v + 1) * LANES))
+                fresh = MOMENTUM * held_m[at] + product[v, s * tall : (s + 1) * tall, :]
+                held_m[at] = fresh
+                held_w[at] = held_w[at] - LEARN_RATE * fresh
+            for copy in stores[s]:
+                copy.start()
+        for pair in stores:
+            for copy in pair:
+                copy.wait()
+
     anywhere = pl.BlockSpec(memory_space=pl.ANY)
     extra = [] if previous is None else list(previous)
     return pl.pallas_call(
         kernel,
-        grid_spec=pltpu.PrefetchScalarGridSpec(
-            num_scalar_prefetch=1,
-            grid=(steps,),
-            in_specs=[big, big, fixed(rows.shape)]
-            + [fixed(value.shape) for value in grads]
-            + [anywhere] * (len(extra) + 1),
-            out_specs=[big, big, fixed((8, LANES))],
-            scratch_shapes=[
-                pltpu.VMEM((n_images, units), LOW),
-                pltpu.VMEM((columns, depth // 2, LANES), WIDE),
-            ],
-        ),
-        out_shape=[like(weight.shape, WIDE)] * 2 + [like((8, LANES), WIDE)],
+        in_specs=[SCALARS, hbm, hbm] + [WHOLE] * (1 + planes) + [hbm] * len(extra) + [anywhere],
+        out_specs=[hbm, hbm, WHOLE],
+        out_shape=[pltpu.HBM(weight.shape, WIDE)] * 2 + [like((8, LANES), WIDE)],
+        scratch_shapes=[
+            pltpu.VMEM((n_images, units), LOW),
+            pltpu.VMEM((columns, depth // 2, LANES), WIDE),
+            pltpu.VMEM((steps, tall, units), WIDE),
+            pltpu.VMEM((steps, tall, units), WIDE),
+            pltpu.SemaphoreType.DMA((steps, 4)),
+        ],
         input_output_aliases={} if previous is None else {4 + planes: 0, 5 + planes: 1},
-        compiler_params=pltpu.CompilerParams(vmem_limit_bytes=14 << 20),
-        cost_estimate=pl.CostEstimate(
-            flops=2 * n_images * depth * units, bytes_accessed=8 * depth * units, transcendentals=0
-        ),
+        compiler_params=pltpu.CompilerParams(vmem_limit_bytes=12 << 20),
+        cost_estimate=BRIEF,
     )(core, weight, moment, rows, *grads, *extra, gate)
 
 
@@ -547,11 +571,11 @@
         out_specs=WHOLE,
         out_shape=like((2, *own.shape), own.dtype),
         compiler_params=pltpu.CompilerParams(vmem_limit_bytes=8 << 20),
-        cost_estimate=pl.CostEstimate(flops=0, bytes_accessed=8 * own.size, transcendentals=0),
+        cost_estimate=BRIEF,
     )(core, own, other)
 
 
-def small_update(gates, pieces, lines, params, moments, core, plane):
+def small_update(gate, ready, pieces, lines, params, moments, core, plane):
     planes = len(pieces)
     height, width_in = pieces[0].shape
     shard = params[1].shape[-1]
@@ -559,11 +583,11 @@
     count = lines - EXTRA
     rates = (LEARN_RATE, BIAS_RATE, STITCH_RATE, STITCH_RATE)
 
-    def kernel(core_ref, plane_ref, done_ref, ready_ref, *refs):
+    def kernel(core_ref, plane_ref, gate_ref, ready_ref, *refs):
         piece_refs = refs[:planes]
         p_refs, m_refs = refs[planes : planes + 4], refs[planes + 4 : planes + 8]
         new_p, new_m = refs[planes + 8 : planes + 12], refs[planes + 12 : planes + 16]
-        whole = refs[planes + 16]
+        whole = refs[planes + 17]
         for k in range(planes):
             at = pl.ds(pl.multiple_of((plane_ref[0] ^ k) * height, height), height)
             whole[at, :] = piece_refs[k][...].astype(WIDE)
@@ -596,13 +620,16 @@
     out_shape = [like(value.shape, WIDE) for value in (*params, *moments)]
     return pl.pallas_call(
         kernel,
-        in_specs=[SCALARS] * 2 + [pl.BlockSpec(memory_space=pl.ANY)] * 2 + [WHOLE] * (planes + 8),
-        out_specs=[WHOLE] * 8,
-        out_shape=out_shape,
+        in_specs=[SCALARS] * 2
+        + [pl.BlockSpec(memory_space=pl.ANY), pl.BlockSpec(memory_space=pltpu.HBM)]
+        + [WHOLE] * (planes + 8),
+        out_specs=[WHOLE] * 8 + [pl.BlockSpec(memory_space=pltpu.HBM)],
+        out_shape=out_shape + [pltpu.HBM(ready.shape, ready.dtype)],
+        input_output_aliases={3: 8},
         scratch_shapes=[pltpu.VMEM((planes * height, width_in), WIDE)],
         compiler_params=pltpu.CompilerParams(vmem_limit_bytes=12 << 20),
-        cost_estimate=pl.CostEstimate(flops=0, bytes_accessed=24 * 2 * lines * width_in, transcendentals=0),
-    )(core, plane, *gates, *pieces, *params, *moments)
+        cost_estimate=BRIEF,
+    )(core, plane, gate, ready, *pieces, *params, *moments)
 
 
 def reorder(parts, place):
@@ -898,7 +925,6 @@
     as_scalar = lambda value: value.reshape(1).astype(jnp.int32)
     core_at, chip_at, plane_at = as_scalar(core), as_scalar(chip), as_scalar(plane)
     swap = lambda value: trade(value, "chan", 1)
-    mine = lambda a, b: jnp.where(core == 0, a, b)
     per_core, side, width_in = images.shape[0], images.shape[2], images.shape[-1]
     shard = conv_weight.shape[-1]
     units = fc_weight.shape[-1]
@@ -906,18 +932,25 @@
 
     as_rows = lambda value: jnp.transpose(value, (0, 1, 2, 4, 3)).reshape(2, TAPS * shard, width_in)
     keep, give = pack_kernels(as_rows(conv_weight), conv_bias, stitch_conv, core_at)
-    got = swap(give)
-    kernel_parts = [part for pair in gather_chips(keep, got, chips) for part in pair]
+    starts = [(plane ^ k).astype(jnp.uint32) * jnp.uint32(PORTION) for k in range(planes)]
+    keep, give, core_at, chip_at, plane_at, first_core, starts = tie(
+        keep, give, core_at, chip_at, plane_at, core == 0, starts
+    )
+    mine = lambda a, b: jnp.where(first_core, a, b)
+    keep_y, give_x = trade(keep, "chan", 4), trade(give, "chan", 3)
+    keep_x, give_y = trade(keep, "chan", 2), trade(give, "chan", 5)
+    keep_d, give_d = trade(keep_y, "chan", 2), trade(give_x, "chan", 4)
+    kernel_parts = [keep, swap(give), keep_x, give_x, keep_y, give_y, keep_d, give_d]
     fc_own, fc_give = fc_prepare(fc_weight, core_at, kernel_parts[3])
     fc_cross = swap(fc_give)
 
-    late_core, kernel_parts[3] = tie(core, kernel_parts[3])
+    late_core, kernel_parts[3] = tie(first_core, kernel_parts[3])
     towers = lax.optimization_barrier(jnp.transpose(images, (1, 2, 3, 0, 4)))
-    keep, give = (jnp.where(late_core == 0, towers[a], towers[1 - a]) for a in range(2))
+    keep, give = (jnp.where(late_core, towers[a], towers[1 - a]) for a in range(2))
     tower_images = jnp.concatenate([keep, swap(give)], axis=2)
     tower_images = jnp.pad(tower_images, ((1, 1), (1, 1), (0, 0), (0, 0)))
 
-    pooled, slope, small_all = conv_forward(tower_images, kernel_parts, core_at, chip_at)
+    pooled, slope, small_all, joined = conv_forward(tower_images, kernel_parts, core_at, chip_at)
     pooled_other = swap(pooled)
     pieces = mix_pieces(pooled, pooled_other, small_all, core_at, plane_at, planes)
     got = exchange_planes(pieces)
@@ -939,10 +972,17 @@
     grad_low = jnp.stack(
         [(slopes[b] * (mix[0][b] * out_grad[0] + mix[1][b] * out_grad[1])).astype(LOW) for b in range(2)]
     )
-    stitch_fc_grad = jnp.stack(
-        [jnp.stack([jnp.sum(out_grad[a] * acts[b], axis=0) for b in range(2)]) for a in range(2)]
-    )
+    stitch_fc_grad = jnp.concatenate(
+        [jnp.sum(out_grad[a] * acts[b], axis=0, keepdims=True) for a in range(2) for b in range(2)]
+    )
+    packed = jnp.concatenate(
+        [
+            jnp.pad(stitch_fc_grad[:, at : at + width_in], ((0, 0), (0, max(0, at + width_in - units))))
+            for at in range(0, units, width_in)
+        ]
+    ).astype(LOW)
     grads = exchange_planes([grad_low] * planes)
+    grads[1], packed = tie(grads[1], packed)
     grads_cross = swap(jnp.stack([value[1] for value in grads]))
 
     step = done = None
@@ -978,12 +1018,7 @@
             preferred_element_type=WIDE,
         ).astype(LOW)
 
-    full_chan = conv_grad.shape[-1]
-    ordered = reorder([(kernel_parts[2 * j], kernel_parts[2 * j + 1]) for j in range(chips)], chip)
-    ordered = [part for a, b in ordered for part in (mine(a, b), mine(b, a))]
-    kernel = jnp.concatenate(
-        [part[: TAPS * shard].reshape(3, 3, shard, width_in) for part in ordered], axis=2
-    )
+    kernel = joined.reshape(3, 3, -1, width_in)
     images_grad = None
 
     def after_sums(gate, value):
@@ -1000,15 +1035,11 @@
     towers = jnp.stack([total(first).astype(LOW), swap(total(second).astype(LOW))])
     lines = towers.shape[1]
 
-    vectors = stitch_fc_grad.reshape(4, units)
-    packed = [vectors[:, at : at + width_in] for at in range(0, units, width_in)]
-    packed = jnp.concatenate(
-        [jnp.pad(value, ((0, 0), (0, width_in - value.shape[1]))) for value in packed]
-    ).astype(LOW)
-    tail = (-(2 * lines + packed.shape[0])) % (planes * EXTRA)
-    flat = jnp.concatenate([towers.reshape(-1, width_in), jnp.pad(packed, ((0, tail), (0, 0)))])
-    flat = flat.reshape(planes, -1, width_in)
-    quarters = [lax.dynamic_index_in_dim(flat, plane ^ k, 0, keepdims=False) for k in range(planes)]
+    flat = jnp.concatenate([towers.reshape(-1, width_in), packed])
+    assert flat.shape[0] <= planes * PORTION
+    flat = jnp.pad(flat, ((0, planes * PORTION - flat.shape[0]), (0, 0)))
+    nothing = jnp.uint32(0)
+    quarters = [lax.dynamic_slice(flat, (start, nothing), (PORTION, width_in)) for start in starts]
     quarters = exchange_planes(quarters)
     *step, done = fc_update(fc_weight, fc_moment, other_rows, grads, core_at, 1, 0, step, quarters[0])
     quarters[1], done = tie(quarters[1], done)
@@ -1021,8 +1052,9 @@
     images_grad = order_towers(keep, got, core_at)
     images_grad = jnp.transpose(images_grad, (3, 1, 2, 0, 4))
 
-    new_small = small_update(
-        (done, images_grad),
+    *new_small, images_grad = small_update(
+        done,
+        images_grad,
         quarters,
         lines,
         (as_rows(conv_weight), conv_bias, stitch_conv, stitch_fc),
@@ -1032,12 +1064,12 @@
     )
 
     fc_bias_grad = sum(jnp.sum(value.astype(WIDE), axis=1) for value in grads)
-    fc_bias_grad = mine(fc_bias_grad, fc_bias_grad[::-1])
+    fc_bias_grad = jnp.stack([mine(fc_bias_grad[a], fc_bias_grad[1 - a]) for a in range(2)])
     new_fc_bias_moment = MOMENTUM * fc_bias_moment + fc_bias_grad
     new_fc_bias = fc_bias - BIAS_RATE * new_fc_bias_moment
 
     as_given = lambda value: jnp.swapaxes(value.reshape(2, 3, 3, shard, width_in), 3, 4)
-    params, fresh = list(new_small[:4]), list(new_small[4:])
+    params, fresh = new_small[:4], new_small[4:]
     params[0], fresh[0] = as_given(params[0]), as_given(fresh[0])
     params[3:3], fresh[3:3] = (step[0], new_fc_bias), (step[1], new_fc_bias_moment)
     images_grad = jnp.transpose(images_grad, (0, 3, 1, 2, 4))

time: 218 us -> 185 us (0.85)
  Pallas kernels: 62.9 us -> 46.4 us
  local copies, waits for them, and re-layouts: 18.9 us -> 6.19 us
  other arithmetic: 9.18 us -> 3.15 us
  waiting for transfers between devices: 57.4 us -> 62 us
    unnamed x96 -> x30, local copies, waits for them, and re-layouts: 14 us -> 2.72 us
    pallas_call x5, Pallas kernels: 27.3 us -> 21.6 us  [the longest x4 20.4 us: fc_update(): pl.pallas_call(kernel, in_specs=[SCALARS, hbm, hbm] + [WHOLE] * (1 + plan...]
    ppermute x52, waiting for transfers between devices: 57.4 us -> 62 us  [trade(): return lax.ppermute(value, axis, [(i, i ^ bit) for i in range(size)])]
    select_n x7 -> x4, other arithmetic: 3.26 us -> 0.2 us  [the longest x1 0.18 us: four_by_four(): jnp.where(late_core, towers[a], towers[1 - a])]
    pallas_call x1, Pallas kernels: 10.1 us -> 7.48 us  [conv_forward(): pl.pallas_call(kernel, in_specs=[SCALARS] * 2 + [WHOLE] * (1 + count), ou...]
  transfers between devices with their start and end apart: 52 -> 52, of which waited for: 23 -> 23; matrix products, arithmetic and copies ran while one was open for 11% -> 9% of each run, Pallas kernels for 25% -> 18%
where the time goes in v2:
time: 185 us
  waiting for transfers between devices  62 us (34%)
  starting transfers between devices  57.4 us (31%)
  Pallas kernels  46.4 us (25%)
  matrix products  8.16 us (4%)
  local copies, waits for them, and re-layouts  6.19 us (3%)
  other arithmetic  3.15 us (2%)
    ppermute x52, waiting for transfers between devices, trade(): return lax.ppermute(value, axis, [(i, i ^ bit) for i in range(size)])  62 us
    ppermute x52, starting transfers between devices, trade(): return lax.ppermute(value, axis, [(i, i ^ bit) for i in range(size)])  57.4 us
    pallas_call x4, Pallas kernels, fc_update(): pl.pallas_call(kernel, in_specs=[SCALARS, hbm, hbm] + [WHOLE] * (1 + plan...  20.4 us
    conv_general_dilated x1, matrix products, turned_conv(): lax.conv_general_dilated(grad, kernel[::-1, ::-1], (1, 1), 'SAME', dimens...  8.16 us
    pallas_call x1, Pallas kernels, conv_backward(): pl.pallas_call(kernel, in_specs=[SCALARS] * 3 + [pl.BlockSpec(memory_spac...  7.51 us
    pallas_call x1, Pallas kernels, conv_forward(): pl.pallas_call(kernel, in_specs=[SCALARS] * 2 + [WHOLE] * (1 + count), ou...  7.48 us
    pallas_call x1, Pallas kernels, fc_prepare(): pl.pallas_call(kernel, grid_spec=pltpu.PrefetchScalarGridSpec(num_scalar_...  4.9 us
  transfers between devices with their start and end apart: 52, of which 23 were waited for; matrix products, arithmetic and copies ran while one was open for 9% of the time, Pallas kernels for 18%

profile of v2, /device:TPU:0, one launch (start us, length us, event | category | flops | bytes accessed | tf_op | source)
XLA Modules:
  0.0 184.7 jit_solution(17240014184788075871)
XLA Ops:
  2.0 2.4 %collective-permute-start = (bf16[304,384]{1,0:T(8,128)(2,1)S(1)}, bf16[304,384]{1,0:T(8,128)(2,1)S(1)}, u32[]{:S(2)}, u32[]{:S(2)}) collective-permute-start(bf16[304,384]{1,0:T(8,128)(2,1)S(1)} %get-tuple-element.102), channel_id=1, source_target_pairs={{0,12},{4,8},{8,4},{12,0},{16,28},{20,24},{24,20},{28,16},{1,13},{... | collective-permute-start | bytes 700424 | tf_op jit(solution)/shard_map/ppermute | solution.py:39
  4.4 1.8 %copy.60 = bf16[8,2,13,13,384]{4,0,3,2,1:T(8,128)(2,1)S(1)} copy(bf16[8,2,13,13,384]{4,1,3,2,0:T(2,128)(2,1)} %param.15) | data formatting | bytes 4153344 | tf_op args[0]
  6.3 4.2 %collective-permute-done.refs_3_._ = bf16[304,384]{1,0:T(8,128)(2,1)S(1)} collective-permute-done((bf16[304,384]{1,0:T(8,128)(2,1)S(1)}, bf16[304,384]{1,0:T(8,128)(2,1)S(1)}, u32[]{:S(2)}, u32[]{:S(2)}) %collective-permute-start) | collective-permute-done | bytes 233504 | tf_op jit(solution)/shard_map/ppermute | solution.py:39
  10.8 2.5 %collective-permute-start.4 = (bf16[304,384]{1,0:T(8,128)(2,1)S(1)}, bf16[304,384]{1,0:T(8,128)(2,1)S(1)}, u32[]{:S(2)}, u32[]{:S(2)}) collective-permute-start(bf16[304,384]{1,0:T(8,128)(2,1)S(1)} %get-tuple-element.104.refs_0_), channel_id=1, source_target_pairs={{0,16},{4,20},{8,24},{12,28},{16,0},{20,4},{24,8},{28,12},{1,17},{... | collective-permute-start | bytes 700424 | tf_op jit(solution)/shard_map/ppermute | solution.py:39
  13.4 1.5 collective-permute-start.3
  15.2 4.9 %shard_map.257 = (bf16[2304,512]{1,0:T(8,128)(2,1)S(1)}, bf16[2304,512]{1,0:T(8,128)(2,1)S(1)}) custom-call(s32[1]{0:T(128)} %bitcast.core_ref, f32[2,2304,512]{2,1,0:T(8,128)} %w_hbm.7, f32[2,2304,512]{2,1,0:T(8,128)} %w_hbm.7, bf16[304,384]{1,0:T(8,128)(2,1)S(1)} %collective-permute-done.refs_3_._), custom_call_target="tpu_custom_call" | custom-call | tf_op jit(solution)/shard_map/pallas_call | solution.py:164
  20.6 1.5 collective-permute-start.7
  24.4 5.3 %collective-permute-done.6.refs_6_ = bf16[304,384]{1,0:T(8,128)(2,1)S(1)} collective-permute-done((bf16[304,384]{1,0:T(8,128)(2,1)S(1)}, bf16[304,384]{1,0:T(8,128)(2,1)S(1)}, u32[]{:S(2)}, u32[]{:S(2)}) %collective-permute-start.6) | collective-permute-done | bytes 233504 | tf_op jit(solution)/shard_map/ppermute | solution.py:39
  29.7 7.5 %shard_map.255 = (f32[36,16,256]{2,1,0:T(8,128)S(1)}, bf16[13,13,16,256]{3,2,1,0:T(8,128)(2,1)}, f32[16,256]{1,0:T(8,128)S(1)}, bf16[9,256,384]{2,1,0:T(8,128)(2,1)}) custom-call(s32[1]{0:T(128)} %bitcast.core_ref, s32[1]{0:T(128)} %bitcast.3.chip_ref, bf16[15,15,16,384]{3,2,1,0:T(8,128)(2,1)S(1)} %fusion.6.x_ref.refs_8_, ...), custom_call_target="tpu_custom_call" | custom-call | tf_op jit(solution)/shard_map/pallas_call | solution.py:243
  37.3 2.0 %collective-permute-done.8.b_ref.refs_6_ = f32[36,16,256]{2,1,0:T(8,128)S(1)} collective-permute-done((f32[36,16,256]{2,1,0:T(8,128)S(1)}, f32[36,16,256]{2,1,0:T(8,128)S(1)}, u32[]{:S(2)}, u32[]{:S(2)}) %collective-permute-start.8) | collective-permute-done | bytes 589856 | tf_op jit(solution)/shard_map/ppermute | solution.py:39
  39.4 2.8 %collective-permute-start.10 = (bf16[16,2304]{1,0:T(8,128)(2,1)S(1)}, bf16[16,2304]{1,0:T(8,128)(2,1)S(1)}, u32[]{:S(2)}, u32[]{:S(2)}) collective-permute-start(bf16[16,2304]{1,0:T(8,128)(2,1)S(1)} %get-tuple-element.110), channel_id=1, source_target_pairs={{0,2},{1,3},{2,0},{3,1},{4,6},{5,7},{6,4},{7,5},{8,10},{9,11},{10,... | collective-permute-start | bytes 221192 | tf_op jit(solution)/shard_map/ppermute | solution.py:39
  43.8 3.7 %collective-permute-done.10 = bf16[16,2304]{1,0:T(8,128)(2,1)S(1)} collective-permute-done((bf16[16,2304]{1,0:T(8,128)(2,1)S(1)}, bf16[16,2304]{1,0:T(8,128)(2,1)S(1)}, u32[]{:S(2)}, u32[]{:S(2)}) %collective-permute-start.10) | collective-permute-done | bytes 73760 | tf_op jit(solution)/shard_map/ppermute | solution.py:39
  48.9 1.6 collective-permute-start.13
  50.5 1.6 collective-permute-start.14
  53.3 2.0 %collective-permute-done.13.refs_3_ = bf16[2,16,2304]{2,1,0:T(8,128)(2,1)S(1)} collective-permute-done((bf16[2,16,2304]{2,1,0:T(8,128)(2,1)S(1)}, bf16[2,16,2304]{2,1,0:T(8,128)(2,1)S(1)}, u32[]{:S(2)}, u32[]{:S(2)}) %collective-permute-start.13) | collective-permute-done | bytes 147488 | tf_op jit(solution)/shard_map/ppermute | solution.py:39
  55.3 1.5 collective-permute-start.17
  59.1 1.6 collective-permute-done.17.refs_7_
  60.7 1.8 collective-permute-done.16.refs_6_
  65.4 2.0 %collective-permute-start.20 = (bf16[64,1024]{1,0:T(8,128)(2,1)S(1)}, bf16[64,1024]{1,0:T(8,128)(2,1)S(1)}, u32[]{:S(2)}, u32[]{:S(2)}) collective-permute-start(bf16[64,1024]{1,0:T(8,128)(2,1)S(1)} %get-tuple-element.116), channel_id=1, source_target_pairs={{0,2},{1,3},{2,0},{3,1},{4,6},{5,7},{6,4},{7,5},{8,10},{9,11},{10,... | collective-permute-start | bytes 393224 | tf_op jit(solution)/shard_map/ppermute | solution.py:39
  70.3 7.7 %collective-permute-done.20 = bf16[64,1024]{1,0:T(8,128)(2,1)S(1)} collective-permute-done((bf16[64,1024]{1,0:T(8,128)(2,1)S(1)}, bf16[64,1024]{1,0:T(8,128)(2,1)S(1)}, u32[]{:S(2)}, u32[]{:S(2)}) %collective-permute-start.20) | collective-permute-done | bytes 131104 | tf_op jit(solution)/shard_map/ppermute | solution.py:39
  79.9 2.0 %collective-permute-start.24 = (bf16[2,64,512]{2,1,0:T(8,128)(2,1)S(1)}, bf16[2,64,512]{2,1,0:T(8,128)(2,1)S(1)}, u32[]{:S(2)}, u32[]{:S(2)}) collective-permute-start(bf16[2,64,512]{2,1,0:T(8,128)(2,1)S(1)} %pad_maximum_fusion.6.refs_0_), channel_id=1, source_target_pairs={{0,1},{1,0},{2,3},{3,2},{4,5},{5,4},{6,7},{7,6},{8,9},{9,8},{10,11... | collective-permute-start | bytes 393224 | tf_op jit(solution)/shard_map/ppermute | solution.py:39
  81.9 2.5 %collective-permute-start.26 = (bf16[2,64,512]{2,1,0:T(8,128)(2,1)S(1)}, bf16[2,64,512]{2,1,0:T(8,128)(2,1)S(1)}, u32[]{:S(2)}, u32[]{:S(2)}) collective-permute-start(bf16[2,64,512]{2,1,0:T(8,128)(2,1)S(1)} %pad_maximum_fusion.6.refs_0_), channel_id=1, source_target_pairs={{0,3},{1,2},{2,1},{3,0},{4,7},{5,6},{6,5},{7,4},{8,11},{9,10},{10,... | collective-permute-start | bytes 393224 | tf_op jit(solution)/shard_map/ppermute | solution.py:39
  85.7 10.0 %collective-permute-done.25.refs_2_ = bf16[2,64,512]{2,1,0:T(8,128)(2,1)S(1)} collective-permute-done((bf16[2,64,512]{2,1,0:T(8,128)(2,1)S(1)}, bf16[2,64,512]{2,1,0:T(8,128)(2,1)S(1)}, u32[]{:S(2)}, u32[]{:S(2)}) %collective-permute-start.25) | collective-permute-done | bytes 131104 | tf_op jit(solution)/shard_map/ppermute | solution.py:39
  95.8 1.5 collective-permute-done.27.refs_4_
  97.4 1.5 shard_map.259
  99.5 1.5 collective-permute-start.28
  101.0 1.5 collective-permute-start.31
  103.0 2.6 %collective-permute-done.32 = bf16[2,16,2304]{2,1,0:T(8,128)(2,1)S(1)} collective-permute-done((bf16[2,16,2304]{2,1,0:T(8,128)(2,1)S(1)}, bf16[2,16,2304]{2,1,0:T(8,128)(2,1)S(1)}, u32[]{:S(2)}, u32[]{:S(2)}) %collective-permute-start.32) | collective-permute-done | bytes 147488 | tf_op jit(solution)/shard_map/ppermute | solution.py:39
  105.7 1.6 collective-permute-start.33
  107.9 5.1 %shard_map.260 = (f32[2,2304,512]{2,1,0:T(8,128)}, f32[2,2304,512]{2,1,0:T(8,128)}, f32[8,128]{1,0:T(8,128)S(1)}) custom-call(s32[1]{0:T(128)} %bitcast.core_ref, f32[2,2304,512]{2,1,0:T(8,128)} %w_hbm.7, f32[2,2304,512]{2,1,0:T(8,128)} %m_hbm.7, bf16[256,2304]{1,0:T(8,128)(2,1)S(1)} %get-tuple-element.118.rows_ref, ...), custom_call_target="tpu_custom_call" | custom-call | tf_op jit(solution)/shard_map/pallas_call | solution.py:545
  113.2 2.8 %collective-permute-start.35 = (bf16[16,2304]{1,0:T(8,128)(2,1)S(1)}, bf16[16,2304]{1,0:T(8,128)(2,1)S(1)}, u32[]{:S(2)}, u32[]{:S(2)}) collective-permute-start(bf16[16,2304]{1,0:T(8,128)(2,1)S(1)} %get-tuple-element.210), channel_id=1, source_target_pairs={{0,2},{1,3},{2,0},{3,1},{4,6},{5,7},{6,4},{7,5},{8,10},{9,11},{10,... | collective-permute-start | bytes 221192 | tf_op jit(solution)/shard_map/ppermute | solution.py:39
  116.0 1.7 collective-permute-start.36
  117.7 5.1 %shard_map.261 = (f32[2,2304,512]{2,1,0:T(8,128)}, f32[2,2304,512]{2,1,0:T(8,128)}, f32[8,128]{1,0:T(8,128)S(1)}) custom-call(s32[1]{0:T(128)} %bitcast.core_ref, f32[2,2304,512]{2,1,0:T(8,128)} %w_hbm.7, f32[2,2304,512]{2,1,0:T(8,128)} %m_hbm.7, bf16[256,2304]{1,0:T(8,128)(2,1)S(1)} %get-tuple-element.118.rows_ref, ...), custom_call_target="tpu_custom_call", output_to_operand_aliasing={{0}: (8, {}), {1}: (9, {})} | custom-call | tf_op jit(solution)/shard_map/pallas_call | solution.py:545
  122.9 1.6 collective-permute-done.37.refs_4_
  124.5 7.5 %shard_map.262 = (bf16[304,384]{1,0:T(8,128)(2,1)S(1)}, bf16[304,384]{1,0:T(8,128)(2,1)S(1)}, bf16[304,384]{1,0:T(8,128)(2,1)S(1)}, bf16[304,384]{1,0:T(8,128)(2...) custom-call(s32[1]{0:T(128)} %bitcast.core_ref, ...), custom_call_target="tpu_custom_call" | custom-call | tf_op jit(solution)/shard_map/pallas_call | solution.py:469
  132.0 1.5 collective-permute-start.41
  136.1 4.5 %collective-permute-done.41 = bf16[304,384]{1,0:T(8,128)(2,1)S(1)} collective-permute-done((bf16[304,384]{1,0:T(8,128)(2,1)S(1)}, bf16[304,384]{1,0:T(8,128)(2,1)S(1)}, u32[]{:S(2)}, u32[]{:S(2)}) %collective-permute-start.41) | collective-permute-done | bytes 233504 | tf_op jit(solution)/shard_map/ppermute | solution.py:39
  142.7 1.5 collective-permute-start.42
  144.3 8.2 %convolution_convert_fusion = bf16[13,13,16,384]{3,2,1,0:T(8,128)(2,1)S(1)} fusion(bf16[13,13,16,256]{3,2,1,0:T(8,128)(2,1)} %get-tuple-element.147, bf16[3,3,256,384]{3,2,1,0:T(8,128)(2,1)S(1)} %bitcast.123), kind=kOutput, calls=%fused_computation.14 | convolution fusion | flops 4307539968 | bytes 5230592 | tf_op jit(solution)/shard_map/conv_general_dilated | solution.py:1012
  154.5 2.7 %collective-permute-start.46 = (bf16[160,384]{1,0:T(8,128)(2,1)S(1)}, bf16[160,384]{1,0:T(8,128)(2,1)S(1)}, u32[]{:S(2)}, u32[]{:S(2)}) collective-permute-start(bf16[160,384]{1,0:T(8,128)(2,1)S(1)} %get-tuple-element.206), channel_id=1, source_target_pairs={{0,2},{1,3},{2,0},{3,1},{4,6},{5,7},{6,4},{7,5},{8,10},{9,11},{10,... | collective-permute-start | bytes 368648 | tf_op jit(solution)/shard_map/ppermute | solution.py:39
  157.2 1.6 collective-permute-start.47
  158.9 5.1 %shard_map.263 = (f32[2,2304,512]{2,1,0:T(8,128)}, f32[2,2304,512]{2,1,0:T(8,128)}, f32[8,128]{1,0:T(8,128)S(1)}) custom-call(s32[1]{0:T(128)} %bitcast.core_ref, f32[2,2304,512]{2,1,0:T(8,128)} %w_hbm.7, f32[2,2304,512]{2,1,0:T(8,128)} %m_hbm.7, ...), custom_call_target="tpu_custom_call", output_to_operand_aliasing={{0}: (8, {}), {1}: (9, {})} | custom-call | tf_op jit(solution)/shard_map/pallas_call | solution.py:545
  164.0 3.0 %collective-permute-done.46 = bf16[160,384]{1,0:T(8,128)(2,1)S(1)} collective-permute-done((bf16[160,384]{1,0:T(8,128)(2,1)S(1)}, bf16[160,384]{1,0:T(8,128)(2,1)S(1)}, u32[]{:S(2)}, u32[]{:S(2)}) %collective-permute-start.46) | collective-permute-done | bytes 122912 | tf_op jit(solution)/shard_map/ppermute | solution.py:39
  168.3 2.5 %collective-permute-start.49 = (bf16[160,384]{1,0:T(8,128)(2,1)S(1)}, bf16[160,384]{1,0:T(8,128)(2,1)S(1)}, u32[]{:S(2)}, u32[]{:S(2)}) collective-permute-start(bf16[160,384]{1,0:T(8,128)(2,1)S(1)} %add_convert_fusion.6.refs_0_), channel_id=1, source_target_pairs={{0,1},{1,0},{2,3},{3,2},{4,5},{5,4},{6,7},{7,6},{8,9},{9,8},{10,11... | collective-permute-start | bytes 368648 | tf_op jit(solution)/shard_map/ppermute | solution.py:39
  171.5 1.7 collective-permute-start.51
  173.8 5.1 %shard_map.264 = (f32[2,2304,512]{2,1,0:T(8,128)}, f32[2,2304,512]{2,1,0:T(8,128)}, f32[8,128]{1,0:T(8,128)S(1)}) custom-call(s32[1]{0:T(128)} %bitcast.core_ref, f32[2,2304,512]{2,1,0:T(8,128)} %w_hbm.7, f32[2,2304,512]{2,1,0:T(8,128)} %m_hbm.7, ...), custom_call_target="tpu_custom_call", output_to_operand_aliasing={{0}: (8, {}), {1}: (9, {})} | custom-call | tf_op jit(solution)/shard_map/pallas_call | solution.py:545
  179.2 2.9 %copy.59 = bf16[2,13,13,8,384]{4,0,2,1,3:T(2,128)(2,1)} copy(bf16[2,13,13,8,384]{4,3,2,1,0:T(8,128)(2,1)S(1)} %shard_map.265) | data formatting | bytes 4153344 | tf_op jit(solution)/shard_map/pallas_call | solution.py:568
  183.2 1.5 shard_map.266
  (145 shorter events, 33.2 us)
Async XLA Ops:
  2.0 8.5 %collective-permute-start = (bf16[304,384]{1,0:T(8,128)(2,1)S(1)}, bf16[304,384]{1,0:T(8,128)(2,1)S(1)}, u32[]{:S(2)}, u32[]{:S(2)}) collective-permute-start(bf16[304,384]{1,0:T(8,128)(2,1)S(1)} %get-tuple-element.102), channel_id=1, source_target_pairs={{0,12},{4,8},{8,4},{12,0},{16,28},{20,24},{24,20},{28,16},{1,13},{... | collective-permute-start | bytes 700424 | tf_op jit(solution)/shard_map/ppermute | solution.py:39
  10.7 11.4 %collective-permute-start.1 = (bf16[13,13,8,384]{3,2,1,0:T(8,128)(2,1)S(1)}, bf16[13,13,8,384]{3,2,1,0:T(8,128)(2,1)S(1)}, u32[]{:S(2)}, u32[]{:S(2)}) collective-permute-start(bf16[13,13,8,384]{3,2,1,0:T(8,128)(2,1)S(1)} %get-tuple-element.205), channel_id=1, source_target_pairs={{0,4},{4,0},{8,12},{12,8},{16,20},{20,16},{24,28},{28,24},{1,5},{5... | collective-permute-start | bytes 3115016 | tf_op jit(solution)/shard_map/ppermute | solution.py:39
  10.8 9.3 %collective-permute-start.4 = (bf16[304,384]{1,0:T(8,128)(2,1)S(1)}, bf16[304,384]{1,0:T(8,128)(2,1)S(1)}, u32[]{:S(2)}, u32[]{:S(2)}) collective-permute-start(bf16[304,384]{1,0:T(8,128)(2,1)S(1)} %get-tuple-element.104.refs_0_), channel_id=1, source_target_pairs={{0,16},{4,20},{8,24},{12,28},{16,0},{20,4},{24,8},{28,12},{1,17},{... | collective-permute-start | bytes 700424 | tf_op jit(solution)/shard_map/ppermute | solution.py:39
  13.3 7.2 %collective-permute-start.2 = (bf16[304,384]{1,0:T(8,128)(2,1)S(1)}, bf16[304,384]{1,0:T(8,128)(2,1)S(1)}, u32[]{:S(2)}, u32[]{:S(2)}) collective-permute-start(bf16[304,384]{1,0:T(8,128)(2,1)S(1)} %get-tuple-element.102), channel_id=1, source_target_pairs={{0,4},{4,0},{8,12},{12,8},{16,20},{20,16},{24,28},{28,24},{1,5},{5... | collective-permute-start | bytes 700424 | tf_op jit(solution)/shard_map/ppermute | solution.py:39
  13.4 10.9 %collective-permute-start.3 = (bf16[304,384]{1,0:T(8,128)(2,1)S(1)}, bf16[304,384]{1,0:T(8,128)(2,1)S(1)}, u32[]{:S(2)}, u32[]{:S(2)}) collective-permute-start(bf16[304,384]{1,0:T(8,128)(2,1)S(1)} %get-tuple-element.104.refs_0_), channel_id=1, source_target_pairs={{0,8},{4,12},{8,0},{12,4},{16,24},{20,28},{24,16},{28,20},{1,9},{5... | collective-permute-start | bytes 700424 | tf_op jit(solution)/shard_map/ppermute | solution.py:39
  14.9 9.4 %collective-permute-start.5 = (bf16[304,384]{1,0:T(8,128)(2,1)S(1)}, bf16[304,384]{1,0:T(8,128)(2,1)S(1)}, u32[]{:S(2)}, u32[]{:S(2)}) collective-permute-start(bf16[304,384]{1,0:T(8,128)(2,1)S(1)} %get-tuple-element.102), channel_id=1, source_target_pairs={{0,20},{4,16},{8,28},{12,24},{16,4},{20,0},{24,12},{28,8},{1,21},{... | collective-permute-start | bytes 700424 | tf_op jit(solution)/shard_map/ppermute | solution.py:39
  20.1 42.4 %collective-permute-start.18 = (bf16[2304,512]{1,0:T(8,128)(2,1)S(1)}, bf16[2304,512]{1,0:T(8,128)(2,1)S(1)}, u32[]{:S(2)}, u32[]{:S(2)}) collective-permute-start(bf16[2304,512]{1,0:T(8,128)(2,1)S(1)} %get-tuple-element.113), channel_id=1, source_target_pairs={{0,4},{4,0},{8,12},{12,8},{16,20},{20,16},{24,28},{28,24},{1,5},{5... | collective-permute-start | bytes 7077896 | tf_op jit(solution)/shard_map/ppermute | solution.py:39
  20.6 9.1 %collective-permute-start.7 = (bf16[304,384]{1,0:T(8,128)(2,1)S(1)}, bf16[304,384]{1,0:T(8,128)(2,1)S(1)}, u32[]{:S(2)}, u32[]{:S(2)}) collective-permute-start(bf16[304,384]{1,0:T(8,128)(2,1)S(1)} %collective-permute-done.refs_3_._), channel_id=1, source_target_pairs={{0,16},{4,20},{8,24},{12,28},{16,0},{20,4},{24,8},{28,12},{1,17},{... | collective-permute-start | bytes 700424 | tf_op jit(solution)/shard_map/ppermute | solution.py:39
  22.1 7.6 %collective-permute-start.6 = (bf16[304,384]{1,0:T(8,128)(2,1)S(1)}, bf16[304,384]{1,0:T(8,128)(2,1)S(1)}, u32[]{:S(2)}, u32[]{:S(2)}) collective-permute-start(bf16[304,384]{1,0:T(8,128)(2,1)S(1)} %collective-permute-done.4.refs_4_), channel_id=1, source_target_pairs={{0,8},{4,12},{8,0},{12,4},{16,24},{20,28},{24,16},{28,20},{1,9},{5... | collective-permute-start | bytes 700424 | tf_op jit(solution)/shard_map/ppermute | solution.py:39
  37.2 2.1 %collective-permute-start.8 = (f32[36,16,256]{2,1,0:T(8,128)S(1)}, f32[36,16,256]{2,1,0:T(8,128)S(1)}, u32[]{:S(2)}, u32[]{:S(2)}) collective-permute-start(f32[36,16,256]{2,1,0:T(8,128)S(1)} %get-tuple-element.106.a_ref.refs_5_), channel_id=1, source_target_pairs={{0,4},{4,0},{8,12},{12,8},{16,20},{20,16},{24,28},{28,24},{1,5},{5... | collective-permute-start | bytes 1769480 | tf_op jit(solution)/shard_map/ppermute | solution.py:39
  39.4 8.1 %collective-permute-start.10 = (bf16[16,2304]{1,0:T(8,128)(2,1)S(1)}, bf16[16,2304]{1,0:T(8,128)(2,1)S(1)}, u32[]{:S(2)}, u32[]{:S(2)}) collective-permute-start(bf16[16,2304]{1,0:T(8,128)(2,1)S(1)} %get-tuple-element.110), channel_id=1, source_target_pairs={{0,2},{1,3},{2,0},{3,1},{4,6},{5,7},{6,4},{7,5},{8,10},{9,11},{10,... | collective-permute-start | bytes 221192 | tf_op jit(solution)/shard_map/ppermute | solution.py:39
  42.2 6.7 %collective-permute-start.11 = (bf16[16,2304]{1,0:T(8,128)(2,1)S(1)}, bf16[16,2304]{1,0:T(8,128)(2,1)S(1)}, u32[]{:S(2)}, u32[]{:S(2)}) collective-permute-start(bf16[16,2304]{1,0:T(8,128)(2,1)S(1)} %get-tuple-element.111), channel_id=1, source_target_pairs={{0,3},{1,2},{2,1},{3,0},{4,7},{5,6},{6,5},{7,4},{8,11},{9,10},{10,... | collective-permute-start | bytes 221192 | tf_op jit(solution)/shard_map/ppermute | solution.py:39
  43.5 6.9 %collective-permute-start.9 = (bf16[16,2304]{1,0:T(8,128)(2,1)S(1)}, bf16[16,2304]{1,0:T(8,128)(2,1)S(1)}, u32[]{:S(2)}, u32[]{:S(2)}) collective-permute-start(bf16[16,2304]{1,0:T(8,128)(2,1)S(1)} %get-tuple-element.109), channel_id=1, source_target_pairs={{0,1},{1,0},{2,3},{3,2},{4,5},{5,4},{6,7},{7,6},{8,9},{9,8},{10,11... | collective-permute-start | bytes 221192 | tf_op jit(solution)/shard_map/ppermute | solution.py:39
  48.9 6.4 %collective-permute-start.13 = (bf16[2,16,2304]{2,1,0:T(8,128)(2,1)S(1)}, bf16[2,16,2304]{2,1,0:T(8,128)(2,1)S(1)}, u32[]{:S(2)}, u32[]{:S(2)}) collective-permute-start(bf16[2,16,2304]{2,1,0:T(8,128)(2,1)S(1)} %pad_maximum_fusion.4.refs_1_), channel_id=1, source_target_pairs={{0,8},{4,12},{8,0},{12,4},{16,24},{20,28},{24,16},{28,20},{1,9},{5... | collective-permute-start | bytes 442376 | tf_op jit(solution)/shard_map/ppermute | solution.py:39
  50.5 6.9 %collective-permute-start.14 = (bf16[2,16,2304]{2,1,0:T(8,128)(2,1)S(1)}, bf16[2,16,2304]{2,1,0:T(8,128)(2,1)S(1)}, u32[]{:S(2)}, u32[]{:S(2)}) collective-permute-start(bf16[2,16,2304]{2,1,0:T(8,128)(2,1)S(1)} %pad_maximum_fusion.3.refs_0_), channel_id=1, source_target_pairs={{0,16},{4,20},{8,24},{12,28},{16,0},{20,4},{24,8},{28,12},{1,17},{... | collective-permute-start | bytes 442376 | tf_op jit(solution)/shard_map/ppermute | solution.py:39
  52.3 6.9 %collective-permute-start.15 = (bf16[2,16,2304]{2,1,0:T(8,128)(2,1)S(1)}, bf16[2,16,2304]{2,1,0:T(8,128)(2,1)S(1)}, u32[]{:S(2)}, u32[]{:S(2)}) collective-permute-start(bf16[2,16,2304]{2,1,0:T(8,128)(2,1)S(1)} %pad_maximum_fusion.4.refs_1_), channel_id=1, source_target_pairs={{0,16},{4,20},{8,24},{12,28},{16,0},{20,4},{24,8},{28,12},{1,17},{... | collective-permute-start | bytes 442376 | tf_op jit(solution)/shard_map/ppermute | solution.py:39
  52.8 6.3 %collective-permute-start.12 = (bf16[2,16,2304]{2,1,0:T(8,128)(2,1)S(1)}, bf16[2,16,2304]{2,1,0:T(8,128)(2,1)S(1)}, u32[]{:S(2)}, u32[]{:S(2)}) collective-permute-start(bf16[2,16,2304]{2,1,0:T(8,128)(2,1)S(1)} %pad_maximum_fusion.3.refs_0_), channel_id=1, source_target_pairs={{0,8},{4,12},{8,0},{12,4},{16,24},{20,28},{24,16},{28,20},{1,9},{5... | collective-permute-start | bytes 442376 | tf_op jit(solution)/shard_map/ppermute | solution.py:39
  55.3 5.4 %collective-permute-start.17 = (bf16[2,16,2304]{2,1,0:T(8,128)(2,1)S(1)}, bf16[2,16,2304]{2,1,0:T(8,128)(2,1)S(1)}, u32[]{:S(2)}, u32[]{:S(2)}) collective-permute-start(bf16[2,16,2304]{2,1,0:T(8,128)(2,1)S(1)} %collective-permute-done.13.refs_3_), channel_id=1, source_target_pairs={{0,16},{4,20},{8,24},{12,28},{16,0},{20,4},{24,8},{28,12},{1,17},{... | collective-permute-start | bytes 442376 | tf_op jit(solution)/shard_map/ppermute | solution.py:39
  57.3 5.1 %collective-permute-start.16 = (bf16[2,16,2304]{2,1,0:T(8,128)(2,1)S(1)}, bf16[2,16,2304]{2,1,0:T(8,128)(2,1)S(1)}, u32[]{:S(2)}, u32[]{:S(2)}) collective-permute-start(bf16[2,16,2304]{2,1,0:T(8,128)(2,1)S(1)} %collective-permute-done.14.refs_4_), channel_id=1, source_target_pairs={{0,8},{4,12},{8,0},{12,4},{16,24},{20,28},{24,16},{28,20},{1,9},{5... | collective-permute-start | bytes 442376 | tf_op jit(solution)/shard_map/ppermute | solution.py:39
  63.9 6.3 %collective-permute-start.19 = (bf16[64,1024]{1,0:T(8,128)(2,1)S(1)}, bf16[64,1024]{1,0:T(8,128)(2,1)S(1)}, u32[]{:S(2)}, u32[]{:S(2)}) collective-permute-start(bf16[64,1024]{1,0:T(8,128)(2,1)S(1)} %get-tuple-element.115), channel_id=1, source_target_pairs={{0,1},{1,0},{2,3},{3,2},{4,5},{5,4},{6,7},{7,6},{8,9},{9,8},{10,11... | collective-permute-start | bytes 393224 | tf_op jit(solution)/shard_map/ppermute | solution.py:39
  65.4 12.6 %collective-permute-start.20 = (bf16[64,1024]{1,0:T(8,128)(2,1)S(1)}, bf16[64,1024]{1,0:T(8,128)(2,1)S(1)}, u32[]{:S(2)}, u32[]{:S(2)}) collective-permute-start(bf16[64,1024]{1,0:T(8,128)(2,1)S(1)} %get-tuple-element.116), channel_id=1, source_target_pairs={{0,2},{1,3},{2,0},{3,1},{4,6},{5,7},{6,4},{7,5},{8,10},{9,11},{10,... | collective-permute-start | bytes 393224 | tf_op jit(solution)/shard_map/ppermute | solution.py:39
  67.4 10.6 %collective-permute-start.21 = (bf16[64,1024]{1,0:T(8,128)(2,1)S(1)}, bf16[64,1024]{1,0:T(8,128)(2,1)S(1)}, u32[]{:S(2)}, u32[]{:S(2)}) collective-permute-start(bf16[64,1024]{1,0:T(8,128)(2,1)S(1)} %get-tuple-element.117), channel_id=1, source_target_pairs={{0,3},{1,2},{2,1},{3,0},{4,7},{5,6},{6,5},{7,4},{8,11},{9,10},{10,... | collective-permute-start | bytes 393224 | tf_op jit(solution)/shard_map/ppermute | solution.py:39
  79.9 5.8 %collective-permute-start.24 = (bf16[2,64,512]{2,1,0:T(8,128)(2,1)S(1)}, bf16[2,64,512]{2,1,0:T(8,128)(2,1)S(1)}, u32[]{:S(2)}, u32[]{:S(2)}) collective-permute-start(bf16[2,64,512]{2,1,0:T(8,128)(2,1)S(1)} %pad_maximum_fusion.6.refs_0_), channel_id=1, source_target_pairs={{0,1},{1,0},{2,3},{3,2},{4,5},{5,4},{6,7},{7,6},{8,9},{9,8},{10,11... | collective-permute-start | bytes 393224 | tf_op jit(solution)/shard_map/ppermute | solution.py:39
  81.9 13.8 %collective-permute-start.26 = (bf16[2,64,512]{2,1,0:T(8,128)(2,1)S(1)}, bf16[2,64,512]{2,1,0:T(8,128)(2,1)S(1)}, u32[]{:S(2)}, u32[]{:S(2)}) collective-permute-start(bf16[2,64,512]{2,1,0:T(8,128)(2,1)S(1)} %pad_maximum_fusion.6.refs_0_), channel_id=1, source_target_pairs={{0,3},{1,2},{2,1},{3,0},{4,7},{5,6},{6,5},{7,4},{8,11},{9,10},{10,... | collective-permute-start | bytes 393224 | tf_op jit(solution)/shard_map/ppermute | solution.py:39
  84.4 11.3 %collective-permute-start.25 = (bf16[2,64,512]{2,1,0:T(8,128)(2,1)S(1)}, bf16[2,64,512]{2,1,0:T(8,128)(2,1)S(1)}, u32[]{:S(2)}, u32[]{:S(2)}) collective-permute-start(bf16[2,64,512]{2,1,0:T(8,128)(2,1)S(1)} %pad_maximum_fusion.6.refs_0_), channel_id=1, source_target_pairs={{0,2},{1,3},{2,0},{3,1},{4,6},{5,7},{6,4},{7,5},{8,10},{9,11},{10,... | collective-permute-start | bytes 393224 | tf_op jit(solution)/shard_map/ppermute | solution.py:39
  98.9 6.8 %collective-permute-start.32 = (bf16[2,16,2304]{2,1,0:T(8,128)(2,1)S(1)}, bf16[2,16,2304]{2,1,0:T(8,128)(2,1)S(1)}, u32[]{:S(2)}, u32[]{:S(2)}) collective-permute-start(bf16[2,16,2304]{2,1,0:T(8,128)(2,1)S(1)} %get-tuple-element.131), channel_id=1, source_target_pairs={{0,8},{4,12},{8,0},{12,4},{16,24},{20,28},{24,16},{28,20},{1,9},{5... | collective-permute-start | bytes 442376 | tf_op jit(solution)/shard_map/ppermute | solution.py:39
  99.5 7.8 %collective-permute-start.28 = (bf16[2,16,2304]{2,1,0:T(8,128)(2,1)S(1)}, bf16[2,16,2304]{2,1,0:T(8,128)(2,1)S(1)}, u32[]{:S(2)}, u32[]{:S(2)}) collective-permute-start(bf16[2,16,2304]{2,1,0:T(8,128)(2,1)S(1)} %get-tuple-element.121), channel_id=1, source_target_pairs={{0,16},{4,20},{8,24},{12,28},{16,0},{20,4},{24,8},{28,12},{1,17},{... | collective-permute-start | bytes 442376 | tf_op jit(solution)/shard_map/ppermute | solution.py:39
  101.0 12.0 %collective-permute-start.31 = (bf16[2,16,2304]{2,1,0:T(8,128)(2,1)S(1)}, bf16[2,16,2304]{2,1,0:T(8,128)(2,1)S(1)}, u32[]{:S(2)}, u32[]{:S(2)}) collective-permute-start(bf16[2,16,2304]{2,1,0:T(8,128)(2,1)S(1)} %get-tuple-element.129), channel_id=1, source_target_pairs={{0,8},{4,12},{8,0},{12,4},{16,24},{20,28},{24,16},{28,20},{1,9},{5... | collective-permute-start | bytes 442376 | tf_op jit(solution)/shard_map/ppermute | solution.py:39
  102.5 10.6 %collective-permute-start.30 = (bf16[2,16,2304]{2,1,0:T(8,128)(2,1)S(1)}, bf16[2,16,2304]{2,1,0:T(8,128)(2,1)S(1)}, u32[]{:S(2)}, u32[]{:S(2)}) collective-permute-start(bf16[2,16,2304]{2,1,0:T(8,128)(2,1)S(1)} %get-tuple-element.125), channel_id=1, source_target_pairs={{0,16},{4,20},{8,24},{12,28},{16,0},{20,4},{24,8},{28,12},{1,17},{... | collective-permute-start | bytes 442376 | tf_op jit(solution)/shard_map/ppermute | solution.py:39
  105.7 7.3 %collective-permute-start.33 = (bf16[2,16,2304]{2,1,0:T(8,128)(2,1)S(1)}, bf16[2,16,2304]{2,1,0:T(8,128)(2,1)S(1)}, u32[]{:S(2)}, u32[]{:S(2)}) collective-permute-start(bf16[2,16,2304]{2,1,0:T(8,128)(2,1)S(1)} %add_convert_fusion.4), channel_id=1, source_target_pairs={{0,16},{4,20},{8,24},{12,28},{16,0},{20,4},{24,8},{28,12},{1,17},{... | collective-permute-start | bytes 442376 | tf_op jit(solution)/shard_map/ppermute | solution.py:39
  107.3 5.8 %collective-permute-start.29 = (bf16[2,16,2304]{2,1,0:T(8,128)(2,1)S(1)}, bf16[2,16,2304]{2,1,0:T(8,128)(2,1)S(1)}, u32[]{:S(2)}, u32[]{:S(2)}) collective-permute-start(bf16[2,16,2304]{2,1,0:T(8,128)(2,1)S(1)} %add_convert_fusion.5.refs_4_), channel_id=1, source_target_pairs={{0,8},{4,12},{8,0},{12,4},{16,24},{20,28},{24,16},{28,20},{1,9},{5... | collective-permute-start | bytes 442376 | tf_op jit(solution)/shard_map/ppermute | solution.py:39
  113.1 9.7 %collective-permute-start.34 = (bf16[16,2304]{1,0:T(8,128)(2,1)S(1)}, bf16[16,2304]{1,0:T(8,128)(2,1)S(1)}, u32[]{:S(2)}, u32[]{:S(2)}) collective-permute-start(bf16[16,2304]{1,0:T(8,128)(2,1)S(1)} %get-tuple-element.213), channel_id=1, source_target_pairs={{0,1},{1,0},{2,3},{3,2},{4,5},{5,4},{6,7},{7,6},{8,9},{9,8},{10,11... | collective-permute-start | bytes 221192 | tf_op jit(solution)/shard_map/ppermute | solution.py:39
  113.2 9.5 %collective-permute-start.35 = (bf16[16,2304]{1,0:T(8,128)(2,1)S(1)}, bf16[16,2304]{1,0:T(8,128)(2,1)S(1)}, u32[]{:S(2)}, u32[]{:S(2)}) collective-permute-start(bf16[16,2304]{1,0:T(8,128)(2,1)S(1)} %get-tuple-element.210), channel_id=1, source_target_pairs={{0,2},{1,3},{2,0},{3,1},{4,6},{5,7},{6,4},{7,5},{8,10},{9,11},{10,... | collective-permute-start | bytes 221192 | tf_op jit(solution)/shard_map/ppermute | solution.py:39
  116.0 6.8 %collective-permute-start.36 = (bf16[16,2304]{1,0:T(8,128)(2,1)S(1)}, bf16[16,2304]{1,0:T(8,128)(2,1)S(1)}, u32[]{:S(2)}, u32[]{:S(2)}) collective-permute-start(bf16[16,2304]{1,0:T(8,128)(2,1)S(1)} %get-tuple-element.211.refs_6_), channel_id=1, source_target_pairs={{0,3},{1,2},{2,1},{3,0},{4,7},{5,6},{6,5},{7,4},{8,11},{9,10},{10,... | collective-permute-start | bytes 221192 | tf_op jit(solution)/shard_map/ppermute | solution.py:39
  132.0 8.6 %collective-permute-start.41 = (bf16[304,384]{1,0:T(8,128)(2,1)S(1)}, bf16[304,384]{1,0:T(8,128)(2,1)S(1)}, u32[]{:S(2)}, u32[]{:S(2)}) collective-permute-start(bf16[304,384]{1,0:T(8,128)(2,1)S(1)} %get-tuple-element.145), channel_id=1, source_target_pairs={{0,16},{4,20},{8,24},{12,28},{16,0},{20,4},{24,8},{28,12},{1,17},{... | collective-permute-start | bytes 700424 | tf_op jit(solution)/shard_map/ppermute | solution.py:39
  133.6 25.3 %collective-permute-start.23 = (bf16[256,2304]{1,0:T(8,128)(2,1)S(1)}, bf16[256,2304]{1,0:T(8,128)(2,1)S(1)}, u32[]{:S(2)}, u32[]{:S(2)}) collective-permute-start(bf16[256,2304]{1,0:T(8,128)(2,1)S(1)} %get-tuple-element.118.rows_ref), channel_id=1, source_target_pairs={{0,4},{4,0},{8,12},{12,8},{16,20},{20,16},{24,28},{28,24},{1,5},{5... | collective-permute-start | bytes 3538952 | tf_op jit(solution)/shard_map/ppermute | solution.py:39
  133.6 8.5 %collective-permute-start.39 = (bf16[304,384]{1,0:T(8,128)(2,1)S(1)}, bf16[304,384]{1,0:T(8,128)(2,1)S(1)}, u32[]{:S(2)}, u32[]{:S(2)}) collective-permute-start(bf16[304,384]{1,0:T(8,128)(2,1)S(1)} %get-tuple-element.143), channel_id=1, source_target_pairs={{0,8},{4,12},{8,0},{12,4},{16,24},{20,28},{24,16},{28,20},{1,9},{5... | collective-permute-start | bytes 700424 | tf_op jit(solution)/shard_map/ppermute | solution.py:39
  134.1 18.5 %collective-permute-start.38 = (bf16[304,384]{1,0:T(8,128)(2,1)S(1)}, bf16[304,384]{1,0:T(8,128)(2,1)S(1)}, u32[]{:S(2)}, u32[]{:S(2)}) collective-permute-start(bf16[304,384]{1,0:T(8,128)(2,1)S(1)} %get-tuple-element.141), channel_id=1, source_target_pairs={{0,8},{4,12},{8,0},{12,4},{16,24},{20,28},{24,16},{28,20},{1,9},{5... | collective-permute-start | bytes 700424 | tf_op jit(solution)/shard_map/ppermute | solution.py:39
  135.6 16.9 %collective-permute-start.43 = (bf16[304,384]{1,0:T(8,128)(2,1)S(1)}, bf16[304,384]{1,0:T(8,128)(2,1)S(1)}, u32[]{:S(2)}, u32[]{:S(2)}) collective-permute-start(bf16[304,384]{1,0:T(8,128)(2,1)S(1)} %get-tuple-element.152), channel_id=1, source_target_pairs={{0,16},{4,20},{8,24},{12,28},{16,0},{20,4},{24,8},{28,12},{1,17},{... | collective-permute-start | bytes 700424 | tf_op jit(solution)/shard_map/ppermute | solution.py:39
  142.1 10.3 %collective-permute-start.40 = (bf16[304,384]{1,0:T(8,128)(2,1)S(1)}, bf16[304,384]{1,0:T(8,128)(2,1)S(1)}, u32[]{:S(2)}, u32[]{:S(2)}) collective-permute-start(bf16[304,384]{1,0:T(8,128)(2,1)S(1)} %add_convert_fusion.3), channel_id=1, source_target_pairs={{0,16},{4,20},{8,24},{12,28},{16,0},{20,4},{24,8},{28,12},{1,17},{... | collective-permute-start | bytes 700424 | tf_op jit(solution)/shard_map/ppermute | solution.py:39
  142.7 9.7 %collective-permute-start.42 = (bf16[304,384]{1,0:T(8,128)(2,1)S(1)}, bf16[304,384]{1,0:T(8,128)(2,1)S(1)}, u32[]{:S(2)}, u32[]{:S(2)}) collective-permute-start(bf16[304,384]{1,0:T(8,128)(2,1)S(1)} %add_convert_fusion.2), channel_id=1, source_target_pairs={{0,8},{4,12},{8,0},{12,4},{16,24},{20,28},{24,16},{28,20},{1,9},{5... | collective-permute-start | bytes 700424 | tf_op jit(solution)/shard_map/ppermute | solution.py:39
  154.4 9.6 %collective-permute-start.45 = (bf16[160,384]{1,0:T(8,128)(2,1)S(1)}, bf16[160,384]{1,0:T(8,128)(2,1)S(1)}, u32[]{:S(2)}, u32[]{:S(2)}) collective-permute-start(bf16[160,384]{1,0:T(8,128)(2,1)S(1)} %get-tuple-element.207), channel_id=1, source_target_pairs={{0,1},{1,0},{2,3},{3,2},{4,5},{5,4},{6,7},{7,6},{8,9},{9,8},{10,11... | collective-permute-start | bytes 368648 | tf_op jit(solution)/shard_map/ppermute | solution.py:39
  154.5 12.4 %collective-permute-start.46 = (bf16[160,384]{1,0:T(8,128)(2,1)S(1)}, bf16[160,384]{1,0:T(8,128)(2,1)S(1)}, u32[]{:S(2)}, u32[]{:S(2)}) collective-permute-start(bf16[160,384]{1,0:T(8,128)(2,1)S(1)} %get-tuple-element.206), channel_id=1, source_target_pairs={{0,2},{1,3},{2,0},{3,1},{4,6},{5,7},{6,4},{7,5},{8,10},{9,11},{10,... | collective-permute-start | bytes 368648 | tf_op jit(solution)/shard_map/ppermute | solution.py:39
  157.2 9.7 %collective-permute-start.47 = (bf16[160,384]{1,0:T(8,128)(2,1)S(1)}, bf16[160,384]{1,0:T(8,128)(2,1)S(1)}, u32[]{:S(2)}, u32[]{:S(2)}) collective-permute-start(bf16[160,384]{1,0:T(8,128)(2,1)S(1)} %get-tuple-element.209), channel_id=1, source_target_pairs={{0,3},{1,2},{2,1},{3,0},{4,7},{5,6},{6,5},{7,4},{8,11},{9,10},{10,... | collective-permute-start | bytes 368648 | tf_op jit(solution)/shard_map/ppermute | solution.py:39
  167.2 11.7 %collective-permute-start.48 = (bf16[13,13,8,384]{3,2,1,0:T(8,128)(2,1)S(1)}, bf16[13,13,8,384]{3,2,1,0:T(8,128)(2,1)S(1)}, u32[]{:S(2)}, u32[]{:S(2)}) collective-permute-start(bf16[13,13,8,384]{3,2,1,0:T(8,128)(2,1)S(1)} %get-tuple-element.202), channel_id=1, source_target_pairs={{0,4},{4,0},{8,12},{12,8},{16,20},{20,16},{24,28},{28,24},{1,5},{5... | collective-permute-start | bytes 3115016 | tf_op jit(solution)/shard_map/ppermute | solution.py:39
  168.3 13.8 %collective-permute-start.49 = (bf16[160,384]{1,0:T(8,128)(2,1)S(1)}, bf16[160,384]{1,0:T(8,128)(2,1)S(1)}, u32[]{:S(2)}, u32[]{:S(2)}) collective-permute-start(bf16[160,384]{1,0:T(8,128)(2,1)S(1)} %add_convert_fusion.6.refs_0_), channel_id=1, source_target_pairs={{0,1},{1,0},{2,3},{3,2},{4,5},{5,4},{6,7},{7,6},{8,9},{9,8},{10,11... | collective-permute-start | bytes 368648 | tf_op jit(solution)/shard_map/ppermute | solution.py:39
  170.8 12.4 %collective-permute-start.50 = (bf16[160,384]{1,0:T(8,128)(2,1)S(1)}, bf16[160,384]{1,0:T(8,128)(2,1)S(1)}, u32[]{:S(2)}, u32[]{:S(2)}) collective-permute-start(bf16[160,384]{1,0:T(8,128)(2,1)S(1)} %add_convert_fusion.6.refs_0_), channel_id=1, source_target_pairs={{0,2},{1,3},{2,0},{3,1},{4,6},{5,7},{6,4},{7,5},{8,10},{9,11},{10,... | collective-permute-start | bytes 368648 | tf_op jit(solution)/shard_map/ppermute | solution.py:39
  171.5 11.6 %collective-permute-start.51 = (bf16[160,384]{1,0:T(8,128)(2,1)S(1)}, bf16[160,384]{1,0:T(8,128)(2,1)S(1)}, u32[]{:S(2)}, u32[]{:S(2)}) collective-permute-start(bf16[160,384]{1,0:T(8,128)(2,1)S(1)} %add_convert_fusion.6.refs_0_), channel_id=1, source_target_pairs={{0,3},{1,2},{2,1},{3,0},{4,7},{5,6},{6,5},{7,4},{8,11},{9,10},{10,... | collective-permute-start | bytes 368648 | tf_op jit(solution)/shard_map/ppermute | solution.py:39
  (18 other events, 150.8 us)

commit v3 on v2

--- a/solution.py
+++ b/solution.py
@@ -16,7 +16,7 @@
 TAPS = 9
 CELLS = 36
 EXTRA = 16
-PORTION = 160
+PORTION = 80
 LANES = 128
 WHOLE = pl.BlockSpec(memory_space=pltpu.VMEM)
 SCALARS = pl.BlockSpec(memory_space=pltpu.SMEM)
@@ -61,12 +61,13 @@
     return (a.astype(WIDE) + b.astype(WIDE)).astype(LOW)
 
 
-def scatter_chips(parts, chips, later=lambda gate, value: (gate, value)):
+def scatter_chips(parts, chips, early=lambda *pair: pair, later=lambda gate, value: (gate, value)):
     if chips == 4:
         from_x = trade(parts[3][0], "chan", 2)
         from_y = trade(parts[3][1], "chan", 4)
         first_x = trade(parts[1][0], "chan", 2)
         second_y = trade(parts[2][1], "chan", 4)
+        from_x, from_y = early(from_x, from_y)
         to_y = add_low(parts[2][0], from_x)
         first_y = trade(to_y, "chan", 4)
         to_x = add_low(parts[1][1], from_y)
@@ -90,6 +91,21 @@
 def exchange_planes(parts):
     got = {k: trade(parts[k], "batch", k) for k in range(len(parts) - 1, 0, -1)}
     return [parts[0]] + [got[k] for k in range(1, len(parts))]
+
+
+def reduce_planes(first, second):
+    passed = [trade(parts[3], "batch", 1) for parts in (first, second)]
+    near = [trade(parts[1], "batch", 1) for parts in (first, second)]
+    sent = [add_low(parts[2], term) for parts, term in zip((first, second), passed)]
+    far = [trade(value, "batch", 2) for value in sent]
+    return [[parts[0], a, b] for parts, a, b in zip((first, second), near, far)]
+
+
+def spread_planes(first, second):
+    far = [trade(value, "batch", 2) for value in (first, second)]
+    near = [trade(value, "batch", 1) for value in (first, second)]
+    passed = [trade(value, "batch", 1) for value in far]
+    return [list(values) for values in zip((first, second), near, far, passed)]
 
 
 def gate_of(value):
@@ -175,7 +191,7 @@
         ),
         out_shape=[like((rows, units), LOW)] * 2,
         compiler_params=pltpu.CompilerParams(vmem_limit_bytes=12 << 20),
-        cost_estimate=BRIEF,
+        cost_estimate=pl.CostEstimate(flops=0, bytes_accessed=6 * fc_weight.size, transcendentals=0),
     )(core, fc_weight, fc_weight, gate)
 
 
@@ -322,24 +338,23 @@
         for n, weight in enumerate((own, cross)):
             part = dot(rows_ref[...], weight[...], NN)
             for k in range(planes):
-                outs[k][:, n * units : (n + 1) * units] = part[k * block : (k + 1) * block].astype(
-                    outs[k].dtype
-                )
+                out = outs[n * planes + k]
+                out[...] = part[k * block : (k + 1) * block].astype(out.dtype)
 
     n_images = planes * block
     return pl.pallas_call(
         kernel,
         in_specs=[SCALARS] + [WHOLE] * (count + 2),
-        out_specs=[WHOLE] * (1 + planes),
+        out_specs=[WHOLE] * (1 + 2 * planes),
         out_shape=[like((n_images, rows), LOW)]
-        + [like((block, 2 * units), LOW if k else WIDE) for k in range(planes)],
+        + [like((block, units), LOW if k else WIDE) for k in range(planes)] * 2,
         compiler_params=pltpu.CompilerParams(vmem_limit_bytes=16 << 20),
         cost_estimate=BRIEF,
     )(chip, *gathered, *weights)
 
 
 def fc_backward(grads, crossed, weights, chip, chips, planes):
-    _, block, units = grads[0].shape
+    block, units = grads[0].shape
     rows = weights[0].shape[0]
     group = block // chips
     half = planes // 2
@@ -351,7 +366,7 @@
         outs = refs[planes + 3 : planes + 3 + 2 * chips]
         held_own, held_cross, held = refs[planes + 3 + 2 * chips :]
         for k in range(planes):
-            held_own[pl.ds(k * block, block), :] = pieces[k][0]
+            held_own[pl.ds(k * block, block), :] = pieces[k][...]
             held_cross[pl.ds(k * block, block), :] = got[k]
         step = rows // 3
         for s in range(3):
@@ -497,54 +512,38 @@
     few = width // 2
     tall = depth // 2 // steps
     hbm = pl.BlockSpec(memory_space=pltpu.HBM)
-    weight, moment = (pltpu.with_memory_space_constraint(value, pltpu.HBM) for value in (weight, moment))
-
-    def kernel(core_ref, w_hbm, m_hbm, rows_ref, *refs):
+
+    def kernel(core_ref, w_ref, m_ref, rows_ref, *refs):
         grad_refs = refs[:planes]
         new_w, new_m, token, joined, product, held_w, held_m, sems = refs[-8:]
         tower = core_ref[0] ^ which
-
-        def copies(pairs, s, first):
-            at = pl.ds((part * steps + s) * tall, tall)
-            return [
-                pltpu.make_async_copy(held.at[s], hbm_ref.at[tower, at, :], sems.at[s, first + i])
-                if first
-                else pltpu.make_async_copy(hbm_ref.at[tower, at, :], held.at[s], sems.at[s, i])
-                for i, (hbm_ref, held) in enumerate(pairs)
-            ]
-
-        loads = [copies(((w_hbm, held_w), (m_hbm, held_m)), s, 0) for s in range(steps)]
-        stores = [copies(((new_w, held_w), (new_m, held_m)), s, 2) for s in range(steps)]
-        for pair in loads:
-            for copy in pair:
-                copy.start()
         token[...] = jnp.zeros_like(token)
         for k in range(planes):
-            joined[pl.ds(k * block, block), :] = grad_refs[k][which]
+            joined[pl.ds(k * block, block), :] = grad_refs[k][...]
         for v in range(columns):
             grad = dot(rows_ref[...], joined[:, v * LANES : (v + 1) * LANES], TN)
             for cell in range(CELLS):
                 start = cell * width + part * few
                 product[v, pl.ds(cell, few, stride=CELLS), :] = grad[start : start + few]
+        stores = []
         for s in range(steps):
-            for copy in loads[s]:
-                copy.wait()
+            at = pl.ds((part * steps + s) * tall, tall)
             for v in range(columns):
-                at = (s, slice(None), slice(v * LANES, (v + 1) * LANES))
-                fresh = MOMENTUM * held_m[at] + product[v, s * tall : (s + 1) * tall, :]
-                held_m[at] = fresh
-                held_w[at] = held_w[at] - LEARN_RATE * fresh
-            for copy in stores[s]:
-                copy.start()
-        for pair in stores:
-            for copy in pair:
-                copy.wait()
+                lanes = slice(v * LANES, (v + 1) * LANES)
+                fresh = MOMENTUM * m_ref[tower, at, lanes] + product[v, s * tall : (s + 1) * tall, :]
+                held_m[s, :, lanes] = fresh
+                held_w[s, :, lanes] = w_ref[tower, at, lanes] - LEARN_RATE * fresh
+            for i, (held, out) in enumerate(((held_w, new_w), (held_m, new_m))):
+                stores.append(pltpu.make_async_copy(held.at[s], out.at[tower, at, :], sems.at[s, i]))
+                stores[-1].start()
+        for copy in stores:
+            copy.wait()
 
     anywhere = pl.BlockSpec(memory_space=pl.ANY)
     extra = [] if previous is None else list(previous)
     return pl.pallas_call(
         kernel,
-        in_specs=[SCALARS, hbm, hbm] + [WHOLE] * (1 + planes) + [hbm] * len(extra) + [anywhere],
+        in_specs=[SCALARS] + [WHOLE] * (3 + planes) + [hbm] * len(extra) + [anywhere],
         out_specs=[hbm, hbm, WHOLE],
         out_shape=[pltpu.HBM(weight.shape, WIDE)] * 2 + [like((8, LANES), WIDE)],
         scratch_shapes=[
@@ -552,11 +551,11 @@
             pltpu.VMEM((columns, depth // 2, LANES), WIDE),
             pltpu.VMEM((steps, tall, units), WIDE),
             pltpu.VMEM((steps, tall, units), WIDE),
-            pltpu.SemaphoreType.DMA((steps, 4)),
+            pltpu.SemaphoreType.DMA((steps, 2)),
         ],
         input_output_aliases={} if previous is None else {4 + planes: 0, 5 + planes: 1},
         compiler_params=pltpu.CompilerParams(vmem_limit_bytes=12 << 20),
-        cost_estimate=BRIEF,
+        cost_estimate=pl.CostEstimate(flops=0, bytes_accessed=8 * depth * units, transcendentals=0),
     )(core, weight, moment, rows, *grads, *extra, gate)
 
 
@@ -578,19 +577,19 @@
 def small_update(gate, ready, pieces, lines, params, moments, core, plane):
     planes = len(pieces)
     height, width_in = pieces[0].shape
+    height = height // 2
     shard = params[1].shape[-1]
     units = params[3].shape[-1]
     count = lines - EXTRA
     rates = (LEARN_RATE, BIAS_RATE, STITCH_RATE, STITCH_RATE)
 
     def kernel(core_ref, plane_ref, gate_ref, ready_ref, *refs):
-        piece_refs = refs[:planes]
-        p_refs, m_refs = refs[planes : planes + 4], refs[planes + 4 : planes + 8]
-        new_p, new_m = refs[planes + 8 : planes + 12], refs[planes + 12 : planes + 16]
-        whole = refs[planes + 17]
-        for k in range(planes):
-            at = pl.ds(pl.multiple_of((plane_ref[0] ^ k) * height, height), height)
-            whole[at, :] = piece_refs[k][...].astype(WIDE)
+        piece_refs, refs = refs[:planes], refs[planes:]
+        p_refs, m_refs, new_p, new_m, whole = refs[:4], refs[4:8], refs[8:12], refs[12:16], refs[17]
+        for a in range(2):
+            for k in range(planes):
+                at = pl.ds(pl.multiple_of((plane_ref[0] ^ k) * height, height), height)
+                whole[a, at, :] = piece_refs[k][a * height : (a + 1) * height, :].astype(WIDE)
 
         def advance(which, at, grad):
             fresh = MOMENTUM * m_refs[which][at] + grad
@@ -599,18 +598,18 @@
 
         first = core_ref[0] == 0
         for a in range(2):
-            advance(0, core_ref[0] ^ a, whole[a * lines : a * lines + count, :])
-        rows = [[whole[a * lines + count + i : a * lines + count + i + 1, :shard] for i in range(3)] for a in range(2)]
+            advance(0, core_ref[0] ^ a, whole[a, :count, :])
+        rows = [[whole[a, count + i : count + i + 1, :shard] for i in range(3)] for a in range(2)]
         rows = [[jnp.where(first, rows[a][i], rows[1 - a][i]) for i in range(3)] for a in range(2)]
         for t in range(2):
             advance(1, (slice(t, t + 1), slice(None)), rows[t][0])
             advance(2, (t, slice(t, t + 1), slice(None)), rows[t][1])
             advance(2, (t, slice(1 - t, 2 - t), slice(None)), rows[t][2])
-        base = 2 * lines
+        base = lines
         parts, start = [], 0
         while start < units:
             step = min(width_in, units - start)
-            parts.append(whole[base : base + 4, :step])
+            parts.append(whole[0, base : base + 4, :step])
             base, start = base + 4, start + step
         packed = jnp.concatenate(parts, axis=1) if len(parts) > 1 else parts[0]
         for i in range(4):
@@ -626,7 +625,7 @@
         out_specs=[WHOLE] * 8 + [pl.BlockSpec(memory_space=pltpu.HBM)],
         out_shape=out_shape + [pltpu.HBM(ready.shape, ready.dtype)],
         input_output_aliases={3: 8},
-        scratch_shapes=[pltpu.VMEM((planes * height, width_in), WIDE)],
+        scratch_shapes=[pltpu.VMEM((2, planes * height, width_in), WIDE)],
         compiler_params=pltpu.CompilerParams(vmem_limit_bytes=12 << 20),
         cost_estimate=BRIEF,
     )(core, plane, gate, ready, *pieces, *params, *moments)
@@ -938,17 +937,17 @@
     )
     mine = lambda a, b: jnp.where(first_core, a, b)
     keep_y, give_x = trade(keep, "chan", 4), trade(give, "chan", 3)
-    keep_x, give_y = trade(keep, "chan", 2), trade(give, "chan", 5)
+    keep_x, give_y = tie(trade(keep, "chan", 2), trade(give, "chan", 5))
     keep_d, give_d = trade(keep_y, "chan", 2), trade(give_x, "chan", 4)
     kernel_parts = [keep, swap(give), keep_x, give_x, keep_y, give_y, keep_d, give_d]
-    fc_own, fc_give = fc_prepare(fc_weight, core_at, kernel_parts[3])
-    fc_cross = swap(fc_give)
-
-    late_core, kernel_parts[3] = tie(first_core, kernel_parts[3])
+
     towers = lax.optimization_barrier(jnp.transpose(images, (1, 2, 3, 0, 4)))
-    keep, give = (jnp.where(late_core, towers[a], towers[1 - a]) for a in range(2))
+    keep, give = (jnp.where(first_core, towers[a], towers[1 - a]) for a in range(2))
     tower_images = jnp.concatenate([keep, swap(give)], axis=2)
     tower_images = jnp.pad(tower_images, ((1, 1), (1, 1), (0, 0), (0, 0)))
+
+    fc_own, fc_give = fc_prepare(fc_weight, core_at, keep_x)
+    fc_cross = swap(fc_give)
 
     pooled, slope, small_all, joined = conv_forward(tower_images, kernel_parts, core_at, chip_at)
     pooled_other = swap(pooled)
@@ -960,8 +959,8 @@
     )
     other_rows = swap(tower_rows)
 
-    fc_sum = total(exchange_planes(partial))
-    fc_out = [fc_sum[:, :units], swap(fc_sum[:, units:])]
+    crossed, own = reduce_planes(partial[planes:], partial[:planes])
+    fc_out = [total(own), swap(total(crossed))]
     fc_out = [fc_out[a] + mine(fc_bias[a], fc_bias[1 - a]) for a in range(2)]
     acts, slopes = zip(*[silu_and_slope(value) for value in fc_out])
     mix = [[mine(stitch_fc[a, b], stitch_fc[1 - a, 1 - b]) for b in range(2)] for a in range(2)]
@@ -969,9 +968,7 @@
     features_out = jnp.stack([mine(features[0], features[1]), mine(features[1], features[0])], axis=1)
     masked = [cotangent[:, t].astype(WIDE) * task_mask[:, t].astype(WIDE)[:, None] for t in range(2)]
     out_grad = [mine(masked[a], masked[1 - a]) for a in range(2)]
-    grad_low = jnp.stack(
-        [(slopes[b] * (mix[0][b] * out_grad[0] + mix[1][b] * out_grad[1])).astype(LOW) for b in range(2)]
-    )
+    grad_low = [(slopes[b] * (mix[0][b] * out_grad[0] + mix[1][b] * out_grad[1])).astype(LOW) for b in range(2)]
     stitch_fc_grad = jnp.concatenate(
         [jnp.sum(out_grad[a] * acts[b], axis=0, keepdims=True) for a in range(2) for b in range(2)]
     )
@@ -981,25 +978,25 @@
             for at in range(0, units, width_in)
         ]
     ).astype(LOW)
-    grads = exchange_planes([grad_low] * planes)
-    grads[1], packed = tie(grads[1], packed)
-    grads_cross = swap(jnp.stack([value[1] for value in grads]))
+    grads_other, grads_own = spread_planes(grad_low[1], grad_low[0])
+    grads_own[1], packed = tie(grads_own[1], packed)
+    grads_cross = swap(jnp.stack(grads_other))
 
     step = done = None
 
     def update_own(gate, value):
         nonlocal step, done
-        *step, done = fc_update(fc_weight, fc_moment, tower_rows, grads, core_at, 0, 0, None, gate)
+        *step, done = fc_update(fc_weight, fc_moment, tower_rows, grads_own, core_at, 0, 0, None, gate)
         value, done = tie(value, done)
         return gate, value
 
-    blocks = fc_backward(grads, grads_cross, (fc_own, fc_cross), chip_at, chips, planes)
+    blocks = fc_backward(grads_own, grads_cross, (fc_own, fc_cross), chip_at, chips, planes)
     first, second = scatter_chips(
         [blocks[2 * j : 2 * j + 2] for j in range(chips)], chips, later=update_own
     )
     sums = [total([value[i] for value in part]).astype(LOW) for part in (first, second) for i in range(half)]
     mixed_grad = exchange_planes(sums)
-    *step, token = fc_update(fc_weight, fc_moment, tower_rows, grads, core_at, 0, 1, step, sums[-1])
+    *step, token = fc_update(fc_weight, fc_moment, tower_rows, grads_own, core_at, 0, 1, step, sums[-1])
     mixed_grad[1], done, token = tie(mixed_grad[1], done, token)
     done = done + token
     mixed_grad_other = swap(jnp.stack(mixed_grad))
@@ -1019,33 +1016,39 @@
         ).astype(LOW)
 
     kernel = joined.reshape(3, 3, -1, width_in)
-    images_grad = None
-
-    def after_sums(gate, value):
-        nonlocal images_grad
-        gate, grad = tie(gate, conv_grad)
-        value, images_grad = tie(value, turned_conv(grad))
+    def update_early(*pair):
+        nonlocal step, done
+        *step, done = fc_update(fc_weight, fc_moment, other_rows, grads_other, core_at, 1, 0, step, blocks[0])
+        *pair, done = tie(*pair, done)
+        return pair
+
+    def update_late(gate, value):
+        nonlocal step, done
+        *step, token = fc_update(fc_weight, fc_moment, other_rows, grads_other, core_at, 1, 1, step, gate)
+        value, done, token = tie(value, done, token)
+        done = done + token
         return gate, value
 
     first, second = scatter_chips(
-        [blocks[2 * j : 2 * j + 2] for j in range(chips)],
-        chips,
-        later=after_sums,
-    )
-    towers = jnp.stack([total(first).astype(LOW), swap(total(second).astype(LOW))])
-    lines = towers.shape[1]
-
-    flat = jnp.concatenate([towers.reshape(-1, width_in), packed])
-    assert flat.shape[0] <= planes * PORTION
-    flat = jnp.pad(flat, ((0, planes * PORTION - flat.shape[0]), (0, 0)))
+        [blocks[2 * j : 2 * j + 2] for j in range(chips)], chips, update_early, update_late
+    )
+    lines = TAPS * shard + EXTRA
+
+    fill = lambda count: jnp.zeros((count, width_in), LOW)
+    spare = planes * PORTION - lines
+    flats = (
+        jnp.concatenate([total(first).astype(LOW), packed, fill(spare - packed.shape[0])]),
+        jnp.concatenate([swap(total(second).astype(LOW)), fill(spare)]),
+    )
     nothing = jnp.uint32(0)
-    quarters = [lax.dynamic_slice(flat, (start, nothing), (PORTION, width_in)) for start in starts]
-    quarters = exchange_planes(quarters)
-    *step, done = fc_update(fc_weight, fc_moment, other_rows, grads, core_at, 1, 0, step, quarters[0])
-    quarters[1], done = tie(quarters[1], done)
+    quarters = [
+        [lax.dynamic_slice(flat, (start, nothing), (PORTION, width_in)) for start in starts] for flat in flats
+    ]
+    quarters = exchange_planes([jnp.concatenate(pair) for pair in zip(*quarters)])
+    quarters[0], conv_grad = tie(quarters[0], conv_grad)
+    quarters[1], images_grad = tie(quarters[1], turned_conv(conv_grad))
     quarter = total(quarters).astype(LOW)
     quarters = exchange_planes([quarter] * planes)
-    *step, done = fc_update(fc_weight, fc_moment, other_rows, grads, core_at, 1, 1, step, done)
 
     images_grad, quarters[0] = tie(images_grad, quarters[0])
     keep, got = images_grad[:, :, :per_core], swap(images_grad[:, :, per_core:])
@@ -1063,7 +1066,7 @@
         plane_at,
     )
 
-    fc_bias_grad = sum(jnp.sum(value.astype(WIDE), axis=1) for value in grads)
+    fc_bias_grad = [sum(jnp.sum(value.astype(WIDE), axis=0) for value in grads) for grads in (grads_own, grads_other)]
     fc_bias_grad = jnp.stack([mine(fc_bias_grad[a], fc_bias_grad[1 - a]) for a in range(2)])
     new_fc_bias_moment = MOMENTUM * fc_bias_moment + fc_bias_grad
     new_fc_bias = fc_bias - BIAS_RATE * new_fc_bias_moment

time: 185 us -> 176 us (0.951)
  waiting for transfers between devices: 62 us -> 58.2 us
  Pallas kernels: 46.4 us -> 42.7 us
    ppermute x52 -> x58, waiting for transfers between devices: 62 us -> 58.2 us  [trade(): return lax.ppermute(value, axis, [(i, i ^ bit) for i in range(size)])]
    pallas_call x4, Pallas kernels: 20.4 us -> 16.6 us  [fc_update(): pl.pallas_call(kernel, in_specs=[SCALARS] + [WHOLE] * (3 + planes) + [hbm...]
    ppermute x52 -> x58, starting transfers between devices: 57.4 us -> 57.4 us  [trade(): return lax.ppermute(value, axis, [(i, i ^ bit) for i in range(size)])]
  transfers between devices with their start and end apart: 52 -> 58, of which waited for: 23 -> 30; matrix products, arithmetic and copies ran while one was open for 9% -> 8% of each run, Pallas kernels for 18% -> 21%
where the time goes in v3:
time: 176 us
  waiting for transfers between devices  58.2 us (33%)
  starting transfers between devices  57.4 us (33%)
  Pallas kernels  42.7 us (24%)
  matrix products  6.82 us (4%)
  local copies, waits for them, and re-layouts  6.31 us (4%)
  other arithmetic  3.18 us (2%)
    ppermute x58, waiting for transfers between devices, trade(): return lax.ppermute(value, axis, [(i, i ^ bit) for i in range(size)])  58.2 us
    ppermute x58, starting transfers between devices, trade(): return lax.ppermute(value, axis, [(i, i ^ bit) for i in range(size)])  57.4 us
    pallas_call x4, Pallas kernels, fc_update(): pl.pallas_call(kernel, in_specs=[SCALARS] + [WHOLE] * (3 + planes) + [hbm...  16.6 us
    pallas_call x1, Pallas kernels, conv_backward(): pl.pallas_call(kernel, in_specs=[SCALARS] * 3 + [pl.BlockSpec(memory_spac...  7.51 us
    pallas_call x1, Pallas kernels, conv_forward(): pl.pallas_call(kernel, in_specs=[SCALARS] * 2 + [WHOLE] * (1 + count), ou...  7.47 us
    conv_general_dilated x1, matrix products, turned_conv(): lax.conv_general_dilated(grad, kernel[::-1, ::-1], (1, 1), 'SAME', dimens...  6.82 us
    pallas_call x1, Pallas kernels, fc_prepare(): pl.pallas_call(kernel, grid_spec=pltpu.PrefetchScalarGridSpec(num_scalar_...  4.9 us
  transfers between devices with their start and end apart: 58, of which 30 were waited for; matrix products, arithmetic and copies ran while one was open for 8% of the time, Pallas kernels for 21%

profile of v3, /device:TPU:0, one launch (start us, length us, event | category | flops | bytes accessed | tf_op | source)
XLA Modules:
  0.0 176.0 jit_solution(12430635278993287491)
XLA Ops:
  0.7 1.3 shard_map.254
  2.0 1.9 %copy.60 = bf16[8,2,13,13,384]{4,0,3,2,1:T(8,128)(2,1)S(1)} copy(bf16[8,2,13,13,384]{4,1,3,2,0:T(2,128)(2,1)} %param.15) | data formatting | bytes 4153344 | tf_op args[0]
  4.5 2.6 %collective-permute-start.2 = (bf16[304,384]{1,0:T(8,128)(2,1)S(1)}, bf16[304,384]{1,0:T(8,128)(2,1)S(1)}, u32[]{:S(2)}, u32[]{:S(2)}) collective-permute-start(bf16[304,384]{1,0:T(8,128)(2,1)S(1)} %get-tuple-element.110.refs_0_), channel_id=1, source_target_pairs={{0,8},{4,12},{8,0},{12,4},{16,24},{20,28},{24,16},{28,20},{1,9},{5... | collective-permute-start | bytes 700424 | tf_op jit(solution)/shard_map/ppermute | solution.py:39
  7.1 1.3 collective-permute-start.3
  8.9 4.7 %collective-permute-done.2.refs_2_._ = bf16[304,384]{1,0:T(8,128)(2,1)S(1)} collective-permute-done((bf16[304,384]{1,0:T(8,128)(2,1)S(1)}, bf16[304,384]{1,0:T(8,128)(2,1)S(1)}, u32[]{:S(2)}, u32[]{:S(2)}) %collective-permute-start.2) | collective-permute-done | bytes 233504 | tf_op jit(solution)/shard_map/ppermute | solution.py:39
  14.7 4.9 %shard_map.257 = (bf16[2304,512]{1,0:T(8,128)(2,1)S(1)}, bf16[2304,512]{1,0:T(8,128)(2,1)S(1)}) custom-call(s32[1]{0:T(128)} %bitcast.core_ref, f32[2,2304,512]{2,1,0:T(8,128)} %w_ref.7, f32[2,2304,512]{2,1,0:T(8,128)} %w_ref.7, bf16[304,384]{1,0:T(8,128)(2,1)S(1)} %collective-permute-done.2.refs_2_._), custom_call_target="tpu_custom_call" | custom-call | bytes 14155776 | tf_op jit(solution)/shard_map/pallas_call | solution.py:180
  21.1 1.5 collective-permute-start.7
  23.6 4.6 %collective-permute-done.6.refs_6_ = bf16[304,384]{1,0:T(8,128)(2,1)S(1)} collective-permute-done((bf16[304,384]{1,0:T(8,128)(2,1)S(1)}, bf16[304,384]{1,0:T(8,128)(2,1)S(1)}, u32[]{:S(2)}, u32[]{:S(2)}) %collective-permute-start.6) | collective-permute-done | bytes 233504 | tf_op jit(solution)/shard_map/ppermute | solution.py:39
  28.5 7.5 %shard_map.255 = (f32[36,16,256]{2,1,0:T(8,128)S(1)}, bf16[13,13,16,256]{3,2,1,0:T(8,128)(2,1)}, f32[16,256]{1,0:T(8,128)S(1)}, bf16[9,256,384]{2,1,0:T(8,128)(2,1)}) custom-call(s32[1]{0:T(128)} %bitcast.core_ref, s32[1]{0:T(128)} %bitcast.3.chip_ref, bf16[15,15,16,384]{3,2,1,0:T(8,128)(2,1)S(1)} %fusion.6.x_ref.refs_8_, ...), custom_call_target="tpu_custom_call" | custom-call | tf_op jit(solution)/shard_map/pallas_call | solution.py:259
  36.0 2.0 %collective-permute-done.8.b_ref.refs_6_ = f32[36,16,256]{2,1,0:T(8,128)S(1)} collective-permute-done((f32[36,16,256]{2,1,0:T(8,128)S(1)}, f32[36,16,256]{2,1,0:T(8,128)S(1)}, u32[]{:S(2)}, u32[]{:S(2)}) %collective-permute-start.8) | collective-permute-done | bytes 589856 | tf_op jit(solution)/shard_map/ppermute | solution.py:39
  38.2 3.7 %collective-permute-start.11 = (bf16[16,2304]{1,0:T(8,128)(2,1)S(1)}, bf16[16,2304]{1,0:T(8,128)(2,1)S(1)}, u32[]{:S(2)}, u32[]{:S(2)}) collective-permute-start(bf16[16,2304]{1,0:T(8,128)(2,1)S(1)} %get-tuple-element.119), channel_id=1, source_target_pairs={{0,3},{1,2},{2,1},{3,0},{4,7},{5,6},{6,5},{7,4},{8,11},{9,10},{10,... | collective-permute-start | bytes 221192 | tf_op jit(solution)/shard_map/ppermute | solution.py:39
  43.0 2.0 %collective-permute-done.11 = bf16[16,2304]{1,0:T(8,128)(2,1)S(1)} collective-permute-done((bf16[16,2304]{1,0:T(8,128)(2,1)S(1)}, bf16[16,2304]{1,0:T(8,128)(2,1)S(1)}, u32[]{:S(2)}, u32[]{:S(2)}) %collective-permute-start.11) | collective-permute-done | bytes 73760 | tf_op jit(solution)/shard_map/ppermute | solution.py:39
  44.9 3.5 %collective-permute-done.10 = bf16[16,2304]{1,0:T(8,128)(2,1)S(1)} collective-permute-done((bf16[16,2304]{1,0:T(8,128)(2,1)S(1)}, bf16[16,2304]{1,0:T(8,128)(2,1)S(1)}, u32[]{:S(2)}, u32[]{:S(2)}) %collective-permute-start.10) | collective-permute-done | bytes 73760 | tf_op jit(solution)/shard_map/ppermute | solution.py:39
  48.4 1.5 collective-permute-start.13
  50.0 1.6 collective-permute-start.14
  52.7 4.0 %collective-permute-done.14.refs_4_ = bf16[2,16,2304]{2,1,0:T(8,128)(2,1)S(1)} collective-permute-done((bf16[2,16,2304]{2,1,0:T(8,128)(2,1)S(1)}, bf16[2,16,2304]{2,1,0:T(8,128)(2,1)S(1)}, u32[]{:S(2)}, u32[]{:S(2)}) %collective-permute-start.14) | collective-permute-done | bytes 147488 | tf_op jit(solution)/shard_map/ppermute | solution.py:39
  56.7 1.9 %collective-permute-start.17 = (bf16[2,16,2304]{2,1,0:T(8,128)(2,1)S(1)}, bf16[2,16,2304]{2,1,0:T(8,128)(2,1)S(1)}, u32[]{:S(2)}, u32[]{:S(2)}) collective-permute-start(bf16[2,16,2304]{2,1,0:T(8,128)(2,1)S(1)} %collective-permute-done.13.refs_3_), channel_id=1, source_target_pairs={{0,16},{4,20},{8,24},{12,28},{16,0},{20,4},{24,8},{28,12},{1,17},{... | collective-permute-start | bytes 442376 | tf_op jit(solution)/shard_map/ppermute | solution.py:39
  59.7 2.1 %collective-permute-done.16.refs_6_ = bf16[2,16,2304]{2,1,0:T(8,128)(2,1)S(1)} collective-permute-done((bf16[2,16,2304]{2,1,0:T(8,128)(2,1)S(1)}, bf16[2,16,2304]{2,1,0:T(8,128)(2,1)S(1)}, u32[]{:S(2)}, u32[]{:S(2)}) %collective-permute-start.16) | collective-permute-done | bytes 147488 | tf_op jit(solution)/shard_map/ppermute | solution.py:39
  61.9 1.4 shard_map.258
  67.7 2.1 %collective-permute-start.24 = (bf16[64,512]{1,0:T(8,128)(2,1)S(1)}, bf16[64,512]{1,0:T(8,128)(2,1)S(1)}, u32[]{:S(2)}, u32[]{:S(2)}) collective-permute-start(bf16[64,512]{1,0:T(8,128)(2,1)S(1)} %add_convert_fusion.11), channel_id=1, source_target_pairs={{0,2},{1,3},{2,0},{3,1},{4,6},{5,7},{6,4},{7,5},{8,10},{9,11},{10,... | collective-permute-start | bytes 196616 | tf_op jit(solution)/shard_map/ppermute | solution.py:39
  71.2 2.4 %collective-permute-done.24 = bf16[64,512]{1,0:T(8,128)(2,1)S(1)} collective-permute-done((bf16[64,512]{1,0:T(8,128)(2,1)S(1)}, bf16[64,512]{1,0:T(8,128)(2,1)S(1)}, u32[]{:S(2)}, u32[]{:S(2)}) %collective-permute-start.24) | collective-permute-done | bytes 65568 | tf_op jit(solution)/shard_map/ppermute | solution.py:39
  73.7 2.1 %collective-permute-done.21 = bf16[64,512]{1,0:T(8,128)(2,1)S(1)} collective-permute-done((bf16[64,512]{1,0:T(8,128)(2,1)S(1)}, bf16[64,512]{1,0:T(8,128)(2,1)S(1)}, u32[]{:S(2)}, u32[]{:S(2)}) %collective-permute-start.21) | collective-permute-done | bytes 65568 | tf_op jit(solution)/shard_map/ppermute | solution.py:39
  76.8 2.3 %collective-permute-start.27 = (bf16[64,512]{1,0:T(8,128)(2,1)S(1)}, bf16[64,512]{1,0:T(8,128)(2,1)S(1)}, u32[]{:S(2)}, u32[]{:S(2)}) collective-permute-start(bf16[64,512]{1,0:T(8,128)(2,1)S(1)} %get-tuple-element.218.refs_0_), channel_id=1, source_target_pairs={{0,2},{1,3},{2,0},{3,1},{4,6},{5,7},{6,4},{7,5},{8,10},{9,11},{10,... | collective-permute-start | bytes 196616 | tf_op jit(solution)/shard_map/ppermute | solution.py:39
  79.5 4.3 %collective-permute-done.30.refs_2_ = bf16[64,512]{1,0:T(8,128)(2,1)S(1)} collective-permute-done((bf16[64,512]{1,0:T(8,128)(2,1)S(1)}, bf16[64,512]{1,0:T(8,128)(2,1)S(1)}, u32[]{:S(2)}, u32[]{:S(2)}) %collective-permute-start.30) | collective-permute-done | bytes 65568 | tf_op jit(solution)/shard_map/ppermute | solution.py:39
  83.8 2.0 %collective-permute-start.26 = (bf16[64,512]{1,0:T(8,128)(2,1)S(1)}, bf16[64,512]{1,0:T(8,128)(2,1)S(1)}, u32[]{:S(2)}, u32[]{:S(2)}) collective-permute-start(bf16[64,512]{1,0:T(8,128)(2,1)S(1)} %get-tuple-element.218.refs_0_), channel_id=1, source_target_pairs={{0,1},{1,0},{2,3},{3,2},{4,5},{5,4},{6,7},{7,6},{8,9},{9,8},{10,11... | collective-permute-start | bytes 196616 | tf_op jit(solution)/shard_map/ppermute | solution.py:39
  85.9 2.2 %collective-permute-done.31.refs_3_ = bf16[64,512]{1,0:T(8,128)(2,1)S(1)} collective-permute-done((bf16[64,512]{1,0:T(8,128)(2,1)S(1)}, bf16[64,512]{1,0:T(8,128)(2,1)S(1)}, u32[]{:S(2)}, u32[]{:S(2)}) %collective-permute-start.31) | collective-permute-done | bytes 65568 | tf_op jit(solution)/shard_map/ppermute | solution.py:39
  88.8 1.3 collective-permute-done.28.refs_3_
  90.1 1.5 shard_map.259
  95.8 2.7 %collective-permute-done.34 = bf16[2,16,2304]{2,1,0:T(8,128)(2,1)S(1)} collective-permute-done((bf16[2,16,2304]{2,1,0:T(8,128)(2,1)S(1)}, bf16[2,16,2304]{2,1,0:T(8,128)(2,1)S(1)}, u32[]{:S(2)}, u32[]{:S(2)}) %collective-permute-start.34) | collective-permute-done | bytes 147488 | tf_op jit(solution)/shard_map/ppermute | solution.py:39
  101.6 4.3 %shard_map.260 = (f32[2,2304,512]{2,1,0:T(8,128)}, f32[2,2304,512]{2,1,0:T(8,128)}, f32[8,128]{1,0:T(8,128)S(1)}) custom-call(s32[1]{0:T(128)} %bitcast.core_ref, f32[2,2304,512]{2,1,0:T(8,128)S(1)} %bitcast.86, f32[2,2304,512]{2,1,0:T(8,128)S(1)} %bitcast.88, bf16[256,2304]{1,0:T(8,128)(2,1)S(1)} %get-tuple-element.135.rows_ref, ...), custom_call_target="tpu_custom_call" | custom-call | bytes 9437184 | tf_op jit(solution)/shard_map/pallas_call | solution.py:544
  107.0 2.5 %collective-permute-start.40 = (bf16[16,2304]{1,0:T(8,128)(2,1)S(1)}, bf16[16,2304]{1,0:T(8,128)(2,1)S(1)}, u32[]{:S(2)}, u32[]{:S(2)}) collective-permute-start(bf16[16,2304]{1,0:T(8,128)(2,1)S(1)} %get-tuple-element.228), channel_id=1, source_target_pairs={{0,2},{1,3},{2,0},{3,1},{4,6},{5,7},{6,4},{7,5},{8,10},{9,11},{10,... | collective-permute-start | bytes 221192 | tf_op jit(solution)/shard_map/ppermute | solution.py:39
  110.7 4.0 %shard_map.261 = (f32[2,2304,512]{2,1,0:T(8,128)}, f32[2,2304,512]{2,1,0:T(8,128)}, f32[8,128]{1,0:T(8,128)S(1)}) custom-call(s32[1]{0:T(128)} %bitcast.core_ref, f32[2,2304,512]{2,1,0:T(8,128)S(1)} %bitcast.86, f32[2,2304,512]{2,1,0:T(8,128)S(1)} %bitcast.88, ...), custom_call_target="tpu_custom_call", output_to_operand_aliasing={{0}: (8, {}), {1}: (9, {})} | custom-call | bytes 9437184 | tf_op jit(solution)/shard_map/pallas_call | solution.py:544
  115.9 1.6 collective-permute-done.42.refs_4_
  117.5 7.5 %shard_map.262 = (bf16[304,384]{1,0:T(8,128)(2,1)S(1)}, bf16[304,384]{1,0:T(8,128)(2,1)S(1)}, bf16[304,384]{1,0:T(8,128)(2,1)S(1)}, bf16[304,384]{1,0:T(8,128)(2...) custom-call(s32[1]{0:T(128)} %bitcast.core_ref, ...), custom_call_target="tpu_custom_call" | custom-call | tf_op jit(solution)/shard_map/pallas_call | solution.py:484
  126.2 1.4 collective-permute-start.44
  128.3 4.0 %shard_map.263 = (f32[2,2304,512]{2,1,0:T(8,128)}, f32[2,2304,512]{2,1,0:T(8,128)}, f32[8,128]{1,0:T(8,128)S(1)}) custom-call(s32[1]{0:T(128)} %bitcast.core_ref, f32[2,2304,512]{2,1,0:T(8,128)S(1)} %bitcast.86, f32[2,2304,512]{2,1,0:T(8,128)S(1)} %bitcast.88, ...), custom_call_target="tpu_custom_call", output_to_operand_aliasing={{0}: (8, {}), {1}: (9, {})} | custom-call | bytes 9437184 | tf_op jit(solution)/shard_map/pallas_call | solution.py:544
  132.8 2.0 %collective-permute-done.44 = bf16[304,384]{1,0:T(8,128)(2,1)S(1)} collective-permute-done((bf16[304,384]{1,0:T(8,128)(2,1)S(1)}, bf16[304,384]{1,0:T(8,128)(2,1)S(1)}, u32[]{:S(2)}, u32[]{:S(2)}) %collective-permute-start.44) | collective-permute-done | bytes 233504 | tf_op jit(solution)/shard_map/ppermute | solution.py:39
  134.9 1.4 collective-permute-start.46
  138.6 4.3 %shard_map.264 = (f32[2,2304,512]{2,1,0:T(8,128)}, f32[2,2304,512]{2,1,0:T(8,128)}, f32[8,128]{1,0:T(8,128)S(1)}) custom-call(s32[1]{0:T(128)} %bitcast.core_ref, f32[2,2304,512]{2,1,0:T(8,128)S(1)} %bitcast.86, f32[2,2304,512]{2,1,0:T(8,128)S(1)} %bitcast.88, ...), custom_call_target="tpu_custom_call", output_to_operand_aliasing={{0}: (8, {}), {1}: (9, {})} | custom-call | bytes 9437184 | tf_op jit(solution)/shard_map/pallas_call | solution.py:544
  144.3 2.3 %collective-permute-done.47 = bf16[304,384]{1,0:T(8,128)(2,1)S(1)} collective-permute-done((bf16[304,384]{1,0:T(8,128)(2,1)S(1)}, bf16[304,384]{1,0:T(8,128)(2,1)S(1)}, u32[]{:S(2)}, u32[]{:S(2)}) %collective-permute-start.47) | collective-permute-done | bytes 233504 | tf_op jit(solution)/shard_map/ppermute | solution.py:39
  147.9 2.7 %collective-permute-start.53 = (bf16[160,384]{1,0:T(8,128)(2,1)S(1)}, bf16[160,384]{1,0:T(8,128)(2,1)S(1)}, u32[]{:S(2)}, u32[]{:S(2)}) collective-permute-start(bf16[160,384]{1,0:T(8,128)(2,1)S(1)} %pad_maximum_fusion.8), channel_id=1, source_target_pairs={{0,3},{1,2},{2,1},{3,0},{4,7},{5,6},{6,5},{7,4},{8,11},{9,10},{10,... | collective-permute-start | bytes 368648 | tf_op jit(solution)/shard_map/ppermute | solution.py:39
  150.7 6.8 %convolution_convert_fusion = bf16[13,13,16,384]{3,2,1,0:T(8,128)(2,1)S(1)} fusion(bf16[13,13,16,256]{3,2,1,0:T(8,128)(2,1)S(1)} %copy-done.14, bf16[3,3,256,384]{3,2,1,0:T(8,128)(2,1)S(1)} %bitcast.125), kind=kOutput, calls=%fused_computation.14 | convolution fusion | flops 4307539968 | bytes 5230592 | tf_op jit(solution)/shard_map/conv_general_dilated | solution.py:1009
  157.6 3.0 %collective-permute-done.52 = bf16[160,384]{1,0:T(8,128)(2,1)S(1)} collective-permute-done((bf16[160,384]{1,0:T(8,128)(2,1)S(1)}, bf16[160,384]{1,0:T(8,128)(2,1)S(1)}, u32[]{:S(2)}, u32[]{:S(2)}) %collective-permute-start.52) | collective-permute-done | bytes 122912 | tf_op jit(solution)/shard_map/ppermute | solution.py:39
  162.0 2.8 %collective-permute-start.56 = (bf16[160,384]{1,0:T(8,128)(2,1)S(1)}, bf16[160,384]{1,0:T(8,128)(2,1)S(1)}, u32[]{:S(2)}, u32[]{:S(2)}) collective-permute-start(bf16[160,384]{1,0:T(8,128)(2,1)S(1)} %add_convert_fusion.6.refs_0_), channel_id=1, source_target_pairs={{0,2},{1,3},{2,0},{3,1},{4,6},{5,7},{6,4},{7,5},{8,10},{9,11},{10,... | collective-permute-start | bytes 368648 | tf_op jit(solution)/shard_map/ppermute | solution.py:39
  164.8 1.5 collective-permute-start.57
  167.3 2.9 %copy.59 = bf16[2,13,13,8,384]{4,0,2,1,3:T(2,128)(2,1)} copy(bf16[2,13,13,8,384]{4,3,2,1,0:T(8,128)(2,1)S(1)} %shard_map.265) | data formatting | bytes 4153344 | tf_op jit(solution)/shard_map/pallas_call | solution.py:567
  170.2 4.2 %collective-permute-done.56.refs_2_ = bf16[160,384]{1,0:T(8,128)(2,1)S(1)} collective-permute-done((bf16[160,384]{1,0:T(8,128)(2,1)S(1)}, bf16[160,384]{1,0:T(8,128)(2,1)S(1)}, u32[]{:S(2)}, u32[]{:S(2)}) %collective-permute-start.56) | collective-permute-done | bytes 122912 | tf_op jit(solution)/shard_map/ppermute | solution.py:39
  174.5 1.5 shard_map.266
  (179 shorter events, 36.8 us)
Async XLA Ops:
  4.0 18.6 %collective-permute-start = (bf16[13,13,8,384]{3,2,1,0:T(8,128)(2,1)S(1)}, bf16[13,13,8,384]{3,2,1,0:T(8,128)(2,1)S(1)}, u32[]{:S(2)}, u32[]{:S(2)}) collective-permute-start(bf16[13,13,8,384]{3,2,1,0:T(8,128)(2,1)S(1)} %get-tuple-element.227), channel_id=1, source_target_pairs={{0,4},{4,0},{8,12},{12,8},{16,20},{20,16},{24,28},{28,24},{1,5},{5... | collective-permute-start | bytes 3115016 | tf_op jit(solution)/shard_map/ppermute | solution.py:39
  4.5 9.1 %collective-permute-start.2 = (bf16[304,384]{1,0:T(8,128)(2,1)S(1)}, bf16[304,384]{1,0:T(8,128)(2,1)S(1)}, u32[]{:S(2)}, u32[]{:S(2)}) collective-permute-start(bf16[304,384]{1,0:T(8,128)(2,1)S(1)} %get-tuple-element.110.refs_0_), channel_id=1, source_target_pairs={{0,8},{4,12},{8,0},{12,4},{16,24},{20,28},{24,16},{28,20},{1,9},{5... | collective-permute-start | bytes 700424 | tf_op jit(solution)/shard_map/ppermute | solution.py:39
  7.1 7.6 %collective-permute-start.3 = (bf16[304,384]{1,0:T(8,128)(2,1)S(1)}, bf16[304,384]{1,0:T(8,128)(2,1)S(1)}, u32[]{:S(2)}, u32[]{:S(2)}) collective-permute-start(bf16[304,384]{1,0:T(8,128)(2,1)S(1)} %get-tuple-element.111), channel_id=1, source_target_pairs={{0,20},{4,16},{8,28},{12,24},{16,4},{20,0},{24,12},{28,8},{1,21},{... | collective-permute-start | bytes 700424 | tf_op jit(solution)/shard_map/ppermute | solution.py:39
  8.4 12.1 %collective-permute-start.5 = (bf16[304,384]{1,0:T(8,128)(2,1)S(1)}, bf16[304,384]{1,0:T(8,128)(2,1)S(1)}, u32[]{:S(2)}, u32[]{:S(2)}) collective-permute-start(bf16[304,384]{1,0:T(8,128)(2,1)S(1)} %get-tuple-element.110.refs_0_), channel_id=1, source_target_pairs={{0,16},{4,20},{8,24},{12,28},{16,0},{20,4},{24,8},{28,12},{1,17},{... | collective-permute-start | bytes 700424 | tf_op jit(solution)/shard_map/ppermute | solution.py:39
  8.9 12.2 %collective-permute-start.4 = (bf16[304,384]{1,0:T(8,128)(2,1)S(1)}, bf16[304,384]{1,0:T(8,128)(2,1)S(1)}, u32[]{:S(2)}, u32[]{:S(2)}) collective-permute-start(bf16[304,384]{1,0:T(8,128)(2,1)S(1)} %get-tuple-element.111), channel_id=1, source_target_pairs={{0,12},{4,8},{8,4},{12,0},{16,28},{20,24},{24,20},{28,16},{1,13},{... | collective-permute-start | bytes 700424 | tf_op jit(solution)/shard_map/ppermute | solution.py:39
  13.6 10.0 %collective-permute-start.1 = (bf16[304,384]{1,0:T(8,128)(2,1)S(1)}, bf16[304,384]{1,0:T(8,128)(2,1)S(1)}, u32[]{:S(2)}, u32[]{:S(2)}) collective-permute-start(bf16[304,384]{1,0:T(8,128)(2,1)S(1)} %get-tuple-element.111), channel_id=1, source_target_pairs={{0,4},{4,0},{8,12},{12,8},{16,20},{20,16},{24,28},{28,24},{1,5},{5... | collective-permute-start | bytes 700424 | tf_op jit(solution)/shard_map/ppermute | solution.py:39
  19.6 42.2 %collective-permute-start.18 = (bf16[2304,512]{1,0:T(8,128)(2,1)S(1)}, bf16[2304,512]{1,0:T(8,128)(2,1)S(1)}, u32[]{:S(2)}, u32[]{:S(2)}) collective-permute-start(bf16[2304,512]{1,0:T(8,128)(2,1)S(1)} %get-tuple-element.121), channel_id=1, source_target_pairs={{0,4},{4,0},{8,12},{12,8},{16,20},{20,16},{24,28},{28,24},{1,5},{5... | collective-permute-start | bytes 7077896 | tf_op jit(solution)/shard_map/ppermute | solution.py:39
  20.5 7.7 %collective-permute-start.6 = (bf16[304,384]{1,0:T(8,128)(2,1)S(1)}, bf16[304,384]{1,0:T(8,128)(2,1)S(1)}, u32[]{:S(2)}, u32[]{:S(2)}) collective-permute-start(bf16[304,384]{1,0:T(8,128)(2,1)S(1)} %collective-permute-done.5.refs_4_), channel_id=1, source_target_pairs={{0,8},{4,12},{8,0},{12,4},{16,24},{20,28},{24,16},{28,20},{1,9},{5... | collective-permute-start | bytes 700424 | tf_op jit(solution)/shard_map/ppermute | solution.py:39
  21.1 7.4 %collective-permute-start.7 = (bf16[304,384]{1,0:T(8,128)(2,1)S(1)}, bf16[304,384]{1,0:T(8,128)(2,1)S(1)}, u32[]{:S(2)}, u32[]{:S(2)}) collective-permute-start(bf16[304,384]{1,0:T(8,128)(2,1)S(1)} %collective-permute-done.4.refs_3_), channel_id=1, source_target_pairs={{0,16},{4,20},{8,24},{12,28},{16,0},{20,4},{24,8},{28,12},{1,17},{... | collective-permute-start | bytes 700424 | tf_op jit(solution)/shard_map/ppermute | solution.py:39
  38.2 6.7 %collective-permute-start.11 = (bf16[16,2304]{1,0:T(8,128)(2,1)S(1)}, bf16[16,2304]{1,0:T(8,128)(2,1)S(1)}, u32[]{:S(2)}, u32[]{:S(2)}) collective-permute-start(bf16[16,2304]{1,0:T(8,128)(2,1)S(1)} %get-tuple-element.119), channel_id=1, source_target_pairs={{0,3},{1,2},{2,1},{3,0},{4,7},{5,6},{6,5},{7,4},{8,11},{9,10},{10,... | collective-permute-start | bytes 221192 | tf_op jit(solution)/shard_map/ppermute | solution.py:39
  41.9 6.5 %collective-permute-start.10 = (bf16[16,2304]{1,0:T(8,128)(2,1)S(1)}, bf16[16,2304]{1,0:T(8,128)(2,1)S(1)}, u32[]{:S(2)}, u32[]{:S(2)}) collective-permute-start(bf16[16,2304]{1,0:T(8,128)(2,1)S(1)} %get-tuple-element.118), channel_id=1, source_target_pairs={{0,2},{1,3},{2,0},{3,1},{4,6},{5,7},{6,4},{7,5},{8,10},{9,11},{10,... | collective-permute-start | bytes 221192 | tf_op jit(solution)/shard_map/ppermute | solution.py:39
  42.1 7.9 %collective-permute-start.9 = (bf16[16,2304]{1,0:T(8,128)(2,1)S(1)}, bf16[16,2304]{1,0:T(8,128)(2,1)S(1)}, u32[]{:S(2)}, u32[]{:S(2)}) collective-permute-start(bf16[16,2304]{1,0:T(8,128)(2,1)S(1)} %get-tuple-element.117), channel_id=1, source_target_pairs={{0,1},{1,0},{2,3},{3,2},{4,5},{5,4},{6,7},{7,6},{8,9},{9,8},{10,11... | collective-permute-start | bytes 221192 | tf_op jit(solution)/shard_map/ppermute | solution.py:39
  48.4 8.3 %collective-permute-start.13 = (bf16[2,16,2304]{2,1,0:T(8,128)(2,1)S(1)}, bf16[2,16,2304]{2,1,0:T(8,128)(2,1)S(1)}, u32[]{:S(2)}, u32[]{:S(2)}) collective-permute-start(bf16[2,16,2304]{2,1,0:T(8,128)(2,1)S(1)} %pad_maximum_fusion.3.refs_1_), channel_id=1, source_target_pairs={{0,8},{4,12},{8,0},{12,4},{16,24},{20,28},{24,16},{28,20},{1,9},{5... | collective-permute-start | bytes 442376 | tf_op jit(solution)/shard_map/ppermute | solution.py:39
  50.0 6.7 %collective-permute-start.14 = (bf16[2,16,2304]{2,1,0:T(8,128)(2,1)S(1)}, bf16[2,16,2304]{2,1,0:T(8,128)(2,1)S(1)}, u32[]{:S(2)}, u32[]{:S(2)}) collective-permute-start(bf16[2,16,2304]{2,1,0:T(8,128)(2,1)S(1)} %pad_maximum_fusion.2.refs_0_), channel_id=1, source_target_pairs={{0,16},{4,20},{8,24},{12,28},{16,0},{20,4},{24,8},{28,12},{1,17},{... | collective-permute-start | bytes 442376 | tf_op jit(solution)/shard_map/ppermute | solution.py:39
  51.6 7.1 %collective-permute-start.12 = (bf16[2,16,2304]{2,1,0:T(8,128)(2,1)S(1)}, bf16[2,16,2304]{2,1,0:T(8,128)(2,1)S(1)}, u32[]{:S(2)}, u32[]{:S(2)}) collective-permute-start(bf16[2,16,2304]{2,1,0:T(8,128)(2,1)S(1)} %pad_maximum_fusion.2.refs_0_), channel_id=1, source_target_pairs={{0,8},{4,12},{8,0},{12,4},{16,24},{20,28},{24,16},{28,20},{1,9},{5... | collective-permute-start | bytes 442376 | tf_op jit(solution)/shard_map/ppermute | solution.py:39
  52.2 7.5 %collective-permute-start.15 = (bf16[2,16,2304]{2,1,0:T(8,128)(2,1)S(1)}, bf16[2,16,2304]{2,1,0:T(8,128)(2,1)S(1)}, u32[]{:S(2)}, u32[]{:S(2)}) collective-permute-start(bf16[2,16,2304]{2,1,0:T(8,128)(2,1)S(1)} %pad_maximum_fusion.3.refs_1_), channel_id=1, source_target_pairs={{0,16},{4,20},{8,24},{12,28},{16,0},{20,4},{24,8},{28,12},{1,17},{... | collective-permute-start | bytes 442376 | tf_op jit(solution)/shard_map/ppermute | solution.py:39
  56.7 5.1 %collective-permute-start.16 = (bf16[2,16,2304]{2,1,0:T(8,128)(2,1)S(1)}, bf16[2,16,2304]{2,1,0:T(8,128)(2,1)S(1)}, u32[]{:S(2)}, u32[]{:S(2)}) collective-permute-start(bf16[2,16,2304]{2,1,0:T(8,128)(2,1)S(1)} %collective-permute-done.14.refs_4_), channel_id=1, source_target_pairs={{0,8},{4,12},{8,0},{12,4},{16,24},{20,28},{24,16},{28,20},{1,9},{5... | collective-permute-start | bytes 442376 | tf_op jit(solution)/shard_map/ppermute | solution.py:39
  56.7 5.1 %collective-permute-start.17 = (bf16[2,16,2304]{2,1,0:T(8,128)(2,1)S(1)}, bf16[2,16,2304]{2,1,0:T(8,128)(2,1)S(1)}, u32[]{:S(2)}, u32[]{:S(2)}) collective-permute-start(bf16[2,16,2304]{2,1,0:T(8,128)(2,1)S(1)} %collective-permute-done.13.refs_3_), channel_id=1, source_target_pairs={{0,16},{4,20},{8,24},{12,28},{16,0},{20,4},{24,8},{28,12},{1,17},{... | collective-permute-start | bytes 442376 | tf_op jit(solution)/shard_map/ppermute | solution.py:39
  64.1 5.7 %collective-permute-start.20 = (bf16[64,512]{1,0:T(8,128)(2,1)S(1)}, bf16[64,512]{1,0:T(8,128)(2,1)S(1)}, u32[]{:S(2)}, u32[]{:S(2)}) collective-permute-start(bf16[64,512]{1,0:T(8,128)(2,1)S(1)} %get-tuple-element.125), channel_id=1, source_target_pairs={{0,1},{1,0},{2,3},{3,2},{4,5},{5,4},{6,7},{7,6},{8,9},{9,8},{10,11... | collective-permute-start | bytes 196616 | tf_op jit(solution)/shard_map/ppermute | solution.py:39
  65.4 8.3 %collective-permute-start.19 = (bf16[64,512]{1,0:T(8,128)(2,1)S(1)}, bf16[64,512]{1,0:T(8,128)(2,1)S(1)}, u32[]{:S(2)}, u32[]{:S(2)}) collective-permute-start(bf16[64,512]{1,0:T(8,128)(2,1)S(1)} %get-tuple-element.123), channel_id=1, source_target_pairs={{0,1},{1,0},{2,3},{3,2},{4,5},{5,4},{6,7},{7,6},{8,9},{9,8},{10,11... | collective-permute-start | bytes 196616 | tf_op jit(solution)/shard_map/ppermute | solution.py:39
  67.7 5.9 %collective-permute-start.24 = (bf16[64,512]{1,0:T(8,128)(2,1)S(1)}, bf16[64,512]{1,0:T(8,128)(2,1)S(1)}, u32[]{:S(2)}, u32[]{:S(2)}) collective-permute-start(bf16[64,512]{1,0:T(8,128)(2,1)S(1)} %add_convert_fusion.11), channel_id=1, source_target_pairs={{0,2},{1,3},{2,0},{3,1},{4,6},{5,7},{6,4},{7,5},{8,10},{9,11},{10,... | collective-permute-start | bytes 196616 | tf_op jit(solution)/shard_map/ppermute | solution.py:39
  69.8 5.9 %collective-permute-start.21 = (bf16[64,512]{1,0:T(8,128)(2,1)S(1)}, bf16[64,512]{1,0:T(8,128)(2,1)S(1)}, u32[]{:S(2)}, u32[]{:S(2)}) collective-permute-start(bf16[64,512]{1,0:T(8,128)(2,1)S(1)} %add_convert_fusion.12), channel_id=1, source_target_pairs={{0,2},{1,3},{2,0},{3,1},{4,6},{5,7},{6,4},{7,5},{8,10},{9,11},{10,... | collective-permute-start | bytes 196616 | tf_op jit(solution)/shard_map/ppermute | solution.py:39
  76.1 7.7 %collective-permute-start.30 = (bf16[64,512]{1,0:T(8,128)(2,1)S(1)}, bf16[64,512]{1,0:T(8,128)(2,1)S(1)}, u32[]{:S(2)}, u32[]{:S(2)}) collective-permute-start(bf16[64,512]{1,0:T(8,128)(2,1)S(1)} %get-tuple-element.243.refs_0_), channel_id=1, source_target_pairs={{0,2},{1,3},{2,0},{3,1},{4,6},{5,7},{6,4},{7,5},{8,10},{9,11},{10,... | collective-permute-start | bytes 196616 | tf_op jit(solution)/shard_map/ppermute | solution.py:39
  76.8 9.1 %collective-permute-start.27 = (bf16[64,512]{1,0:T(8,128)(2,1)S(1)}, bf16[64,512]{1,0:T(8,128)(2,1)S(1)}, u32[]{:S(2)}, u32[]{:S(2)}) collective-permute-start(bf16[64,512]{1,0:T(8,128)(2,1)S(1)} %get-tuple-element.218.refs_0_), channel_id=1, source_target_pairs={{0,2},{1,3},{2,0},{3,1},{4,6},{5,7},{6,4},{7,5},{8,10},{9,11},{10,... | collective-permute-start | bytes 196616 | tf_op jit(solution)/shard_map/ppermute | solution.py:39
  79.1 6.8 %collective-permute-start.29 = (bf16[64,512]{1,0:T(8,128)(2,1)S(1)}, bf16[64,512]{1,0:T(8,128)(2,1)S(1)}, u32[]{:S(2)}, u32[]{:S(2)}) collective-permute-start(bf16[64,512]{1,0:T(8,128)(2,1)S(1)} %get-tuple-element.243.refs_0_), channel_id=1, source_target_pairs={{0,1},{1,0},{2,3},{3,2},{4,5},{5,4},{6,7},{7,6},{8,9},{9,8},{10,11... | collective-permute-start | bytes 196616 | tf_op jit(solution)/shard_map/ppermute | solution.py:39
  91.7 6.8 %collective-permute-start.34 = (bf16[2,16,2304]{2,1,0:T(8,128)(2,1)S(1)}, bf16[2,16,2304]{2,1,0:T(8,128)(2,1)S(1)}, u32[]{:S(2)}, u32[]{:S(2)}) collective-permute-start(bf16[2,16,2304]{2,1,0:T(8,128)(2,1)S(1)} %get-tuple-element.134), channel_id=1, source_target_pairs={{0,8},{4,12},{8,0},{12,4},{16,24},{20,28},{24,16},{28,20},{1,9},{5... | collective-permute-start | bytes 442376 | tf_op jit(solution)/shard_map/ppermute | solution.py:39
  92.7 35.6 %collective-permute-start.45 = (bf16[256,2304]{1,0:T(8,128)(2,1)S(1)}, bf16[256,2304]{1,0:T(8,128)(2,1)S(1)}, u32[]{:S(2)}, u32[]{:S(2)}) collective-permute-start(bf16[256,2304]{1,0:T(8,128)(2,1)S(1)} %get-tuple-element.135.rows_ref), channel_id=1, source_target_pairs={{0,4},{4,0},{8,12},{12,8},{16,20},{20,16},{24,28},{28,24},{1,5},{5... | collective-permute-start | bytes 3538952 | tf_op jit(solution)/shard_map/ppermute | solution.py:39
  92.7 13.4 %collective-permute-start.33 = (bf16[2,16,2304]{2,1,0:T(8,128)(2,1)S(1)}, bf16[2,16,2304]{2,1,0:T(8,128)(2,1)S(1)}, u32[]{:S(2)}, u32[]{:S(2)}) collective-permute-start(bf16[2,16,2304]{2,1,0:T(8,128)(2,1)S(1)} %get-tuple-element.132), channel_id=1, source_target_pairs={{0,8},{4,12},{8,0},{12,4},{16,24},{20,28},{24,16},{28,20},{1,9},{5... | collective-permute-start | bytes 442376 | tf_op jit(solution)/shard_map/ppermute | solution.py:39
  93.8 6.7 %collective-permute-start.36 = (bf16[2,16,2304]{2,1,0:T(8,128)(2,1)S(1)}, bf16[2,16,2304]{2,1,0:T(8,128)(2,1)S(1)}, u32[]{:S(2)}, u32[]{:S(2)}) collective-permute-start(bf16[2,16,2304]{2,1,0:T(8,128)(2,1)S(1)} %get-tuple-element.137), channel_id=1, source_target_pairs={{0,16},{4,20},{8,24},{12,28},{16,0},{20,4},{24,8},{28,12},{1,17},{... | collective-permute-start | bytes 442376 | tf_op jit(solution)/shard_map/ppermute | solution.py:39
  94.7 12.2 %collective-permute-start.39 = (bf16[2,16,2304]{2,1,0:T(8,128)(2,1)S(1)}, bf16[2,16,2304]{2,1,0:T(8,128)(2,1)S(1)}, u32[]{:S(2)}, u32[]{:S(2)}) collective-permute-start(bf16[2,16,2304]{2,1,0:T(8,128)(2,1)S(1)} %get-tuple-element.144), channel_id=1, source_target_pairs={{0,16},{4,20},{8,24},{12,28},{16,0},{20,4},{24,8},{28,12},{1,17},{... | collective-permute-start | bytes 442376 | tf_op jit(solution)/shard_map/ppermute | solution.py:39
  98.5 7.5 %collective-permute-start.35 = (bf16[2,16,2304]{2,1,0:T(8,128)(2,1)S(1)}, bf16[2,16,2304]{2,1,0:T(8,128)(2,1)S(1)}, u32[]{:S(2)}, u32[]{:S(2)}) collective-permute-start(bf16[2,16,2304]{2,1,0:T(8,128)(2,1)S(1)} %add_convert_fusion.5), channel_id=1, source_target_pairs={{0,16},{4,20},{8,24},{12,28},{16,0},{20,4},{24,8},{28,12},{1,17},{... | collective-permute-start | bytes 442376 | tf_op jit(solution)/shard_map/ppermute | solution.py:39
  100.5 6.4 %collective-permute-start.38 = (bf16[2,16,2304]{2,1,0:T(8,128)(2,1)S(1)}, bf16[2,16,2304]{2,1,0:T(8,128)(2,1)S(1)}, u32[]{:S(2)}, u32[]{:S(2)}) collective-permute-start(bf16[2,16,2304]{2,1,0:T(8,128)(2,1)S(1)} %add_convert_fusion.4.refs_4_), channel_id=1, source_target_pairs={{0,8},{4,12},{8,0},{12,4},{16,24},{20,28},{24,16},{28,20},{1,9},{5... | collective-permute-start | bytes 442376 | tf_op jit(solution)/shard_map/ppermute | solution.py:39
  106.1 8.6 %collective-permute-start.37 = (bf16[16,2304]{1,0:T(8,128)(2,1)S(1)}, bf16[16,2304]{1,0:T(8,128)(2,1)S(1)}, u32[]{:S(2)}, u32[]{:S(2)}) collective-permute-start(bf16[16,2304]{1,0:T(8,128)(2,1)S(1)} %get-tuple-element.231), channel_id=1, source_target_pairs={{0,1},{1,0},{2,3},{3,2},{4,5},{5,4},{6,7},{7,6},{8,9},{9,8},{10,11... | collective-permute-start | bytes 221192 | tf_op jit(solution)/shard_map/ppermute | solution.py:39
  107.0 7.8 %collective-permute-start.40 = (bf16[16,2304]{1,0:T(8,128)(2,1)S(1)}, bf16[16,2304]{1,0:T(8,128)(2,1)S(1)}, u32[]{:S(2)}, u32[]{:S(2)}) collective-permute-start(bf16[16,2304]{1,0:T(8,128)(2,1)S(1)} %get-tuple-element.228), channel_id=1, source_target_pairs={{0,2},{1,3},{2,0},{3,1},{4,6},{5,7},{6,4},{7,5},{8,10},{9,11},{10,... | collective-permute-start | bytes 221192 | tf_op jit(solution)/shard_map/ppermute | solution.py:39
  109.5 6.3 %collective-permute-start.41 = (bf16[16,2304]{1,0:T(8,128)(2,1)S(1)}, bf16[16,2304]{1,0:T(8,128)(2,1)S(1)}, u32[]{:S(2)}, u32[]{:S(2)}) collective-permute-start(bf16[16,2304]{1,0:T(8,128)(2,1)S(1)} %get-tuple-element.229.refs_6_), channel_id=1, source_target_pairs={{0,3},{1,2},{2,1},{3,0},{4,7},{5,6},{6,5},{7,4},{8,11},{9,10},{10,... | collective-permute-start | bytes 221192 | tf_op jit(solution)/shard_map/ppermute | solution.py:39
  125.0 7.8 %collective-permute-start.43 = (bf16[304,384]{1,0:T(8,128)(2,1)S(1)}, bf16[304,384]{1,0:T(8,128)(2,1)S(1)}, u32[]{:S(2)}, u32[]{:S(2)}) collective-permute-start(bf16[304,384]{1,0:T(8,128)(2,1)S(1)} %get-tuple-element.151), channel_id=1, source_target_pairs={{0,8},{4,12},{8,0},{12,4},{16,24},{20,28},{24,16},{28,20},{1,9},{5... | collective-permute-start | bytes 700424 | tf_op jit(solution)/shard_map/ppermute | solution.py:39
  126.2 8.6 %collective-permute-start.44 = (bf16[304,384]{1,0:T(8,128)(2,1)S(1)}, bf16[304,384]{1,0:T(8,128)(2,1)S(1)}, u32[]{:S(2)}, u32[]{:S(2)}) collective-permute-start(bf16[304,384]{1,0:T(8,128)(2,1)S(1)} %get-tuple-element.152), channel_id=1, source_target_pairs={{0,16},{4,20},{8,24},{12,28},{16,0},{20,4},{24,8},{28,12},{1,17},{... | collective-permute-start | bytes 700424 | tf_op jit(solution)/shard_map/ppermute | solution.py:39
  127.7 16.0 %collective-permute-start.49 = (bf16[304,384]{1,0:T(8,128)(2,1)S(1)}, bf16[304,384]{1,0:T(8,128)(2,1)S(1)}, u32[]{:S(2)}, u32[]{:S(2)}) collective-permute-start(bf16[304,384]{1,0:T(8,128)(2,1)S(1)} %get-tuple-element.171), channel_id=1, source_target_pairs={{0,16},{4,20},{8,24},{12,28},{16,0},{20,4},{24,8},{28,12},{1,17},{... | collective-permute-start | bytes 700424 | tf_op jit(solution)/shard_map/ppermute | solution.py:39
  134.9 8.8 %collective-permute-start.46 = (bf16[304,384]{1,0:T(8,128)(2,1)S(1)}, bf16[304,384]{1,0:T(8,128)(2,1)S(1)}, u32[]{:S(2)}, u32[]{:S(2)}) collective-permute-start(bf16[304,384]{1,0:T(8,128)(2,1)S(1)} %add_convert_fusion.3), channel_id=1, source_target_pairs={{0,16},{4,20},{8,24},{12,28},{16,0},{20,4},{24,8},{28,12},{1,17},{... | collective-permute-start | bytes 700424 | tf_op jit(solution)/shard_map/ppermute | solution.py:39
  136.3 7.7 %collective-permute-start.48 = (bf16[304,384]{1,0:T(8,128)(2,1)S(1)}, bf16[304,384]{1,0:T(8,128)(2,1)S(1)}, u32[]{:S(2)}, u32[]{:S(2)}) collective-permute-start(bf16[304,384]{1,0:T(8,128)(2,1)S(1)} %add_convert_fusion.2.refs_6_), channel_id=1, source_target_pairs={{0,8},{4,12},{8,0},{12,4},{16,24},{20,28},{24,16},{28,20},{1,9},{5... | collective-permute-start | bytes 700424 | tf_op jit(solution)/shard_map/ppermute | solution.py:39
  137.4 9.1 %collective-permute-start.47 = (bf16[304,384]{1,0:T(8,128)(2,1)S(1)}, bf16[304,384]{1,0:T(8,128)(2,1)S(1)}, u32[]{:S(2)}, u32[]{:S(2)}) collective-permute-start(bf16[304,384]{1,0:T(8,128)(2,1)S(1)} %get-tuple-element.166), channel_id=1, source_target_pairs={{0,8},{4,12},{8,0},{12,4},{16,24},{20,28},{24,16},{28,20},{1,9},{5... | collective-permute-start | bytes 700424 | tf_op jit(solution)/shard_map/ppermute | solution.py:39
  147.0 10.6 %collective-permute-start.51 = (bf16[160,384]{1,0:T(8,128)(2,1)S(1)}, bf16[160,384]{1,0:T(8,128)(2,1)S(1)}, u32[]{:S(2)}, u32[]{:S(2)}) collective-permute-start(bf16[160,384]{1,0:T(8,128)(2,1)S(1)} %pad_maximum_fusion.5), channel_id=1, source_target_pairs={{0,1},{1,0},{2,3},{3,2},{4,5},{5,4},{6,7},{7,6},{8,9},{9,8},{10,11... | collective-permute-start | bytes 368648 | tf_op jit(solution)/shard_map/ppermute | solution.py:39
  147.9 9.7 %collective-permute-start.53 = (bf16[160,384]{1,0:T(8,128)(2,1)S(1)}, bf16[160,384]{1,0:T(8,128)(2,1)S(1)}, u32[]{:S(2)}, u32[]{:S(2)}) collective-permute-start(bf16[160,384]{1,0:T(8,128)(2,1)S(1)} %pad_maximum_fusion.8), channel_id=1, source_target_pairs={{0,3},{1,2},{2,1},{3,0},{4,7},{5,6},{6,5},{7,4},{8,11},{9,10},{10,... | collective-permute-start | bytes 368648 | tf_op jit(solution)/shard_map/ppermute | solution.py:39
  150.6 10.0 %collective-permute-start.52 = (bf16[160,384]{1,0:T(8,128)(2,1)S(1)}, bf16[160,384]{1,0:T(8,128)(2,1)S(1)}, u32[]{:S(2)}, u32[]{:S(2)}) collective-permute-start(bf16[160,384]{1,0:T(8,128)(2,1)S(1)} %pad_maximum_fusion.7), channel_id=1, source_target_pairs={{0,2},{1,3},{2,0},{3,1},{4,6},{5,7},{6,4},{7,5},{8,10},{9,11},{10,... | collective-permute-start | bytes 368648 | tf_op jit(solution)/shard_map/ppermute | solution.py:39
  160.9 6.1 %collective-permute-start.54 = (bf16[13,13,8,384]{3,2,1,0:T(8,128)(2,1)S(1)}, bf16[13,13,8,384]{3,2,1,0:T(8,128)(2,1)S(1)}, u32[]{:S(2)}, u32[]{:S(2)}) collective-permute-start(bf16[13,13,8,384]{3,2,1,0:T(8,128)(2,1)S(1)} %get-tuple-element.224), channel_id=1, source_target_pairs={{0,4},{4,0},{8,12},{12,8},{16,20},{20,16},{24,28},{28,24},{1,5},{5... | collective-permute-start | bytes 3115016 | tf_op jit(solution)/shard_map/ppermute | solution.py:39
  161.9 8.3 %collective-permute-start.55 = (bf16[160,384]{1,0:T(8,128)(2,1)S(1)}, bf16[160,384]{1,0:T(8,128)(2,1)S(1)}, u32[]{:S(2)}, u32[]{:S(2)}) collective-permute-start(bf16[160,384]{1,0:T(8,128)(2,1)S(1)} %add_convert_fusion.6.refs_0_), channel_id=1, source_target_pairs={{0,1},{1,0},{2,3},{3,2},{4,5},{5,4},{6,7},{7,6},{8,9},{9,8},{10,11... | collective-permute-start | bytes 368648 | tf_op jit(solution)/shard_map/ppermute | solution.py:39
  162.0 12.4 %collective-permute-start.56 = (bf16[160,384]{1,0:T(8,128)(2,1)S(1)}, bf16[160,384]{1,0:T(8,128)(2,1)S(1)}, u32[]{:S(2)}, u32[]{:S(2)}) collective-permute-start(bf16[160,384]{1,0:T(8,128)(2,1)S(1)} %add_convert_fusion.6.refs_0_), channel_id=1, source_target_pairs={{0,2},{1,3},{2,0},{3,1},{4,6},{5,7},{6,4},{7,5},{8,10},{9,11},{10,... | collective-permute-start | bytes 368648 | tf_op jit(solution)/shard_map/ppermute | solution.py:39
  164.8 9.6 %collective-permute-start.57 = (bf16[160,384]{1,0:T(8,128)(2,1)S(1)}, bf16[160,384]{1,0:T(8,128)(2,1)S(1)}, u32[]{:S(2)}, u32[]{:S(2)}) collective-permute-start(bf16[160,384]{1,0:T(8,128)(2,1)S(1)} %add_convert_fusion.6.refs_0_), channel_id=1, source_target_pairs={{0,3},{1,2},{2,1},{3,0},{4,7},{5,6},{6,5},{7,4},{8,11},{9,10},{10,... | collective-permute-start | bytes 368648 | tf_op jit(solution)/shard_map/ppermute | solution.py:39
  (31 other events, 575.9 us)

commit v4 on v3

--- a/solution.py
+++ b/solution.py
@@ -3,6 +3,7 @@
 import jax
 import jax.numpy as jnp
 from jax import lax
+from jax.experimental.layout import Layout, with_layout_constraint
 from jax.experimental import pallas as pl
 from jax.experimental.pallas import tpu as pltpu
 from jax.sharding import PartitionSpec as P
@@ -61,18 +62,17 @@
     return (a.astype(WIDE) + b.astype(WIDE)).astype(LOW)
 
 
-def scatter_chips(parts, chips, early=lambda *pair: pair, later=lambda gate, value: (gate, value)):
+def scatter_chips(parts, chips, early=lambda *values: values, later=lambda gate, *values: values):
     if chips == 4:
         from_x = trade(parts[3][0], "chan", 2)
         from_y = trade(parts[3][1], "chan", 4)
-        first_x = trade(parts[1][0], "chan", 2)
-        second_y = trade(parts[2][1], "chan", 4)
+        first_x, second_y = trade(parts[1][0], "chan", 2), trade(parts[2][1], "chan", 4)
         from_x, from_y = early(from_x, from_y)
         to_y = add_low(parts[2][0], from_x)
         first_y = trade(to_y, "chan", 4)
         to_x = add_low(parts[1][1], from_y)
-        to_x, first_y = later(to_x, first_y)
         second_x = trade(to_x, "chan", 2)
+        first_x, second_y, first_y = later(to_x, first_x, second_y, first_y)
         return (parts[0][0], first_x, first_y), (parts[0][1], second_x, second_y)
     got = [(trade(parts[j][0], "chan", 2 * j), trade(parts[j][1], "chan", 2 * j)) for j in range(1, chips)]
     return (
@@ -93,12 +93,11 @@
     return [parts[0]] + [got[k] for k in range(1, len(parts))]
 
 
-def reduce_planes(first, second):
-    passed = [trade(parts[3], "batch", 1) for parts in (first, second)]
-    near = [trade(parts[1], "batch", 1) for parts in (first, second)]
-    sent = [add_low(parts[2], term) for parts, term in zip((first, second), passed)]
-    far = [trade(value, "batch", 2) for value in sent]
-    return [[parts[0], a, b] for parts, a, b in zip((first, second), near, far)]
+def reduce_planes(*lists):
+    passed = [trade(parts[3], "batch", 1) for parts in lists]
+    near = [trade(parts[1], "batch", 1) for parts in lists]
+    far = [trade(add_low(parts[2], term), "batch", 2) for parts, term in zip(lists, passed)]
+    return [[parts[0], a, b] for parts, a, b in zip(lists, near, far)]
 
 
 def spread_planes(first, second):
@@ -165,17 +164,14 @@
     )(core, *(pltpu.with_memory_space_constraint(value, pltpu.HBM) for value in sources))
 
 
-def fc_prepare(fc_weight, core, gate):
+def fc_prepare(fc_weight, core, which, gate):
     _, rows, units = fc_weight.shape
     width = rows // CELLS
     fc_weight = pltpu.with_memory_space_constraint(fc_weight, pltpu.HBM)
 
-    def kernel(core_ref, own_ref, other_ref, _, keep_ref, give_ref):
-        for source, out in ((own_ref, keep_ref), (other_ref, give_ref)):
-            for cell in range(CELLS):
-                out[pl.ds(cell * width, width), :] = source[
-                    0, pl.ds(cell, width, stride=CELLS), :
-                ].astype(LOW)
+    def kernel(core_ref, source, _, out):
+        for cell in range(CELLS):
+            out[pl.ds(cell * width, width), :] = source[0, pl.ds(cell, width, stride=CELLS), :].astype(LOW)
 
     return pl.pallas_call(
         kernel,
@@ -183,16 +179,15 @@
             num_scalar_prefetch=1,
             grid=(units // LANES,),
             in_specs=[
-                pl.BlockSpec((1, rows, LANES), lambda j, core: (core[0], 0, j)),
-                pl.BlockSpec((1, rows, LANES), lambda j, core: (core[0] ^ 1, 0, j)),
+                pl.BlockSpec((1, rows, LANES), lambda j, core: (core[0] ^ which, 0, j)),
                 pl.BlockSpec(memory_space=pl.ANY),
             ],
-            out_specs=[pl.BlockSpec((rows, LANES), lambda j, core: (0, j))] * 2,
+            out_specs=pl.BlockSpec((rows, LANES), lambda j, core: (0, j)),
         ),
-        out_shape=[like((rows, units), LOW)] * 2,
-        compiler_params=pltpu.CompilerParams(vmem_limit_bytes=12 << 20),
-        cost_estimate=pl.CostEstimate(flops=0, bytes_accessed=6 * fc_weight.size, transcendentals=0),
-    )(core, fc_weight, fc_weight, gate)
+        out_shape=like((rows, units), LOW),
+        compiler_params=pltpu.CompilerParams(vmem_limit_bytes=6 << 20),
+        cost_estimate=pl.CostEstimate(flops=0, bytes_accessed=6 * rows * units, transcendentals=0),
+    )(core, fc_weight, gate)
 
 
 def conv_forward(images, parts, core, chip):
@@ -205,8 +200,8 @@
 
     def kernel(core_ref, chip_ref, x_ref, *refs):
         pieces = refs[:count]
-        pooled_ref, slope_out, small_ref, weights_out = refs[count : count + 4]
-        weights, acc, slope_ref, sems = refs[count + 4 :]
+        pooled_ref, low_ref, slope_out, small_ref, weights_out = refs[count : count + 5]
+        weights, acc, slope_ref, sems = refs[count + 5 :]
         copies = [pltpu.make_async_copy(slope_ref.at[h], slope_out.at[h], sems.at[h]) for h in range(side)]
         copies += [
             pltpu.make_async_copy(
@@ -235,23 +230,34 @@
             copy.start()
         line = side * group
         bias = small_ref[0:1, :]
-        for low, high_row in ((0, (side + 1) // 2), ((side + 1) // 2, side)):
+        def products(low, high_row):
             tall = high_row - low
             windows = [
                 x_ref[tap // 3 + low : tap // 3 + high_row, tap % 3 : tap % 3 + side].reshape(tall * line, width_in)
                 for tap in range(TAPS)
             ]
             acc[low * line : high_row * line, :] = dot(jnp.concatenate(windows, axis=1), weights[...], NT)
-        for h in range(side):
-            value, slope = silu_and_slope(acc[h * line : (h + 1) * line, :] + bias)
-            slope_ref[h] = slope.reshape(side, group, full).astype(LOW)
-            acc[h * line : (h + 1) * line, :] = value
-            copies[h].start()
+
+        def activate(low, high_row):
+            for h in range(low, high_row):
+                value, slope = silu_and_slope(acc[h * line : (h + 1) * line, :] + bias)
+                slope_ref[h] = slope.reshape(side, group, full).astype(LOW)
+                acc[h * line : (h + 1) * line, :] = value
+                copies[h].start()
+
+        blocks = [(low, min(low + 2, side)) for low in range(0, side, 2)]
+        for n, block in enumerate(blocks):
+            products(*block)
+            if n:
+                activate(*blocks[n - 1])
+        activate(*blocks[-1])
         cell = lambda h, w: acc[(h * side + w) * group : (h * side + w + 1) * group, :]
         for r in range(6):
             rows = [cell(2 * r, w) + cell(2 * r + 1, w) + cell(2 * r + 2, w) for w in range(side)]
             for c in range(6):
-                pooled_ref[6 * r + c] = (rows[2 * c] + rows[2 * c + 1] + rows[2 * c + 2]) * (1.0 / 9.0)
+                value = (rows[2 * c] + rows[2 * c + 1] + rows[2 * c + 2]) * (1.0 / 9.0)
+                pooled_ref[6 * r + c] = value
+                low_ref[6 * r + c] = value.astype(LOW)
         for copy in copies:
             copy.wait()
 
@@ -259,9 +265,10 @@
     return pl.pallas_call(
         kernel,
         in_specs=[SCALARS] * 2 + [WHOLE] * (1 + count),
-        out_specs=[WHOLE, pl.BlockSpec(memory_space=pltpu.HBM), WHOLE, pl.BlockSpec(memory_space=pltpu.HBM)],
+        out_specs=[WHOLE, WHOLE, pl.BlockSpec(memory_space=pltpu.HBM), WHOLE, pl.BlockSpec(memory_space=pltpu.HBM)],
         out_shape=[
             like((CELLS, group, full), WIDE),
+            like((CELLS, group, full), LOW),
             pltpu.HBM((side, side, group, full), LOW),
             like((EXTRA, full), WIDE),
             pltpu.HBM((TAPS, full, width_in), LOW),
@@ -294,7 +301,7 @@
         one, two = small_ref[1:2, :], small_ref[2:3, :]
         for start in range(0, cells, per):
             mixed = [
-                one * a_ref[start + i] + two * turn(b_ref[start + i]) for i in range(per)
+                one * a_ref[start + i] + two * turn(b_ref[start + i].astype(WIDE)) for i in range(per)
             ]
             mixed = [jnp.where(first, value, turn(value)) for value in mixed]
             for p in range(planes):
@@ -353,18 +360,18 @@
     )(chip, *gathered, *weights)
 
 
-def fc_backward(grads, crossed, weights, chip, chips, planes):
+def fc_backward(ready, grads, crossed, weights, chip, chips, planes):
     block, units = grads[0].shape
     rows = weights[0].shape[0]
     group = block // chips
     half = planes // 2
     n_images = planes * block
 
-    def kernel(chip_ref, *refs):
+    def kernel(chip_ref, _, *refs):
         pieces, got = refs[:planes], refs[planes]
         own, cross = refs[planes + 1 : planes + 3]
         outs = refs[planes + 3 : planes + 3 + 2 * chips]
-        held_own, held_cross, held = refs[planes + 3 + 2 * chips :]
+        held_own, held_cross, held = refs[planes + 4 + 2 * chips :]
         for k in range(planes):
             held_own[pl.ds(k * block, block), :] = pieces[k][...]
             held_cross[pl.ds(k * block, block), :] = got[k]
@@ -381,9 +388,10 @@
 
     return pl.pallas_call(
         kernel,
-        in_specs=[SCALARS] + [WHOLE] * (planes + 3),
-        out_specs=[WHOLE] * (2 * chips),
-        out_shape=[like((half, group, rows), LOW)] * (2 * chips),
+        in_specs=[SCALARS, pl.BlockSpec(memory_space=pltpu.HBM)] + [WHOLE] * (planes + 3),
+        out_specs=[WHOLE] * (2 * chips) + [pl.BlockSpec(memory_space=pltpu.HBM)],
+        out_shape=[like((half, group, rows), LOW)] * (2 * chips) + [pltpu.HBM(ready.shape, ready.dtype)],
+        input_output_aliases={1: 2 * chips},
         scratch_shapes=[
             pltpu.VMEM((n_images, units), LOW),
             pltpu.VMEM((n_images, units), LOW),
@@ -391,7 +399,7 @@
         ],
         compiler_params=pltpu.CompilerParams(vmem_limit_bytes=20 << 20),
         cost_estimate=BRIEF,
-    )(chip, *grads, crossed, *weights)
+    )(chip, ready, *grads, crossed, *weights)
 
 
 def conv_backward(gate, own, other, pooled, pooled_other, slope, images, small, core, chip, plane):
@@ -440,7 +448,7 @@
                     blocks.append(out)
                 both.append(jnp.concatenate(blocks, axis=1))
             sum_one += both[0] * a_ref[cell]
-            sum_two += both[0] * turn(b_ref[cell])
+            sum_two += both[0] * turn(b_ref[cell].astype(WIDE))
             pool_grad[cell] = one * both[0] + back * both[1]
         sum_bias = jnp.zeros((group, full), WIDE)
         for h in range(side):
@@ -936,23 +944,30 @@
         keep, give, core_at, chip_at, plane_at, core == 0, starts
     )
     mine = lambda a, b: jnp.where(first_core, a, b)
-    keep_y, give_x = trade(keep, "chan", 4), trade(give, "chan", 3)
-    keep_x, give_y = tie(trade(keep, "chan", 2), trade(give, "chan", 5))
-    keep_d, give_d = trade(keep_y, "chan", 2), trade(give_x, "chan", 4)
-    kernel_parts = [keep, swap(give), keep_x, give_x, keep_y, give_y, keep_d, give_d]
-
+    fc_own, fc_give = (fc_prepare(fc_weight, core_at, which, keep) for which in range(2))
+    images, fc_own, fc_give = tie(images, fc_own, fc_give)
+    images = with_layout_constraint(images, Layout(major_to_minor=(0, 2, 3, 1, 4)))
     towers = lax.optimization_barrier(jnp.transpose(images, (1, 2, 3, 0, 4)))
-    keep, give = (jnp.where(first_core, towers[a], towers[1 - a]) for a in range(2))
-    tower_images = jnp.concatenate([keep, swap(give)], axis=2)
+    own_images, given = (jnp.where(first_core, towers[a], towers[1 - a]) for a in range(2))
+    got, keep_y, give_x, keep_x, give_y, own_images, given = tie(
+        swap(give),
+        trade(keep, "chan", 4),
+        trade(give, "chan", 3),
+        trade(keep, "chan", 2),
+        trade(give, "chan", 5),
+        own_images,
+        given,
+    )
+    tower_images = jnp.concatenate([own_images, swap(given)], axis=2)
     tower_images = jnp.pad(tower_images, ((1, 1), (1, 1), (0, 0), (0, 0)))
-
-    fc_own, fc_give = fc_prepare(fc_weight, core_at, keep_x)
-    fc_cross = swap(fc_give)
-
-    pooled, slope, small_all, joined = conv_forward(tower_images, kernel_parts, core_at, chip_at)
-    pooled_other = swap(pooled)
+    keep_d, give_d, tower_images = tie(trade(keep_y, "chan", 2), trade(give_x, "chan", 4), tower_images)
+    kernel_parts = [keep, got, keep_x, give_x, keep_y, give_y, keep_d, give_d]
+
+    pooled, pooled_low, slope, small_all, joined = conv_forward(tower_images, kernel_parts, core_at, chip_at)
+    pooled_other = swap(pooled_low)
     pieces = mix_pieces(pooled, pooled_other, small_all, core_at, plane_at, planes)
     got = exchange_planes(pieces)
+    fc_cross = swap(fc_give)
     gathered = gather_chips(jnp.stack(got[:half]), jnp.stack(got[half:]), chips)
     tower_rows, *partial = fc_forward(
         [part for pair in gathered for part in pair], (fc_own, fc_cross), chip_at, chips, planes
@@ -966,6 +981,7 @@
     mix = [[mine(stitch_fc[a, b], stitch_fc[1 - a, 1 - b]) for b in range(2)] for a in range(2)]
     features = [mix[a][0] * acts[0] + mix[a][1] * acts[1] for a in range(2)]
     features_out = jnp.stack([mine(features[0], features[1]), mine(features[1], features[0])], axis=1)
+    features_out = features_out.astype(LOW)
     masked = [cotangent[:, t].astype(WIDE) * task_mask[:, t].astype(WIDE)[:, None] for t in range(2)]
     out_grad = [mine(masked[a], masked[1 - a]) for a in range(2)]
     grad_low = [(slopes[b] * (mix[0][b] * out_grad[0] + mix[1][b] * out_grad[1])).astype(LOW) for b in range(2)]
@@ -984,13 +1000,13 @@
 
     step = done = None
 
-    def update_own(gate, value):
+    def update_own(gate, first_x, second_y, first_y):
         nonlocal step, done
         *step, done = fc_update(fc_weight, fc_moment, tower_rows, grads_own, core_at, 0, 0, None, gate)
-        value, done = tie(value, done)
-        return gate, value
-
-    blocks = fc_backward(grads_own, grads_cross, (fc_own, fc_cross), chip_at, chips, planes)
+        first_y, done = tie(first_y, done)
+        return first_x, second_y, first_y
+
+    *blocks, features_out = fc_backward(features_out, grads_own, grads_cross, (fc_own, fc_cross), chip_at, chips, planes)
     first, second = scatter_chips(
         [blocks[2 * j : 2 * j + 2] for j in range(chips)], chips, later=update_own
     )
@@ -1016,29 +1032,30 @@
         ).astype(LOW)
 
     kernel = joined.reshape(3, 3, -1, width_in)
-    def update_early(*pair):
+    def update_early(*values):
         nonlocal step, done
         *step, done = fc_update(fc_weight, fc_moment, other_rows, grads_other, core_at, 1, 0, step, blocks[0])
-        *pair, done = tie(*pair, done)
-        return pair
-
-    def update_late(gate, value):
+        *values, done = tie(*values, done)
+        return values
+
+    def update_late(gate, first_x, second_y, first_y):
         nonlocal step, done
+        gate, first_x, second_y = tie(gate, first_x, second_y)
         *step, token = fc_update(fc_weight, fc_moment, other_rows, grads_other, core_at, 1, 1, step, gate)
-        value, done, token = tie(value, done, token)
+        first_y, done, token = tie(first_y, done, token)
         done = done + token
-        return gate, value
-
-    first, second = scatter_chips(
-        [blocks[2 * j : 2 * j + 2] for j in range(chips)], chips, update_early, update_late
+        return first_x, second_y, first_y
+
+    other, own = scatter_chips(
+        [(blocks[2 * j + 1], blocks[2 * j]) for j in range(chips)], chips, update_early, update_late
     )
     lines = TAPS * shard + EXTRA
 
     fill = lambda count: jnp.zeros((count, width_in), LOW)
     spare = planes * PORTION - lines
     flats = (
-        jnp.concatenate([total(first).astype(LOW), packed, fill(spare - packed.shape[0])]),
-        jnp.concatenate([swap(total(second).astype(LOW)), fill(spare)]),
+        jnp.concatenate([total(own).astype(LOW), packed, fill(spare - packed.shape[0])]),
+        jnp.concatenate([swap(total(other).astype(LOW)), fill(spare)]),
     )
     nothing = jnp.uint32(0)
     quarters = [
@@ -1076,7 +1093,7 @@
     params[0], fresh[0] = as_given(params[0]), as_given(fresh[0])
     params[3:3], fresh[3:3] = (step[0], new_fc_bias), (step[1], new_fc_bias_moment)
     images_grad = jnp.transpose(images_grad, (0, 3, 1, 2, 4))
-    return (features_out.astype(LOW), images_grad, *params, *fresh)
+    return (features_out, images_grad, *params, *fresh)
 
 
 def solution(mesh):

time: 176 us -> 172 us (0.977)
  waiting for transfers between devices: 58.2 us -> 53.2 us
  starting transfers between devices: 57.4 us -> 59.2 us
    ppermute x58, waiting for transfers between devices: 58.2 us -> 53.2 us  [trade(): return lax.ppermute(value, axis, [(i, i ^ bit) for i in range(size)])]
    unnamed x44, local copies, waits for them, and re-layouts: 2.76 us -> 0.13 us
    pallas_call x1 -> x2, Pallas kernels: 4.9 us -> 6.88 us  [fc_prepare(): pl.pallas_call(kernel, grid_spec=pltpu.PrefetchScalarGridSpec(num_scalar_...]
  transfers between devices with their start and end apart: 58 -> 58, of which waited for: 30 -> 30; matrix products, arithmetic and copies ran while one was open for 8% -> 8% of each run, Pallas kernels for 21% -> 22%
where the time goes in v4:
time: 172 us
  starting transfers between devices  59.2 us (34%)
  waiting for transfers between devices  53.2 us (31%)
  Pallas kernels  43.7 us (25%)
  matrix products  6.81 us (4%)
  local copies, waits for them, and re-layouts  4.73 us (3%)
  other arithmetic  3.16 us (2%)
    ppermute x58, starting transfers between devices, trade(): return lax.ppermute(value, axis, [(i, i ^ bit) for i in range(size)])  59.2 us
    ppermute x58, waiting for transfers between devices, trade(): return lax.ppermute(value, axis, [(i, i ^ bit) for i in range(size)])  53.2 us
    pallas_call x4, Pallas kernels, fc_update(): pl.pallas_call(kernel, in_specs=[SCALARS] + [WHOLE] * (3 + planes) + [hbm...  16.4 us
    pallas_call x1, Pallas kernels, conv_backward(): pl.pallas_call(kernel, in_specs=[SCALARS] * 3 + [pl.BlockSpec(memory_spac...  7.51 us
    pallas_call x2, Pallas kernels, fc_prepare(): pl.pallas_call(kernel, grid_spec=pltpu.PrefetchScalarGridSpec(num_scalar_...  6.88 us
    conv_general_dilated x1, matrix products, turned_conv(): lax.conv_general_dilated(grad, kernel[::-1, ::-1], (1, 1), 'SAME', dimens...  6.81 us
    pallas_call x1, Pallas kernels, conv_forward(): pl.pallas_call(kernel, in_specs=[SCALARS] * 2 + [WHOLE] * (1 + count), ou...  6.71 us
  transfers between devices with their start and end apart: 58, of which 30 were waited for; matrix products, arithmetic and copies ran while one was open for 8% of the time, Pallas kernels for 22%

profile of v4, /device:TPU:0, one launch (start us, length us, event | category | flops | bytes accessed | tf_op | source)
XLA Modules:
  0.0 172.1 jit_solution(7950396193097756575)
XLA Ops:
  2.5 2.6 %collective-permute-start.2 = (bf16[304,384]{1,0:T(8,128)(2,1)S(1)}, bf16[304,384]{1,0:T(8,128)(2,1)S(1)}, u32[]{:S(2)}, u32[]{:S(2)}) collective-permute-start(bf16[304,384]{1,0:T(8,128)(2,1)S(1)} %get-tuple-element.124), channel_id=1, source_target_pairs={{0,12},{4,8},{8,4},{12,0},{16,28},{20,24},{24,20},{28,16},{1,13},{... | collective-permute-start | bytes 700424 | tf_op jit(solution)/shard_map/ppermute | solution.py:40
  5.1 1.5 collective-permute-start.1
  7.2 3.4 %shard_map.255.refs_8_.refs_5_ = bf16[2304,512]{1,0:T(8,128)(2,1)S(1)} custom-call(s32[1]{0:T(128)} %bitcast.core_ref, f32[2,2304,512]{2,1,0:T(8,128)} %w_ref.7, bf16[304,384]{1,0:T(8,128)(2,1)S(1)} %get-tuple-element.125._.refs_0_), custom_call_target="tpu_custom_call" | custom-call | bytes 7077888 | tf_op jit(solution)/shard_map/pallas_call | solution.py:176
  10.5 3.5 %shard_map.256 = bf16[2304,512]{1,0:T(8,128)(2,1)S(1)} custom-call(s32[1]{0:T(128)} %bitcast.core_ref, f32[2,2304,512]{2,1,0:T(8,128)} %w_ref.7, bf16[304,384]{1,0:T(8,128)(2,1)S(1)} %get-tuple-element.125._.refs_0_), custom_call_target="tpu_custom_call" | custom-call | bytes 7077888 | tf_op jit(solution)/shard_map/pallas_call | solution.py:176
  14.6 1.8 %collective-permute-done.3.refs_2_ = bf16[304,384]{1,0:T(8,128)(2,1)S(1)} collective-permute-done((bf16[304,384]{1,0:T(8,128)(2,1)S(1)}, bf16[304,384]{1,0:T(8,128)(2,1)S(1)}, u32[]{:S(2)}, u32[]{:S(2)}) %collective-permute-start.3) | collective-permute-done | bytes 233504 | tf_op jit(solution)/shard_map/ppermute | solution.py:40
  18.6 1.5 collective-permute-start.6
  21.0 4.7 %collective-permute-done.5.refs_6_ = bf16[304,384]{1,0:T(8,128)(2,1)S(1)} collective-permute-done((bf16[304,384]{1,0:T(8,128)(2,1)S(1)}, bf16[304,384]{1,0:T(8,128)(2,1)S(1)}, u32[]{:S(2)}, u32[]{:S(2)}) %collective-permute-start.5) | collective-permute-done | bytes 233504 | tf_op jit(solution)/shard_map/ppermute | solution.py:40
  26.0 6.7 %shard_map.257 = (f32[36,16,256]{2,1,0:T(8,128)S(1)}, bf16[36,16,256]{2,1,0:T(8,128)(2,1)S(1)}, bf16[13,13,16,256]{3,2,1,0:T(8,128)(2,1)}, f32[16,256]{1,0:T(8,128)S(1)}, bf16[9,256,384]{2,1,0:T(8,128)(2,1)}) custom-call(s32[1]{0:T(128)} %bitcast.core_ref, s32[1]{0:T(128)} %bitcast.3.chip_ref, bf16[15,15,16,384]{3,2,1,0:T(8,128)(2,1)S(1)} %fusion.6.x_ref.refs_8_, ...), custom_call_target="tpu_custom_call" | custom-call | tf_op jit(solution)/shard_map/pallas_call | solution.py:265
  32.8 1.6 collective-permute-done.8.b_ref.refs_6_
  34.6 3.7 %collective-permute-start.11 = (bf16[16,2304]{1,0:T(8,128)(2,1)S(1)}, bf16[16,2304]{1,0:T(8,128)(2,1)S(1)}, u32[]{:S(2)}, u32[]{:S(2)}) collective-permute-start(bf16[16,2304]{1,0:T(8,128)(2,1)S(1)} %get-tuple-element.143), channel_id=1, source_target_pairs={{0,3},{1,2},{2,1},{3,0},{4,7},{5,6},{6,5},{7,4},{8,11},{9,10},{10,... | collective-permute-start | bytes 221192 | tf_op jit(solution)/shard_map/ppermute | solution.py:40
  39.3 2.0 %collective-permute-done.11 = bf16[16,2304]{1,0:T(8,128)(2,1)S(1)} collective-permute-done((bf16[16,2304]{1,0:T(8,128)(2,1)S(1)}, bf16[16,2304]{1,0:T(8,128)(2,1)S(1)}, u32[]{:S(2)}, u32[]{:S(2)}) %collective-permute-start.11) | collective-permute-done | bytes 73760 | tf_op jit(solution)/shard_map/ppermute | solution.py:40
  41.3 3.5 %collective-permute-done.10 = bf16[16,2304]{1,0:T(8,128)(2,1)S(1)} collective-permute-done((bf16[16,2304]{1,0:T(8,128)(2,1)S(1)}, bf16[16,2304]{1,0:T(8,128)(2,1)S(1)}, u32[]{:S(2)}, u32[]{:S(2)}) %collective-permute-start.10) | collective-permute-done | bytes 73760 | tf_op jit(solution)/shard_map/ppermute | solution.py:40
  44.8 1.5 collective-permute-start.13
  46.3 1.6 collective-permute-start.14
  49.1 4.0 %collective-permute-done.14.refs_4_ = bf16[2,16,2304]{2,1,0:T(8,128)(2,1)S(1)} collective-permute-done((bf16[2,16,2304]{2,1,0:T(8,128)(2,1)S(1)}, bf16[2,16,2304]{2,1,0:T(8,128)(2,1)S(1)}, u32[]{:S(2)}, u32[]{:S(2)}) %collective-permute-start.14) | collective-permute-done | bytes 147488 | tf_op jit(solution)/shard_map/ppermute | solution.py:40
  53.0 1.9 %collective-permute-start.17 = (bf16[2,16,2304]{2,1,0:T(8,128)(2,1)S(1)}, bf16[2,16,2304]{2,1,0:T(8,128)(2,1)S(1)}, u32[]{:S(2)}, u32[]{:S(2)}) collective-permute-start(bf16[2,16,2304]{2,1,0:T(8,128)(2,1)S(1)} %collective-permute-done.13.refs_3_), channel_id=1, source_target_pairs={{0,16},{4,20},{8,24},{12,28},{16,0},{20,4},{24,8},{28,12},{1,17},{... | collective-permute-start | bytes 442376 | tf_op jit(solution)/shard_map/ppermute | solution.py:40
  56.1 2.1 %collective-permute-done.16.refs_6_ = bf16[2,16,2304]{2,1,0:T(8,128)(2,1)S(1)} collective-permute-done((bf16[2,16,2304]{2,1,0:T(8,128)(2,1)S(1)}, bf16[2,16,2304]{2,1,0:T(8,128)(2,1)S(1)}, u32[]{:S(2)}, u32[]{:S(2)}) %collective-permute-start.16) | collective-permute-done | bytes 147488 | tf_op jit(solution)/shard_map/ppermute | solution.py:40
  58.2 1.4 shard_map.259
  64.0 2.1 %collective-permute-start.24 = (bf16[64,512]{1,0:T(8,128)(2,1)S(1)}, bf16[64,512]{1,0:T(8,128)(2,1)S(1)}, u32[]{:S(2)}, u32[]{:S(2)}) collective-permute-start(bf16[64,512]{1,0:T(8,128)(2,1)S(1)} %add_convert_fusion.11), channel_id=1, source_target_pairs={{0,2},{1,3},{2,0},{3,1},{4,6},{5,7},{6,4},{7,5},{8,10},{9,11},{10,... | collective-permute-start | bytes 196616 | tf_op jit(solution)/shard_map/ppermute | solution.py:40
  67.5 2.4 %collective-permute-done.24 = bf16[64,512]{1,0:T(8,128)(2,1)S(1)} collective-permute-done((bf16[64,512]{1,0:T(8,128)(2,1)S(1)}, bf16[64,512]{1,0:T(8,128)(2,1)S(1)}, u32[]{:S(2)}, u32[]{:S(2)}) %collective-permute-start.24) | collective-permute-done | bytes 65568 | tf_op jit(solution)/shard_map/ppermute | solution.py:40
  70.0 2.0 %collective-permute-done.21 = bf16[64,512]{1,0:T(8,128)(2,1)S(1)} collective-permute-done((bf16[64,512]{1,0:T(8,128)(2,1)S(1)}, bf16[64,512]{1,0:T(8,128)(2,1)S(1)}, u32[]{:S(2)}, u32[]{:S(2)}) %collective-permute-start.21) | collective-permute-done | bytes 65568 | tf_op jit(solution)/shard_map/ppermute | solution.py:40
  73.1 2.4 %collective-permute-start.30 = (bf16[64,512]{1,0:T(8,128)(2,1)S(1)}, bf16[64,512]{1,0:T(8,128)(2,1)S(1)}, u32[]{:S(2)}, u32[]{:S(2)}) collective-permute-start(bf16[64,512]{1,0:T(8,128)(2,1)S(1)} %get-tuple-element.257.refs_0_), channel_id=1, source_target_pairs={{0,2},{1,3},{2,0},{3,1},{4,6},{5,7},{6,4},{7,5},{8,10},{9,11},{10,... | collective-permute-start | bytes 196616 | tf_op jit(solution)/shard_map/ppermute | solution.py:40
  75.9 2.9 %collective-permute-done.27.refs_2_ = bf16[64,512]{1,0:T(8,128)(2,1)S(1)} collective-permute-done((bf16[64,512]{1,0:T(8,128)(2,1)S(1)}, bf16[64,512]{1,0:T(8,128)(2,1)S(1)}, u32[]{:S(2)}, u32[]{:S(2)}) %collective-permute-start.27) | collective-permute-done | bytes 65568 | tf_op jit(solution)/shard_map/ppermute | solution.py:40
  78.8 2.0 %collective-permute-start.29 = (bf16[64,512]{1,0:T(8,128)(2,1)S(1)}, bf16[64,512]{1,0:T(8,128)(2,1)S(1)}, u32[]{:S(2)}, u32[]{:S(2)}) collective-permute-start(bf16[64,512]{1,0:T(8,128)(2,1)S(1)} %get-tuple-element.257.refs_0_), channel_id=1, source_target_pairs={{0,1},{1,0},{2,3},{3,2},{4,5},{5,4},{6,7},{7,6},{8,9},{9,8},{10,11... | collective-permute-start | bytes 196616 | tf_op jit(solution)/shard_map/ppermute | solution.py:40
  80.9 2.9 %collective-permute-done.29.refs_1_ = bf16[64,512]{1,0:T(8,128)(2,1)S(1)} collective-permute-done((bf16[64,512]{1,0:T(8,128)(2,1)S(1)}, bf16[64,512]{1,0:T(8,128)(2,1)S(1)}, u32[]{:S(2)}, u32[]{:S(2)}) %collective-permute-start.29) | collective-permute-done | bytes 65568 | tf_op jit(solution)/shard_map/ppermute | solution.py:40
  86.7 1.5 shard_map.260
  90.3 1.6 collective-permute-start.36
  92.4 2.6 %collective-permute-done.34 = bf16[2,16,2304]{2,1,0:T(8,128)(2,1)S(1)} collective-permute-done((bf16[2,16,2304]{2,1,0:T(8,128)(2,1)S(1)}, bf16[2,16,2304]{2,1,0:T(8,128)(2,1)S(1)}, u32[]{:S(2)}, u32[]{:S(2)}) %collective-permute-start.34) | collective-permute-done | bytes 147488 | tf_op jit(solution)/shard_map/ppermute | solution.py:40
  95.0 1.6 collective-permute-start.35
  98.4 4.1 %shard_map.261 = (f32[2,2304,512]{2,1,0:T(8,128)}, f32[2,2304,512]{2,1,0:T(8,128)}, f32[8,128]{1,0:T(8,128)S(1)}) custom-call(s32[1]{0:T(128)} %bitcast.core_ref, f32[2,2304,512]{2,1,0:T(8,128)S(1)} %bitcast.86, f32[2,2304,512]{2,1,0:T(8,128)S(1)} %bitcast.88, bf16[256,2304]{1,0:T(8,128)(2,1)S(1)} %get-tuple-element.160.rows_ref, ...), custom_call_target="tpu_custom_call" | custom-call | bytes 9437184 | tf_op jit(solution)/shard_map/pallas_call | solution.py:552
  102.7 1.3 collective-permute-start.37
  104.1 2.3 %collective-permute-start.40 = (bf16[16,2304]{1,0:T(8,128)(2,1)S(1)}, bf16[16,2304]{1,0:T(8,128)(2,1)S(1)}, u32[]{:S(2)}, u32[]{:S(2)}) collective-permute-start(bf16[16,2304]{1,0:T(8,128)(2,1)S(1)} %get-tuple-element.242), channel_id=1, source_target_pairs={{0,2},{1,3},{2,0},{3,1},{4,6},{5,7},{6,4},{7,5},{8,10},{9,11},{10,... | collective-permute-start | bytes 221192 | tf_op jit(solution)/shard_map/ppermute | solution.py:40
  107.5 4.0 %shard_map.262 = (f32[2,2304,512]{2,1,0:T(8,128)}, f32[2,2304,512]{2,1,0:T(8,128)}, f32[8,128]{1,0:T(8,128)S(1)}) custom-call(s32[1]{0:T(128)} %bitcast.core_ref, f32[2,2304,512]{2,1,0:T(8,128)S(1)} %bitcast.86, f32[2,2304,512]{2,1,0:T(8,128)S(1)} %bitcast.88, ...), custom_call_target="tpu_custom_call", output_to_operand_aliasing={{0}: (8, {}), {1}: (9, {})} | custom-call | bytes 9437184 | tf_op jit(solution)/shard_map/pallas_call | solution.py:552
  112.8 1.6 collective-permute-done.42.refs_4_
  114.3 7.5 %shard_map.263 = (bf16[304,384]{1,0:T(8,128)(2,1)S(1)}, bf16[304,384]{1,0:T(8,128)(2,1)S(1)}, bf16[304,384]{1,0:T(8,128)(2,1)S(1)}, bf16[304,384]{1,0:T(8,128)(2...) custom-call(s32[1]{0:T(128)} %bitcast.core_ref, ...), custom_call_target="tpu_custom_call" | custom-call | tf_op jit(solution)/shard_map/pallas_call | solution.py:492
  121.8 1.4 collective-permute-start.43
  126.2 4.0 %shard_map.264 = (f32[2,2304,512]{2,1,0:T(8,128)}, f32[2,2304,512]{2,1,0:T(8,128)}, f32[8,128]{1,0:T(8,128)S(1)}) custom-call(s32[1]{0:T(128)} %bitcast.core_ref, f32[2,2304,512]{2,1,0:T(8,128)S(1)} %bitcast.86, f32[2,2304,512]{2,1,0:T(8,128)S(1)} %bitcast.88, ...), custom_call_target="tpu_custom_call", output_to_operand_aliasing={{0}: (8, {}), {1}: (9, {})} | custom-call | bytes 9437184 | tf_op jit(solution)/shard_map/pallas_call | solution.py:552
  130.4 1.4 collective-permute-done.44
  135.4 1.4 collective-permute-done.48
  136.9 4.3 %shard_map.265 = (f32[2,2304,512]{2,1,0:T(8,128)}, f32[2,2304,512]{2,1,0:T(8,128)}, f32[8,128]{1,0:T(8,128)S(1)}) custom-call(s32[1]{0:T(128)} %bitcast.core_ref, f32[2,2304,512]{2,1,0:T(8,128)S(1)} %bitcast.86, f32[2,2304,512]{2,1,0:T(8,128)S(1)} %bitcast.88, ...), custom_call_target="tpu_custom_call", output_to_operand_aliasing={{0}: (8, {}), {1}: (9, {})} | custom-call | bytes 9437184 | tf_op jit(solution)/shard_map/pallas_call | solution.py:552
  144.1 2.4 %collective-permute-start.53 = (bf16[160,384]{1,0:T(8,128)(2,1)S(1)}, bf16[160,384]{1,0:T(8,128)(2,1)S(1)}, u32[]{:S(2)}, u32[]{:S(2)}) collective-permute-start(bf16[160,384]{1,0:T(8,128)(2,1)S(1)} %pad_maximum_fusion.8), channel_id=1, source_target_pairs={{0,3},{1,2},{2,1},{3,0},{4,7},{5,6},{6,5},{7,4},{8,11},{9,10},{10,... | collective-permute-start | bytes 368648 | tf_op jit(solution)/shard_map/ppermute | solution.py:40
  146.7 6.8 %convolution_convert_fusion = bf16[13,13,16,384]{3,2,1,0:T(8,128)(2,1)S(1)} fusion(bf16[13,13,16,256]{3,2,1,0:T(8,128)(2,1)S(1)} %copy-done.15, bf16[3,3,256,384]{3,2,1,0:T(8,128)(2,1)S(1)} %bitcast.125), kind=kOutput, calls=%fused_computation.14 | convolution fusion | flops 4307539968 | bytes 5230592 | tf_op jit(solution)/shard_map/conv_general_dilated | solution.py:1025
  153.5 4.0 %collective-permute-done.52 = bf16[160,384]{1,0:T(8,128)(2,1)S(1)} collective-permute-done((bf16[160,384]{1,0:T(8,128)(2,1)S(1)}, bf16[160,384]{1,0:T(8,128)(2,1)S(1)}, u32[]{:S(2)}, u32[]{:S(2)}) %collective-permute-start.52) | collective-permute-done | bytes 122912 | tf_op jit(solution)/shard_map/ppermute | solution.py:40
  158.2 2.6 %collective-permute-start.56 = (bf16[160,384]{1,0:T(8,128)(2,1)S(1)}, bf16[160,384]{1,0:T(8,128)(2,1)S(1)}, u32[]{:S(2)}, u32[]{:S(2)}) collective-permute-start(bf16[160,384]{1,0:T(8,128)(2,1)S(1)} %add_convert_fusion.6.refs_0_), channel_id=1, source_target_pairs={{0,2},{1,3},{2,0},{3,1},{4,6},{5,7},{6,4},{7,5},{8,10},{9,11},{10,... | collective-permute-start | bytes 368648 | tf_op jit(solution)/shard_map/ppermute | solution.py:40
  160.7 1.8 %collective-permute-start.57 = (bf16[160,384]{1,0:T(8,128)(2,1)S(1)}, bf16[160,384]{1,0:T(8,128)(2,1)S(1)}, u32[]{:S(2)}, u32[]{:S(2)}) collective-permute-start(bf16[160,384]{1,0:T(8,128)(2,1)S(1)} %add_convert_fusion.6.refs_0_), channel_id=1, source_target_pairs={{0,3},{1,2},{2,1},{3,0},{4,7},{5,6},{6,5},{7,4},{8,11},{9,10},{10,... | collective-permute-start | bytes 368648 | tf_op jit(solution)/shard_map/ppermute | solution.py:40
  163.4 2.9 %copy.60 = bf16[2,13,13,8,384]{4,0,2,1,3:T(2,128)(2,1)} copy(bf16[2,13,13,8,384]{4,3,2,1,0:T(8,128)(2,1)S(1)} %shard_map.266) | data formatting | bytes 4153344 | tf_op jit(solution)/shard_map/pallas_call | solution.py:575
  166.3 4.2 %collective-permute-done.56.refs_2_ = bf16[160,384]{1,0:T(8,128)(2,1)S(1)} collective-permute-done((bf16[160,384]{1,0:T(8,128)(2,1)S(1)}, bf16[160,384]{1,0:T(8,128)(2,1)S(1)}, u32[]{:S(2)}, u32[]{:S(2)}) %collective-permute-start.56) | collective-permute-done | bytes 122912 | tf_op jit(solution)/shard_map/ppermute | solution.py:40
  170.6 1.5 shard_map.267
  (182 shorter events, 38.0 us)
Async XLA Ops:
  2.0 12.6 %collective-permute-start = (bf16[304,384]{1,0:T(8,128)(2,1)S(1)}, bf16[304,384]{1,0:T(8,128)(2,1)S(1)}, u32[]{:S(2)}, u32[]{:S(2)}) collective-permute-start(bf16[304,384]{1,0:T(8,128)(2,1)S(1)} %get-tuple-element.124), channel_id=1, source_target_pairs={{0,4},{4,0},{8,12},{12,8},{16,20},{20,16},{24,28},{28,24},{1,5},{5... | collective-permute-start | bytes 700424 | tf_op jit(solution)/shard_map/ppermute | solution.py:40
  2.5 12.1 %collective-permute-start.2 = (bf16[304,384]{1,0:T(8,128)(2,1)S(1)}, bf16[304,384]{1,0:T(8,128)(2,1)S(1)}, u32[]{:S(2)}, u32[]{:S(2)}) collective-permute-start(bf16[304,384]{1,0:T(8,128)(2,1)S(1)} %get-tuple-element.124), channel_id=1, source_target_pairs={{0,12},{4,8},{8,4},{12,0},{16,28},{20,24},{24,20},{28,16},{1,13},{... | collective-permute-start | bytes 700424 | tf_op jit(solution)/shard_map/ppermute | solution.py:40
  5.1 9.5 %collective-permute-start.1 = (bf16[304,384]{1,0:T(8,128)(2,1)S(1)}, bf16[304,384]{1,0:T(8,128)(2,1)S(1)}, u32[]{:S(2)}, u32[]{:S(2)}) collective-permute-start(bf16[304,384]{1,0:T(8,128)(2,1)S(1)} %get-tuple-element.125._.refs_0_), channel_id=1, source_target_pairs={{0,16},{4,20},{8,24},{12,28},{16,0},{20,4},{24,8},{28,12},{1,17},{... | collective-permute-start | bytes 700424 | tf_op jit(solution)/shard_map/ppermute | solution.py:40
  6.6 9.7 %collective-permute-start.3 = (bf16[304,384]{1,0:T(8,128)(2,1)S(1)}, bf16[304,384]{1,0:T(8,128)(2,1)S(1)}, u32[]{:S(2)}, u32[]{:S(2)}) collective-permute-start(bf16[304,384]{1,0:T(8,128)(2,1)S(1)} %get-tuple-element.125._.refs_0_), channel_id=1, source_target_pairs={{0,8},{4,12},{8,0},{12,4},{16,24},{20,28},{24,16},{28,20},{1,9},{5... | collective-permute-start | bytes 700424 | tf_op jit(solution)/shard_map/ppermute | solution.py:40
  7.2 9.7 %collective-permute-start.4 = (bf16[304,384]{1,0:T(8,128)(2,1)S(1)}, bf16[304,384]{1,0:T(8,128)(2,1)S(1)}, u32[]{:S(2)}, u32[]{:S(2)}) collective-permute-start(bf16[304,384]{1,0:T(8,128)(2,1)S(1)} %get-tuple-element.124), channel_id=1, source_target_pairs={{0,20},{4,16},{8,28},{12,24},{16,4},{20,0},{24,12},{28,8},{1,21},{... | collective-permute-start | bytes 700424 | tf_op jit(solution)/shard_map/ppermute | solution.py:40
  17.6 40.6 %collective-permute-start.18 = (bf16[2304,512]{1,0:T(8,128)(2,1)S(1)}, bf16[2304,512]{1,0:T(8,128)(2,1)S(1)}, u32[]{:S(2)}, u32[]{:S(2)}) collective-permute-start(bf16[2304,512]{1,0:T(8,128)(2,1)S(1)} %shard_map.256), channel_id=1, source_target_pairs={{0,4},{4,0},{8,12},{12,8},{16,20},{20,16},{24,28},{28,24},{1,5},{5... | collective-permute-start | bytes 7077896 | tf_op jit(solution)/shard_map/ppermute | solution.py:40
  17.6 8.1 %collective-permute-start.5 = (bf16[304,384]{1,0:T(8,128)(2,1)S(1)}, bf16[304,384]{1,0:T(8,128)(2,1)S(1)}, u32[]{:S(2)}, u32[]{:S(2)}) collective-permute-start(bf16[304,384]{1,0:T(8,128)(2,1)S(1)} %collective-permute-done.1.refs_4_), channel_id=1, source_target_pairs={{0,8},{4,12},{8,0},{12,4},{16,24},{20,28},{24,16},{28,20},{1,9},{5... | collective-permute-start | bytes 700424 | tf_op jit(solution)/shard_map/ppermute | solution.py:40
  18.6 7.4 %collective-permute-start.6 = (bf16[304,384]{1,0:T(8,128)(2,1)S(1)}, bf16[304,384]{1,0:T(8,128)(2,1)S(1)}, u32[]{:S(2)}, u32[]{:S(2)}) collective-permute-start(bf16[304,384]{1,0:T(8,128)(2,1)S(1)} %collective-permute-done.2.refs_3_), channel_id=1, source_target_pairs={{0,16},{4,20},{8,24},{12,28},{16,0},{20,4},{24,8},{28,12},{1,17},{... | collective-permute-start | bytes 700424 | tf_op jit(solution)/shard_map/ppermute | solution.py:40
  34.6 6.7 %collective-permute-start.11 = (bf16[16,2304]{1,0:T(8,128)(2,1)S(1)}, bf16[16,2304]{1,0:T(8,128)(2,1)S(1)}, u32[]{:S(2)}, u32[]{:S(2)}) collective-permute-start(bf16[16,2304]{1,0:T(8,128)(2,1)S(1)} %get-tuple-element.143), channel_id=1, source_target_pairs={{0,3},{1,2},{2,1},{3,0},{4,7},{5,6},{6,5},{7,4},{8,11},{9,10},{10,... | collective-permute-start | bytes 221192 | tf_op jit(solution)/shard_map/ppermute | solution.py:40
  38.2 6.5 %collective-permute-start.10 = (bf16[16,2304]{1,0:T(8,128)(2,1)S(1)}, bf16[16,2304]{1,0:T(8,128)(2,1)S(1)}, u32[]{:S(2)}, u32[]{:S(2)}) collective-permute-start(bf16[16,2304]{1,0:T(8,128)(2,1)S(1)} %get-tuple-element.142), channel_id=1, source_target_pairs={{0,2},{1,3},{2,0},{3,1},{4,6},{5,7},{6,4},{7,5},{8,10},{9,11},{10,... | collective-permute-start | bytes 221192 | tf_op jit(solution)/shard_map/ppermute | solution.py:40
  38.4 7.8 %collective-permute-start.9 = (bf16[16,2304]{1,0:T(8,128)(2,1)S(1)}, bf16[16,2304]{1,0:T(8,128)(2,1)S(1)}, u32[]{:S(2)}, u32[]{:S(2)}) collective-permute-start(bf16[16,2304]{1,0:T(8,128)(2,1)S(1)} %get-tuple-element.141), channel_id=1, source_target_pairs={{0,1},{1,0},{2,3},{3,2},{4,5},{5,4},{6,7},{7,6},{8,9},{9,8},{10,11... | collective-permute-start | bytes 221192 | tf_op jit(solution)/shard_map/ppermute | solution.py:40
  44.8 8.3 %collective-permute-start.13 = (bf16[2,16,2304]{2,1,0:T(8,128)(2,1)S(1)}, bf16[2,16,2304]{2,1,0:T(8,128)(2,1)S(1)}, u32[]{:S(2)}, u32[]{:S(2)}) collective-permute-start(bf16[2,16,2304]{2,1,0:T(8,128)(2,1)S(1)} %pad_maximum_fusion.3.refs_1_), channel_id=1, source_target_pairs={{0,8},{4,12},{8,0},{12,4},{16,24},{20,28},{24,16},{28,20},{1,9},{5... | collective-permute-start | bytes 442376 | tf_op jit(solution)/shard_map/ppermute | solution.py:40
  46.3 6.7 %collective-permute-start.14 = (bf16[2,16,2304]{2,1,0:T(8,128)(2,1)S(1)}, bf16[2,16,2304]{2,1,0:T(8,128)(2,1)S(1)}, u32[]{:S(2)}, u32[]{:S(2)}) collective-permute-start(bf16[2,16,2304]{2,1,0:T(8,128)(2,1)S(1)} %pad_maximum_fusion.2.refs_0_), channel_id=1, source_target_pairs={{0,16},{4,20},{8,24},{12,28},{16,0},{20,4},{24,8},{28,12},{1,17},{... | collective-permute-start | bytes 442376 | tf_op jit(solution)/shard_map/ppermute | solution.py:40
  47.9 7.1 %collective-permute-start.12 = (bf16[2,16,2304]{2,1,0:T(8,128)(2,1)S(1)}, bf16[2,16,2304]{2,1,0:T(8,128)(2,1)S(1)}, u32[]{:S(2)}, u32[]{:S(2)}) collective-permute-start(bf16[2,16,2304]{2,1,0:T(8,128)(2,1)S(1)} %pad_maximum_fusion.2.refs_0_), channel_id=1, source_target_pairs={{0,8},{4,12},{8,0},{12,4},{16,24},{20,28},{24,16},{28,20},{1,9},{5... | collective-permute-start | bytes 442376 | tf_op jit(solution)/shard_map/ppermute | solution.py:40
  48.5 7.5 %collective-permute-start.15 = (bf16[2,16,2304]{2,1,0:T(8,128)(2,1)S(1)}, bf16[2,16,2304]{2,1,0:T(8,128)(2,1)S(1)}, u32[]{:S(2)}, u32[]{:S(2)}) collective-permute-start(bf16[2,16,2304]{2,1,0:T(8,128)(2,1)S(1)} %pad_maximum_fusion.3.refs_1_), channel_id=1, source_target_pairs={{0,16},{4,20},{8,24},{12,28},{16,0},{20,4},{24,8},{28,12},{1,17},{... | collective-permute-start | bytes 442376 | tf_op jit(solution)/shard_map/ppermute | solution.py:40
  53.0 5.1 %collective-permute-start.16 = (bf16[2,16,2304]{2,1,0:T(8,128)(2,1)S(1)}, bf16[2,16,2304]{2,1,0:T(8,128)(2,1)S(1)}, u32[]{:S(2)}, u32[]{:S(2)}) collective-permute-start(bf16[2,16,2304]{2,1,0:T(8,128)(2,1)S(1)} %collective-permute-done.14.refs_4_), channel_id=1, source_target_pairs={{0,8},{4,12},{8,0},{12,4},{16,24},{20,28},{24,16},{28,20},{1,9},{5... | collective-permute-start | bytes 442376 | tf_op jit(solution)/shard_map/ppermute | solution.py:40
  53.0 5.1 %collective-permute-start.17 = (bf16[2,16,2304]{2,1,0:T(8,128)(2,1)S(1)}, bf16[2,16,2304]{2,1,0:T(8,128)(2,1)S(1)}, u32[]{:S(2)}, u32[]{:S(2)}) collective-permute-start(bf16[2,16,2304]{2,1,0:T(8,128)(2,1)S(1)} %collective-permute-done.13.refs_3_), channel_id=1, source_target_pairs={{0,16},{4,20},{8,24},{12,28},{16,0},{20,4},{24,8},{28,12},{1,17},{... | collective-permute-start | bytes 442376 | tf_op jit(solution)/shard_map/ppermute | solution.py:40
  60.5 5.7 %collective-permute-start.20 = (bf16[64,512]{1,0:T(8,128)(2,1)S(1)}, bf16[64,512]{1,0:T(8,128)(2,1)S(1)}, u32[]{:S(2)}, u32[]{:S(2)}) collective-permute-start(bf16[64,512]{1,0:T(8,128)(2,1)S(1)} %get-tuple-element.149), channel_id=1, source_target_pairs={{0,1},{1,0},{2,3},{3,2},{4,5},{5,4},{6,7},{7,6},{8,9},{9,8},{10,11... | collective-permute-start | bytes 196616 | tf_op jit(solution)/shard_map/ppermute | solution.py:40
  61.7 8.3 %collective-permute-start.19 = (bf16[64,512]{1,0:T(8,128)(2,1)S(1)}, bf16[64,512]{1,0:T(8,128)(2,1)S(1)}, u32[]{:S(2)}, u32[]{:S(2)}) collective-permute-start(bf16[64,512]{1,0:T(8,128)(2,1)S(1)} %get-tuple-element.147), channel_id=1, source_target_pairs={{0,1},{1,0},{2,3},{3,2},{4,5},{5,4},{6,7},{7,6},{8,9},{9,8},{10,11... | collective-permute-start | bytes 196616 | tf_op jit(solution)/shard_map/ppermute | solution.py:40
  64.0 5.9 %collective-permute-start.24 = (bf16[64,512]{1,0:T(8,128)(2,1)S(1)}, bf16[64,512]{1,0:T(8,128)(2,1)S(1)}, u32[]{:S(2)}, u32[]{:S(2)}) collective-permute-start(bf16[64,512]{1,0:T(8,128)(2,1)S(1)} %add_convert_fusion.11), channel_id=1, source_target_pairs={{0,2},{1,3},{2,0},{3,1},{4,6},{5,7},{6,4},{7,5},{8,10},{9,11},{10,... | collective-permute-start | bytes 196616 | tf_op jit(solution)/shard_map/ppermute | solution.py:40
  66.2 5.9 %collective-permute-start.21 = (bf16[64,512]{1,0:T(8,128)(2,1)S(1)}, bf16[64,512]{1,0:T(8,128)(2,1)S(1)}, u32[]{:S(2)}, u32[]{:S(2)}) collective-permute-start(bf16[64,512]{1,0:T(8,128)(2,1)S(1)} %add_convert_fusion.12), channel_id=1, source_target_pairs={{0,2},{1,3},{2,0},{3,1},{4,6},{5,7},{6,4},{7,5},{8,10},{9,11},{10,... | collective-permute-start | bytes 196616 | tf_op jit(solution)/shard_map/ppermute | solution.py:40
  72.2 6.5 %collective-permute-start.27 = (bf16[64,512]{1,0:T(8,128)(2,1)S(1)}, bf16[64,512]{1,0:T(8,128)(2,1)S(1)}, u32[]{:S(2)}, u32[]{:S(2)}) collective-permute-start(bf16[64,512]{1,0:T(8,128)(2,1)S(1)} %get-tuple-element.232.refs_0_), channel_id=1, source_target_pairs={{0,2},{1,3},{2,0},{3,1},{4,6},{5,7},{6,4},{7,5},{8,10},{9,11},{10,... | collective-permute-start | bytes 196616 | tf_op jit(solution)/shard_map/ppermute | solution.py:40
  73.1 7.7 %collective-permute-start.30 = (bf16[64,512]{1,0:T(8,128)(2,1)S(1)}, bf16[64,512]{1,0:T(8,128)(2,1)S(1)}, u32[]{:S(2)}, u32[]{:S(2)}) collective-permute-start(bf16[64,512]{1,0:T(8,128)(2,1)S(1)} %get-tuple-element.257.refs_0_), channel_id=1, source_target_pairs={{0,2},{1,3},{2,0},{3,1},{4,6},{5,7},{6,4},{7,5},{8,10},{9,11},{10,... | collective-permute-start | bytes 196616 | tf_op jit(solution)/shard_map/ppermute | solution.py:40
  75.5 10.6 %collective-permute-start.26 = (bf16[64,512]{1,0:T(8,128)(2,1)S(1)}, bf16[64,512]{1,0:T(8,128)(2,1)S(1)}, u32[]{:S(2)}, u32[]{:S(2)}) collective-permute-start(bf16[64,512]{1,0:T(8,128)(2,1)S(1)} %get-tuple-element.232.refs_0_), channel_id=1, source_target_pairs={{0,1},{1,0},{2,3},{3,2},{4,5},{5,4},{6,7},{7,6},{8,9},{9,8},{10,11... | collective-permute-start | bytes 196616 | tf_op jit(solution)/shard_map/ppermute | solution.py:40
  78.8 7.3 %collective-permute-start.28 = (bf16[64,512]{1,0:T(8,128)(2,1)S(1)}, bf16[64,512]{1,0:T(8,128)(2,1)S(1)}, u32[]{:S(2)}, u32[]{:S(2)}) collective-permute-start(bf16[64,512]{1,0:T(8,128)(2,1)S(1)} %collective-permute-done.27.refs_2_), channel_id=1, source_target_pairs={{0,1},{1,0},{2,3},{3,2},{4,5},{5,4},{6,7},{7,6},{8,9},{9,8},{10,11... | collective-permute-start | bytes 196616 | tf_op jit(solution)/shard_map/ppermute | solution.py:40
  88.2 6.8 %collective-permute-start.34 = (bf16[2,16,2304]{2,1,0:T(8,128)(2,1)S(1)}, bf16[2,16,2304]{2,1,0:T(8,128)(2,1)S(1)}, u32[]{:S(2)}, u32[]{:S(2)}) collective-permute-start(bf16[2,16,2304]{2,1,0:T(8,128)(2,1)S(1)} %get-tuple-element.159), channel_id=1, source_target_pairs={{0,8},{4,12},{8,0},{12,4},{16,24},{20,28},{24,16},{28,20},{1,9},{5... | collective-permute-start | bytes 442376 | tf_op jit(solution)/shard_map/ppermute | solution.py:40
  89.5 36.6 %collective-permute-start.45 = (bf16[256,2304]{1,0:T(8,128)(2,1)S(1)}, bf16[256,2304]{1,0:T(8,128)(2,1)S(1)}, u32[]{:S(2)}, u32[]{:S(2)}) collective-permute-start(bf16[256,2304]{1,0:T(8,128)(2,1)S(1)} %get-tuple-element.160.rows_ref), channel_id=1, source_target_pairs={{0,4},{4,0},{8,12},{12,8},{16,20},{20,16},{24,28},{28,24},{1,5},{5... | collective-permute-start | bytes 3538952 | tf_op jit(solution)/shard_map/ppermute | solution.py:40
  89.5 13.1 %collective-permute-start.33 = (bf16[2,16,2304]{2,1,0:T(8,128)(2,1)S(1)}, bf16[2,16,2304]{2,1,0:T(8,128)(2,1)S(1)}, u32[]{:S(2)}, u32[]{:S(2)}) collective-permute-start(bf16[2,16,2304]{2,1,0:T(8,128)(2,1)S(1)} %get-tuple-element.157), channel_id=1, source_target_pairs={{0,8},{4,12},{8,0},{12,4},{16,24},{20,28},{24,16},{28,20},{1,9},{5... | collective-permute-start | bytes 442376 | tf_op jit(solution)/shard_map/ppermute | solution.py:40
  90.3 6.7 %collective-permute-start.36 = (bf16[2,16,2304]{2,1,0:T(8,128)(2,1)S(1)}, bf16[2,16,2304]{2,1,0:T(8,128)(2,1)S(1)}, u32[]{:S(2)}, u32[]{:S(2)}) collective-permute-start(bf16[2,16,2304]{2,1,0:T(8,128)(2,1)S(1)} %get-tuple-element.162), channel_id=1, source_target_pairs={{0,16},{4,20},{8,24},{12,28},{16,0},{20,4},{24,8},{28,12},{1,17},{... | collective-permute-start | bytes 442376 | tf_op jit(solution)/shard_map/ppermute | solution.py:40
  91.9 12.1 %collective-permute-start.39 = (bf16[2,16,2304]{2,1,0:T(8,128)(2,1)S(1)}, bf16[2,16,2304]{2,1,0:T(8,128)(2,1)S(1)}, u32[]{:S(2)}, u32[]{:S(2)}) collective-permute-start(bf16[2,16,2304]{2,1,0:T(8,128)(2,1)S(1)} %get-tuple-element.169), channel_id=1, source_target_pairs={{0,16},{4,20},{8,24},{12,28},{16,0},{20,4},{24,8},{28,12},{1,17},{... | collective-permute-start | bytes 442376 | tf_op jit(solution)/shard_map/ppermute | solution.py:40
  95.0 7.6 %collective-permute-start.35 = (bf16[2,16,2304]{2,1,0:T(8,128)(2,1)S(1)}, bf16[2,16,2304]{2,1,0:T(8,128)(2,1)S(1)}, u32[]{:S(2)}, u32[]{:S(2)}) collective-permute-start(bf16[2,16,2304]{2,1,0:T(8,128)(2,1)S(1)} %add_convert_fusion.5), channel_id=1, source_target_pairs={{0,16},{4,20},{8,24},{12,28},{16,0},{20,4},{24,8},{28,12},{1,17},{... | collective-permute-start | bytes 442376 | tf_op jit(solution)/shard_map/ppermute | solution.py:40
  97.0 7.0 %collective-permute-start.38 = (bf16[2,16,2304]{2,1,0:T(8,128)(2,1)S(1)}, bf16[2,16,2304]{2,1,0:T(8,128)(2,1)S(1)}, u32[]{:S(2)}, u32[]{:S(2)}) collective-permute-start(bf16[2,16,2304]{2,1,0:T(8,128)(2,1)S(1)} %add_convert_fusion.4.refs_4_), channel_id=1, source_target_pairs={{0,8},{4,12},{8,0},{12,4},{16,24},{20,28},{24,16},{28,20},{1,9},{5... | collective-permute-start | bytes 442376 | tf_op jit(solution)/shard_map/ppermute | solution.py:40
  102.7 8.8 %collective-permute-start.37 = (bf16[16,2304]{1,0:T(8,128)(2,1)S(1)}, bf16[16,2304]{1,0:T(8,128)(2,1)S(1)}, u32[]{:S(2)}, u32[]{:S(2)}) collective-permute-start(bf16[16,2304]{1,0:T(8,128)(2,1)S(1)} %get-tuple-element.245), channel_id=1, source_target_pairs={{0,1},{1,0},{2,3},{3,2},{4,5},{5,4},{6,7},{7,6},{8,9},{9,8},{10,11... | collective-permute-start | bytes 221192 | tf_op jit(solution)/shard_map/ppermute | solution.py:40
  104.1 7.4 %collective-permute-start.40 = (bf16[16,2304]{1,0:T(8,128)(2,1)S(1)}, bf16[16,2304]{1,0:T(8,128)(2,1)S(1)}, u32[]{:S(2)}, u32[]{:S(2)}) collective-permute-start(bf16[16,2304]{1,0:T(8,128)(2,1)S(1)} %get-tuple-element.242), channel_id=1, source_target_pairs={{0,2},{1,3},{2,0},{3,1},{4,6},{5,7},{6,4},{7,5},{8,10},{9,11},{10,... | collective-permute-start | bytes 221192 | tf_op jit(solution)/shard_map/ppermute | solution.py:40
  106.4 6.3 %collective-permute-start.41 = (bf16[16,2304]{1,0:T(8,128)(2,1)S(1)}, bf16[16,2304]{1,0:T(8,128)(2,1)S(1)}, u32[]{:S(2)}, u32[]{:S(2)}) collective-permute-start(bf16[16,2304]{1,0:T(8,128)(2,1)S(1)} %get-tuple-element.243.refs_6_), channel_id=1, source_target_pairs={{0,3},{1,2},{2,1},{3,0},{4,7},{5,6},{6,5},{7,4},{8,11},{9,10},{10,... | collective-permute-start | bytes 221192 | tf_op jit(solution)/shard_map/ppermute | solution.py:40
  121.8 8.6 %collective-permute-start.43 = (bf16[304,384]{1,0:T(8,128)(2,1)S(1)}, bf16[304,384]{1,0:T(8,128)(2,1)S(1)}, u32[]{:S(2)}, u32[]{:S(2)}) collective-permute-start(bf16[304,384]{1,0:T(8,128)(2,1)S(1)} %get-tuple-element.176), channel_id=1, source_target_pairs={{0,8},{4,12},{8,0},{12,4},{16,24},{20,28},{24,16},{28,20},{1,9},{5... | collective-permute-start | bytes 700424 | tf_op jit(solution)/shard_map/ppermute | solution.py:40
  123.3 8.6 %collective-permute-start.44 = (bf16[304,384]{1,0:T(8,128)(2,1)S(1)}, bf16[304,384]{1,0:T(8,128)(2,1)S(1)}, u32[]{:S(2)}, u32[]{:S(2)}) collective-permute-start(bf16[304,384]{1,0:T(8,128)(2,1)S(1)} %get-tuple-element.177), channel_id=1, source_target_pairs={{0,16},{4,20},{8,24},{12,28},{16,0},{20,4},{24,8},{28,12},{1,17},{... | collective-permute-start | bytes 700424 | tf_op jit(solution)/shard_map/ppermute | solution.py:40
  124.6 10.9 %collective-permute-start.47 = (bf16[304,384]{1,0:T(8,128)(2,1)S(1)}, bf16[304,384]{1,0:T(8,128)(2,1)S(1)}, u32[]{:S(2)}, u32[]{:S(2)}) collective-permute-start(bf16[304,384]{1,0:T(8,128)(2,1)S(1)} %get-tuple-element.188), channel_id=1, source_target_pairs={{0,8},{4,12},{8,0},{12,4},{16,24},{20,28},{24,16},{28,20},{1,9},{5... | collective-permute-start | bytes 700424 | tf_op jit(solution)/shard_map/ppermute | solution.py:40
  125.9 11.0 %collective-permute-start.48 = (bf16[304,384]{1,0:T(8,128)(2,1)S(1)}, bf16[304,384]{1,0:T(8,128)(2,1)S(1)}, u32[]{:S(2)}, u32[]{:S(2)}) collective-permute-start(bf16[304,384]{1,0:T(8,128)(2,1)S(1)} %get-tuple-element.189), channel_id=1, source_target_pairs={{0,16},{4,20},{8,24},{12,28},{16,0},{20,4},{24,8},{28,12},{1,17},{... | collective-permute-start | bytes 700424 | tf_op jit(solution)/shard_map/ppermute | solution.py:40
  131.9 9.2 %collective-permute-start.46 = (bf16[304,384]{1,0:T(8,128)(2,1)S(1)}, bf16[304,384]{1,0:T(8,128)(2,1)S(1)}, u32[]{:S(2)}, u32[]{:S(2)}) collective-permute-start(bf16[304,384]{1,0:T(8,128)(2,1)S(1)} %add_convert_fusion.3), channel_id=1, source_target_pairs={{0,16},{4,20},{8,24},{12,28},{16,0},{20,4},{24,8},{28,12},{1,17},{... | collective-permute-start | bytes 700424 | tf_op jit(solution)/shard_map/ppermute | solution.py:40
  133.2 8.2 %collective-permute-start.49 = (bf16[304,384]{1,0:T(8,128)(2,1)S(1)}, bf16[304,384]{1,0:T(8,128)(2,1)S(1)}, u32[]{:S(2)}, u32[]{:S(2)}) collective-permute-start(bf16[304,384]{1,0:T(8,128)(2,1)S(1)} %add_convert_fusion.2.refs_6_), channel_id=1, source_target_pairs={{0,8},{4,12},{8,0},{12,4},{16,24},{20,28},{24,16},{28,20},{1,9},{5... | collective-permute-start | bytes 700424 | tf_op jit(solution)/shard_map/ppermute | solution.py:40
  142.9 10.6 %collective-permute-start.51 = (bf16[160,384]{1,0:T(8,128)(2,1)S(1)}, bf16[160,384]{1,0:T(8,128)(2,1)S(1)}, u32[]{:S(2)}, u32[]{:S(2)}) collective-permute-start(bf16[160,384]{1,0:T(8,128)(2,1)S(1)} %pad_maximum_fusion.5), channel_id=1, source_target_pairs={{0,1},{1,0},{2,3},{3,2},{4,5},{5,4},{6,7},{7,6},{8,9},{9,8},{10,11... | collective-permute-start | bytes 368648 | tf_op jit(solution)/shard_map/ppermute | solution.py:40
  144.1 9.4 %collective-permute-start.53 = (bf16[160,384]{1,0:T(8,128)(2,1)S(1)}, bf16[160,384]{1,0:T(8,128)(2,1)S(1)}, u32[]{:S(2)}, u32[]{:S(2)}) collective-permute-start(bf16[160,384]{1,0:T(8,128)(2,1)S(1)} %pad_maximum_fusion.8), channel_id=1, source_target_pairs={{0,3},{1,2},{2,1},{3,0},{4,7},{5,6},{6,5},{7,4},{8,11},{9,10},{10,... | collective-permute-start | bytes 368648 | tf_op jit(solution)/shard_map/ppermute | solution.py:40
  146.5 11.1 %collective-permute-start.52 = (bf16[160,384]{1,0:T(8,128)(2,1)S(1)}, bf16[160,384]{1,0:T(8,128)(2,1)S(1)}, u32[]{:S(2)}, u32[]{:S(2)}) collective-permute-start(bf16[160,384]{1,0:T(8,128)(2,1)S(1)} %pad_maximum_fusion.7), channel_id=1, source_target_pairs={{0,2},{1,3},{2,0},{3,1},{4,6},{5,7},{6,4},{7,5},{8,10},{9,11},{10,... | collective-permute-start | bytes 368648 | tf_op jit(solution)/shard_map/ppermute | solution.py:40
  157.9 5.3 %collective-permute-start.54 = (bf16[13,13,8,384]{3,2,1,0:T(8,128)(2,1)S(1)}, bf16[13,13,8,384]{3,2,1,0:T(8,128)(2,1)S(1)}, u32[]{:S(2)}, u32[]{:S(2)}) collective-permute-start(bf16[13,13,8,384]{3,2,1,0:T(8,128)(2,1)S(1)} %get-tuple-element.238), channel_id=1, source_target_pairs={{0,4},{4,0},{8,12},{12,8},{16,20},{20,16},{24,28},{28,24},{1,5},{5... | collective-permute-start | bytes 3115016 | tf_op jit(solution)/shard_map/ppermute | solution.py:40
  158.1 8.3 %collective-permute-start.55 = (bf16[160,384]{1,0:T(8,128)(2,1)S(1)}, bf16[160,384]{1,0:T(8,128)(2,1)S(1)}, u32[]{:S(2)}, u32[]{:S(2)}) collective-permute-start(bf16[160,384]{1,0:T(8,128)(2,1)S(1)} %add_convert_fusion.6.refs_0_), channel_id=1, source_target_pairs={{0,1},{1,0},{2,3},{3,2},{4,5},{5,4},{6,7},{7,6},{8,9},{9,8},{10,11... | collective-permute-start | bytes 368648 | tf_op jit(solution)/shard_map/ppermute | solution.py:40
  158.2 12.4 %collective-permute-start.56 = (bf16[160,384]{1,0:T(8,128)(2,1)S(1)}, bf16[160,384]{1,0:T(8,128)(2,1)S(1)}, u32[]{:S(2)}, u32[]{:S(2)}) collective-permute-start(bf16[160,384]{1,0:T(8,128)(2,1)S(1)} %add_convert_fusion.6.refs_0_), channel_id=1, source_target_pairs={{0,2},{1,3},{2,0},{3,1},{4,6},{5,7},{6,4},{7,5},{8,10},{9,11},{10,... | collective-permute-start | bytes 368648 | tf_op jit(solution)/shard_map/ppermute | solution.py:40
  160.7 9.8 %collective-permute-start.57 = (bf16[160,384]{1,0:T(8,128)(2,1)S(1)}, bf16[160,384]{1,0:T(8,128)(2,1)S(1)}, u32[]{:S(2)}, u32[]{:S(2)}) collective-permute-start(bf16[160,384]{1,0:T(8,128)(2,1)S(1)} %add_convert_fusion.6.refs_0_), channel_id=1, source_target_pairs={{0,3},{1,2},{2,1},{3,0},{4,7},{5,6},{6,5},{7,4},{8,11},{9,10},{10,... | collective-permute-start | bytes 368648 | tf_op jit(solution)/shard_map/ppermute | solution.py:40
  (32 other events, 542.0 us)

commit v5 on v4

--- a/solution.py
+++ b/solution.py
@@ -16,7 +16,7 @@
 WIDE = jnp.float32
 TAPS = 9
 CELLS = 36
-EXTRA = 16
+EXTRA = 8
 PORTION = 80
 LANES = 128
 WHOLE = pl.BlockSpec(memory_space=pltpu.VMEM)

time: 172 us -> 171 us (level)
  no operation moved by 1% of the time
where the time goes in v5:
time: 171 us
  starting transfers between devices  59 us (35%)
  waiting for transfers between devices  52.4 us (31%)
  Pallas kernels  43.5 us (25%)
  matrix products  6.81 us (4%)
  local copies, waits for them, and re-layouts  4.74 us (3%)
  other arithmetic  3.37 us (2%)
    ppermute x58, starting transfers between devices, trade(): return lax.ppermute(value, axis, [(i, i ^ bit) for i in range(size)])  59 us
    ppermute x58, waiting for transfers between devices, trade(): return lax.ppermute(value, axis, [(i, i ^ bit) for i in range(size)])  52.4 us
    pallas_call x4, Pallas kernels, fc_update(): pl.pallas_call(kernel, in_specs=[SCALARS] + [WHOLE] * (3 + planes) + [hbm...  16.2 us
    pallas_call x1, Pallas kernels, conv_backward(): pl.pallas_call(kernel, in_specs=[SCALARS] * 3 + [pl.BlockSpec(memory_spac...  7.51 us
    pallas_call x2, Pallas kernels, fc_prepare(): pl.pallas_call(kernel, grid_spec=pltpu.PrefetchScalarGridSpec(num_scalar_...  6.88 us
    conv_general_dilated x1, matrix products, turned_conv(): lax.conv_general_dilated(grad, kernel[::-1, ::-1], (1, 1), 'SAME', dimens...  6.81 us
    pallas_call x1, Pallas kernels, conv_forward(): pl.pallas_call(kernel, in_specs=[SCALARS] * 2 + [WHOLE] * (1 + count), ou...  6.71 us
  transfers between devices with their start and end apart: 58, of which 30 were waited for; matrix products, arithmetic and copies ran while one was open for 8% of the time, Pallas kernels for 22%

profile of v5, /device:TPU:0, one launch (start us, length us, event | category | flops | bytes accessed | tf_op | source)
XLA Modules:
  0.0 171.3 jit_solution(1568379838746767833)
XLA Ops:
  2.5 2.6 %collective-permute-start.2 = (bf16[296,384]{1,0:T(8,128)(2,1)S(1)}, bf16[296,384]{1,0:T(8,128)(2,1)S(1)}, u32[]{:S(2)}, u32[]{:S(2)}) collective-permute-start(bf16[296,384]{1,0:T(8,128)(2,1)S(1)} %get-tuple-element.124), channel_id=1, source_target_pairs={{0,12},{4,8},{8,4},{12,0},{16,28},{20,24},{24,20},{28,16},{1,13},{... | collective-permute-start | bytes 681992 | tf_op jit(solution)/shard_map/ppermute | solution.py:40
  5.1 1.5 collective-permute-start.1
  7.2 3.4 %shard_map.255.refs_8_.refs_5_ = bf16[2304,512]{1,0:T(8,128)(2,1)S(1)} custom-call(s32[1]{0:T(128)} %bitcast.core_ref, f32[2,2304,512]{2,1,0:T(8,128)} %w_ref.7, bf16[296,384]{1,0:T(8,128)(2,1)S(1)} %get-tuple-element.125._.refs_0_), custom_call_target="tpu_custom_call" | custom-call | bytes 7077888 | tf_op jit(solution)/shard_map/pallas_call | solution.py:176
  10.5 3.5 %shard_map.256 = bf16[2304,512]{1,0:T(8,128)(2,1)S(1)} custom-call(s32[1]{0:T(128)} %bitcast.core_ref, f32[2,2304,512]{2,1,0:T(8,128)} %w_ref.7, bf16[296,384]{1,0:T(8,128)(2,1)S(1)} %get-tuple-element.125._.refs_0_), custom_call_target="tpu_custom_call" | custom-call | bytes 7077888 | tf_op jit(solution)/shard_map/pallas_call | solution.py:176
  14.6 1.5 collective-permute-done.3.refs_2_
  18.3 1.5 collective-permute-start.6
  20.7 4.5 %collective-permute-done.5.refs_6_ = bf16[296,384]{1,0:T(8,128)(2,1)S(1)} collective-permute-done((bf16[296,384]{1,0:T(8,128)(2,1)S(1)}, bf16[296,384]{1,0:T(8,128)(2,1)S(1)}, u32[]{:S(2)}, u32[]{:S(2)}) %collective-permute-start.5) | collective-permute-done | bytes 227360 | tf_op jit(solution)/shard_map/ppermute | solution.py:40
  25.6 6.7 %shard_map.257 = (f32[36,16,256]{2,1,0:T(8,128)S(1)}, bf16[36,16,256]{2,1,0:T(8,128)(2,1)S(1)}, bf16[13,13,16,256]{3,2,1,0:T(8,128)(2,1)}, f32[8,256]{1,0:T(8,128)S(1)}, bf16[9,256,384]{2,1,0:T(8,128)(2,1)}) custom-call(s32[1]{0:T(128)} %bitcast.core_ref, s32[1]{0:T(128)} %bitcast.3.chip_ref, bf16[15,15,16,384]{3,2,1,0:T(8,128)(2,1)S(1)} %fusion.6.x_ref.refs_8_, ...), custom_call_target="tpu_custom_call" | custom-call | tf_op jit(solution)/shard_map/pallas_call | solution.py:265
  32.4 1.6 collective-permute-done.8.b_ref.refs_6_
  34.2 3.7 %collective-permute-start.11 = (bf16[16,2304]{1,0:T(8,128)(2,1)S(1)}, bf16[16,2304]{1,0:T(8,128)(2,1)S(1)}, u32[]{:S(2)}, u32[]{:S(2)}) collective-permute-start(bf16[16,2304]{1,0:T(8,128)(2,1)S(1)} %get-tuple-element.143), channel_id=1, source_target_pairs={{0,3},{1,2},{2,1},{3,0},{4,7},{5,6},{6,5},{7,4},{8,11},{9,10},{10,... | collective-permute-start | bytes 221192 | tf_op jit(solution)/shard_map/ppermute | solution.py:40
  38.9 2.0 %collective-permute-done.11 = bf16[16,2304]{1,0:T(8,128)(2,1)S(1)} collective-permute-done((bf16[16,2304]{1,0:T(8,128)(2,1)S(1)}, bf16[16,2304]{1,0:T(8,128)(2,1)S(1)}, u32[]{:S(2)}, u32[]{:S(2)}) %collective-permute-start.11) | collective-permute-done | bytes 73760 | tf_op jit(solution)/shard_map/ppermute | solution.py:40
  40.9 3.5 %collective-permute-done.10 = bf16[16,2304]{1,0:T(8,128)(2,1)S(1)} collective-permute-done((bf16[16,2304]{1,0:T(8,128)(2,1)S(1)}, bf16[16,2304]{1,0:T(8,128)(2,1)S(1)}, u32[]{:S(2)}, u32[]{:S(2)}) %collective-permute-start.10) | collective-permute-done | bytes 73760 | tf_op jit(solution)/shard_map/ppermute | solution.py:40
  44.4 1.5 collective-permute-start.13
  45.9 1.6 collective-permute-start.14
  48.7 4.0 %collective-permute-done.14.refs_4_ = bf16[2,16,2304]{2,1,0:T(8,128)(2,1)S(1)} collective-permute-done((bf16[2,16,2304]{2,1,0:T(8,128)(2,1)S(1)}, bf16[2,16,2304]{2,1,0:T(8,128)(2,1)S(1)}, u32[]{:S(2)}, u32[]{:S(2)}) %collective-permute-start.14) | collective-permute-done | bytes 147488 | tf_op jit(solution)/shard_map/ppermute | solution.py:40
  52.6 1.9 %collective-permute-start.17 = (bf16[2,16,2304]{2,1,0:T(8,128)(2,1)S(1)}, bf16[2,16,2304]{2,1,0:T(8,128)(2,1)S(1)}, u32[]{:S(2)}, u32[]{:S(2)}) collective-permute-start(bf16[2,16,2304]{2,1,0:T(8,128)(2,1)S(1)} %collective-permute-done.13.refs_3_), channel_id=1, source_target_pairs={{0,16},{4,20},{8,24},{12,28},{16,0},{20,4},{24,8},{28,12},{1,17},{... | collective-permute-start | bytes 442376 | tf_op jit(solution)/shard_map/ppermute | solution.py:40
  55.7 2.1 %collective-permute-done.16.refs_6_ = bf16[2,16,2304]{2,1,0:T(8,128)(2,1)S(1)} collective-permute-done((bf16[2,16,2304]{2,1,0:T(8,128)(2,1)S(1)}, bf16[2,16,2304]{2,1,0:T(8,128)(2,1)S(1)}, u32[]{:S(2)}, u32[]{:S(2)}) %collective-permute-start.16) | collective-permute-done | bytes 147488 | tf_op jit(solution)/shard_map/ppermute | solution.py:40
  57.8 1.4 shard_map.259
  63.6 2.1 %collective-permute-start.24 = (bf16[64,512]{1,0:T(8,128)(2,1)S(1)}, bf16[64,512]{1,0:T(8,128)(2,1)S(1)}, u32[]{:S(2)}, u32[]{:S(2)}) collective-permute-start(bf16[64,512]{1,0:T(8,128)(2,1)S(1)} %add_convert_fusion.11), channel_id=1, source_target_pairs={{0,2},{1,3},{2,0},{3,1},{4,6},{5,7},{6,4},{7,5},{8,10},{9,11},{10,... | collective-permute-start | bytes 196616 | tf_op jit(solution)/shard_map/ppermute | solution.py:40
  67.2 2.4 %collective-permute-done.24 = bf16[64,512]{1,0:T(8,128)(2,1)S(1)} collective-permute-done((bf16[64,512]{1,0:T(8,128)(2,1)S(1)}, bf16[64,512]{1,0:T(8,128)(2,1)S(1)}, u32[]{:S(2)}, u32[]{:S(2)}) %collective-permute-start.24) | collective-permute-done | bytes 65568 | tf_op jit(solution)/shard_map/ppermute | solution.py:40
  69.6 2.1 %collective-permute-done.21 = bf16[64,512]{1,0:T(8,128)(2,1)S(1)} collective-permute-done((bf16[64,512]{1,0:T(8,128)(2,1)S(1)}, bf16[64,512]{1,0:T(8,128)(2,1)S(1)}, u32[]{:S(2)}, u32[]{:S(2)}) %collective-permute-start.21) | collective-permute-done | bytes 65568 | tf_op jit(solution)/shard_map/ppermute | solution.py:40
  72.7 2.4 %collective-permute-start.30 = (bf16[64,512]{1,0:T(8,128)(2,1)S(1)}, bf16[64,512]{1,0:T(8,128)(2,1)S(1)}, u32[]{:S(2)}, u32[]{:S(2)}) collective-permute-start(bf16[64,512]{1,0:T(8,128)(2,1)S(1)} %get-tuple-element.257.refs_0_), channel_id=1, source_target_pairs={{0,2},{1,3},{2,0},{3,1},{4,6},{5,7},{6,4},{7,5},{8,10},{9,11},{10,... | collective-permute-start | bytes 196616 | tf_op jit(solution)/shard_map/ppermute | solution.py:40
  75.5 2.9 %collective-permute-done.27.refs_2_ = bf16[64,512]{1,0:T(8,128)(2,1)S(1)} collective-permute-done((bf16[64,512]{1,0:T(8,128)(2,1)S(1)}, bf16[64,512]{1,0:T(8,128)(2,1)S(1)}, u32[]{:S(2)}, u32[]{:S(2)}) %collective-permute-start.27) | collective-permute-done | bytes 65568 | tf_op jit(solution)/shard_map/ppermute | solution.py:40
  78.4 2.0 %collective-permute-start.29 = (bf16[64,512]{1,0:T(8,128)(2,1)S(1)}, bf16[64,512]{1,0:T(8,128)(2,1)S(1)}, u32[]{:S(2)}, u32[]{:S(2)}) collective-permute-start(bf16[64,512]{1,0:T(8,128)(2,1)S(1)} %get-tuple-element.257.refs_0_), channel_id=1, source_target_pairs={{0,1},{1,0},{2,3},{3,2},{4,5},{5,4},{6,7},{7,6},{8,9},{9,8},{10,11... | collective-permute-start | bytes 196616 | tf_op jit(solution)/shard_map/ppermute | solution.py:40
  80.5 2.9 %collective-permute-done.29.refs_1_ = bf16[64,512]{1,0:T(8,128)(2,1)S(1)} collective-permute-done((bf16[64,512]{1,0:T(8,128)(2,1)S(1)}, bf16[64,512]{1,0:T(8,128)(2,1)S(1)}, u32[]{:S(2)}, u32[]{:S(2)}) %collective-permute-start.29) | collective-permute-done | bytes 65568 | tf_op jit(solution)/shard_map/ppermute | solution.py:40
  86.3 1.5 shard_map.260
  89.9 1.6 collective-permute-start.36
  92.0 2.6 %collective-permute-done.34 = bf16[2,16,2304]{2,1,0:T(8,128)(2,1)S(1)} collective-permute-done((bf16[2,16,2304]{2,1,0:T(8,128)(2,1)S(1)}, bf16[2,16,2304]{2,1,0:T(8,128)(2,1)S(1)}, u32[]{:S(2)}, u32[]{:S(2)}) %collective-permute-start.34) | collective-permute-done | bytes 147488 | tf_op jit(solution)/shard_map/ppermute | solution.py:40
  94.6 1.6 collective-permute-start.35
  98.0 4.1 %shard_map.261 = (f32[2,2304,512]{2,1,0:T(8,128)}, f32[2,2304,512]{2,1,0:T(8,128)}, f32[8,128]{1,0:T(8,128)S(1)}) custom-call(s32[1]{0:T(128)} %bitcast.core_ref, f32[2,2304,512]{2,1,0:T(8,128)S(1)} %bitcast.86, f32[2,2304,512]{2,1,0:T(8,128)S(1)} %bitcast.88, bf16[256,2304]{1,0:T(8,128)(2,1)S(1)} %get-tuple-element.160.rows_ref, ...), custom_call_target="tpu_custom_call" | custom-call | bytes 9437184 | tf_op jit(solution)/shard_map/pallas_call | solution.py:552
  102.3 1.3 collective-permute-start.37
  103.7 2.3 %collective-permute-start.40 = (bf16[16,2304]{1,0:T(8,128)(2,1)S(1)}, bf16[16,2304]{1,0:T(8,128)(2,1)S(1)}, u32[]{:S(2)}, u32[]{:S(2)}) collective-permute-start(bf16[16,2304]{1,0:T(8,128)(2,1)S(1)} %get-tuple-element.242), channel_id=1, source_target_pairs={{0,2},{1,3},{2,0},{3,1},{4,6},{5,7},{6,4},{7,5},{8,10},{9,11},{10,... | collective-permute-start | bytes 221192 | tf_op jit(solution)/shard_map/ppermute | solution.py:40
  107.1 4.1 %shard_map.262 = (f32[2,2304,512]{2,1,0:T(8,128)}, f32[2,2304,512]{2,1,0:T(8,128)}, f32[8,128]{1,0:T(8,128)S(1)}) custom-call(s32[1]{0:T(128)} %bitcast.core_ref, f32[2,2304,512]{2,1,0:T(8,128)S(1)} %bitcast.86, f32[2,2304,512]{2,1,0:T(8,128)S(1)} %bitcast.88, ...), custom_call_target="tpu_custom_call", output_to_operand_aliasing={{0}: (8, {}), {1}: (9, {})} | custom-call | bytes 9437184 | tf_op jit(solution)/shard_map/pallas_call | solution.py:552
  112.5 1.5 collective-permute-done.42.refs_4_
  113.9 7.5 %shard_map.263 = (bf16[296,384]{1,0:T(8,128)(2,1)S(1)}, bf16[296,384]{1,0:T(8,128)(2,1)S(1)}, bf16[296,384]{1,0:T(8,128)(2,1)S(1)}, bf16[296,384]{1,0:T(8,128)(2...) custom-call(s32[1]{0:T(128)} %bitcast.core_ref, ...), custom_call_target="tpu_custom_call" | custom-call | tf_op jit(solution)/shard_map/pallas_call | solution.py:492
  121.5 1.4 collective-permute-start.43
  125.7 4.1 %shard_map.264 = (f32[2,2304,512]{2,1,0:T(8,128)}, f32[2,2304,512]{2,1,0:T(8,128)}, f32[8,128]{1,0:T(8,128)S(1)}) custom-call(s32[1]{0:T(128)} %bitcast.core_ref, f32[2,2304,512]{2,1,0:T(8,128)S(1)} %bitcast.86, f32[2,2304,512]{2,1,0:T(8,128)S(1)} %bitcast.88, ...), custom_call_target="tpu_custom_call", output_to_operand_aliasing={{0}: (8, {}), {1}: (9, {})} | custom-call | bytes 9437184 | tf_op jit(solution)/shard_map/pallas_call | solution.py:552
  129.9 1.4 collective-permute-done.44
  134.8 1.4 collective-permute-done.48
  136.2 4.1 %shard_map.265 = (f32[2,2304,512]{2,1,0:T(8,128)}, f32[2,2304,512]{2,1,0:T(8,128)}, f32[8,128]{1,0:T(8,128)S(1)}) custom-call(s32[1]{0:T(128)} %bitcast.core_ref, f32[2,2304,512]{2,1,0:T(8,128)S(1)} %bitcast.86, f32[2,2304,512]{2,1,0:T(8,128)S(1)} %bitcast.88, ...), custom_call_target="tpu_custom_call", output_to_operand_aliasing={{0}: (8, {}), {1}: (9, {})} | custom-call | bytes 9437184 | tf_op jit(solution)/shard_map/pallas_call | solution.py:552
  143.2 2.4 %collective-permute-start.53 = (bf16[160,384]{1,0:T(8,128)(2,1)S(1)}, bf16[160,384]{1,0:T(8,128)(2,1)S(1)}, u32[]{:S(2)}, u32[]{:S(2)}) collective-permute-start(bf16[160,384]{1,0:T(8,128)(2,1)S(1)} %pad_maximum_fusion.8), channel_id=1, source_target_pairs={{0,3},{1,2},{2,1},{3,0},{4,7},{5,6},{6,5},{7,4},{8,11},{9,10},{10,... | collective-permute-start | bytes 368648 | tf_op jit(solution)/shard_map/ppermute | solution.py:40
  145.8 6.8 %convolution_convert_fusion = bf16[13,13,16,384]{3,2,1,0:T(8,128)(2,1)S(1)} fusion(bf16[13,13,16,256]{3,2,1,0:T(8,128)(2,1)S(1)} %copy-done.15, bf16[3,3,256,384]{3,2,1,0:T(8,128)(2,1)S(1)} %bitcast.125), kind=kOutput, calls=%fused_computation.14 | convolution fusion | flops 4307539968 | bytes 5230592 | tf_op jit(solution)/shard_map/conv_general_dilated | solution.py:1025
  152.6 4.0 %collective-permute-done.52 = bf16[160,384]{1,0:T(8,128)(2,1)S(1)} collective-permute-done((bf16[160,384]{1,0:T(8,128)(2,1)S(1)}, bf16[160,384]{1,0:T(8,128)(2,1)S(1)}, u32[]{:S(2)}, u32[]{:S(2)}) %collective-permute-start.52) | collective-permute-done | bytes 122912 | tf_op jit(solution)/shard_map/ppermute | solution.py:40
  157.3 2.6 %collective-permute-start.56 = (bf16[160,384]{1,0:T(8,128)(2,1)S(1)}, bf16[160,384]{1,0:T(8,128)(2,1)S(1)}, u32[]{:S(2)}, u32[]{:S(2)}) collective-permute-start(bf16[160,384]{1,0:T(8,128)(2,1)S(1)} %add_convert_fusion.6.refs_0_), channel_id=1, source_target_pairs={{0,2},{1,3},{2,0},{3,1},{4,6},{5,7},{6,4},{7,5},{8,10},{9,11},{10,... | collective-permute-start | bytes 368648 | tf_op jit(solution)/shard_map/ppermute | solution.py:40
  159.9 1.8 %collective-permute-start.57 = (bf16[160,384]{1,0:T(8,128)(2,1)S(1)}, bf16[160,384]{1,0:T(8,128)(2,1)S(1)}, u32[]{:S(2)}, u32[]{:S(2)}) collective-permute-start(bf16[160,384]{1,0:T(8,128)(2,1)S(1)} %add_convert_fusion.6.refs_0_), channel_id=1, source_target_pairs={{0,3},{1,2},{2,1},{3,0},{4,7},{5,6},{6,5},{7,4},{8,11},{9,10},{10,... | collective-permute-start | bytes 368648 | tf_op jit(solution)/shard_map/ppermute | solution.py:40
  162.5 2.9 %copy.60 = bf16[2,13,13,8,384]{4,0,2,1,3:T(2,128)(2,1)} copy(bf16[2,13,13,8,384]{4,3,2,1,0:T(8,128)(2,1)S(1)} %shard_map.266) | data formatting | bytes 4153344 | tf_op jit(solution)/shard_map/pallas_call | solution.py:575
  165.5 4.2 %collective-permute-done.56.refs_2_ = bf16[160,384]{1,0:T(8,128)(2,1)S(1)} collective-permute-done((bf16[160,384]{1,0:T(8,128)(2,1)S(1)}, bf16[160,384]{1,0:T(8,128)(2,1)S(1)}, u32[]{:S(2)}, u32[]{:S(2)}) %collective-permute-start.56) | collective-permute-done | bytes 122912 | tf_op jit(solution)/shard_map/ppermute | solution.py:40
  169.7 1.5 shard_map.267
  (182 shorter events, 37.9 us)
Async XLA Ops:
  2.0 12.6 %collective-permute-start = (bf16[296,384]{1,0:T(8,128)(2,1)S(1)}, bf16[296,384]{1,0:T(8,128)(2,1)S(1)}, u32[]{:S(2)}, u32[]{:S(2)}) collective-permute-start(bf16[296,384]{1,0:T(8,128)(2,1)S(1)} %get-tuple-element.124), channel_id=1, source_target_pairs={{0,4},{4,0},{8,12},{12,8},{16,20},{20,16},{24,28},{28,24},{1,5},{5... | collective-permute-start | bytes 681992 | tf_op jit(solution)/shard_map/ppermute | solution.py:40
  2.5 12.1 %collective-permute-start.2 = (bf16[296,384]{1,0:T(8,128)(2,1)S(1)}, bf16[296,384]{1,0:T(8,128)(2,1)S(1)}, u32[]{:S(2)}, u32[]{:S(2)}) collective-permute-start(bf16[296,384]{1,0:T(8,128)(2,1)S(1)} %get-tuple-element.124), channel_id=1, source_target_pairs={{0,12},{4,8},{8,4},{12,0},{16,28},{20,24},{24,20},{28,16},{1,13},{... | collective-permute-start | bytes 681992 | tf_op jit(solution)/shard_map/ppermute | solution.py:40
  5.1 9.5 %collective-permute-start.1 = (bf16[296,384]{1,0:T(8,128)(2,1)S(1)}, bf16[296,384]{1,0:T(8,128)(2,1)S(1)}, u32[]{:S(2)}, u32[]{:S(2)}) collective-permute-start(bf16[296,384]{1,0:T(8,128)(2,1)S(1)} %get-tuple-element.125._.refs_0_), channel_id=1, source_target_pairs={{0,16},{4,20},{8,24},{12,28},{16,0},{20,4},{24,8},{28,12},{1,17},{... | collective-permute-start | bytes 681992 | tf_op jit(solution)/shard_map/ppermute | solution.py:40
  6.6 9.5 %collective-permute-start.3 = (bf16[296,384]{1,0:T(8,128)(2,1)S(1)}, bf16[296,384]{1,0:T(8,128)(2,1)S(1)}, u32[]{:S(2)}, u32[]{:S(2)}) collective-permute-start(bf16[296,384]{1,0:T(8,128)(2,1)S(1)} %get-tuple-element.125._.refs_0_), channel_id=1, source_target_pairs={{0,8},{4,12},{8,0},{12,4},{16,24},{20,28},{24,16},{28,20},{1,9},{5... | collective-permute-start | bytes 681992 | tf_op jit(solution)/shard_map/ppermute | solution.py:40
  7.2 9.5 %collective-permute-start.4 = (bf16[296,384]{1,0:T(8,128)(2,1)S(1)}, bf16[296,384]{1,0:T(8,128)(2,1)S(1)}, u32[]{:S(2)}, u32[]{:S(2)}) collective-permute-start(bf16[296,384]{1,0:T(8,128)(2,1)S(1)} %get-tuple-element.124), channel_id=1, source_target_pairs={{0,20},{4,16},{8,28},{12,24},{16,4},{20,0},{24,12},{28,8},{1,21},{... | collective-permute-start | bytes 681992 | tf_op jit(solution)/shard_map/ppermute | solution.py:40
  17.3 40.5 %collective-permute-start.18 = (bf16[2304,512]{1,0:T(8,128)(2,1)S(1)}, bf16[2304,512]{1,0:T(8,128)(2,1)S(1)}, u32[]{:S(2)}, u32[]{:S(2)}) collective-permute-start(bf16[2304,512]{1,0:T(8,128)(2,1)S(1)} %shard_map.256), channel_id=1, source_target_pairs={{0,4},{4,0},{8,12},{12,8},{16,20},{20,16},{24,28},{28,24},{1,5},{5... | collective-permute-start | bytes 7077896 | tf_op jit(solution)/shard_map/ppermute | solution.py:40
  17.3 8.0 %collective-permute-start.5 = (bf16[296,384]{1,0:T(8,128)(2,1)S(1)}, bf16[296,384]{1,0:T(8,128)(2,1)S(1)}, u32[]{:S(2)}, u32[]{:S(2)}) collective-permute-start(bf16[296,384]{1,0:T(8,128)(2,1)S(1)} %collective-permute-done.1.refs_4_), channel_id=1, source_target_pairs={{0,8},{4,12},{8,0},{12,4},{16,24},{20,28},{24,16},{28,20},{1,9},{5... | collective-permute-start | bytes 681992 | tf_op jit(solution)/shard_map/ppermute | solution.py:40
  18.3 7.3 %collective-permute-start.6 = (bf16[296,384]{1,0:T(8,128)(2,1)S(1)}, bf16[296,384]{1,0:T(8,128)(2,1)S(1)}, u32[]{:S(2)}, u32[]{:S(2)}) collective-permute-start(bf16[296,384]{1,0:T(8,128)(2,1)S(1)} %collective-permute-done.2.refs_3_), channel_id=1, source_target_pairs={{0,16},{4,20},{8,24},{12,28},{16,0},{20,4},{24,8},{28,12},{1,17},{... | collective-permute-start | bytes 681992 | tf_op jit(solution)/shard_map/ppermute | solution.py:40
  34.2 6.7 %collective-permute-start.11 = (bf16[16,2304]{1,0:T(8,128)(2,1)S(1)}, bf16[16,2304]{1,0:T(8,128)(2,1)S(1)}, u32[]{:S(2)}, u32[]{:S(2)}) collective-permute-start(bf16[16,2304]{1,0:T(8,128)(2,1)S(1)} %get-tuple-element.143), channel_id=1, source_target_pairs={{0,3},{1,2},{2,1},{3,0},{4,7},{5,6},{6,5},{7,4},{8,11},{9,10},{10,... | collective-permute-start | bytes 221192 | tf_op jit(solution)/shard_map/ppermute | solution.py:40
  37.9 6.5 %collective-permute-start.10 = (bf16[16,2304]{1,0:T(8,128)(2,1)S(1)}, bf16[16,2304]{1,0:T(8,128)(2,1)S(1)}, u32[]{:S(2)}, u32[]{:S(2)}) collective-permute-start(bf16[16,2304]{1,0:T(8,128)(2,1)S(1)} %get-tuple-element.142), channel_id=1, source_target_pairs={{0,2},{1,3},{2,0},{3,1},{4,6},{5,7},{6,4},{7,5},{8,10},{9,11},{10,... | collective-permute-start | bytes 221192 | tf_op jit(solution)/shard_map/ppermute | solution.py:40
  38.0 7.8 %collective-permute-start.9 = (bf16[16,2304]{1,0:T(8,128)(2,1)S(1)}, bf16[16,2304]{1,0:T(8,128)(2,1)S(1)}, u32[]{:S(2)}, u32[]{:S(2)}) collective-permute-start(bf16[16,2304]{1,0:T(8,128)(2,1)S(1)} %get-tuple-element.141), channel_id=1, source_target_pairs={{0,1},{1,0},{2,3},{3,2},{4,5},{5,4},{6,7},{7,6},{8,9},{9,8},{10,11... | collective-permute-start | bytes 221192 | tf_op jit(solution)/shard_map/ppermute | solution.py:40
  44.4 8.3 %collective-permute-start.13 = (bf16[2,16,2304]{2,1,0:T(8,128)(2,1)S(1)}, bf16[2,16,2304]{2,1,0:T(8,128)(2,1)S(1)}, u32[]{:S(2)}, u32[]{:S(2)}) collective-permute-start(bf16[2,16,2304]{2,1,0:T(8,128)(2,1)S(1)} %pad_maximum_fusion.3.refs_1_), channel_id=1, source_target_pairs={{0,8},{4,12},{8,0},{12,4},{16,24},{20,28},{24,16},{28,20},{1,9},{5... | collective-permute-start | bytes 442376 | tf_op jit(solution)/shard_map/ppermute | solution.py:40
  45.9 6.7 %collective-permute-start.14 = (bf16[2,16,2304]{2,1,0:T(8,128)(2,1)S(1)}, bf16[2,16,2304]{2,1,0:T(8,128)(2,1)S(1)}, u32[]{:S(2)}, u32[]{:S(2)}) collective-permute-start(bf16[2,16,2304]{2,1,0:T(8,128)(2,1)S(1)} %pad_maximum_fusion.2.refs_0_), channel_id=1, source_target_pairs={{0,16},{4,20},{8,24},{12,28},{16,0},{20,4},{24,8},{28,12},{1,17},{... | collective-permute-start | bytes 442376 | tf_op jit(solution)/shard_map/ppermute | solution.py:40
  47.5 7.1 %collective-permute-start.12 = (bf16[2,16,2304]{2,1,0:T(8,128)(2,1)S(1)}, bf16[2,16,2304]{2,1,0:T(8,128)(2,1)S(1)}, u32[]{:S(2)}, u32[]{:S(2)}) collective-permute-start(bf16[2,16,2304]{2,1,0:T(8,128)(2,1)S(1)} %pad_maximum_fusion.2.refs_0_), channel_id=1, source_target_pairs={{0,8},{4,12},{8,0},{12,4},{16,24},{20,28},{24,16},{28,20},{1,9},{5... | collective-permute-start | bytes 442376 | tf_op jit(solution)/shard_map/ppermute | solution.py:40
  48.1 7.5 %collective-permute-start.15 = (bf16[2,16,2304]{2,1,0:T(8,128)(2,1)S(1)}, bf16[2,16,2304]{2,1,0:T(8,128)(2,1)S(1)}, u32[]{:S(2)}, u32[]{:S(2)}) collective-permute-start(bf16[2,16,2304]{2,1,0:T(8,128)(2,1)S(1)} %pad_maximum_fusion.3.refs_1_), channel_id=1, source_target_pairs={{0,16},{4,20},{8,24},{12,28},{16,0},{20,4},{24,8},{28,12},{1,17},{... | collective-permute-start | bytes 442376 | tf_op jit(solution)/shard_map/ppermute | solution.py:40
  52.6 5.1 %collective-permute-start.16 = (bf16[2,16,2304]{2,1,0:T(8,128)(2,1)S(1)}, bf16[2,16,2304]{2,1,0:T(8,128)(2,1)S(1)}, u32[]{:S(2)}, u32[]{:S(2)}) collective-permute-start(bf16[2,16,2304]{2,1,0:T(8,128)(2,1)S(1)} %collective-permute-done.14.refs_4_), channel_id=1, source_target_pairs={{0,8},{4,12},{8,0},{12,4},{16,24},{20,28},{24,16},{28,20},{1,9},{5... | collective-permute-start | bytes 442376 | tf_op jit(solution)/shard_map/ppermute | solution.py:40
  52.6 5.1 %collective-permute-start.17 = (bf16[2,16,2304]{2,1,0:T(8,128)(2,1)S(1)}, bf16[2,16,2304]{2,1,0:T(8,128)(2,1)S(1)}, u32[]{:S(2)}, u32[]{:S(2)}) collective-permute-start(bf16[2,16,2304]{2,1,0:T(8,128)(2,1)S(1)} %collective-permute-done.13.refs_3_), channel_id=1, source_target_pairs={{0,16},{4,20},{8,24},{12,28},{16,0},{20,4},{24,8},{28,12},{1,17},{... | collective-permute-start | bytes 442376 | tf_op jit(solution)/shard_map/ppermute | solution.py:40
  60.1 5.7 %collective-permute-start.20 = (bf16[64,512]{1,0:T(8,128)(2,1)S(1)}, bf16[64,512]{1,0:T(8,128)(2,1)S(1)}, u32[]{:S(2)}, u32[]{:S(2)}) collective-permute-start(bf16[64,512]{1,0:T(8,128)(2,1)S(1)} %get-tuple-element.149), channel_id=1, source_target_pairs={{0,1},{1,0},{2,3},{3,2},{4,5},{5,4},{6,7},{7,6},{8,9},{9,8},{10,11... | collective-permute-start | bytes 196616 | tf_op jit(solution)/shard_map/ppermute | solution.py:40
  61.3 8.3 %collective-permute-start.19 = (bf16[64,512]{1,0:T(8,128)(2,1)S(1)}, bf16[64,512]{1,0:T(8,128)(2,1)S(1)}, u32[]{:S(2)}, u32[]{:S(2)}) collective-permute-start(bf16[64,512]{1,0:T(8,128)(2,1)S(1)} %get-tuple-element.147), channel_id=1, source_target_pairs={{0,1},{1,0},{2,3},{3,2},{4,5},{5,4},{6,7},{7,6},{8,9},{9,8},{10,11... | collective-permute-start | bytes 196616 | tf_op jit(solution)/shard_map/ppermute | solution.py:40
  63.6 5.9 %collective-permute-start.24 = (bf16[64,512]{1,0:T(8,128)(2,1)S(1)}, bf16[64,512]{1,0:T(8,128)(2,1)S(1)}, u32[]{:S(2)}, u32[]{:S(2)}) collective-permute-start(bf16[64,512]{1,0:T(8,128)(2,1)S(1)} %add_convert_fusion.11), channel_id=1, source_target_pairs={{0,2},{1,3},{2,0},{3,1},{4,6},{5,7},{6,4},{7,5},{8,10},{9,11},{10,... | collective-permute-start | bytes 196616 | tf_op jit(solution)/shard_map/ppermute | solution.py:40
  65.8 5.9 %collective-permute-start.21 = (bf16[64,512]{1,0:T(8,128)(2,1)S(1)}, bf16[64,512]{1,0:T(8,128)(2,1)S(1)}, u32[]{:S(2)}, u32[]{:S(2)}) collective-permute-start(bf16[64,512]{1,0:T(8,128)(2,1)S(1)} %add_convert_fusion.12), channel_id=1, source_target_pairs={{0,2},{1,3},{2,0},{3,1},{4,6},{5,7},{6,4},{7,5},{8,10},{9,11},{10,... | collective-permute-start | bytes 196616 | tf_op jit(solution)/shard_map/ppermute | solution.py:40
  71.8 6.5 %collective-permute-start.27 = (bf16[64,512]{1,0:T(8,128)(2,1)S(1)}, bf16[64,512]{1,0:T(8,128)(2,1)S(1)}, u32[]{:S(2)}, u32[]{:S(2)}) collective-permute-start(bf16[64,512]{1,0:T(8,128)(2,1)S(1)} %get-tuple-element.232.refs_0_), channel_id=1, source_target_pairs={{0,2},{1,3},{2,0},{3,1},{4,6},{5,7},{6,4},{7,5},{8,10},{9,11},{10,... | collective-permute-start | bytes 196616 | tf_op jit(solution)/shard_map/ppermute | solution.py:40
  72.7 7.7 %collective-permute-start.30 = (bf16[64,512]{1,0:T(8,128)(2,1)S(1)}, bf16[64,512]{1,0:T(8,128)(2,1)S(1)}, u32[]{:S(2)}, u32[]{:S(2)}) collective-permute-start(bf16[64,512]{1,0:T(8,128)(2,1)S(1)} %get-tuple-element.257.refs_0_), channel_id=1, source_target_pairs={{0,2},{1,3},{2,0},{3,1},{4,6},{5,7},{6,4},{7,5},{8,10},{9,11},{10,... | collective-permute-start | bytes 196616 | tf_op jit(solution)/shard_map/ppermute | solution.py:40
  75.1 10.6 %collective-permute-start.26 = (bf16[64,512]{1,0:T(8,128)(2,1)S(1)}, bf16[64,512]{1,0:T(8,128)(2,1)S(1)}, u32[]{:S(2)}, u32[]{:S(2)}) collective-permute-start(bf16[64,512]{1,0:T(8,128)(2,1)S(1)} %get-tuple-element.232.refs_0_), channel_id=1, source_target_pairs={{0,1},{1,0},{2,3},{3,2},{4,5},{5,4},{6,7},{7,6},{8,9},{9,8},{10,11... | collective-permute-start | bytes 196616 | tf_op jit(solution)/shard_map/ppermute | solution.py:40
  78.4 7.3 %collective-permute-start.28 = (bf16[64,512]{1,0:T(8,128)(2,1)S(1)}, bf16[64,512]{1,0:T(8,128)(2,1)S(1)}, u32[]{:S(2)}, u32[]{:S(2)}) collective-permute-start(bf16[64,512]{1,0:T(8,128)(2,1)S(1)} %collective-permute-done.27.refs_2_), channel_id=1, source_target_pairs={{0,1},{1,0},{2,3},{3,2},{4,5},{5,4},{6,7},{7,6},{8,9},{9,8},{10,11... | collective-permute-start | bytes 196616 | tf_op jit(solution)/shard_map/ppermute | solution.py:40
  87.8 6.8 %collective-permute-start.34 = (bf16[2,16,2304]{2,1,0:T(8,128)(2,1)S(1)}, bf16[2,16,2304]{2,1,0:T(8,128)(2,1)S(1)}, u32[]{:S(2)}, u32[]{:S(2)}) collective-permute-start(bf16[2,16,2304]{2,1,0:T(8,128)(2,1)S(1)} %get-tuple-element.159), channel_id=1, source_target_pairs={{0,8},{4,12},{8,0},{12,4},{16,24},{20,28},{24,16},{28,20},{1,9},{5... | collective-permute-start | bytes 442376 | tf_op jit(solution)/shard_map/ppermute | solution.py:40
  89.1 36.6 %collective-permute-start.45 = (bf16[256,2304]{1,0:T(8,128)(2,1)S(1)}, bf16[256,2304]{1,0:T(8,128)(2,1)S(1)}, u32[]{:S(2)}, u32[]{:S(2)}) collective-permute-start(bf16[256,2304]{1,0:T(8,128)(2,1)S(1)} %get-tuple-element.160.rows_ref), channel_id=1, source_target_pairs={{0,4},{4,0},{8,12},{12,8},{16,20},{20,16},{24,28},{28,24},{1,5},{5... | collective-permute-start | bytes 3538952 | tf_op jit(solution)/shard_map/ppermute | solution.py:40
  89.1 13.1 %collective-permute-start.33 = (bf16[2,16,2304]{2,1,0:T(8,128)(2,1)S(1)}, bf16[2,16,2304]{2,1,0:T(8,128)(2,1)S(1)}, u32[]{:S(2)}, u32[]{:S(2)}) collective-permute-start(bf16[2,16,2304]{2,1,0:T(8,128)(2,1)S(1)} %get-tuple-element.157), channel_id=1, source_target_pairs={{0,8},{4,12},{8,0},{12,4},{16,24},{20,28},{24,16},{28,20},{1,9},{5... | collective-permute-start | bytes 442376 | tf_op jit(solution)/shard_map/ppermute | solution.py:40
  89.9 6.7 %collective-permute-start.36 = (bf16[2,16,2304]{2,1,0:T(8,128)(2,1)S(1)}, bf16[2,16,2304]{2,1,0:T(8,128)(2,1)S(1)}, u32[]{:S(2)}, u32[]{:S(2)}) collective-permute-start(bf16[2,16,2304]{2,1,0:T(8,128)(2,1)S(1)} %get-tuple-element.162), channel_id=1, source_target_pairs={{0,16},{4,20},{8,24},{12,28},{16,0},{20,4},{24,8},{28,12},{1,17},{... | collective-permute-start | bytes 442376 | tf_op jit(solution)/shard_map/ppermute | solution.py:40
  91.5 12.1 %collective-permute-start.39 = (bf16[2,16,2304]{2,1,0:T(8,128)(2,1)S(1)}, bf16[2,16,2304]{2,1,0:T(8,128)(2,1)S(1)}, u32[]{:S(2)}, u32[]{:S(2)}) collective-permute-start(bf16[2,16,2304]{2,1,0:T(8,128)(2,1)S(1)} %get-tuple-element.169), channel_id=1, source_target_pairs={{0,16},{4,20},{8,24},{12,28},{16,0},{20,4},{24,8},{28,12},{1,17},{... | collective-permute-start | bytes 442376 | tf_op jit(solution)/shard_map/ppermute | solution.py:40
  94.6 7.6 %collective-permute-start.35 = (bf16[2,16,2304]{2,1,0:T(8,128)(2,1)S(1)}, bf16[2,16,2304]{2,1,0:T(8,128)(2,1)S(1)}, u32[]{:S(2)}, u32[]{:S(2)}) collective-permute-start(bf16[2,16,2304]{2,1,0:T(8,128)(2,1)S(1)} %add_convert_fusion.5), channel_id=1, source_target_pairs={{0,16},{4,20},{8,24},{12,28},{16,0},{20,4},{24,8},{28,12},{1,17},{... | collective-permute-start | bytes 442376 | tf_op jit(solution)/shard_map/ppermute | solution.py:40
  96.7 7.0 %collective-permute-start.38 = (bf16[2,16,2304]{2,1,0:T(8,128)(2,1)S(1)}, bf16[2,16,2304]{2,1,0:T(8,128)(2,1)S(1)}, u32[]{:S(2)}, u32[]{:S(2)}) collective-permute-start(bf16[2,16,2304]{2,1,0:T(8,128)(2,1)S(1)} %add_convert_fusion.4.refs_4_), channel_id=1, source_target_pairs={{0,8},{4,12},{8,0},{12,4},{16,24},{20,28},{24,16},{28,20},{1,9},{5... | collective-permute-start | bytes 442376 | tf_op jit(solution)/shard_map/ppermute | solution.py:40
  102.3 8.8 %collective-permute-start.37 = (bf16[16,2304]{1,0:T(8,128)(2,1)S(1)}, bf16[16,2304]{1,0:T(8,128)(2,1)S(1)}, u32[]{:S(2)}, u32[]{:S(2)}) collective-permute-start(bf16[16,2304]{1,0:T(8,128)(2,1)S(1)} %get-tuple-element.245), channel_id=1, source_target_pairs={{0,1},{1,0},{2,3},{3,2},{4,5},{5,4},{6,7},{7,6},{8,9},{9,8},{10,11... | collective-permute-start | bytes 221192 | tf_op jit(solution)/shard_map/ppermute | solution.py:40
  103.7 7.5 %collective-permute-start.40 = (bf16[16,2304]{1,0:T(8,128)(2,1)S(1)}, bf16[16,2304]{1,0:T(8,128)(2,1)S(1)}, u32[]{:S(2)}, u32[]{:S(2)}) collective-permute-start(bf16[16,2304]{1,0:T(8,128)(2,1)S(1)} %get-tuple-element.242), channel_id=1, source_target_pairs={{0,2},{1,3},{2,0},{3,1},{4,6},{5,7},{6,4},{7,5},{8,10},{9,11},{10,... | collective-permute-start | bytes 221192 | tf_op jit(solution)/shard_map/ppermute | solution.py:40
  106.0 6.3 %collective-permute-start.41 = (bf16[16,2304]{1,0:T(8,128)(2,1)S(1)}, bf16[16,2304]{1,0:T(8,128)(2,1)S(1)}, u32[]{:S(2)}, u32[]{:S(2)}) collective-permute-start(bf16[16,2304]{1,0:T(8,128)(2,1)S(1)} %get-tuple-element.243.refs_6_), channel_id=1, source_target_pairs={{0,3},{1,2},{2,1},{3,0},{4,7},{5,6},{6,5},{7,4},{8,11},{9,10},{10,... | collective-permute-start | bytes 221192 | tf_op jit(solution)/shard_map/ppermute | solution.py:40
  121.5 8.5 %collective-permute-start.43 = (bf16[296,384]{1,0:T(8,128)(2,1)S(1)}, bf16[296,384]{1,0:T(8,128)(2,1)S(1)}, u32[]{:S(2)}, u32[]{:S(2)}) collective-permute-start(bf16[296,384]{1,0:T(8,128)(2,1)S(1)} %get-tuple-element.176), channel_id=1, source_target_pairs={{0,8},{4,12},{8,0},{12,4},{16,24},{20,28},{24,16},{28,20},{1,9},{5... | collective-permute-start | bytes 681992 | tf_op jit(solution)/shard_map/ppermute | solution.py:40
  122.9 8.4 %collective-permute-start.44 = (bf16[296,384]{1,0:T(8,128)(2,1)S(1)}, bf16[296,384]{1,0:T(8,128)(2,1)S(1)}, u32[]{:S(2)}, u32[]{:S(2)}) collective-permute-start(bf16[296,384]{1,0:T(8,128)(2,1)S(1)} %get-tuple-element.177), channel_id=1, source_target_pairs={{0,16},{4,20},{8,24},{12,28},{16,0},{20,4},{24,8},{28,12},{1,17},{... | collective-permute-start | bytes 681992 | tf_op jit(solution)/shard_map/ppermute | solution.py:40
  124.1 10.7 %collective-permute-start.47 = (bf16[296,384]{1,0:T(8,128)(2,1)S(1)}, bf16[296,384]{1,0:T(8,128)(2,1)S(1)}, u32[]{:S(2)}, u32[]{:S(2)}) collective-permute-start(bf16[296,384]{1,0:T(8,128)(2,1)S(1)} %get-tuple-element.188), channel_id=1, source_target_pairs={{0,8},{4,12},{8,0},{12,4},{16,24},{20,28},{24,16},{28,20},{1,9},{5... | collective-permute-start | bytes 681992 | tf_op jit(solution)/shard_map/ppermute | solution.py:40
  125.3 10.9 %collective-permute-start.48 = (bf16[296,384]{1,0:T(8,128)(2,1)S(1)}, bf16[296,384]{1,0:T(8,128)(2,1)S(1)}, u32[]{:S(2)}, u32[]{:S(2)}) collective-permute-start(bf16[296,384]{1,0:T(8,128)(2,1)S(1)} %get-tuple-element.189), channel_id=1, source_target_pairs={{0,16},{4,20},{8,24},{12,28},{16,0},{20,4},{24,8},{28,12},{1,17},{... | collective-permute-start | bytes 681992 | tf_op jit(solution)/shard_map/ppermute | solution.py:40
  131.4 8.9 %collective-permute-start.46 = (bf16[296,384]{1,0:T(8,128)(2,1)S(1)}, bf16[296,384]{1,0:T(8,128)(2,1)S(1)}, u32[]{:S(2)}, u32[]{:S(2)}) collective-permute-start(bf16[296,384]{1,0:T(8,128)(2,1)S(1)} %add_convert_fusion.3), channel_id=1, source_target_pairs={{0,16},{4,20},{8,24},{12,28},{16,0},{20,4},{24,8},{28,12},{1,17},{... | collective-permute-start | bytes 681992 | tf_op jit(solution)/shard_map/ppermute | solution.py:40
  132.7 7.8 %collective-permute-start.49 = (bf16[296,384]{1,0:T(8,128)(2,1)S(1)}, bf16[296,384]{1,0:T(8,128)(2,1)S(1)}, u32[]{:S(2)}, u32[]{:S(2)}) collective-permute-start(bf16[296,384]{1,0:T(8,128)(2,1)S(1)} %add_convert_fusion.2.refs_6_), channel_id=1, source_target_pairs={{0,8},{4,12},{8,0},{12,4},{16,24},{20,28},{24,16},{28,20},{1,9},{5... | collective-permute-start | bytes 681992 | tf_op jit(solution)/shard_map/ppermute | solution.py:40
  142.1 10.6 %collective-permute-start.51 = (bf16[160,384]{1,0:T(8,128)(2,1)S(1)}, bf16[160,384]{1,0:T(8,128)(2,1)S(1)}, u32[]{:S(2)}, u32[]{:S(2)}) collective-permute-start(bf16[160,384]{1,0:T(8,128)(2,1)S(1)} %pad_maximum_fusion.5), channel_id=1, source_target_pairs={{0,1},{1,0},{2,3},{3,2},{4,5},{5,4},{6,7},{7,6},{8,9},{9,8},{10,11... | collective-permute-start | bytes 368648 | tf_op jit(solution)/shard_map/ppermute | solution.py:40
  143.2 9.4 %collective-permute-start.53 = (bf16[160,384]{1,0:T(8,128)(2,1)S(1)}, bf16[160,384]{1,0:T(8,128)(2,1)S(1)}, u32[]{:S(2)}, u32[]{:S(2)}) collective-permute-start(bf16[160,384]{1,0:T(8,128)(2,1)S(1)} %pad_maximum_fusion.8), channel_id=1, source_target_pairs={{0,3},{1,2},{2,1},{3,0},{4,7},{5,6},{6,5},{7,4},{8,11},{9,10},{10,... | collective-permute-start | bytes 368648 | tf_op jit(solution)/shard_map/ppermute | solution.py:40
  145.6 11.0 %collective-permute-start.52 = (bf16[160,384]{1,0:T(8,128)(2,1)S(1)}, bf16[160,384]{1,0:T(8,128)(2,1)S(1)}, u32[]{:S(2)}, u32[]{:S(2)}) collective-permute-start(bf16[160,384]{1,0:T(8,128)(2,1)S(1)} %pad_maximum_fusion.7), channel_id=1, source_target_pairs={{0,2},{1,3},{2,0},{3,1},{4,6},{5,7},{6,4},{7,5},{8,10},{9,11},{10,... | collective-permute-start | bytes 368648 | tf_op jit(solution)/shard_map/ppermute | solution.py:40
  157.0 5.3 %collective-permute-start.54 = (bf16[13,13,8,384]{3,2,1,0:T(8,128)(2,1)S(1)}, bf16[13,13,8,384]{3,2,1,0:T(8,128)(2,1)S(1)}, u32[]{:S(2)}, u32[]{:S(2)}) collective-permute-start(bf16[13,13,8,384]{3,2,1,0:T(8,128)(2,1)S(1)} %get-tuple-element.238), channel_id=1, source_target_pairs={{0,4},{4,0},{8,12},{12,8},{16,20},{20,16},{24,28},{28,24},{1,5},{5... | collective-permute-start | bytes 3115016 | tf_op jit(solution)/shard_map/ppermute | solution.py:40
  157.2 8.3 %collective-permute-start.55 = (bf16[160,384]{1,0:T(8,128)(2,1)S(1)}, bf16[160,384]{1,0:T(8,128)(2,1)S(1)}, u32[]{:S(2)}, u32[]{:S(2)}) collective-permute-start(bf16[160,384]{1,0:T(8,128)(2,1)S(1)} %add_convert_fusion.6.refs_0_), channel_id=1, source_target_pairs={{0,1},{1,0},{2,3},{3,2},{4,5},{5,4},{6,7},{7,6},{8,9},{9,8},{10,11... | collective-permute-start | bytes 368648 | tf_op jit(solution)/shard_map/ppermute | solution.py:40
  157.3 12.4 %collective-permute-start.56 = (bf16[160,384]{1,0:T(8,128)(2,1)S(1)}, bf16[160,384]{1,0:T(8,128)(2,1)S(1)}, u32[]{:S(2)}, u32[]{:S(2)}) collective-permute-start(bf16[160,384]{1,0:T(8,128)(2,1)S(1)} %add_convert_fusion.6.refs_0_), channel_id=1, source_target_pairs={{0,2},{1,3},{2,0},{3,1},{4,6},{5,7},{6,4},{7,5},{8,10},{9,11},{10,... | collective-permute-start | bytes 368648 | tf_op jit(solution)/shard_map/ppermute | solution.py:40
  159.9 9.8 %collective-permute-start.57 = (bf16[160,384]{1,0:T(8,128)(2,1)S(1)}, bf16[160,384]{1,0:T(8,128)(2,1)S(1)}, u32[]{:S(2)}, u32[]{:S(2)}) collective-permute-start(bf16[160,384]{1,0:T(8,128)(2,1)S(1)} %add_convert_fusion.6.refs_0_), channel_id=1, source_target_pairs={{0,3},{1,2},{2,1},{3,0},{4,7},{5,6},{6,5},{7,4},{8,11},{9,10},{10,... | collective-permute-start | bytes 368648 | tf_op jit(solution)/shard_map/ppermute | solution.py:40
  (32 other events, 541.2 us)
